TPU v7x, 32 devices: a whole 2x2x4 slice. The times are simulated.
32 devices in a mesh: blk: 8 (over z, core), head: 4 (over y, x).
Axes of the slice: x: 2, y: 2, z: 4, core: 2. Of those that a mesh axis runs over, the one named last changes fastest.
Arguments:
- hidden_in: bfloat16 [4096, 2304], P(('blk', 'head')), may hold values from -6 to 6
- out_grad: bfloat16 [4096, 2304], P(('blk', 'head')), may hold values from -6 to 6
- span_order: int32 [16], replicated, may hold values from 0 to 15, as said below
- w_query: bfloat16 [2304, 2048], P('blk', 'head'), may hold values from -0.5 to 0.5
- w_key: bfloat16 [2304, 1024], P('blk'), may hold values from -0.125 to 0.125
- w_value: bfloat16 [2304, 1024], P('blk'), may hold values from -0.125 to 0.125
- w_output: bfloat16 [2048, 2304], P('head', 'blk'), may hold values from -0.125 to 0.125
- w_gate: bfloat16 [2304, 9216], P('blk', 'head'), may hold values from -0.125 to 0.125
- w_up: bfloat16 [2304, 9216], P('blk', 'head'), may hold values from -0.125 to 0.125
- w_down: bfloat16 [9216, 2304], P('head', 'blk'), may hold values from -0.0625 to 0.0625
- norm_scales: bfloat16 [4, 2304], P(None, 'blk'), may hold values from 0.5 to 1.5
Outputs:
- layer_out: bfloat16 [4096, 2304], P(('blk', 'head'))
- grad_in: float32 [4096, 2304], P(('blk', 'head'))
- grad_query: float32 [2304, 2048], P('blk', 'head')
- grad_key: float32 [2304, 1024], P('blk')
- grad_value: float32 [2304, 1024], P('blk')
- grad_output: float32 [2048, 2304], P('head', 'blk')
- grad_gate: float32 [2304, 9216], P('blk', 'head')
- grad_up: float32 [2304, 9216], P('blk', 'head')
- grad_down: float32 [9216, 2304], P('head', 'blk')
- grad_scales: float32 [4, 2304], P(None, 'blk')
Inputs may be any that keep to these rules, and one draw needn't show every extreme that they name: span_order is a permutation of 0 to 15 in which entries 2 i and 2 i + 1 sum to 15.
All inputs are finite; a program needn't handle non-finite values.
Results may differ from a plain program's by a relative error of at most 0.03.
The roundings to bfloat16 on the way count: a program that leaves them out, or rounds other values in their place, can miss the bound.
Values may be sent and summed in bfloat16 or wider, within the bound.
No kernel may reach another device: no remote copies, remote signals or barrier semaphores. Data moves between devices by JAX's collectives and lax.ppermute only.
A program may use at most 256 MiB of HBM per device.

v0:
```python
import math

import jax
import jax.numpy as jnp
from jax import lax
from jax.sharding import PartitionSpec as P

H = 8
KVH = 4
HD = 256


norm_eps = 1e-06
cap_value = 50.0
theta_base = 10000.0
masked_value = -1e30


def rms_scale(value, scale):
    inverse = lax.rsqrt(jnp.mean(value * value, axis=-1, keepdims=True) + norm_eps)
    return value * inverse * scale


def rms_back(value, scale, grad):
    inverse = lax.rsqrt(jnp.mean(value * value, axis=-1, keepdims=True) + norm_eps)
    scaled = grad * scale
    inner = jnp.mean(scaled * value, axis=-1, keepdims=True)
    grad_value = inverse * scaled - value * (inverse * inverse * inverse) * inner
    grad_scale = jnp.sum(grad * value * inverse, axis=0)
    return (grad_value, grad_scale)


def rotate(value, position, sign, head_dim):
    row_count, total_width = value.shape
    quarter = head_dim // 4
    groups = total_width // (2 * quarter)
    shaped = value.reshape(row_count, groups, 2, quarter)
    halves = jnp.arange(groups, dtype=jnp.int32) % 2
    pair_index = halves[:, None] * quarter + jnp.arange(quarter, dtype=jnp.int32)[None, :]
    frequency = jnp.power(theta_base, -2.0 * pair_index.astype(jnp.float32) / head_dim)
    angles = position.astype(jnp.float32)[:, None, None] * frequency[None, :, :]
    cosine = jnp.cos(angles)
    sine_part = jnp.sin(angles)
    first_part = shaped[:, :, 0]
    second_part = shaped[:, :, 1]
    new_first = first_part * cosine - sign * second_part * sine_part
    new_second = sign * first_part * sine_part + second_part * cosine
    return jnp.stack([new_first, new_second], axis=2).reshape(row_count, total_width)


def positions(span_table, first_row, row_total, span_len):
    row_index = first_row + jnp.arange(row_total, dtype=jnp.int32)
    slot_index = row_index // span_len
    slot_table = jnp.arange(span_table.shape[0], dtype=jnp.int32)
    picked = jnp.sum(
        jnp.where(slot_index[:, None] == slot_table[None, :], span_table[None, :], 0), axis=1
    )
    return picked * span_len + row_index % span_len


def tiled(arrays, first_row, span_len, span_table):
    piece_len = arrays[0].shape[0]
    tile_count = piece_len // span_len
    shaped = tuple(
        (array_item.reshape((tile_count, span_len) + array_item.shape[1:]) for array_item in arrays)
    )
    tile_pos = positions(span_table, first_row, piece_len, span_len).reshape(tile_count, span_len)
    return (shaped, tile_pos)


def gelu_tanh(value):
    return jax.nn.gelu(value, approximate=True)


def tile_forward(attn_state, query_tile, query_pos, key_tile, value_tile, key_pos):
    row_top, row_total, accum = attn_state
    score_scale = 1.0 / math.sqrt(query_tile.shape[-1])
    raw_score = jnp.einsum(
        "qkgd,mkd->qkgm", query_tile, key_tile, preferred_element_type=jnp.float32
    )
    capped = cap_value * jnp.tanh(raw_score * (score_scale / cap_value))
    visible = (key_pos[None, :] <= query_pos[:, None])[:, None, None, :]
    masked = jnp.where(visible, capped, masked_value)
    new_top = jnp.maximum(row_top, jnp.max(masked, axis=-1))
    weights = jnp.where(visible, jnp.exp(masked - new_top[..., None]), 0.0)
    factor = jnp.exp(row_top - new_top)
    row_total = row_total * factor + jnp.sum(weights, axis=-1)
    accum = accum * factor[..., None] + jnp.einsum(
        "qkgm,mkd->qkgd",
        weights.astype(jnp.bfloat16),
        value_tile,
        preferred_element_type=jnp.float32,
    )
    return (new_top, row_total, accum)


def tile_backward(
    query_tile, grad_tile, lse_tile, delta_tile, query_pos, key_tile, value_tile, key_pos
):
    score_scale = 1.0 / math.sqrt(query_tile.shape[-1])
    raw_score = jnp.einsum(
        "qkgd,mkd->qkgm", query_tile, key_tile, preferred_element_type=jnp.float32
    )
    tangent = jnp.tanh(raw_score * (score_scale / cap_value))
    visible = (key_pos[None, :] <= query_pos[:, None])[:, None, None, :]
    probability = jnp.where(visible, jnp.exp(cap_value * tangent - lse_tile[..., None]), 0.0)
    grad_prob = jnp.einsum(
        "qkgd,mkd->qkgm", grad_tile, value_tile, preferred_element_type=jnp.float32
    )
    grad_capped = probability * (grad_prob - delta_tile[..., None])
    grad_raw = (grad_capped * (1.0 - tangent * tangent) * score_scale).astype(jnp.bfloat16)
    grad_query = jnp.einsum(
        "qkgm,mkd->qkgd", grad_raw, key_tile, preferred_element_type=jnp.float32
    )
    grad_key = jnp.einsum(
        "qkgm,qkgd->mkgd", grad_raw, query_tile, preferred_element_type=jnp.float32
    )
    grad_value = jnp.einsum(
        "qkgm,qkgd->mkgd",
        probability.astype(jnp.bfloat16),
        grad_tile,
        preferred_element_type=jnp.float32,
    )
    return (grad_query, grad_key, grad_value)


def head_rows(value):
    return lax.all_gather(value, "head", axis=0, tiled=True)


def head_sum(pairs):
    result = None
    for left, right in pairs:
        product = jnp.dot(left, right, preferred_element_type=jnp.float32)
        result = product if result is None else result + product
    return lax.psum_scatter(
        result.astype(jnp.bfloat16), "head", scatter_dimension=0, tiled=True
    ).astype(jnp.float32)


def on_device(
    hidden_in,
    out_grad,
    span_order,
    w_query,
    w_key,
    w_value,
    w_output,
    w_gate,
    w_up,
    w_down,
    norm_scales,
):
    local_rows = hidden_in.shape[0]
    head_count = lax.axis_size("head")
    block_count = lax.axis_size("blk")
    group_rows = local_rows * head_count
    span_len = group_rows // 2
    block_index = lax.axis_index("blk")
    head_index = lax.axis_index("head")
    query_full, key_full, value_full, output_full, scales_full = (
        lax.all_gather(w_query, "blk", axis=0, tiled=True),
        lax.all_gather(w_key, "blk", axis=0, tiled=True),
        lax.all_gather(w_value, "blk", axis=0, tiled=True),
        lax.all_gather(w_output, "blk", axis=1, tiled=True),
        lax.all_gather(norm_scales, "blk", axis=1, tiled=True),
    )
    head_dim = HD
    model_width = key_full.shape[0]
    query_width = query_full.shape[1]
    query_heads = query_width // head_dim
    kv_heads = max(1, KVH // head_count)
    group_size = query_heads // kv_heads
    kv_first = head_index * query_heads // (H // KVH)
    key_cols = lax.dynamic_slice_in_dim(key_full, kv_first * head_dim, kv_heads * head_dim, 1)
    value_cols = lax.dynamic_slice_in_dim(value_full, kv_first * head_dim, kv_heads * head_dim, 1)
    scale_rows = scales_full.astype(jnp.float32)
    residual_in = hidden_in.astype(jnp.float32)
    query_pos = positions(span_order, block_index * group_rows, group_rows, span_len)
    normed = rms_scale(residual_in, scale_rows[0]).astype(jnp.bfloat16)
    normed_full = head_rows(normed)
    query_lin = jnp.dot(normed_full, query_full, preferred_element_type=jnp.float32)
    queries = (
        rotate(query_lin, query_pos, 1.0, head_dim)
        .astype(jnp.bfloat16)
        .reshape(group_rows, kv_heads, group_size, head_dim)
    )
    key_lin = jnp.dot(normed_full, key_cols, preferred_element_type=jnp.float32)
    value_lin = jnp.dot(normed_full, value_cols, preferred_element_type=jnp.float32)
    keys = (
        rotate(key_lin, query_pos, 1.0, head_dim)
        .astype(jnp.bfloat16)
        .reshape(group_rows, kv_heads, head_dim)
    )
    values = value_lin.astype(jnp.bfloat16).reshape(group_rows, kv_heads, head_dim)
    stat_shape = (span_len, kv_heads, group_size)
    state_init = (
        (
            jnp.full(stat_shape, masked_value, jnp.float32),
            jnp.zeros(stat_shape, jnp.float32),
            jnp.zeros(stat_shape + (head_dim,), jnp.float32),
        ),
        (
            jnp.full(stat_shape, masked_value, jnp.float32),
            jnp.zeros(stat_shape, jnp.float32),
            jnp.zeros(stat_shape + (head_dim,), jnp.float32),
        ),
    )
    tiles, tile_positions = tiled(
        (
            lax.all_gather(keys, "blk", axis=0, tiled=True),
            lax.all_gather(values, "blk", axis=0, tiled=True),
        ),
        jnp.int32(0),
        span_len,
        span_order,
    )

    def forward_advance(tile_carry, tile_item):
        tile_keys, tile_values, tile_pos = tile_item
        updated = []
        for half_index in range(2):
            lower_row = half_index * span_len
            half_query = queries[lower_row : lower_row + span_len]
            half_pos = query_pos[lower_row : lower_row + span_len]
            visible = jnp.min(tile_pos) <= jnp.max(half_pos)
            updated.append(
                lax.cond(
                    visible,
                    lambda attn_state: tile_forward(
                        attn_state, half_query, half_pos, tile_keys, tile_values, tile_pos
                    ),
                    lambda attn_state: attn_state,
                    tile_carry[half_index],
                )
            )
        return (tuple(updated), None)

    result, unused = lax.scan(forward_advance, state_init, tiles + (tile_positions,))
    row_top = jnp.concatenate([result[0][0], result[1][0]], 0)
    row_total = jnp.concatenate([result[0][1], result[1][1]], 0)
    accum = jnp.concatenate([result[0][2], result[1][2]], 0)
    out_exact = accum / row_total[..., None]
    log_total = row_top + jnp.log(row_total)
    mixed_flat = out_exact.astype(jnp.bfloat16).reshape(group_rows, query_width)
    attn_out = head_sum([(mixed_flat, output_full)])
    resid = residual_in + rms_scale(attn_out, scale_rows[1])
    ffn_in = rms_scale(resid, scale_rows[2]).astype(jnp.bfloat16)
    ffn_full = head_rows(ffn_in)
    gate_full, up_full, down_full = (
        lax.all_gather(w_gate, "blk", axis=0, tiled=True),
        lax.all_gather(w_up, "blk", axis=0, tiled=True),
        lax.all_gather(w_down, "blk", axis=1, tiled=True),
    )
    gate = jnp.dot(ffn_full, gate_full, preferred_element_type=jnp.float32)
    up_value = jnp.dot(ffn_full, up_full, preferred_element_type=jnp.float32)
    activated, gelu_back = jax.vjp(gelu_tanh, gate)
    hidden = (activated * up_value).astype(jnp.bfloat16)
    ffn_out = head_sum([(hidden, down_full)])
    layer_out = (resid + rms_scale(ffn_out, scale_rows[3])).astype(jnp.bfloat16)
    grad_top = out_grad.astype(jnp.float32)
    grad_ffn_out, scale_grad3 = rms_back(ffn_out, scale_rows[3], grad_top)
    grad_ffn_full = head_rows(grad_ffn_out.astype(jnp.bfloat16))
    grad_hidden = jnp.dot(grad_ffn_full, down_full.T, preferred_element_type=jnp.float32)
    grad_down = jnp.dot(hidden.T, grad_ffn_full, preferred_element_type=jnp.float32)
    gelu_grad = gelu_back(grad_hidden * up_value)[0]
    grad_gate_act = gelu_grad.astype(jnp.bfloat16)
    grad_up_act = (grad_hidden * activated).astype(jnp.bfloat16)
    grad_wgate = jnp.dot(ffn_full.T, grad_gate_act, preferred_element_type=jnp.float32)
    grad_wup = jnp.dot(ffn_full.T, grad_up_act, preferred_element_type=jnp.float32)
    grad_ffn_in = head_sum([(grad_gate_act, gate_full.T), (grad_up_act, up_full.T)])
    grad_resid_part, scale_grad2 = rms_back(resid, scale_rows[2], grad_ffn_in)
    grad_resid = grad_top + grad_resid_part
    grad_attn, scale_grad1 = rms_back(attn_out, scale_rows[1], grad_resid)
    grad_attn_full = head_rows(grad_attn.astype(jnp.bfloat16))
    grad_woutput = jnp.dot(mixed_flat.T, grad_attn_full, preferred_element_type=jnp.float32)
    grad_mixed = (
        jnp.dot(grad_attn_full, output_full.T, preferred_element_type=jnp.float32)
        .astype(jnp.bfloat16)
        .reshape(group_rows, kv_heads, group_size, head_dim)
    )
    delta_rows = jnp.sum(grad_mixed.astype(jnp.float32) * out_exact, axis=-1)
    query_init = (
        jnp.zeros(stat_shape + (head_dim,), jnp.float32),
        jnp.zeros(stat_shape + (head_dim,), jnp.float32),
    )

    def query_side(grads, tile_keys, tile_values, tile_pos):
        copy_shape = tile_keys.shape[:2] + (group_size, head_dim)
        key_sum = jnp.zeros(copy_shape, jnp.float32)
        value_sum = jnp.zeros(copy_shape, jnp.float32)
        updated = []
        for half_index in range(2):
            lower_row = half_index * span_len
            half_query = queries[lower_row : lower_row + span_len]
            half_grad = grad_mixed[lower_row : lower_row + span_len]
            half_lse = log_total[lower_row : lower_row + span_len]
            half_delta = delta_rows[lower_row : lower_row + span_len]
            half_pos = query_pos[lower_row : lower_row + span_len]
            visible = jnp.min(tile_pos) <= jnp.max(half_pos)

            def compute(previous):
                part_query, part_key, part_value = tile_backward(
                    half_query,
                    half_grad,
                    half_lse,
                    half_delta,
                    half_pos,
                    tile_keys,
                    tile_values,
                    tile_pos,
                )
                return (previous + part_query, part_key, part_value)

            def bypass(previous):
                return (
                    previous,
                    jnp.zeros(copy_shape, jnp.float32),
                    jnp.zeros(copy_shape, jnp.float32),
                )

            new_grad, key_grad, value_grad = lax.cond(visible, compute, bypass, grads[half_index])
            updated.append(new_grad)
            key_sum = key_sum + key_grad
            value_sum = value_sum + value_grad
        return (tuple(updated), key_sum, value_sum)

    all_shape = (block_count * group_rows, kv_heads, group_size, head_dim)
    piece_pair = (
        lax.all_gather(keys, "blk", axis=0, tiled=True),
        lax.all_gather(values, "blk", axis=0, tiled=True),
    )
    tiles, tile_positions = tiled(piece_pair, jnp.int32(0), span_len, span_order)

    def collect_advance(grads, tile_item):
        updated, key_sum, value_sum = query_side(grads, tile_item[0], tile_item[1], tile_item[2])
        return (updated, (key_sum, value_sum))

    grads, tile_grads = lax.scan(
        collect_advance,
        (query_init, jnp.zeros(all_shape, jnp.float32), jnp.zeros(all_shape, jnp.float32))[0],
        tiles + (tile_positions,),
    )
    piece_len = piece_pair[0].shape[0]
    key_piece = tile_grads[0].reshape(piece_len, kv_heads, group_size, head_dim)
    value_piece = tile_grads[1].reshape(piece_len, kv_heads, group_size, head_dim)
    key_all = key_piece
    value_all = value_piece
    query_grads, key_all, value_all = (grads, key_all, value_all)
    key_grad_rows, value_grad_rows = (
        lax.psum_scatter(
            key_all.astype(jnp.bfloat16), "blk", scatter_dimension=0, tiled=True
        ).astype(jnp.float32),
        lax.psum_scatter(
            value_all.astype(jnp.bfloat16), "blk", scatter_dimension=0, tiled=True
        ).astype(jnp.float32),
    )
    query_grad = jnp.concatenate([query_grads[0], query_grads[1]], 0).reshape(
        group_rows, query_width
    )
    grad_key_lin = rotate(
        key_grad_rows.reshape(group_rows, query_width), query_pos, -1.0, head_dim
    ).astype(jnp.bfloat16)
    grad_value_lin = value_grad_rows.reshape(group_rows, query_width).astype(jnp.bfloat16)
    grad_query_lin = rotate(query_grad, query_pos, -1.0, head_dim).astype(jnp.bfloat16)
    grad_wquery = jnp.dot(normed_full.T, grad_query_lin, preferred_element_type=jnp.float32)
    grad_wkey = jnp.sum(
        jnp.dot(normed_full.T, grad_key_lin, preferred_element_type=jnp.float32).reshape(
            model_width, kv_heads, group_size, head_dim
        ),
        axis=2,
    ).reshape(model_width, kv_heads * head_dim)
    grad_wvalue = jnp.sum(
        jnp.dot(normed_full.T, grad_value_lin, preferred_element_type=jnp.float32).reshape(
            model_width, kv_heads, group_size, head_dim
        ),
        axis=2,
    ).reshape(model_width, kv_heads * head_dim)

    def spread(columns):
        shaped = columns.reshape(model_width, kv_heads, 1, head_dim)
        return jnp.broadcast_to(shaped, (model_width, kv_heads, group_size, head_dim)).reshape(
            model_width, query_width
        )

    grad_normed = head_sum(
        [
            (grad_query_lin, query_full.T),
            (grad_key_lin, spread(key_cols).T),
            (grad_value_lin, spread(value_cols).T),
        ]
    )
    grad_in_part, scale_grad0 = rms_back(residual_in, scale_rows[0], grad_normed)
    grad_in = grad_resid + grad_in_part
    scale_grad = jnp.stack([scale_grad0, scale_grad1, scale_grad2, scale_grad3])
    summed = (
        lax.psum_scatter(
            grad_wquery.astype(jnp.bfloat16), "blk", scatter_dimension=0, tiled=True
        ).astype(jnp.float32),
        lax.psum_scatter(
            grad_wkey.astype(jnp.bfloat16), "blk", scatter_dimension=0, tiled=True
        ).astype(jnp.float32),
        lax.psum_scatter(
            grad_wvalue.astype(jnp.bfloat16), "blk", scatter_dimension=0, tiled=True
        ).astype(jnp.float32),
        lax.psum_scatter(
            grad_woutput.astype(jnp.bfloat16), "blk", scatter_dimension=1, tiled=True
        ).astype(jnp.float32),
        lax.psum_scatter(
            grad_wgate.astype(jnp.bfloat16), "blk", scatter_dimension=0, tiled=True
        ).astype(jnp.float32),
        lax.psum_scatter(
            grad_wup.astype(jnp.bfloat16), "blk", scatter_dimension=0, tiled=True
        ).astype(jnp.float32),
        lax.psum_scatter(
            grad_down.astype(jnp.bfloat16), "blk", scatter_dimension=1, tiled=True
        ).astype(jnp.float32),
        lax.psum_scatter(
            scale_grad.astype(jnp.bfloat16), "blk", scatter_dimension=1, tiled=True
        ).astype(jnp.float32),
    )
    shard_rows = summed[1].shape[0]
    key_place = lax.dynamic_update_slice_in_dim(
        jnp.zeros((shard_rows, key_full.shape[1]), jnp.float32), summed[1], kv_first * head_dim, 1
    )
    value_place = lax.dynamic_update_slice_in_dim(
        jnp.zeros((shard_rows, value_full.shape[1]), jnp.float32), summed[2], kv_first * head_dim, 1
    )
    key_total, value_total, scale_total = (
        lax.psum(key_place.astype(jnp.bfloat16), "head").astype(jnp.float32),
        lax.psum(value_place.astype(jnp.bfloat16), "head").astype(jnp.float32),
        lax.psum(summed[7].astype(jnp.bfloat16), "head").astype(jnp.float32),
    )
    return (
        layer_out,
        grad_in,
        summed[0],
        key_total,
        value_total,
        summed[3],
        summed[4],
        summed[5],
        summed[6],
        scale_total,
    )


def solution(mesh):
    placed = (
        P(("blk", "head"), None),
        P(("blk", "head"), None),
        P(),
        P("blk", "head"),
        P("blk", None),
        P("blk", None),
        P("head", "blk"),
        P("blk", "head"),
        P("blk", "head"),
        P("head", "blk"),
        P(None, "blk"),
    )
    return jax.shard_map(
        on_device,
        mesh=mesh,
        in_specs=placed,
        out_specs=(
            P(("blk", "head"), None),
            P(("blk", "head"), None),
            P("blk", "head"),
            P("blk", None),
            P("blk", None),
            P("head", "blk"),
            P("blk", "head"),
            P("blk", "head"),
            P("head", "blk"),
            P(None, "blk"),
        ),
        check_vma=False,
    )
```

profile of v0, /device:TPU:0, one launch (start us, length us, event | category | flops | bytes accessed | tf_op | source)
XLA Modules:
  0.0 1846.7 jit_solution(17567172505339224051)
XLA Ops:
  8.0 15.7 all-gather.1
  29.5 34.7 %all-gather.18.cloned.1.call-done = bf16[2304,1024]{1,0:T(8,128)(2,1)} async-done(((bf16[288,1024]{1,0:T(8,128)(2,1)}), bf16[2304,1024]{1,0:T(8,128)(2,1)}) %all-gather.18.cloned.1.call-update) | async-done | bytes 4718608 | tf_op jit(solution)/shard_map/all_gather | solution.py:163
  65.5 37.4 %all-gather.16.cloned.1.call-done = bf16[512,2304]{1,0:T(8,128)(2,1)} async-done(((bf16[128,2304]{1,0:T(8,128)(2,1)}), bf16[512,2304]{1,0:T(8,128)(2,1)}) %all-gather.16.cloned.1.call-update) | async-done | bytes 2359312 | tf_op jit(solution)/shard_map/all_gather | solution.py:128
  107.5 48.8 %all-gather.22.cloned.1.call-done = bf16[2304,1024]{1,0:T(8,128)(2,1)} async-done(((bf16[288,1024]{1,0:T(8,128)(2,1)}), bf16[2304,1024]{1,0:T(8,128)(2,1)}) %all-gather.22.cloned.1.call-update) | async-done | bytes 4718608 | tf_op jit(solution)/shard_map/all_gather | solution.py:164
  163.7 24.5 %all-gather.24.cloned.1.call-done = bf16[2304,512]{1,0:T(8,128)(2,1)} async-done(((bf16[288,512]{1,0:T(8,128)(2,1)}), bf16[2304,512]{1,0:T(8,128)(2,1)}) %all-gather.24.cloned.1.call-update) | async-done | bytes 2359312 | tf_op jit(solution)/shard_map/all_gather | solution.py:162
  193.9 24.6 %all-gather.20.cloned.1.call-done = bf16[4096,1,256]{2,0,1:T(8,128)(2,1)} async-done(((bf16[512,1,256]{2,0,1:T(8,128)(2,1)}), bf16[4096,1,256]{2,0,1:T(8,128)(2,1)}) %all-gather.20.cloned.1.call-update) | async-done | bytes 2097168 | tf_op jit(solution)/shard_map/all_gather | solution.py:211
  218.5 30.7 %all-gather.40.cloned.1.call-done = bf16[4096,256]{1,0:T(8,128)(2,1)} async-done(((bf16[512,256]{1,0:T(8,128)(2,1)}), bf16[4096,256]{1,0:T(8,128)(2,1)}) %all-gather.40.cloned.1.call-update) | async-done | bytes 2097168 | tf_op jit(solution)/shard_map/all_gather | solution.py:212
  249.2 87.5 %while.44 = (s32[]{:T(128)}, f32[256,1,2]{0,2,1:T(2,128)S(1)}, f32[256,1,2]{0,2,1:T(2,128)S(1)}, f32[256,1,2,256]{3,0,2,1:T(8,128)S(1)}, f32[256,1,2]{0,2,1:T(2,...) while((s32[]{:T(128)}, f32[256,1,2]{0,2,1:T(2,128)S(1)}, ...), condition=%wide.region_15.16_spmd, body=%wide.region_5.15_spmd.sunk | while | flops 271715584 | bytes 7416229 | solution.py:239
  342.9 36.3 %reduce-scatter.17.cloned.1.call-done = bf16[128,2304]{1,0:T(8,128)(2,1)} async-done(((bf16[512,2304]{1,0:T(8,128)(2,1)}), bf16[128,2304]{1,0:T(8,128)(2,1)}) %reduce-scatter.17.cloned.1.call-update) | async-done | bytes 589840 | tf_op jit(solution)/shard_map/reduce_scatter | solution.py:136
  385.8 95.5 %all-gather.30.cloned.1.call-done = bf16[2304,2304]{1,0:T(8,128)(2,1)} async-done(((bf16[288,2304]{1,0:T(8,128)(2,1)}), bf16[2304,2304]{1,0:T(8,128)(2,1)}) %all-gather.30.cloned.1.call-update) | async-done | bytes 10616848 | tf_op jit(solution)/shard_map/all_gather | solution.py:251
  481.3 38.1 %all-gather.28.cloned.1.call-done = bf16[512,2304]{1,0:T(8,128)(2,1)} async-done(((bf16[128,2304]{1,0:T(8,128)(2,1)}), bf16[512,2304]{1,0:T(8,128)(2,1)}) %all-gather.28.cloned.1.call-update) | async-done | bytes 2359312 | tf_op jit(solution)/shard_map/all_gather | solution.py:128
  519.4 11.6 fusion.206
  531.1 90.5 %all-gather.32.cloned.1.call-done = bf16[2304,2304]{1,0:T(8,128)(2,1)} async-done(((bf16[288,2304]{1,0:T(8,128)(2,1)}), bf16[2304,2304]{1,0:T(8,128)(2,1)}) %all-gather.32.cloned.1.call-update) | async-done | bytes 10616848 | tf_op jit(solution)/shard_map/all_gather | solution.py:252
  621.6 12.8 multiply_convert_fusion.1
  634.4 87.5 %all-gather.34.cloned.1.call-done = bf16[2304,2304]{0,1:T(8,128)(2,1)} async-done(((bf16[2304,288]{0,1:T(8,128)(2,1)}), bf16[2304,2304]{0,1:T(8,128)(2,1)}) %all-gather.34.cloned.1.call-update) | async-done | bytes 10616848 | tf_op jit(solution)/shard_map/all_gather | solution.py:253
  733.4 35.9 %reduce-scatter.19.cloned.1.call-done = bf16[128,2304]{1,0:T(8,128)(2,1)} async-done(((bf16[512,2304]{1,0:T(8,128)(2,1)}), bf16[128,2304]{1,0:T(8,128)(2,1)}) %reduce-scatter.19.cloned.1.call-update) | async-done | bytes 589840 | tf_op jit(solution)/shard_map/reduce_scatter | solution.py:136
  775.4 37.2 %all-gather.36.cloned.1.call-done = bf16[512,2304]{1,0:T(8,128)(2,1)} async-done(((bf16[128,2304]{1,0:T(8,128)(2,1)}), bf16[512,2304]{1,0:T(8,128)(2,1)}) %all-gather.36.cloned.1.call-update) | async-done | bytes 2359312 | tf_op jit(solution)/shard_map/all_gather | solution.py:128
  812.6 14.2 multiply_convert_fusion
  847.7 37.5 %reduce-scatter.21.cloned.1.call-done = bf16[128,2304]{1,0:T(8,128)(2,1)} async-done(((bf16[512,2304]{1,0:T(8,128)(2,1)}), bf16[128,2304]{1,0:T(8,128)(2,1)}) %reduce-scatter.21.cloned.1.call-update) | async-done | bytes 589840 | tf_op jit(solution)/shard_map/reduce_scatter | solution.py:136
  892.8 37.4 %all-gather.38.cloned.1.call-done = bf16[512,2304]{1,0:T(8,128)(2,1)} async-done(((bf16[128,2304]{1,0:T(8,128)(2,1)}), bf16[512,2304]{1,0:T(8,128)(2,1)}) %all-gather.38.cloned.1.call-update) | async-done | bytes 2359312 | tf_op jit(solution)/shard_map/all_gather | solution.py:128
  938.0 175.2 %while.45 = (s32[]{:T(128)}, f32[256,1,2,256]{3,0,2,1:T(8,128)}, f32[256,1,2,256]{3,0,2,1:T(8,128)}, bf16[16,256,1,2,256]{4,1,0,3,2:T(8,128)(2,1)}, bf16[16,256,...) while((s32[]{:T(128)}, f32[256,1,2,256]{3,0,2,1:T(8,128)}, ...), condition=%wide.region_32.33_spmd, body=%wide.region_26.32_spmd.sunk | while | flops 675676416 | bytes 20093880 | solution.py:339
  1113.9 56.0 %reduce-scatter.23.cloned.1.call-done = bf16[512,1,2,256]{3,0,2,1:T(8,128)(2,1)} async-done(((bf16[4096,1,2,256]{3,0,2,1:T(8,128)(2,1)}), bf16[512,1,2,256]{3,0,2,1:T(8,128)(2,1)}) %reduce-scatter.23.cloned.1.call-update) | async-done | bytes 524304 | tf_op jit(solution)/shard_map/reduce_scatter | solution.py:351
  1176.2 44.0 %reduce-scatter.25.cloned.1.call-done = bf16[512,1,2,256]{3,0,2,1:T(8,128)(2,1)} async-done(((bf16[4096,1,2,256]{3,0,2,1:T(8,128)(2,1)}), bf16[512,1,2,256]{3,0,2,1:T(8,128)(2,1)}) %reduce-scatter.25.cloned.1.call-update) | async-done | bytes 524304 | tf_op jit(solution)/shard_map/reduce_scatter | solution.py:354
  1239.3 14.3 reduce-scatter.31.cloned.1.call-done
  1254.6 32.3 %reduce-scatter.33.cloned.1.call-done = bf16[288,256]{1,0:T(8,128)(2,1)} async-done(((bf16[2304,256]{1,0:T(8,128)(2,1)}), bf16[288,256]{1,0:T(8,128)(2,1)}) %reduce-scatter.33.cloned.1.call-update) | async-done | bytes 147472 | tf_op jit(solution)/shard_map/reduce_scatter | solution.py:403
  1333.6 28.9 %reduce-scatter.35.cloned.1.call-done = bf16[512,288]{0,1:T(8,128)(2,1)} async-done(((bf16[512,2304]{0,1:T(8,128)(2,1)}), bf16[512,288]{0,1:T(8,128)(2,1)}) %reduce-scatter.35.cloned.1.call-update) | async-done | bytes 294928 | tf_op jit(solution)/shard_map/reduce_scatter | solution.py:406
  1364.4 55.2 %all-reduce.3.cloned.1.call-done = (bf16[288,1024]{1,0:T(8,128)(2,1)}, bf16[288,1024]{1,0:T(8,128)(2,1)}) async-done(((bf16[288,1024]{1,0:T(8,128)(2,1)}, bf16[288,1024]{1,0:T(8,128)(2,1)}), (bf16[288,1024]{1,0:T(8,128)(2,1)}, bf16[288,1024]{1,0:T(8,128)(2,1)})) %all-reduce.3.cloned.1.call-update) | async-done | bytes 1179664 | tf_op jit(solution)/shard_map/psum | solution.py:430
  1424.0 108.5 %reduce-scatter.41.cloned.1.call-done = bf16[2304,288]{0,1:T(8,128)(2,1)} async-done(((bf16[2304,2304]{0,1:T(8,128)(2,1)}), bf16[2304,288]{0,1:T(8,128)(2,1)}) %reduce-scatter.41.cloned.1.call-update) | async-done | bytes 1327120 | tf_op jit(solution)/shard_map/reduce_scatter | solution.py:415
  1535.6 108.4 %reduce-scatter.37.cloned.1.call-done = bf16[288,2304]{1,0:T(8,128)(2,1)} async-done(((bf16[2304,2304]{1,0:T(8,128)(2,1)}), bf16[288,2304]{1,0:T(8,128)(2,1)}) %reduce-scatter.37.cloned.1.call-update) | async-done | bytes 1327120 | tf_op jit(solution)/shard_map/reduce_scatter | solution.py:409
  1647.0 108.3 %reduce-scatter.39.cloned.1.call-done = bf16[288,2304]{1,0:T(8,128)(2,1)} async-done(((bf16[2304,2304]{1,0:T(8,128)(2,1)}), bf16[288,2304]{1,0:T(8,128)(2,1)}) %reduce-scatter.39.cloned.1.call-update) | async-done | bytes 1327120 | tf_op jit(solution)/shard_map/reduce_scatter | solution.py:412
  1758.2 35.7 %reduce-scatter.27.cloned.1.call-done = bf16[128,2304]{1,0:T(8,128)(2,1)} async-done(((bf16[512,2304]{1,0:T(8,128)(2,1)}), bf16[128,2304]{1,0:T(8,128)(2,1)}) %reduce-scatter.27.cloned.1.call-update) | async-done | bytes 589840 | tf_op jit(solution)/shard_map/reduce_scatter | solution.py:136
  1798.2 29.7 %reduce-scatter.43.cloned.1.call-done = bf16[288,4]{1,0:T(8,128)(2,1)} async-done(((bf16[2304,4]{1,0:T(8,128)(2,1)}), bf16[288,4]{1,0:T(8,128)(2,1)}) %reduce-scatter.43.cloned.1.call-update) | async-done | bytes 2320
  (730 shorter events, 474.9 us)
Async XLA Ops:
  7.2 56.9 %all-gather.18.cloned.1.call-start = ((), (), s32[]{:S(2)}) async-start(), calls=%async_computation.15 | async-start | bytes 5308416 | tf_op jit(solution)/shard_map/all_gather | solution.py:163
  7.9 94.9 %all-gather.16.cloned.1.call-start = ((), (), s32[]{:S(2)}) async-start(), calls=%async_computation.14 | async-start | bytes 2949120 | tf_op jit(solution)/shard_map/all_gather | solution.py:128
  27.8 128.4 %all-gather.22.cloned.1.call-start = ((), (), s32[]{:S(2)}) async-start(), calls=%async_computation.17 | async-start | bytes 5308416 | tf_op jit(solution)/shard_map/all_gather | solution.py:164
  28.6 159.6 %all-gather.24.cloned.1.call-start = ((), (), s32[]{:S(2)}) async-start(), calls=%async_computation.18 | async-start | bytes 2654208 | tf_op jit(solution)/shard_map/all_gather | solution.py:162
  29.1 189.3 %all-gather.20.cloned.1.call-start = ((), (), s32[]{:S(2)}) async-start(), calls=%async_computation.16 | async-start | bytes 2359296 | tf_op jit(solution)/shard_map/all_gather | solution.py:211
  29.4 161.8 %copy-start.24 = (f32[512]{0:T(512)}, f32[512]{0:T(512)S(1)}, u32[]{:S(2)}) copy-start(f32[512]{0:T(512)S(1)} %get-tuple-element.643) | copy-start | bytes 6148
  107.4 141.7 %all-gather.40.cloned.1.call-start = ((), (), s32[]{:S(2)}) async-start(), calls=%async_computation.39 | async-start | bytes 2359296 | tf_op jit(solution)/shard_map/all_gather | solution.py:212
  161.9 175.4 %all-gather.26.cloned.1.call-start = ((), (), s32[]{:S(2)}) async-start(), calls=%async_computation.19 | async-start | bytes 2654208 | tf_op jit(solution)/shard_map/all_gather | solution.py:165
  162.7 216.5 %reduce-scatter.17.cloned.1.call-start = ((), (), s32[]{:S(2)}) async-start(), calls=%async_computation.20 | async-start | bytes 2949120 | tf_op jit(solution)/shard_map/reduce_scatter | solution.py:136
  342.1 139.2 %all-gather.30.cloned.1.call-start = ((), (), s32[]{:S(2)}) async-start(), calls=%async_computation.22 | async-start | bytes 11943936 | tf_op jit(solution)/shard_map/all_gather | solution.py:251
  342.8 176.6 %all-gather.28.cloned.1.call-start = ((), (), s32[]{:S(2)}) async-start(), calls=%async_computation.21 | async-start | bytes 2949120 | tf_op jit(solution)/shard_map/all_gather | solution.py:128
  384.2 237.4 %all-gather.32.cloned.1.call-start = ((), (), s32[]{:S(2)}) async-start(), calls=%async_computation.23 | async-start | bytes 11943936 | tf_op jit(solution)/shard_map/all_gather | solution.py:252
  384.9 337.0 %all-gather.34.cloned.1.call-start = ((), (), s32[]{:S(2)}) async-start(), calls=%async_computation.24 | async-start | bytes 11943936 | tf_op jit(solution)/shard_map/all_gather | solution.py:253
  385.5 383.7 %reduce-scatter.19.cloned.1.call-start = ((), (), s32[]{:S(2)}) async-start(), calls=%async_computation.25 | async-start | bytes 2949120 | tf_op jit(solution)/shard_map/reduce_scatter | solution.py:136
  733.3 79.3 %all-gather.36.cloned.1.call-start = ((), (), s32[]{:S(2)}) async-start(), calls=%async_computation.26 | async-start | bytes 2949120 | tf_op jit(solution)/shard_map/all_gather | solution.py:128
  774.9 110.3 %reduce-scatter.21.cloned.1.call-start = ((), (), s32[]{:S(2)}) async-start(), calls=%async_computation.27 | async-start | bytes 2949120 | tf_op jit(solution)/shard_map/reduce_scatter | solution.py:136
  847.6 82.5 %all-gather.38.cloned.1.call-start = ((), (), s32[]{:S(2)}) async-start(), calls=%async_computation.28 | async-start | bytes 2949120 | tf_op jit(solution)/shard_map/all_gather | solution.py:128
  892.5 277.4 %reduce-scatter.23.cloned.1.call-start = ((), (), s32[]{:S(2)}) async-start(), calls=%async_computation.29 | async-start | bytes 4718592 | tf_op jit(solution)/shard_map/reduce_scatter | solution.py:351
  1113.2 107.0 %reduce-scatter.25.cloned.1.call-start = ((), (), s32[]{:S(2)}) async-start(), calls=%async_computation.30 | async-start | bytes 4718592 | tf_op jit(solution)/shard_map/reduce_scatter | solution.py:354
  1113.8 139.8 %reduce-scatter.31.cloned.1.call-start = ((), (), s32[]{:S(2)}) async-start(), calls=%async_computation.33 | async-start | bytes 1327104 | tf_op jit(solution)/shard_map/reduce_scatter | solution.py:400
  1176.1 110.7 %reduce-scatter.33.cloned.1.call-start = ((), (), s32[]{:S(2)}) async-start(), calls=%async_computation.34 | async-start | bytes 1327104 | tf_op jit(solution)/shard_map/reduce_scatter | solution.py:403
  1225.9 105.9 %reduce-scatter.29.cloned.1.call-start = ((), (), s32[]{:S(2)}) async-start(), calls=%async_computation.32 | async-start | bytes 2654208 | tf_op jit(solution)/shard_map/reduce_scatter | solution.py:397
  1233.7 128.9 %reduce-scatter.35.cloned.1.call-start = ((), (), s32[]{:S(2)}) async-start(), calls=%async_computation.35 | async-start | bytes 2654208 | tf_op jit(solution)/shard_map/reduce_scatter | solution.py:406
  1239.2 180.4 %all-reduce.3.cloned.1.call-start = ((), (), s32[]{:S(2)}) async-start(), calls=%async_computation.41 | async-start | bytes 2359296 | tf_op jit(solution)/shard_map/psum | solution.py:430
  1288.8 243.8 %reduce-scatter.41.cloned.1.call-start = ((), (), s32[]{:S(2)}) async-start(), calls=%async_computation.38 | async-start | bytes 11943936 | tf_op jit(solution)/shard_map/reduce_scatter | solution.py:415
  1299.2 344.7 %reduce-scatter.37.cloned.1.call-start = ((), (), s32[]{:S(2)}) async-start(), calls=%async_computation.36 | async-start | bytes 11943936 | tf_op jit(solution)/shard_map/reduce_scatter | solution.py:409
  1310.8 444.4 %reduce-scatter.39.cloned.1.call-start = ((), (), s32[]{:S(2)}) async-start(), calls=%async_computation.37 | async-start | bytes 11943936 | tf_op jit(solution)/shard_map/reduce_scatter | solution.py:412
  1321.0 472.9 %reduce-scatter.27.cloned.1.call-start = ((), (), s32[]{:S(2)}) async-start(), calls=%async_computation.31 | async-start | bytes 2949120 | tf_op jit(solution)/shard_map/reduce_scatter | solution.py:136
  1331.0 496.9 %reduce-scatter.43.cloned.1.call-start = ((), (), s32[]{:S(2)}) async-start(), calls=%async_computation.40 | async-start | bytes 663552
  1646.9 147.0 %copy-start.30 = (f32[128]{0:T(128)S(1)}, f32[128]{0:T(128)}, u32[]{:S(2)}) copy-start(f32[128]{0:T(128)} %copy-done.29) | copy-start | bytes 1540
  1646.9 149.7 %copy-start.6 = (f32[128,2304]{1,0:T(8,128)S(1)}, f32[128,2304]{1,0:T(8,128)}, u32[]{:S(2)}) copy-start(f32[128,2304]{1,0:T(8,128)} %copy-done.5) | copy-start | bytes 3538948
  1646.9 149.7 %copy-start.32 = (f32[128]{0:T(128)S(1)}, f32[128]{0:T(128)}, u32[]{:S(2)}) copy-start(f32[128]{0:T(128)} %get-tuple-element.668) | copy-start | bytes 1540
  (45 other events, 687.2 us)
Sparse Core Ops, SparseCore 0:
  9.7 54.3 all-gather.17
  66.5 36.2 all-gather.15
  104.5 51.6 all-gather.21
  157.7 30.4 all-gather.23
  190.2 28.2 all-gather.19
  220.5 28.5 all-gather.39
  250.7 31.1 all-gather.25
  342.2 36.9 reduce-scatter.16
  380.8 100.4 all-gather.29
  483.6 35.8 all-gather.27
  521.1 100.4 all-gather.31
  623.1 98.8 all-gather.33
  733.4 35.7 reduce-scatter.18
  775.1 37.4 all-gather.35
  847.8 37.3 reduce-scatter.20
  892.6 37.4 all-gather.37
  1113.4 56.4 reduce-scatter.22
  1172.0 48.1 reduce-scatter.24
  1222.5 31.0 reduce-scatter.30
  1255.7 31.1 reduce-scatter.32
  1289.8 34.4 reduce-scatter.28
  1327.2 35.3 reduce-scatter.34
  1365.7 53.8 all-reduce.2
  1421.9 110.6 reduce-scatter.40
  1534.9 109.0 reduce-scatter.36
  1646.2 108.9 reduce-scatter.38
  1758.1 35.7 reduce-scatter.26
  1796.8 31.1 reduce-scatter.42
where the time goes:
time: 1860 us; the launch traced here: 1850 us
  waiting for transfers between devices  1320 us (71%)
  matrix products  229 us (12%)
  other arithmetic  95.3 us (5%)
  loops' own time  85.1 us (5%)
  local copies, waits for them, and re-layouts  70.6 us (4%)
  blocking collectives  25.6 us (1%)
    all_gather x4, waiting for transfers between devices, head_rows(): return lax.all_gather(value, 'head', axis=0, tiled=True)  150 us
    reduce_scatter x4, waiting for transfers between devices, head_sum(): lax.psum_scatter(result.astype(jnp.bfloat16), 'head', scatter_dimension=0...  145 us
    reduce_scatter x1, waiting for transfers between devices, on_device(): lax.psum_scatter(grad_down.astype(jnp.bfloat16), 'blk', scatter_dimension...  109 us
    reduce_scatter x1, waiting for transfers between devices, on_device(): lax.psum_scatter(grad_wgate.astype(jnp.bfloat16), 'blk', scatter_dimensio...  108 us
    reduce_scatter x1, waiting for transfers between devices, on_device(): lax.psum_scatter(grad_wup.astype(jnp.bfloat16), 'blk', scatter_dimension=...  108 us
    all_gather x1, waiting for transfers between devices, on_device(): lax.all_gather(w_gate, 'blk', axis=0, tiled=True)  95.5 us
    all_gather x1, waiting for transfers between devices, on_device(): lax.all_gather(w_up, 'blk', axis=0, tiled=True)  90.5 us
    all_gather x1, waiting for transfers between devices, on_device(): lax.all_gather(w_down, 'blk', axis=1, tiled=True)  87.5 us
  transfers between devices with their start and end apart: 28, of which 26 were waited for; matrix products, arithmetic and copies ran while one was open for 10% of the time, Pallas kernels for 0%

commit v1 on v0

v1 whole, which is shorter than its diff:
```python
import functools
import math

import jax
import jax.numpy as jnp
from jax import lax
from jax.experimental import pallas as pl
from jax.experimental.pallas import tpu as pltpu
from jax.sharding import PartitionSpec as P

H = 8
KVH = 4
HD = 256

norm_eps = 1e-06
cap_value = 50.0
theta_base = 10000.0
f32 = jnp.float32
bf16 = jnp.bfloat16


def rms_scale(value, scale):
    inverse = lax.rsqrt(jnp.mean(value * value, axis=-1, keepdims=True) + norm_eps)
    return value * inverse * scale


def rms_back(value, scale, grad):
    inverse = lax.rsqrt(jnp.mean(value * value, axis=-1, keepdims=True) + norm_eps)
    scaled = grad * scale
    inner = jnp.mean(scaled * value, axis=-1, keepdims=True)
    grad_value = inverse * scaled - value * (inverse * inverse * inverse) * inner
    grad_scale = jnp.sum(grad * value * inverse, axis=0)
    return (grad_value, grad_scale)


def rotation(position, head_dim):
    quarter = head_dim // 4
    pair_index = jnp.arange(2, dtype=jnp.int32)[:, None] * quarter + jnp.arange(quarter, dtype=jnp.int32)[None, :]
    frequency = jnp.power(theta_base, -2.0 * pair_index.astype(f32) / head_dim)
    angles = position.astype(f32)[:, None, None] * frequency[None, :, :]
    return jnp.cos(angles), jnp.sin(angles)


def rotate(value, table, sign):
    cosine, sine = table
    row_count, total_width = value.shape
    quarter = cosine.shape[2]
    copies = total_width // (4 * quarter)
    shaped = value.reshape(row_count, copies, 2, 2, quarter)
    first = shaped[:, :, :, 0]
    second = shaped[:, :, :, 1]
    cosine = cosine[:, None]
    sine = sign * sine[:, None]
    new_first = first * cosine - second * sine
    new_second = first * sine + second * cosine
    return jnp.stack([new_first, new_second], axis=3).reshape(row_count, total_width)


def gelu_tanh(value):
    return jax.nn.gelu(value, approximate=True)


def swap(value, axis):
    blk_mask, head_mask = axis
    block_count, head_count = lax.axis_size("blk"), lax.axis_size("head")
    if blk_mask == 0:
        return lax.ppermute(value, "head", [(i, i ^ head_mask) for i in range(head_count)])
    return lax.ppermute(value, "blk", [(i, i ^ blk_mask) for i in range(block_count)])


def bits(count):
    return [1 << i for i in range(count.bit_length() - 1)]


def route(subset, axis_total):
    members = [i for i in range(axis_total) if subset >> i & 1]
    if len(members) >= 2 and len(members) == axis_total:
        return members
    if len(members) == 2 and members[1] - members[0] != 1:
        return members[1:]
    return members[:1]


def shares(row_total, parts):
    unit = row_total // 16
    cuts = [unit * i // parts * 16 for i in range(parts + 1)]
    cuts[-1] = row_total
    return list(zip(cuts[:-1], cuts[1:]))


def gather_rows(value, axes):
    pieces = [value]
    total = len(axes)
    for subset in sorted(range(1, 1 << total), key=lambda t: (bin(t).count("1"), t)):
        pieces.append(None)
    for subset in sorted(range(1, 1 << total), key=lambda t: (bin(t).count("1"), t)):
        ways = route(subset, total)
        parts = []
        for way, (low, high) in zip(ways, shares(value.shape[0], len(ways))):
            source = pieces[subset ^ (1 << way)]
            parts.append(swap(source if len(ways) == 1 else source[low:high], axes[way]))
        pieces[subset] = parts[0] if len(parts) == 1 else jnp.concatenate(parts, 0)
    return pieces


def joined(left, right):
    return (left.astype(f32) + right.astype(f32)).astype(bf16)


def scatter_rows(pieces, axes):
    total = len(axes)
    pieces = list(pieces)
    rows = pieces[0].shape[0]
    last = []
    for subset in sorted(range(1, 1 << total), key=lambda t: (-bin(t).count("1"), t)):
        ways = route(subset, total)
        for way, (low, high) in zip(ways, shares(rows, len(ways))):
            target = subset ^ (1 << way)
            if len(ways) == 1:
                moved = swap(pieces[subset], axes[way])
                if target == 0:
                    last.append(moved)
                else:
                    pieces[target] = joined(pieces[target], moved)
            else:
                moved = swap(pieces[subset][low:high], axes[way])
                old = pieces[target]
                cut = [old[:low], joined(old[low:high], moved), old[high:]]
                pieces[target] = jnp.concatenate([c for c in cut if c.shape[0]], 0)
    result = pieces[0].astype(f32)
    for moved in last:
        result = result + moved.astype(f32)
    return result


def gather_blocks(value, masks):
    held = {0: value}
    for mask in masks:
        for have in list(held):
            held[have ^ mask] = swap(held[have], (mask, 0))
    return held


def stack_rows(held, block_index):
    rows, columns = held[0].shape
    whole = jnp.zeros((len(held) * rows, columns), held[0].dtype)
    for mask, piece in held.items():
        whole = lax.dynamic_update_slice(whole, piece, ((block_index ^ mask) * rows, 0))
    return whole


def scatter_blocks(pick, masks):
    pending = {}

    def term(target):
        value = pick(target)
        return value

    terms = {}
    every = [0]
    for mask in masks:
        every = every + [t ^ mask for t in every]
    for target in every:
        terms[target] = term(target)
    left = list(every)
    for step, mask in enumerate(masks):
        rest = masks[step + 1 :]
        keep = [0]
        for other in rest:
            keep = keep + [t ^ other for t in keep]
        final = not rest
        for target in keep:
            moved = swap(terms[target ^ mask].astype(bf16), (mask, 0))
            total = terms[target].astype(f32) + moved.astype(f32)
            terms[target] = total if final else total.astype(bf16)
        left = keep
    return terms[0]


def scores(query, key, score_scale):
    raw = lax.dot_general(query, key, (((1,), (1,)), ((), ())), preferred_element_type=f32)
    return jnp.tanh(raw * (score_scale / cap_value))


def forward_kernel(group, span_len, tiles, spans_ref, q_ref, kv_ref, mixed_ref, exact_ref, lse_ref, q_all, acc, total):
    step = pl.program_id(0)
    score_scale = 1.0 / math.sqrt(HD)
    rows = group * span_len

    @pl.when(step == 0)
    def _():
        for half in range(2):
            for g in range(group):
                q_all[half, g * span_len : (g + 1) * span_len, :] = q_ref[
                    half * span_len : (half + 1) * span_len, g * HD : (g + 1) * HD
                ]
        acc[...] = jnp.zeros_like(acc)
        total[...] = jnp.zeros_like(total)

    tile_span = spans_ref[step]
    key = kv_ref[:, :HD]
    value = kv_ref[:, HD:]

    def visit(half, diagonal):
        weights = jnp.exp(cap_value * scores(q_all[half], key, score_scale))
        if diagonal:
            flip = spans_ref[tiles + 2]
            shape = (rows, span_len)
            q_pos = (lax.broadcasted_iota(jnp.int32, shape, 0) % span_len) ^ flip
            k_pos = lax.broadcasted_iota(jnp.int32, shape, 1) ^ flip
            weights = jnp.where(k_pos <= q_pos, weights, 0.0)
        part = weights[:, :128]
        for at in range(128, span_len, 128):
            part = part + weights[:, at : at + 128]
        total[half] += part
        acc[half] += jnp.dot(weights.astype(bf16), value, preferred_element_type=f32)

    for half in range(2):
        own = spans_ref[tiles + half]

        @pl.when(tile_span < own)
        def _():
            visit(half, False)

        @pl.when(tile_span == own)
        def _():
            visit(half, True)

    @pl.when(step == tiles - 1)
    def _():
        for half in range(2):
            sums = jnp.sum(total[half], axis=1, keepdims=True)
            exact = acc[half] / sums
            lse_ref[half] = jnp.log(jnp.sum(total[half].T, axis=0, keepdims=True))
            for g in range(group):
                piece = exact[g * span_len : (g + 1) * span_len]
                place = (slice(half * span_len, (half + 1) * span_len), slice(g * HD, (g + 1) * HD))
                exact_ref[place] = piece
                mixed_ref[place] = piece.astype(bf16)


def backward_kernel(
    group, span_len, tiles, spans_ref, q_ref, g_ref, exact_ref, lse_ref, kv_ref, dq_ref, dkv_ref, q_all, g_all, delta, dq_acc
):
    step = pl.program_id(0)
    score_scale = 1.0 / math.sqrt(HD)
    rows = group * span_len

    @pl.when(step == 0)
    def _():
        for half in range(2):
            for g in range(group):
                place = (slice(half * span_len, (half + 1) * span_len), slice(g * HD, (g + 1) * HD))
                here = slice(g * span_len, (g + 1) * span_len)
                q_all[half, here, :] = q_ref[place]
                g_all[half, here, :] = g_ref[place]
                product = g_ref[place].astype(f32) * exact_ref[place]
                folded = product[:, :128] + product[:, 128:]
                delta[half, :, here] = jnp.sum(folded.T, axis=0, keepdims=True)
        dq_acc[...] = jnp.zeros_like(dq_acc)

    tile_span = spans_ref[step]
    key = kv_ref[:, :HD]
    value = kv_ref[:, HD:]

    def visit(half, diagonal):
        query = q_all[half]
        grad = g_all[half]
        tangent = scores(key, query, score_scale)
        probability = jnp.exp(cap_value * tangent - lse_ref[half])
        if diagonal:
            flip = spans_ref[tiles + 2]
            shape = (span_len, rows)
            q_pos = (lax.broadcasted_iota(jnp.int32, shape, 1) % span_len) ^ flip
            k_pos = lax.broadcasted_iota(jnp.int32, shape, 0) ^ flip
            probability = jnp.where(k_pos <= q_pos, probability, 0.0)
        grad_prob = lax.dot_general(value, grad, (((1,), (1,)), ((), ())), preferred_element_type=f32)
        grad_raw = probability * (grad_prob - delta[half]) * ((1.0 - tangent * tangent) * score_scale)
        grad_raw = grad_raw.astype(bf16)
        dv = jnp.dot(probability.astype(bf16), grad, preferred_element_type=f32)
        dk = jnp.dot(grad_raw, query, preferred_element_type=f32)
        dq_acc[half] += lax.dot_general(grad_raw, key, (((0,), (0,)), ((), ())), preferred_element_type=f32)
        return dk, dv

    low, high = spans_ref[tiles], spans_ref[tiles + 1]

    @pl.when(jnp.logical_and(tile_span > low, tile_span > high))
    def _():
        dkv_ref[...] = jnp.zeros_like(dkv_ref)

    for half in range(2):
        own = spans_ref[tiles + half]
        other = spans_ref[tiles + 1 - half]

        def store(diagonal, half=half, own=own, other=other):
            dk, dv = visit(half, diagonal)

            @pl.when(jnp.logical_and(half == 1, tile_span <= other))
            def _():
                dkv_ref[:, :HD] = (dkv_ref[:, :HD].astype(f32) + dk).astype(dkv_ref.dtype)
                dkv_ref[:, HD:] = (dkv_ref[:, HD:].astype(f32) + dv).astype(dkv_ref.dtype)

            @pl.when(jnp.logical_or(half == 0, tile_span > other))
            def _():
                dkv_ref[:, :HD] = dk.astype(dkv_ref.dtype)
                dkv_ref[:, HD:] = dv.astype(dkv_ref.dtype)

        @pl.when(tile_span < own)
        def _():
            store(False)

        @pl.when(tile_span == own)
        def _():
            store(True)

    @pl.when(step == tiles - 1)
    def _():
        for half in range(2):
            for g in range(group):
                dq_ref[half * span_len : (half + 1) * span_len, g * HD : (g + 1) * HD] = dq_acc[
                    half, g * span_len : (g + 1) * span_len
                ]


def attention_forward(spans, queries, kv, span_len):
    tiles = kv.shape[0] // span_len
    width = queries.shape[1]
    group = width // HD
    rows = group * span_len
    whole = lambda s, t: (0, 0)
    visits = tiles + 1
    return pl.pallas_call(
        functools.partial(forward_kernel, group, span_len, tiles),
        grid_spec=pltpu.PrefetchScalarGridSpec(
            num_scalar_prefetch=1,
            grid=(tiles,),
            in_specs=[
                pl.BlockSpec(queries.shape, whole),
                pl.BlockSpec((span_len, 2 * HD), lambda s, t: (s, 0)),
            ],
            out_specs=[
                pl.BlockSpec(queries.shape, whole),
                pl.BlockSpec(queries.shape, whole),
                pl.BlockSpec((2, 1, rows), lambda s, t: (0, 0, 0)),
            ],
            scratch_shapes=[
                pltpu.VMEM((2, rows, HD), bf16),
                pltpu.VMEM((2, rows, HD), f32),
                pltpu.VMEM((2, rows, 128), f32),
            ],
        ),
        out_shape=[
            jax.ShapeDtypeStruct(queries.shape, bf16),
            jax.ShapeDtypeStruct(queries.shape, f32),
            jax.ShapeDtypeStruct((2, 1, rows), f32),
        ],
        compiler_params=pltpu.CompilerParams(vmem_limit_bytes=40 * 1024 * 1024),
        cost_estimate=pl.CostEstimate(
            flops=visits * rows * span_len * HD * 4,
            bytes_accessed=kv.size * 2 + queries.size * 12,
            transcendentals=visits * rows * span_len * 2,
        ),
        name="attention_forward",
    )(spans, queries, kv)


def attention_backward(spans, queries, grads, exact, lse, kv, span_len):
    tiles = kv.shape[0] // span_len
    width = queries.shape[1]
    group = width // HD
    rows = group * span_len
    whole = lambda s, t: (0, 0)
    visits = tiles + 1
    return pl.pallas_call(
        functools.partial(backward_kernel, group, span_len, tiles),
        grid_spec=pltpu.PrefetchScalarGridSpec(
            num_scalar_prefetch=1,
            grid=(tiles,),
            in_specs=[
                pl.BlockSpec(queries.shape, whole),
                pl.BlockSpec(queries.shape, whole),
                pl.BlockSpec(queries.shape, whole),
                pl.BlockSpec((2, 1, rows), lambda s, t: (0, 0, 0)),
                pl.BlockSpec((span_len, 2 * HD), lambda s, t: (s, 0)),
            ],
            out_specs=[
                pl.BlockSpec(queries.shape, whole),
                pl.BlockSpec((span_len, 2 * HD), lambda s, t: (s, 0)),
            ],
            scratch_shapes=[
                pltpu.VMEM((2, rows, HD), bf16),
                pltpu.VMEM((2, rows, HD), bf16),
                pltpu.VMEM((2, 1, rows), f32),
                pltpu.VMEM((2, rows, HD), f32),
            ],
        ),
        out_shape=[
            jax.ShapeDtypeStruct(queries.shape, f32),
            jax.ShapeDtypeStruct(kv.shape, bf16),
        ],
        compiler_params=pltpu.CompilerParams(vmem_limit_bytes=40 * 1024 * 1024),
        cost_estimate=pl.CostEstimate(
            flops=visits * rows * span_len * HD * 10,
            bytes_accessed=kv.size * 4 + queries.size * 16,
            transcendentals=visits * rows * span_len * 2,
        ),
        name="attention_backward",
    )(spans, queries, grads, exact, lse, kv)


def product(left, right, left_dim, right_dim, out=f32):
    result = lax.dot_general(left, right, (((left_dim,), (right_dim,)), ((), ())), preferred_element_type=f32)
    return result.astype(out)


def on_device(
    hidden_in,
    out_grad,
    span_order,
    w_query,
    w_key,
    w_value,
    w_output,
    w_gate,
    w_up,
    w_down,
    norm_scales,
):
    local_rows = hidden_in.shape[0]
    head_count = lax.axis_size("head")
    block_count = lax.axis_size("blk")
    block_index = lax.axis_index("blk")
    head_index = lax.axis_index("head")
    group_rows = local_rows * head_count
    span_len = group_rows // 2
    model_rows, query_width = w_query.shape
    model_width = hidden_in.shape[1]
    query_heads = query_width // HD
    half_units = w_gate.shape[1] // 2

    chip_masks = bits(block_count)[1:]
    pair = chip_masks[0]
    down_masks = chip_masks[::-1] + [1]
    head_axes = [(0, mask) for mask in bits(head_count)]
    unit_axes = head_axes + [(pair, 0)]
    unit_side = (block_index // pair) % 2

    held = gather_blocks(norm_scales, down_masks)
    scale_rows = jnp.zeros((block_count,) + norm_scales.shape, norm_scales.dtype)
    for mask, piece in held.items():
        scale_rows = lax.dynamic_update_slice(scale_rows, piece[None], (block_index ^ mask, 0, 0))
    scale_rows = scale_rows.transpose(1, 0, 2).reshape(norm_scales.shape[0], model_width).astype(f32)

    kv_at = head_index * query_heads // (H // KVH) * HD
    kv_local = jnp.concatenate(
        [
            lax.dynamic_slice_in_dim(w_key, kv_at, HD, 1),
            lax.dynamic_slice_in_dim(w_value, kv_at, HD, 1),
        ],
        1,
    )
    kv_weight = stack_rows(gather_blocks(kv_local, down_masks), block_index)
    query_weight = stack_rows(gather_blocks(w_query, down_masks), block_index)
    output_weight = stack_rows(gather_blocks(w_output.T, down_masks), block_index)

    def unit_weight(local):
        mine = lax.dynamic_slice_in_dim(local, unit_side * half_units, half_units, 1)
        theirs = lax.dynamic_slice_in_dim(local, (1 - unit_side) * half_units, half_units, 1)
        held = {0: mine, pair: swap(theirs, (pair, 0))}
        for mask in [m for m in down_masks if m != pair]:
            for have in list(held):
                held[have ^ mask] = swap(held[have], (mask, 0))
        return stack_rows(held, block_index)

    gate_weight = unit_weight(w_gate)
    up_weight = unit_weight(w_up)
    down_weight = unit_weight(w_down.T)

    def unit_gradient(partial):
        shaped = partial.reshape(block_count, model_rows, half_units)

        def pick(mask):
            return lax.dynamic_index_in_dim(shaped, block_index ^ mask, 0, keepdims=False)

        masks = [1] + [m for m in down_masks if m not in (1, pair)]

        mine = scatter_blocks(pick, masks)
        theirs = scatter_blocks(lambda mask: pick(mask ^ pair), masks)
        other = swap(theirs.astype(bf16), (pair, 0))
        mine = mine.astype(bf16)
        low = jnp.where(unit_side == 0, mine, other)
        high = jnp.where(unit_side == 0, other, mine)
        return jnp.concatenate([low, high], 1).astype(f32)

    def block_gradient(partial):
        shaped = partial.reshape(block_count, model_rows, partial.shape[1])
        return scatter_blocks(
            lambda mask: lax.dynamic_index_in_dim(shaped, block_index ^ mask, 0, keepdims=False),
            [1] + chip_masks[::-1],
        )

    hidden_full = jnp.concatenate(gather_rows(hidden_in, head_axes), 0).astype(f32)
    slot = jnp.arange(head_count, dtype=jnp.int32) ^ head_index
    in_block = (slot[:, None] * local_rows + jnp.arange(local_rows, dtype=jnp.int32)[None, :]).reshape(-1)
    side = head_index // (head_count // 2)
    own_spans = jnp.stack([span_order[2 * block_index + side], span_order[2 * block_index + 1 - side]])
    row_spans = jnp.repeat(own_spans, span_len)
    position = row_spans * span_len + in_block % span_len
    tile_blocks = jnp.arange(block_count, dtype=jnp.int32) ^ block_index
    tile_slots = (2 * tile_blocks[:, None] + jnp.stack([side, 1 - side])[None, :]).reshape(-1)
    flip = (head_index % (head_count // 2)) * local_rows
    spans = jnp.concatenate([span_order[tile_slots], own_spans, flip[None]]).astype(jnp.int32)
    table = rotation(position, HD)

    residual_in = hidden_in.astype(f32)
    normed_full = rms_scale(hidden_full, scale_rows[0]).astype(bf16)
    kv_lin = product(normed_full, kv_weight, 1, 0)
    kv_rows = jnp.concatenate(
        [rotate(kv_lin[:, :HD], table, 1.0).astype(bf16), kv_lin[:, HD:].astype(bf16)], 1
    )
    kv_held = gather_blocks(kv_rows, down_masks)
    kv = jnp.concatenate([kv_held[mask] for mask in range(block_count)], 0)
    query_lin = product(normed_full, query_weight, 1, 0)
    queries = rotate(query_lin, table, 1.0).astype(bf16)

    mixed, exact, lse = attention_forward(spans, queries, kv, span_len)

    def row_sum(partial, axes):
        shaped = partial.reshape(1 << len(axes), local_rows, model_width)
        return scatter_rows([shaped[i] for i in range(1 << len(axes))], axes)

    attn_out = row_sum(product(mixed, output_weight, 1, 1, bf16), head_axes)
    resid = residual_in + rms_scale(attn_out, scale_rows[1])
    ffn_in = rms_scale(resid, scale_rows[2]).astype(bf16)
    ffn_full = jnp.concatenate(gather_rows(ffn_in, unit_axes), 0)
    gate = product(ffn_full, gate_weight, 1, 0)
    up_value = product(ffn_full, up_weight, 1, 0)
    activated, gelu_back = jax.vjp(gelu_tanh, gate)
    hidden = (activated * up_value).astype(bf16)
    ffn_out = row_sum(product(hidden, down_weight, 1, 1, bf16), unit_axes)
    layer_out = (resid + rms_scale(ffn_out, scale_rows[3])).astype(bf16)

    grad_top = out_grad.astype(f32)
    grad_ffn_out, scale_grad3 = rms_back(ffn_out, scale_rows[3], grad_top)
    grad_ffn_full = jnp.concatenate(gather_rows(grad_ffn_out.astype(bf16), unit_axes), 0)
    grad_hidden = product(grad_ffn_full, down_weight, 1, 0)
    grad_down = product(grad_ffn_full, hidden, 0, 0, bf16)
    grad_gate_act = gelu_back(grad_hidden * up_value)[0].astype(bf16)
    grad_up_act = (grad_hidden * activated).astype(bf16)
    grad_ffn_part = product(grad_gate_act, gate_weight, 1, 1) + product(grad_up_act, up_weight, 1, 1)
    grad_ffn_in = row_sum(grad_ffn_part.astype(bf16), unit_axes)
    grad_wgate = product(ffn_full, grad_gate_act, 0, 0, bf16)
    grad_wup = product(ffn_full, grad_up_act, 0, 0, bf16)
    out_down = unit_gradient(grad_down).T
    out_gate = unit_gradient(grad_wgate)
    out_up = unit_gradient(grad_wup)

    grad_resid_part, scale_grad2 = rms_back(resid, scale_rows[2], grad_ffn_in)
    grad_resid = grad_top + grad_resid_part
    grad_attn, scale_grad1 = rms_back(attn_out, scale_rows[1], grad_resid)
    grad_attn_full = jnp.concatenate(gather_rows(grad_attn.astype(bf16), head_axes), 0)
    grad_mixed = product(grad_attn_full, output_weight, 1, 0, bf16)
    grad_woutput = product(grad_attn_full, mixed, 0, 0, bf16)
    out_output = block_gradient(grad_woutput).T

    grad_query, grad_kv = attention_backward(spans, queries, grad_mixed, exact, lse, kv, span_len)
    grad_query_lin = rotate(grad_query, table, -1.0).astype(bf16)
    grad_wquery = product(normed_full, grad_query_lin, 0, 0, bf16)
    out_query = block_gradient(grad_wquery)
    kv_shaped = grad_kv.reshape(block_count, group_rows, 2 * HD)
    kv_grad_rows = scatter_blocks(lambda mask: kv_shaped[mask], [1] + chip_masks[::-1])
    grad_kv_lin = jnp.concatenate(
        [rotate(kv_grad_rows[:, :HD], table, -1.0).astype(bf16), kv_grad_rows[:, HD:].astype(bf16)], 1
    )
    grad_wkv = block_gradient(product(normed_full, grad_kv_lin, 0, 0, bf16))
    grad_normed_part = product(grad_query_lin, query_weight, 1, 1) + product(grad_kv_lin, kv_weight, 1, 1)
    grad_normed = row_sum(grad_normed_part.astype(bf16), head_axes)
    grad_in_part, scale_grad0 = rms_back(residual_in, scale_rows[0], grad_normed)
    grad_in = grad_resid + grad_in_part

    kv_pieces = jnp.stack(gather_rows(grad_wkv.astype(bf16), head_axes))
    kv_ordered = jnp.zeros_like(kv_pieces)
    for mask in range(head_count):
        kv_ordered = lax.dynamic_update_slice(kv_ordered, kv_pieces[mask][None], (head_index ^ mask, 0, 0))
    kv_ordered = kv_ordered.astype(f32).reshape(KVH, head_count // KVH, model_rows, 2, HD).sum(1)
    out_key = kv_ordered[:, :, 0].transpose(1, 0, 2).reshape(model_rows, KVH * HD)
    out_value = kv_ordered[:, :, 1].transpose(1, 0, 2).reshape(model_rows, KVH * HD)

    scale_grad = jnp.stack([scale_grad0, scale_grad1, scale_grad2, scale_grad3])
    scale_shaped = scale_grad.reshape(4, block_count, model_rows).transpose(1, 0, 2)
    scale_total = scatter_blocks(
        lambda mask: lax.dynamic_index_in_dim(scale_shaped, block_index ^ mask, 0, keepdims=False),
        [1] + chip_masks[::-1],
    )
    for axis in head_axes:
        scale_total = scale_total + swap(scale_total, axis)

    return (
        layer_out,
        grad_in,
        out_query,
        out_key,
        out_value,
        out_output,
        out_gate,
        out_up,
        out_down,
        scale_total,
    )


def solution(mesh):
    placed = (
        P(("blk", "head"), None),
        P(("blk", "head"), None),
        P(),
        P("blk", "head"),
        P("blk", None),
        P("blk", None),
        P("head", "blk"),
        P("blk", "head"),
        P("blk", "head"),
        P("head", "blk"),
        P(None, "blk"),
    )
    return jax.shard_map(
        on_device,
        mesh=mesh,
        in_specs=placed,
        out_specs=(
            P(("blk", "head"), None),
            P(("blk", "head"), None),
            P("blk", "head"),
            P("blk", None),
            P("blk", None),
            P("head", "blk"),
            P("blk", "head"),
            P("blk", "head"),
            P("head", "blk"),
            P(None, "blk"),
        ),
        check_vma=False,
    )
```

time: 1860 us -> 1020 us (0.55)
  waiting for transfers between devices: 1320 us -> 572 us
  starting transfers between devices: 2.39 us -> 119 us
  matrix products: 229 us -> 113 us
  loops' own time: 85.1 us -> 0 us
  local copies, waits for them, and re-layouts: 70.6 us -> 103 us
  blocking collectives: 25.6 us -> 0 us
  Pallas kernels: 0 us -> 23.7 us
    reduce_scatter x13 -> x0, waiting for transfers between devices: 646 us -> none  [the longest x4 145 us: head_sum(): lax.psum_scatter(result.astype(jnp.bfloat16), 'head', scatter_dimension=0...]
    all_gather x13 -> x0, waiting for transfers between devices: 587 us -> none  [the longest x4 150 us: head_rows(): return lax.all_gather(value, 'head', axis=0, tiled=True)]
    ppermute x0 -> x170, waiting for transfers between devices: none -> 572 us  [the longest x124 470 us: swap(): lax.ppermute(value, 'blk', [(i, i ^ blk_mask) for i in range(block_count)])]
    ppermute x0 -> x170, starting transfers between devices: none -> 119 us  [the longest x124 78.8 us: swap(): lax.ppermute(value, 'blk', [(i, i ^ blk_mask) for i in range(block_count)])]
    dot_general x140 -> x18, matrix products: 229 us -> 113 us  [product(): lax.dot_general(left, right, (((left_dim,), (right_dim,)), ((), ())), pre...]
    another operation x66 -> x0, loops' own time: 85.1 us -> none  [the longest x1 42.4 us: on_device(): lax.scan(forward_advance, state_init, tiles + (tile_positions,))]
    psum x1 -> x0, waiting for transfers between devices: 55.2 us -> none  [on_device(): lax.psum(key_place.astype(jnp.bfloat16), 'head').astype(jnp.float32)]
    dynamic_update_slice x0 -> x57, local copies, waits for them, and re-layouts: none -> 46.8 us  [the longest x47 44.6 us: stack_rows(): lax.dynamic_update_slice(whole, piece, ((block_index ^ mask) * rows, 0))]
  transfers between devices with their start and end apart: 28 -> 170, of which waited for: 26 -> 65; matrix products, arithmetic and copies ran while one was open for 10% -> 17% of each run, Pallas kernels for 0% -> 1%
where the time goes in v1:
time: 1020 us; the launch traced here: 1010 us
  waiting for transfers between devices  572 us (56%)
  starting transfers between devices  119 us (12%)
  matrix products  113 us (11%)
  local copies, waits for them, and re-layouts  103 us (10%)
  other arithmetic  78.3 us (8%)
  Pallas kernels  23.7 us (2%)
    ppermute x124, waiting for transfers between devices, swap(): lax.ppermute(value, 'blk', [(i, i ^ blk_mask) for i in range(block_count)])  470 us
    dot_general x18, matrix products, product(): lax.dot_general(left, right, (((left_dim,), (right_dim,)), ((), ())), pre...  113 us
    ppermute x46, waiting for transfers between devices, swap(): lax.ppermute(value, 'head', [(i, i ^ head_mask) for i in range(head_count)])  102 us
    ppermute x124, starting transfers between devices, swap(): lax.ppermute(value, 'blk', [(i, i ^ blk_mask) for i in range(block_count)])  78.8 us
    dynamic_update_slice x47, local copies, waits for them, and re-layouts, stack_rows(): lax.dynamic_update_slice(whole, piece, ((block_index ^ mask) * rows, 0))  44.6 us
    ppermute x46, starting transfers between devices, swap(): lax.ppermute(value, 'head', [(i, i ^ head_mask) for i in range(head_count)])  39.7 us
  transfers between devices with their start and end apart: 170, of which 65 were waited for; matrix products, arithmetic and copies ran while one was open for 17% of the time, Pallas kernels for 1%

profile of v1, /device:TPU:0, one launch (start us, length us, event | category | flops | bytes accessed | tf_op | source)
XLA Modules:
  0.0 1011.6 jit_solution(14236309739232920207)
XLA Ops:
  51.6 11.2 %collective-permute-done.18 = bf16[288,512]{1,0:T(8,128)(2,1)} collective-permute-done((bf16[288,512]{1,0:T(8,128)(2,1)}, bf16[288,512]{1,0:T(8,128)(2,1)}, u32[]{:S(2)}, u32[]{:S(2)}) %collective-permute-start.18) | collective-permute-done | bytes 294944 | tf_op jit(solution)/shard_map/ppermute | solution.py:68
  106.2 24.0 %collective-permute-done.34 = bf16[288,512]{1,0:T(8,128)(2,1)S(1)} collective-permute-done((bf16[288,512]{1,0:T(8,128)(2,1)S(1)}, bf16[288,512]{1,0:T(8,128)(2,1)S(1)}, u32[]{:S(2)}, u32[]{:S(2)}) %collective-permute-start.34) | collective-permute-done | bytes 294944 | tf_op jit(solution)/shard_map/ppermute | solution.py:68
  140.9 20.0 %collective-permute-done.59 = bf16[288,1152]{1,0:T(8,128)(2,1)S(1)} collective-permute-done((bf16[288,1152]{1,0:T(8,128)(2,1)S(1)}, bf16[288,1152]{1,0:T(8,128)(2,1)S(1)}, u32[]{:S(2)}, u32[]{:S(2)}) %collective-permute-start.59) | collective-permute-done | bytes 663584 | tf_op jit(solution)/shard_map/ppermute | solution.py:68
  168.8 19.6 %collective-permute-done.66 = bf16[288,1152]{1,0:T(8,128)(2,1)S(1)} collective-permute-done((bf16[288,1152]{1,0:T(8,128)(2,1)S(1)}, bf16[288,1152]{1,0:T(8,128)(2,1)S(1)}, u32[]{:S(2)}, u32[]{:S(2)}) %collective-permute-start.66) | collective-permute-done | bytes 663584 | tf_op jit(solution)/shard_map/ppermute | solution.py:68
  205.5 12.3 %fusion.65 = (bf16[512,1,2,1,64]{0,4,3,2,1:T(8,128)(2,1)S(1)}, bf16[512,1,2,1,64]{0,4,3,2,1:T(8,128)(2,1)S(1)}) fusion(f32[512,1,2,2,64]{0,4,3,2,1:T(8,128)S(1)} %bitcast.304, f32[2,64]{1,0:T(2,128)S(1)} %multiply_power_fusion, f32[512]{0:T(512)S(1)} %fusion.90), kind=kLoop, calls=%fused_computation.233 | loop fusion | flops 589824 | bytes 788992 | tf_op jit(solution)/shard_map/convert.33
  219.7 10.2 %collective-permute-done.54 = bf16[288,1152]{1,0:T(8,128)(2,1)} collective-permute-done((bf16[288,1152]{1,0:T(8,128)(2,1)}, bf16[288,1152]{1,0:T(8,128)(2,1)}, u32[]{:S(2)}, u32[]{:S(2)}) %collective-permute-start.54) | collective-permute-done | bytes 663584 | tf_op jit(solution)/shard_map/ppermute | solution.py:68
  240.6 33.1 %collective-permute-done.61 = bf16[288,1152]{1,0:T(8,128)(2,1)S(1)} collective-permute-done((bf16[288,1152]{1,0:T(8,128)(2,1)S(1)}, bf16[288,1152]{1,0:T(8,128)(2,1)S(1)}, u32[]{:S(2)}, u32[]{:S(2)}) %collective-permute-start.61) | collective-permute-done | bytes 663584 | tf_op jit(solution)/shard_map/ppermute | solution.py:68
  287.5 9.6 collective-permute-done.30
  315.1 14.3 %collective-permute-done.68 = bf16[288,1152]{1,0:T(8,128)(2,1)S(1)} collective-permute-done((bf16[288,1152]{1,0:T(8,128)(2,1)S(1)}, bf16[288,1152]{1,0:T(8,128)(2,1)S(1)}, u32[]{:S(2)}, u32[]{:S(2)}) %collective-permute-start.68) | collective-permute-done | bytes 663584 | tf_op jit(solution)/shard_map/ppermute | solution.py:68
  336.5 9.8 collective-permute-done.42
  353.5 11.0 %collective-permute-done.44 = bf16[128,2304]{1,0:T(8,128)(2,1)S(1)} collective-permute-done((bf16[128,2304]{1,0:T(8,128)(2,1)S(1)}, bf16[128,2304]{1,0:T(8,128)(2,1)S(1)}, u32[]{:S(2)}, u32[]{:S(2)}) %collective-permute-start.44) | collective-permute-done | bytes 589856 | tf_op jit(solution)/shard_map/ppermute | solution.py:67
  366.6 12.5 %collective-permute-done.48 = bf16[128,2304]{1,0:T(8,128)(2,1)S(1)} collective-permute-done((bf16[128,2304]{1,0:T(8,128)(2,1)S(1)}, bf16[128,2304]{1,0:T(8,128)(2,1)S(1)}, u32[]{:S(2)}, u32[]{:S(2)}) %collective-permute-start.48) | collective-permute-done | bytes 589856 | tf_op jit(solution)/shard_map/ppermute | solution.py:67
  392.9 12.6 %multiply_convert_fusion.1 = (bf16[1024,1152]{1,0:T(8,128)(2,1)S(1)}, f32[1024,1152]{1,0:T(8,128)}) fusion(f32[1024,1152]{1,0:T(8,128)S(1)} %fusion.110, bf16[1024,2304]{1,0:T(8,128)(2,1)S(1)} %constant_dynamic-update-slice_fusion.13, bf16[2304,1152]{1,0:T(8,128)(2,1)} %constant_dynamic-update-slice_fusion.46), kind=kOutput, calls=%fused_computation.22 | convolution fusion | flops 5447614464 | bytes 21823488 | tf_op jit(solution)/shard_map/dot_general | solution.py:412
  406.9 9.5 convolution_convert_fusion.3
  446.5 12.3 %collective-permute-done.81 = bf16[128,2304]{1,0:T(8,128)(2,1)} collective-permute-done((bf16[128,2304]{1,0:T(8,128)(2,1)}, bf16[128,2304]{1,0:T(8,128)(2,1)}, u32[]{:S(2)}, u32[]{:S(2)}) %collective-permute-start.81) | collective-permute-done | bytes 589856 | tf_op jit(solution)/shard_map/ppermute | solution.py:68
  501.1 15.3 %fusion.9 = (bf16[1024,1152]{1,0:T(8,128)(2,1)}, bf16[1024,1152]{1,0:T(8,128)(2,1)S(1)}) fusion(f32[1024,1152]{1,0:T(8,128)} %copy-done.90, f32[1024,1152]{1,0:T(8,128)} %get-tuple-element.171, bf16[1024,2304]{1,0:T(8,128)(2,1)} %constant_dynamic-update-slice_fusion.23, bf16[2304,1152]{1,0:T(8,128)(2,1)} %constant_dynamic-update-slice_fusion.38), kind=kOutput, calls=%fused_computation.20 | convolution fusion | flops 5464129536 | bytes 24182784 | tf_op jit(solution)/shard_map/dot_general | solution.py:412
  516.5 12.2 %fusion.111 = f32[1024,2304]{1,0:T(8,128)} fusion(bf16[1024,1152]{1,0:T(8,128)(2,1)S(1)} %get-tuple-element.58, bf16[2304,1152]{1,0:T(8,128)(2,1)} %constant_dynamic-update-slice_fusion.46), kind=kOutput, calls=%fused_computation.421 | convolution fusion | flops 5435817984 | bytes 17104896 | tf_op jit(solution)/shard_map/dot_general | solution.py:412
  528.7 9.6 add_convert_fusion
  547.0 10.2 %convolution_convert_fusion.1 = bf16[2304,1152]{1,0:T(8,128)(2,1)S(1)} fusion(bf16[1024,2304]{1,0:T(8,128)(2,1)} %copy-done.77, bf16[1024,1152]{1,0:T(8,128)(2,1)S(1)} %copy-done.92), kind=kOutput, calls=%fused_computation.2 | convolution fusion | flops 5438472192 | bytes 12386304 | tf_op jit(solution)/shard_map/dot_general | solution.py:412
  595.3 54.8 %collective-permute-done.145 = bf16[288,1152]{1,0:T(8,128)(2,1)S(1)} collective-permute-done((bf16[288,1152]{1,0:T(8,128)(2,1)S(1)}, bf16[288,1152]{1,0:T(8,128)(2,1)S(1)}, u32[]{:S(2)}, u32[]{:S(2)}) %collective-permute-start.145) | collective-permute-done | bytes 663584 | tf_op jit(solution)/shard_map/ppermute | solution.py:68
  651.9 12.5 %collective-permute-done.152 = bf16[288,1152]{1,0:T(8,128)(2,1)S(1)} collective-permute-done((bf16[288,1152]{1,0:T(8,128)(2,1)S(1)}, bf16[288,1152]{1,0:T(8,128)(2,1)S(1)}, u32[]{:S(2)}, u32[]{:S(2)}) %collective-permute-start.152) | collective-permute-done | bytes 663584 | tf_op jit(solution)/shard_map/ppermute | solution.py:68
  666.2 11.9 %collective-permute-done.159 = bf16[288,1152]{1,0:T(8,128)(2,1)S(1)} collective-permute-done((bf16[288,1152]{1,0:T(8,128)(2,1)S(1)}, bf16[288,1152]{1,0:T(8,128)(2,1)S(1)}, u32[]{:S(2)}, u32[]{:S(2)}) %collective-permute-start.159) | collective-permute-done | bytes 663584 | tf_op jit(solution)/shard_map/ppermute | solution.py:68
  679.3 11.4 %collective-permute-done.99 = bf16[128,2304]{1,0:T(8,128)(2,1)S(1)} collective-permute-done((bf16[128,2304]{1,0:T(8,128)(2,1)S(1)}, bf16[128,2304]{1,0:T(8,128)(2,1)S(1)}, u32[]{:S(2)}, u32[]{:S(2)}) %collective-permute-start.99) | collective-permute-done | bytes 589856 | tf_op jit(solution)/shard_map/ppermute | solution.py:68
  699.8 23.3 %collective-permute-done.142 = bf16[288,1152]{1,0:T(8,128)(2,1)} collective-permute-done((bf16[288,1152]{1,0:T(8,128)(2,1)}, bf16[288,1152]{1,0:T(8,128)(2,1)}, u32[]{:S(2)}, u32[]{:S(2)}) %collective-permute-start.142) | collective-permute-done | bytes 663584 | tf_op jit(solution)/shard_map/ppermute | solution.py:68
  728.8 36.8 %collective-permute-done.149 = bf16[288,1152]{1,0:T(8,128)(2,1)S(1)} collective-permute-done((bf16[288,1152]{1,0:T(8,128)(2,1)}, bf16[288,1152]{1,0:T(8,128)(2,1)S(1)}, u32[]{:S(2)}, u32[]{:S(2)}) %collective-permute-start.149) | collective-permute-done | bytes 663584 | tf_op jit(solution)/shard_map/ppermute | solution.py:68
  800.9 14.2 %attention_backward.1 = (f32[512,512]{1,0:T(8,128)S(1)}, bf16[4096,512]{1,0:T(8,128)(2,1)S(1)}) custom-call(s32[19]{0:T(128)S(1)} %copy-done.7, bf16[512,512]{1,0:T(8,128)(2,1)S(1)} %copy-done.3, bf16[512,512]{1,0:T(8,128)(2,1)S(1)} %convolution_convert_fusion.8.g_ref, f32[512,512]{1,0:T(8,128)S(1)} %get-tuple-element.16.exact_ref, ...), custom_call_target="tpu_custom_call" | custom-call | flops 5704253440 | bytes 12582912 | tf_op jit(solution)/shard_map/attention_backward/pallas_call | solution.py:374
  831.0 21.1 %collective-permute-done.109 = bf16[512,512]{1,0:T(8,128)(2,1)S(1)} collective-permute-done((bf16[512,512]{1,0:T(8,128)(2,1)S(1)}, bf16[512,512]{1,0:T(8,128)(2,1)S(1)}, u32[]{:S(2)}, u32[]{:S(2)}) %collective-permute-start.109) | collective-permute-done | bytes 524320 | tf_op jit(solution)/shard_map/ppermute | solution.py:68
  859.0 19.8 %collective-permute-done.120 = bf16[288,512]{1,0:T(8,128)(2,1)S(1)} collective-permute-done((bf16[288,512]{1,0:T(8,128)(2,1)S(1)}, bf16[288,512]{1,0:T(8,128)(2,1)S(1)}, u32[]{:S(2)}, u32[]{:S(2)}) %collective-permute-start.120) | collective-permute-done | bytes 294944 | tf_op jit(solution)/shard_map/ppermute | solution.py:68
  879.7 16.7 %collective-permute-done.106 = bf16[512,512]{1,0:T(8,128)(2,1)S(1)} collective-permute-done((bf16[512,512]{1,0:T(8,128)(2,1)S(1)}, bf16[512,512]{1,0:T(8,128)(2,1)S(1)}, u32[]{:S(2)}, u32[]{:S(2)}) %collective-permute-start.106) | collective-permute-done | bytes 524320 | tf_op jit(solution)/shard_map/ppermute | solution.py:68
  917.0 10.6 %collective-permute-done.138 = bf16[288,512]{1,0:T(8,128)(2,1)S(1)} collective-permute-done((bf16[288,512]{1,0:T(8,128)(2,1)S(1)}, bf16[288,512]{1,0:T(8,128)(2,1)S(1)}, u32[]{:S(2)}, u32[]{:S(2)}) %collective-permute-start.138) | collective-permute-done | bytes 294944 | tf_op jit(solution)/shard_map/ppermute | solution.py:68
  946.4 15.4 %collective-permute-done.127 = bf16[288,512]{1,0:T(8,128)(2,1)} collective-permute-done((bf16[288,512]{1,0:T(8,128)(2,1)}, bf16[288,512]{1,0:T(8,128)(2,1)}, u32[]{:S(2)}, u32[]{:S(2)}) %collective-permute-start.127) | collective-permute-done | bytes 294944 | tf_op jit(solution)/shard_map/ppermute | solution.py:68
  969.4 10.1 %collective-permute-done.166 = bf16[4,288]{1,0:T(4,128)(2,1)S(1)} collective-permute-done((bf16[4,288]{1,0:T(4,128)(2,1)S(1)}, bf16[4,288]{1,0:T(4,128)(2,1)S(1)}, u32[]{:S(2)}, u32[]{:S(2)}) %collective-permute-start.166) | collective-permute-done | bytes 2336 | tf_op jit(solution)/shard_map/ppermute | solution.py:68
  (794 shorter events, 480.5 us)
Async XLA Ops:
  6.3 42.7 %collective-permute-start.11 = (bf16[288,512]{1,0:T(8,128)(2,1)}, bf16[288,512]{1,0:T(8,128)(2,1)}, u32[]{:S(2)}, u32[]{:S(2)}) collective-permute-start(bf16[288,512]{1,0:T(8,128)(2,1)} %param.14), channel_id=1, source_target_pairs={{0,16},{4,20},{8,24},{12,28},{16,0},{20,4},{24,8},{28,12},{1,17},{... | collective-permute-start | bytes 884744 | tf_op jit(solution)/shard_map/ppermute | solution.py:68
  6.7 57.8 %collective-permute-start.12 = (bf16[288,512]{1,0:T(8,128)(2,1)}, bf16[288,512]{1,0:T(8,128)(2,1)}, u32[]{:S(2)}, u32[]{:S(2)}) collective-permute-start(bf16[288,512]{1,0:T(8,128)(2,1)} %param.14), channel_id=1, source_target_pairs={{0,8},{4,12},{8,0},{12,4},{16,24},{20,28},{24,16},{28,20},{1,9},{5... | collective-permute-start | bytes 884744 | tf_op jit(solution)/shard_map/ppermute | solution.py:68
  37.1 61.0 %collective-permute-start.14 = (bf16[288,512]{1,0:T(8,128)(2,1)}, bf16[288,512]{1,0:T(8,128)(2,1)}, u32[]{:S(2)}, u32[]{:S(2)}) collective-permute-start(bf16[288,512]{1,0:T(8,128)(2,1)} %param.14), channel_id=1, source_target_pairs={{0,4},{4,0},{8,12},{12,8},{16,20},{20,16},{24,28},{28,24},{1,5},{5... | collective-permute-start | bytes 884744 | tf_op jit(solution)/shard_map/ppermute | solution.py:68
  40.9 40.1 %collective-permute-start = (bf16[128,2304]{1,0:T(8,128)(2,1)S(1)}, bf16[128,2304]{1,0:T(8,128)(2,1)}, u32[]{:S(2)}, u32[]{:S(2)}) collective-permute-start(bf16[128,2304]{1,0:T(8,128)(2,1)S(1)} %copy-done.12), channel_id=1, source_target_pairs={{0,1},{1,0},{2,3},{3,2},{4,5},{5,4},{6,7},{7,6},{8,9},{9,8},{10,11... | collective-permute-start | bytes 1769480 | tf_op jit(solution)/shard_map/ppermute | solution.py:67
  80.3 50.7 %collective-permute-start.35 = (bf16[288,512]{1,0:T(8,128)(2,1)}, bf16[288,512]{1,0:T(8,128)(2,1)S(1)}, u32[]{:S(2)}, u32[]{:S(2)}) collective-permute-start(bf16[288,512]{1,0:T(8,128)(2,1)} %bitcast.312), channel_id=1, source_target_pairs={{0,4},{4,0},{8,12},{12,8},{16,20},{20,16},{24,28},{28,24},{1,5},{5... | collective-permute-start | bytes 884744 | tf_op jit(solution)/shard_map/ppermute | solution.py:68
  91.0 45.8 %collective-permute-start.52 = (bf16[288,1152]{1,0:T(8,128)(2,1)S(1)}, bf16[288,1152]{1,0:T(8,128)(2,1)}, u32[]{:S(2)}, u32[]{:S(2)}) collective-permute-start(bf16[288,1152]{1,0:T(8,128)(2,1)S(1)} %copy-done.61), channel_id=1, source_target_pairs={{0,8},{4,12},{8,0},{12,4},{16,24},{20,28},{24,16},{28,20},{1,9},{5... | collective-permute-start | bytes 1990664 | tf_op jit(solution)/shard_map/ppermute | solution.py:68
  101.8 37.0 %collective-permute-start.53 = (bf16[288,1152]{1,0:T(8,128)(2,1)}, bf16[288,1152]{1,0:T(8,128)(2,1)}, u32[]{:S(2)}, u32[]{:S(2)}) collective-permute-start(bf16[288,1152]{1,0:T(8,128)(2,1)} %get-tuple-element.50), channel_id=1, source_target_pairs={{0,16},{4,20},{8,24},{12,28},{16,0},{20,4},{24,8},{28,12},{1,17},{... | collective-permute-start | bytes 1990664 | tf_op jit(solution)/shard_map/ppermute | solution.py:68
  131.0 101.0 %collective-permute-start.55 = (bf16[288,1152]{1,0:T(8,128)(2,1)}, bf16[288,1152]{1,0:T(8,128)(2,1)}, u32[]{:S(2)}, u32[]{:S(2)}) collective-permute-start(bf16[288,1152]{1,0:T(8,128)(2,1)} %get-tuple-element.50), channel_id=1, source_target_pairs={{0,4},{4,0},{8,12},{12,8},{16,20},{20,16},{24,28},{28,24},{1,5},{5... | collective-permute-start | bytes 1990664 | tf_op jit(solution)/shard_map/ppermute | solution.py:68
  136.9 137.7 %collective-permute-start.62 = (bf16[288,1152]{1,0:T(8,128)(2,1)}, bf16[288,1152]{1,0:T(8,128)(2,1)}, u32[]{:S(2)}, u32[]{:S(2)}) collective-permute-start(bf16[288,1152]{1,0:T(8,128)(2,1)} %get-tuple-element.52), channel_id=1, source_target_pairs={{0,4},{4,0},{8,12},{12,8},{16,20},{20,16},{24,28},{28,24},{1,5},{5... | collective-permute-start | bytes 1990664 | tf_op jit(solution)/shard_map/ppermute | solution.py:68
  138.9 49.5 %collective-permute-start.66 = (bf16[288,1152]{1,0:T(8,128)(2,1)S(1)}, bf16[288,1152]{1,0:T(8,128)(2,1)S(1)}, u32[]{:S(2)}, u32[]{:S(2)}) collective-permute-start(bf16[288,1152]{1,0:T(8,128)(2,1)S(1)} %copy-done.51), channel_id=1, source_target_pairs={{0,8},{4,12},{8,0},{12,4},{16,24},{20,28},{24,16},{28,20},{1,9},{5... | collective-permute-start | bytes 1990664 | tf_op jit(solution)/shard_map/ppermute | solution.py:68
  229.9 43.7 %collective-permute-start.61 = (bf16[288,1152]{1,0:T(8,128)(2,1)S(1)}, bf16[288,1152]{1,0:T(8,128)(2,1)S(1)}, u32[]{:S(2)}, u32[]{:S(2)}) collective-permute-start(bf16[288,1152]{1,0:T(8,128)(2,1)S(1)} %copy-done.59), channel_id=1, source_target_pairs={{0,16},{4,20},{8,24},{12,28},{16,0},{20,4},{24,8},{28,12},{1,17},{... | collective-permute-start | bytes 1990664 | tf_op jit(solution)/shard_map/ppermute | solution.py:68
  232.0 43.1 %collective-permute-start.26 = (bf16[512,512]{1,0:T(8,128)(2,1)S(1)}, bf16[512,512]{1,0:T(8,128)(2,1)S(1)}, u32[]{:S(2)}, u32[]{:S(2)}) collective-permute-start(bf16[512,512]{1,0:T(8,128)(2,1)S(1)} %get-tuple-element.147), channel_id=1, source_target_pairs={{0,8},{4,12},{8,0},{12,4},{16,24},{20,28},{24,16},{28,20},{1,9},{5... | collective-permute-start | bytes 1572872 | tf_op jit(solution)/shard_map/ppermute | solution.py:68
  237.5 46.5 %collective-permute-start.28 = (bf16[512,512]{1,0:T(8,128)(2,1)S(1)}, bf16[512,512]{1,0:T(8,128)(2,1)S(1)}, u32[]{:S(2)}, u32[]{:S(2)}) collective-permute-start(bf16[512,512]{1,0:T(8,128)(2,1)S(1)} %get-tuple-element.147), channel_id=1, source_target_pairs={{0,16},{4,20},{8,24},{12,28},{16,0},{20,4},{24,8},{28,12},{1,17},{... | collective-permute-start | bytes 1572872 | tf_op jit(solution)/shard_map/ppermute | solution.py:68
  238.4 47.6 %collective-permute-start.63 = (bf16[288,1152]{1,0:T(8,128)(2,1)S(1)}, bf16[288,1152]{1,0:T(8,128)(2,1)S(1)}, u32[]{:S(2)}, u32[]{:S(2)}) collective-permute-start(bf16[288,1152]{1,0:T(8,128)(2,1)S(1)} %copy-done.59), channel_id=1, source_target_pairs={{0,4},{4,0},{8,12},{12,8},{16,20},{20,16},{24,28},{28,24},{1,5},{5... | collective-permute-start | bytes 1990664 | tf_op jit(solution)/shard_map/ppermute | solution.py:68
  274.5 58.1 %collective-permute-start.69 = (bf16[288,1152]{1,0:T(8,128)(2,1)S(1)}, bf16[288,1152]{1,0:T(8,128)(2,1)S(1)}, u32[]{:S(2)}, u32[]{:S(2)}) collective-permute-start(bf16[288,1152]{1,0:T(8,128)(2,1)S(1)} %copy-done.50), channel_id=1, source_target_pairs={{0,4},{4,0},{8,12},{12,8},{16,20},{20,16},{24,28},{28,24},{1,5},{5... | collective-permute-start | bytes 1990664 | tf_op jit(solution)/shard_map/ppermute | solution.py:68
  578.1 73.1 %collective-permute-start.150 = (bf16[288,1152]{1,0:T(8,128)(2,1)S(1)}, bf16[288,1152]{1,0:T(8,128)(2,1)S(1)}, u32[]{:S(2)}, u32[]{:S(2)}) collective-permute-start(bf16[288,1152]{1,0:T(8,128)(2,1)S(1)} %get-tuple-element.67), channel_id=1, source_target_pairs={{0,4},{4,0},{8,12},{12,8},{16,20},{20,16},{24,28},{28,24},{1,5},{5... | collective-permute-start | bytes 1990664 | tf_op jit(solution)/shard_map/ppermute | solution.py:68
  588.0 78.2 %collective-permute-start.157 = (bf16[288,1152]{1,0:T(8,128)(2,1)S(1)}, bf16[288,1152]{1,0:T(8,128)(2,1)S(1)}, u32[]{:S(2)}, u32[]{:S(2)}) collective-permute-start(bf16[288,1152]{1,0:T(8,128)(2,1)S(1)} %get-tuple-element.61), channel_id=1, source_target_pairs={{0,4},{4,0},{8,12},{12,8},{16,20},{20,16},{24,28},{28,24},{1,5},{5... | collective-permute-start | bytes 1990664 | tf_op jit(solution)/shard_map/ppermute | solution.py:68
  590.3 59.9 %collective-permute-start.145 = (bf16[288,1152]{1,0:T(8,128)(2,1)S(1)}, bf16[288,1152]{1,0:T(8,128)(2,1)S(1)}, u32[]{:S(2)}, u32[]{:S(2)}) collective-permute-start(bf16[288,1152]{1,0:T(8,128)(2,1)S(1)} %get-tuple-element.76), channel_id=1, source_target_pairs={{0,16},{4,20},{8,24},{12,28},{16,0},{20,4},{24,8},{28,12},{1,17},{... | collective-permute-start | bytes 1990664 | tf_op jit(solution)/shard_map/ppermute | solution.py:68
  591.8 72.6 %collective-permute-start.152 = (bf16[288,1152]{1,0:T(8,128)(2,1)S(1)}, bf16[288,1152]{1,0:T(8,128)(2,1)S(1)}, u32[]{:S(2)}, u32[]{:S(2)}) collective-permute-start(bf16[288,1152]{1,0:T(8,128)(2,1)S(1)} %get-tuple-element.70), channel_id=1, source_target_pairs={{0,16},{4,20},{8,24},{12,28},{16,0},{20,4},{24,8},{28,12},{1,17},{... | collective-permute-start | bytes 1990664 | tf_op jit(solution)/shard_map/ppermute | solution.py:68
  593.7 84.4 %collective-permute-start.159 = (bf16[288,1152]{1,0:T(8,128)(2,1)S(1)}, bf16[288,1152]{1,0:T(8,128)(2,1)S(1)}, u32[]{:S(2)}, u32[]{:S(2)}) collective-permute-start(bf16[288,1152]{1,0:T(8,128)(2,1)S(1)} %get-tuple-element.64), channel_id=1, source_target_pairs={{0,16},{4,20},{8,24},{12,28},{16,0},{20,4},{24,8},{28,12},{1,17},{... | collective-permute-start | bytes 1990664 | tf_op jit(solution)/shard_map/ppermute | solution.py:68
  650.1 40.5 %collective-permute-start.99 = (bf16[128,2304]{1,0:T(8,128)(2,1)S(1)}, bf16[128,2304]{1,0:T(8,128)(2,1)S(1)}, u32[]{:S(2)}, u32[]{:S(2)}) collective-permute-start(bf16[128,2304]{1,0:T(8,128)(2,1)S(1)} %get-tuple-element.78), channel_id=1, source_target_pairs={{0,8},{4,12},{8,0},{12,4},{16,24},{20,28},{24,16},{28,20},{1,9},{5... | collective-permute-start | bytes 1769480 | tf_op jit(solution)/shard_map/ppermute | solution.py:68
  651.2 39.5 %collective-permute-start.96 = (bf16[128,2304]{1,0:T(8,128)(2,1)S(1)}, bf16[128,2304]{1,0:T(8,128)(2,1)S(1)}, u32[]{:S(2)}, u32[]{:S(2)}) collective-permute-start(bf16[128,2304]{1,0:T(8,128)(2,1)S(1)} %get-tuple-element.79), channel_id=1, source_target_pairs={{0,2},{1,3},{2,0},{3,1},{4,6},{5,7},{6,4},{7,5},{8,10},{9,11},{10,... | collective-permute-start | bytes 1769480 | tf_op jit(solution)/shard_map/ppermute | solution.py:67
  678.1 50.5 %collective-permute-start.147 = (bf16[288,1152]{1,0:T(8,128)(2,1)}, bf16[288,1152]{1,0:T(8,128)(2,1)}, u32[]{:S(2)}, u32[]{:S(2)}) collective-permute-start(bf16[288,1152]{1,0:T(8,128)(2,1)} %get-tuple-element.65), channel_id=1, source_target_pairs={{0,4},{4,0},{8,12},{12,8},{16,20},{20,16},{24,28},{28,24},{1,5},{5... | collective-permute-start | bytes 1990664 | tf_op jit(solution)/shard_map/ppermute | solution.py:68
  690.7 80.0 %collective-permute-start.154 = (bf16[288,1152]{1,0:T(8,128)(2,1)}, bf16[288,1152]{1,0:T(8,128)(2,1)}, u32[]{:S(2)}, u32[]{:S(2)}) collective-permute-start(bf16[288,1152]{1,0:T(8,128)(2,1)} %get-tuple-element.59), channel_id=1, source_target_pairs={{0,4},{4,0},{8,12},{12,8},{16,20},{20,16},{24,28},{28,24},{1,5},{5... | collective-permute-start | bytes 1990664 | tf_op jit(solution)/shard_map/ppermute | solution.py:68
  699.4 66.1 %collective-permute-start.149 = (bf16[288,1152]{1,0:T(8,128)(2,1)}, bf16[288,1152]{1,0:T(8,128)(2,1)S(1)}, u32[]{:S(2)}, u32[]{:S(2)}) collective-permute-start(bf16[288,1152]{1,0:T(8,128)(2,1)} %get-tuple-element.69), channel_id=1, source_target_pairs={{0,16},{4,20},{8,24},{12,28},{16,0},{20,4},{24,8},{28,12},{1,17},{... | collective-permute-start | bytes 1990664 | tf_op jit(solution)/shard_map/ppermute | solution.py:68
  723.1 56.6 %collective-permute-start.156 = (bf16[288,1152]{1,0:T(8,128)(2,1)}, bf16[288,1152]{1,0:T(8,128)(2,1)S(1)}, u32[]{:S(2)}, u32[]{:S(2)}) collective-permute-start(bf16[288,1152]{1,0:T(8,128)(2,1)} %get-tuple-element.63), channel_id=1, source_target_pairs={{0,16},{4,20},{8,24},{12,28},{16,0},{20,4},{24,8},{28,12},{1,17},{... | collective-permute-start | bytes 1990664 | tf_op jit(solution)/shard_map/ppermute | solution.py:68
  723.2 43.0 %collective-permute-start.153 = (bf16[288,1152]{1,0:T(8,128)(2,1)}, bf16[288,1152]{1,0:T(8,128)(2,1)S(1)}, u32[]{:S(2)}, u32[]{:S(2)}) collective-permute-start(bf16[288,1152]{1,0:T(8,128)(2,1)} %add_convert_fusion.3), channel_id=1, source_target_pairs={{0,8},{4,12},{8,0},{12,4},{16,24},{20,28},{24,16},{28,20},{1,9},{5... | collective-permute-start | bytes 1990664 | tf_op jit(solution)/shard_map/ppermute | solution.py:68
  728.7 54.5 %collective-permute-start.160 = (bf16[288,1152]{1,0:T(8,128)(2,1)S(1)}, bf16[288,1152]{1,0:T(8,128)(2,1)S(1)}, u32[]{:S(2)}, u32[]{:S(2)}) collective-permute-start(bf16[288,1152]{1,0:T(8,128)(2,1)S(1)} %copy-done.62), channel_id=1, source_target_pairs={{0,8},{4,12},{8,0},{12,4},{16,24},{20,28},{24,16},{28,20},{1,9},{5... | collective-permute-start | bytes 1990664 | tf_op jit(solution)/shard_map/ppermute | solution.py:68
  827.8 51.8 %collective-permute-start.104 = (bf16[512,512]{1,0:T(8,128)(2,1)S(1)}, bf16[512,512]{1,0:T(8,128)(2,1)S(1)}, u32[]{:S(2)}, u32[]{:S(2)}) collective-permute-start(bf16[512,512]{1,0:T(8,128)(2,1)S(1)} %copy-done.63), channel_id=1, source_target_pairs={{0,4},{4,0},{8,12},{12,8},{16,20},{20,16},{24,28},{28,24},{1,5},{5... | collective-permute-start | bytes 1572872 | tf_op jit(solution)/shard_map/ppermute | solution.py:68
  853.3 43.0 %collective-permute-start.106 = (bf16[512,512]{1,0:T(8,128)(2,1)S(1)}, bf16[512,512]{1,0:T(8,128)(2,1)S(1)}, u32[]{:S(2)}, u32[]{:S(2)}) collective-permute-start(bf16[512,512]{1,0:T(8,128)(2,1)S(1)} %get-tuple-element.101), channel_id=1, source_target_pairs={{0,16},{4,20},{8,24},{12,28},{16,0},{20,4},{24,8},{28,12},{1,17},{... | collective-permute-start | bytes 1572872 | tf_op jit(solution)/shard_map/ppermute | solution.py:68
  856.3 40.0 %collective-permute-start.110 = (bf16[512,512]{1,0:T(8,128)(2,1)S(1)}, bf16[512,512]{1,0:T(8,128)(2,1)S(1)}, u32[]{:S(2)}, u32[]{:S(2)}) collective-permute-start(bf16[512,512]{1,0:T(8,128)(2,1)S(1)} %add_convert_fusion.14), channel_id=1, source_target_pairs={{0,8},{4,12},{8,0},{12,4},{16,24},{20,28},{24,16},{28,20},{1,9},{5... | collective-permute-start | bytes 1572872 | tf_op jit(solution)/shard_map/ppermute | solution.py:68
  859.0 56.8 %collective-permute-start.115 = (bf16[288,512]{1,0:T(8,128)(2,1)}, bf16[288,512]{1,0:T(8,128)(2,1)}, u32[]{:S(2)}, u32[]{:S(2)}) collective-permute-start(bf16[288,512]{1,0:T(8,128)(2,1)} %get-tuple-element.117), channel_id=1, source_target_pairs={{0,4},{4,0},{8,12},{12,8},{16,20},{20,16},{24,28},{28,24},{1,5},{5... | collective-permute-start | bytes 884744 | tf_op jit(solution)/shard_map/ppermute | solution.py:68
  (241 other events, 5869.4 us)

commit v2 on v1

v2 whole, which is shorter than its diff:
```python
import functools
import math

import jax
import jax.numpy as jnp
from jax import lax
from jax.experimental import pallas as pl
from jax.experimental.pallas import tpu as pltpu
from jax.sharding import PartitionSpec as P

H = 8
KVH = 4
HD = 256

norm_eps = 1e-06
cap_value = 50.0
theta_base = 10000.0
f32 = jnp.float32
bf16 = jnp.bfloat16


def inverse_rms(value):
    return lax.rsqrt(jnp.mean(value * value, axis=-1, keepdims=True) + norm_eps)


def rms_back(value, scale, grad):
    inverse = inverse_rms(value)
    scaled = grad * scale
    inner = jnp.mean(scaled * value, axis=-1, keepdims=True)
    grad_value = inverse * scaled - value * (inverse * inverse * inverse) * inner
    grad_scale = jnp.sum(grad * value * inverse, axis=0, keepdims=True)
    return (grad_value, grad_scale)


def rotation(position):
    entry = jnp.arange(HD, dtype=jnp.int32)
    quarter = HD // 4
    pair_index = entry // (2 * quarter) * quarter + entry % quarter
    frequency = jnp.power(theta_base, -2.0 * pair_index.astype(f32) / HD)
    angles = position.astype(f32)[:, None] * frequency[None, :]
    sign = jnp.where(entry % (2 * quarter) < quarter, -1.0, 1.0)
    return jnp.cos(angles), jnp.sin(angles) * sign[None, :]


def rotated(value, cosine, sine, sign):
    half = HD // 2
    parts = []
    for at in range(0, HD, half):
        piece = value[:, at : at + half]
        partner = pltpu.roll(piece, half // 2, 1)
        parts.append(piece * cosine[:, at : at + half] + partner * (sign * sine[:, at : at + half]))
    return jnp.concatenate(parts, 1)


def swap(value, axis):
    blk_mask, head_mask = axis
    block_count, head_count = lax.axis_size("blk"), lax.axis_size("head")
    if blk_mask == 0:
        return lax.ppermute(value, "head", [(i, i ^ head_mask) for i in range(head_count)])
    return lax.ppermute(value, "blk", [(i, i ^ blk_mask) for i in range(block_count)])


def bits(count):
    return [1 << i for i in range(count.bit_length() - 1)]


def route(subset, total, light):
    members = [i for i in range(total) if subset >> i & 1]
    if light and len(members) > 1 and members[-1] == total - 1:
        members = members[:-1]
        return members if len(members) == total - 1 else members[:1]
    if len(members) >= 2 and len(members) == total - light:
        return members
    if not light and len(members) == 2 and members[1] - members[0] != 1:
        return members[1:]
    return members[:1]


def hops(total, light):
    size = lambda t: bin(t).count("1")
    last = 1 << (total - 1)
    subsets = range(1, 1 << total)
    if not light:
        return [[t for t in subsets if size(t) == n] for n in range(1, total + 1)]
    result = [[t for t in subsets if size(t) == 1]]
    for high in (0, last):
        for n in range(2, total + 1):
            result.append([t for t in subsets if size(t) == n and t & last == high])
    return [hop for hop in result if hop]


def shares(row_total, parts):
    unit = row_total // 16
    cuts = [unit * i // parts * 16 for i in range(parts + 1)]
    cuts[-1] = row_total
    return list(zip(cuts[:-1], cuts[1:]))


def gather_hop(parts, axes, light, subsets, before=()):
    rows = parts[0][0].shape[0]
    came = {}
    for subset in subsets:
        ways = route(subset, len(axes), light)
        cuts = shares(rows, len(ways)) if len(ways) > 1 else [(0, rows)]
        came[subset] = []
        for way, (low, high) in zip(ways, cuts):
            source = parts[subset ^ (1 << way)][0]
            came[subset].append(swap(tie(source[low:high] if len(ways) > 1 else source, *before), axes[way]))
    return came


def gather_rows(value, axes, light=False, parts=None):
    last = 1 << (len(axes) - 1)
    parts, before = parts or {0: [value]}, ()
    for subsets in hops(len(axes), light):
        if subsets[0] in parts:
            continue
        if light and last in parts:
            before = [x for x in before if x is not parts[last][0]]
            before += parts[last] * any(t & last for t in subsets)
        came = gather_hop(parts, axes, light, subsets, before)
        parts = parts | came
        before = [part for pieces in came.values() for part in pieces]
    return parts


def join_kernel(plan, *refs):
    step = pl.program_id(0)
    out = refs[-1]
    for at, (slot, first, rows) in enumerate(plan):

        @pl.when(step == slot)
        def _():
            out[first : first + rows, :] = refs[at][...]


def join_rows(parts):
    plan, arrays = [], []
    for slot in sorted(parts):
        first = 0
        for array in parts[slot]:
            plan.append((slot, first, array.shape[0]))
            arrays.append(array)
            first += array.shape[0]
    rows, columns = parts[0][0].shape
    return pl.pallas_call(
        functools.partial(join_kernel, plan),
        grid=(len(parts),),
        in_specs=[pl.BlockSpec(a.shape, lambda m: (0, 0), pipeline_mode=pl.Buffered(1)) for a in arrays],
        out_specs=pl.BlockSpec((rows, columns), lambda m: (m, 0)),
        out_shape=jax.ShapeDtypeStruct((len(parts) * rows, columns), arrays[0].dtype),
        compiler_params=pltpu.CompilerParams(vmem_limit_bytes=32 * 1024 * 1024),
        cost_estimate=pl.CostEstimate(flops=0, bytes_accessed=4 * len(parts) * rows * columns, transcendentals=0),
        name="join_rows",
    )(*arrays)


def two_products_kernel(a_ref, u_ref, b_ref, v_ref, out_ref):
    nt = (((1,), (1,)), ((), ()))
    total = lax.dot_general(a_ref[...], u_ref[...], nt, preferred_element_type=f32)
    total += lax.dot_general(b_ref[...], v_ref[...], nt, preferred_element_type=f32)
    out_ref[...] = total.astype(out_ref.dtype)


def two_products(a, u, b, v):
    rows, depth = a.shape
    columns = u.shape[0]
    step = 256
    resident = pl.BlockSpec((rows, depth), lambda n: (0, 0), pipeline_mode=pl.Buffered(1))
    return pl.pallas_call(
        two_products_kernel,
        grid=(columns // step,),
        in_specs=[resident, pl.BlockSpec((step, depth), lambda n: (n, 0))] * 2,
        out_specs=pl.BlockSpec((rows, step), lambda n: (0, n)),
        out_shape=jax.ShapeDtypeStruct((rows, columns), bf16),
        compiler_params=pltpu.CompilerParams(vmem_limit_bytes=40 * 1024 * 1024),
        cost_estimate=pl.CostEstimate(
            flops=4 * rows * columns * depth,
            bytes_accessed=4 * (rows * depth + columns * depth) + 2 * rows * columns,
            transcendentals=0,
        ),
        name="two_products",
    )(a, u, b, v)


def joined(left, right):
    return (left.astype(f32) + right.astype(f32)).astype(bf16)


def scatter_plan(total, light):
    plan = [list(hop) for hop in hops(total, light)[::-1]]
    last = 1 << (total - 1)
    if light:
        plan[-1].remove(last)
        plan[next(i for i, hop in enumerate(plan) if not any(t & last for t in hop))].append(last)
    return plan


def scatter_hop(pieces, axes, light, subsets, before=(), beside=None):
    last = 1 << (len(axes) - 1)
    pieces = dict(pieces)
    rows = pieces[0][0].shape[0]
    sent, result = [], None
    for subset in subsets:
        (piece,) = pieces.pop(subset)
        ways = route(subset, len(axes), light)
        cuts = shares(rows, len(ways)) if len(ways) > 1 else [(0, rows)]
        for way, (low, high) in zip(ways, cuts):
            part = piece if len(ways) == 1 else piece[low:high]
            sent.append((subset, subset ^ (1 << way), low, high, swap(tie(part, *before), axes[way])))
    if beside:
        result, came = beside([item[4] for item in sent])
        sent = [item[:4] + (moved,) for item, moved in zip(sent, came)]
    for subset, target, low, high, moved in sent:
        if target == 0:
            pieces[0] = pieces[0] + [moved]
        elif high - low == rows:
            pieces[target] = [joined(pieces[target][0], moved)]
        else:
            old = pieces[target][0]
            cut = [old[:low], joined(old[low:high], moved), old[high:]]
            pieces[target] = [jnp.concatenate([c for c in cut if c.shape[0]], 0)]
    came = [item[4] for item in sent if not (light and item[0] == last)]
    return pieces, came, result


def scatter_rows(pieces, axes, light=False):
    pieces, came = {t: [piece] for t, piece in enumerate(pieces)}, ()
    for subsets in scatter_plan(len(axes), light):
        pieces, came, _ = scatter_hop(pieces, axes, light, subsets, came)
    return pieces[0]


def tie(value, *after):
    return lax.optimization_barrier((value, *after))[0] if after else value


def tie_all(held, *after):
    return {mask: tie(block, *after) for mask, block in held.items()}


def scale_kernel(count, index_ref, *refs):
    step = pl.program_id(0)
    for at in range(count):

        @pl.when(step == at)
        def _():
            refs[count][...] = refs[at][...]


def place_scales(held, rows, block_index):
    count = len(held)
    shape = (16, held[0].shape[1])
    return pl.pallas_call(
        functools.partial(scale_kernel, count),
        grid_spec=pltpu.PrefetchScalarGridSpec(
            num_scalar_prefetch=1,
            grid=(count,),
            in_specs=[pl.BlockSpec(shape, lambda m, b: (rows // 16, 0), pipeline_mode=pl.Buffered(1))] * count,
            out_specs=pl.BlockSpec(shape, lambda m, b: (b[0] ^ m, 0)),
        ),
        out_shape=jax.ShapeDtypeStruct((count * 16, shape[1]), bf16),
        cost_estimate=pl.CostEstimate(flops=0, bytes_accessed=4 * count * 16 * shape[1], transcendentals=0),
        name="place_scales",
    )(block_index[None].astype(jnp.int32), *[held[mask] for mask in range(count)])


def placed_kernel(body, plans, counts, steps, index_ref, *refs):
    refs = list(refs)
    arrays, inputs, outs, wholes, weights = [[refs.pop(0) for _ in range(count)] for count in counts]
    in_sems, out_sems = refs
    step = pl.program_id(0)
    came, at = [], 0
    for weight, plan in zip(weights, plans):
        copies = []
        rows = weight.shape[0] // len(plan)
        for mask, (source, column) in enumerate(plan):
            row = pl.multiple_of((index_ref[0] ^ mask) * rows, 16)
            block = arrays[source].at[pl.ds(0, rows)]
            if arrays[source].shape[1] != weight.shape[1]:
                block = arrays[source].at[pl.ds(0, rows), pl.ds(column, weight.shape[1])]
            copies.append(pltpu.make_async_copy(block, weight.at[pl.ds(row, rows)], in_sems.at[at]))
            at += 1
        came.append(copies)
    gone = [
        pltpu.make_async_copy(weight, whole, out_sems.at[n]) for n, (weight, whole) in enumerate(zip(weights, wholes))
    ]

    @pl.when(step == 0)
    def _():
        for copies in came:
            for copy in copies:
                copy.start()
        for copies, copy_out in zip(came, gone):
            for copy in copies:
                copy.wait()
            copy_out.start()

    body(step, inputs, outs, weights)

    @pl.when(step == steps - 1)
    def _():
        for copy_out in gone:
            copy_out.wait()


def placed(body, steps, held, columns, inputs, in_specs, outs, out_specs, block_index, name, flops):
    arrays, plans = [], []
    for blocks, width in zip(held, columns):
        plan = []
        for mask in range(len(blocks)):
            array, column = blocks[mask]
            if width % 128 or column % 128:
                array, column = array[:, column : column + width], 0
            where = next((n for n, known in enumerate(arrays) if known is array), len(arrays))
            if where == len(arrays):
                arrays.append(array)
            plan.append((where, column))
        plans.append(plan)
    rows = min(array.shape[0] for array in arrays) // 16 * 16
    rows = rows - (16 if name == "key_rows" else 0)
    shapes = [(len(plan) * rows, width) for plan, width in zip(plans, columns)]
    anywhere = pl.BlockSpec(memory_space=pl.ANY)
    counts = (len(arrays), len(inputs), len(outs), len(plans), len(plans))
    return pl.pallas_call(
        functools.partial(placed_kernel, body, plans, counts, steps),
        grid_spec=pltpu.PrefetchScalarGridSpec(
            num_scalar_prefetch=1,
            grid=(steps,),
            in_specs=[anywhere] * len(arrays) + in_specs,
            out_specs=out_specs + [anywhere] * len(plans),
            scratch_shapes=[pltpu.VMEM(shape, bf16) for shape in shapes]
            + [
                pltpu.SemaphoreType.DMA((sum(len(plan) for plan in plans),)),
                pltpu.SemaphoreType.DMA((len(plans),)),
            ],
        ),
        out_shape=outs + [jax.ShapeDtypeStruct(shape, bf16) for shape in shapes],
        compiler_params=pltpu.CompilerParams(vmem_limit_bytes=56 * 1024 * 1024),
        cost_estimate=pl.CostEstimate(
            flops=flops, bytes_accessed=4 * sum(h * w for h, w in shapes), transcendentals=0
        ),
        name=name,
    )(block_index[None].astype(jnp.int32), *arrays, *inputs)


def in_turn(held):
    came = []
    for block in held.values():
        came.append(swap(tie(block, *came[-2:-1]), (1, 0)))
    return dict(zip(held, came))


def both_cores(held):
    return held | {mask ^ 1: swap(block, (1, 0)) for mask, block in held.items()}


def pick(value, dim, index):
    return lax.dynamic_index_in_dim(value, index, dim, keepdims=False)


def plus(left, right):
    return left.astype(f32) + right.astype(f32)


def whole_call(body, outs, *inputs, name):
    size = sum(x.size * x.dtype.itemsize for x in inputs)
    return pl.pallas_call(
        body,
        out_shape=[jax.ShapeDtypeStruct(shape, dtype) for shape, dtype in outs],
        compiler_params=pltpu.CompilerParams(vmem_limit_bytes=40 * 1024 * 1024),
        cost_estimate=pl.CostEstimate(flops=0, bytes_accessed=2 * size, transcendentals=0),
        name=name,
    )(*inputs)


def summed(refs):
    total = refs[0][...].astype(f32)
    for ref in refs[1:]:
        total = total + ref[...].astype(f32)
    return total


def norm_full_kernel(count, *refs):
    parts, (scale, normed, inverse) = refs[:count], refs[count:]
    first = 0
    for part in parts:
        value = part[...].astype(f32)
        here = slice(first, first + part.shape[0])
        first += part.shape[0]
        factor = inverse_rms(value)
        inverse[here, :] = factor
        normed[here, :] = (value * factor * scale[0:1, :]).astype(bf16)


def after_attention_kernel(count, *refs):
    terms, (hidden, scales, attn_out, resid_out, ffn_in) = refs[:count], refs[count:]
    attn = summed(terms)
    attn_out[...] = attn
    resid = hidden[...].astype(f32) + attn * inverse_rms(attn) * scales[1:2, :]
    resid_out[...] = resid
    ffn_in[...] = (resid * inverse_rms(resid) * scales[2:3, :]).astype(bf16)


def after_ffn_kernel(count, *refs):
    terms, (resid, out_grad, scales, layer_out, grad_out, grad_scale) = refs[:count], refs[count:]
    ffn_out = summed(terms)
    grad, grad_scale[...] = rms_back(ffn_out, scales[3:4, :], out_grad[...].astype(f32))
    grad_out[...] = grad.astype(bf16)
    layer_out[...] = (resid[...] + ffn_out * inverse_rms(ffn_out) * scales[3:4, :]).astype(bf16)


def after_ffn_back_kernel(count, *refs):
    terms, (resid, attn, out_grad, scales, grad_resid, grad_attn, grad_scale2, grad_scale1) = refs[:count], refs[count:]
    grad, grad_scale2[...] = rms_back(resid[...], scales[2:3, :], summed(terms))
    grad = out_grad[...].astype(f32) + grad
    grad_resid[...] = grad
    back, grad_scale1[...] = rms_back(attn[...], scales[1:2, :], grad)
    grad_attn[...] = back.astype(bf16)


def after_all_kernel(count, *refs):
    terms, (hidden, grad_resid, scales, grad_in) = refs[:count], refs[count:]
    grad, _ = rms_back(hidden[...].astype(f32), scales[0:1, :], summed(terms))
    grad_in[...] = grad_resid[...] + grad


def key_value_grad_kernel(kept, came, cosine, sine, out):
    total = kept[...].astype(f32) + came[...].astype(f32)
    out[:, :HD] = rotated(total[:, :HD], cosine[...], sine[...], -1.0).astype(bf16)
    out[:, HD:] = total[:, HD:].astype(bf16)


def project(rows, held, columns, table, turning, block_index, name):
    count, depth = rows.shape
    heads = columns[0] // HD
    fixed = lambda n, b: (0, 0)
    once = pl.Buffered(1)

    def body(step, inputs, outs, weights):
        rows_ref, cosine_ref, sine_ref = inputs
        (out_ref,) = outs
        here = pl.ds(pl.multiple_of(step * HD, HD), HD)
        value = jnp.dot(rows_ref[...], weights[0][:, here], preferred_element_type=f32)

        @pl.when(step < turning)
        def _():
            out_ref[...] = rotated(value, cosine_ref[...], sine_ref[...], 1.0).astype(bf16)

        @pl.when(step >= turning)
        def _():
            out_ref[...] = value.astype(bf16)

    return placed(
        body,
        heads,
        held,
        columns,
        [rows, *table],
        [
            pl.BlockSpec((count, depth), fixed, pipeline_mode=once),
            pl.BlockSpec((count, HD), fixed, pipeline_mode=once),
            pl.BlockSpec((count, HD), fixed, pipeline_mode=once),
        ],
        [jax.ShapeDtypeStruct((count, columns[0]), bf16)],
        [pl.BlockSpec((count, HD), lambda n, b: (0, n))],
        block_index,
        name,
        2 * rows.size * columns[0],
    )


def hidden_units(rows, held, width, block_index):
    count, depth = rows.shape
    step = 256

    def body(number, inputs, outs, weights):
        hidden_ref, active_ref, slope_ref = outs
        gate = jnp.dot(inputs[0][...], weights[0][...], preferred_element_type=f32)
        up = jnp.dot(inputs[0][...], weights[1][...], preferred_element_type=f32)
        inner = math.sqrt(2.0 / math.pi)
        square = gate * gate
        tangent = jnp.tanh(inner * gate * (1.0 + 0.044715 * square))
        share = 0.5 * (1.0 + tangent)
        active = gate * share
        slope = share + (0.5 * inner) * gate * (1.0 - tangent * tangent) * (1.0 + (3 * 0.044715) * square)
        hidden_ref[...] = (active * up).astype(bf16)
        active_ref[...] = active
        slope_ref[...] = slope * up

    return placed(
        body,
        count // step,
        held,
        [width, width],
        [rows],
        [pl.BlockSpec((step, depth), lambda n, b: (n, 0))],
        [jax.ShapeDtypeStruct((count, width), dtype) for dtype in (bf16, f32, f32)],
        [pl.BlockSpec((step, width), lambda n, b: (n, 0))] * 3,
        block_index,
        "hidden_units",
        4 * rows.size * width,
    )


def down_rows(hidden, held, block_index):
    count, width = hidden.shape
    depth = len(held) * held[0][0].shape[0]
    step = 768 if depth % 768 == 0 else 256

    def body(number, inputs, outs, weights):
        here = pl.ds(pl.multiple_of(number * step, step), step)
        value = lax.dot_general(
            inputs[0][...], weights[0][here, :], (((1,), (1,)), ((), ())), preferred_element_type=f32
        )
        outs[0][...] = value.astype(bf16)

    return placed(
        body,
        depth // step,
        [held],
        [width],
        [hidden],
        [pl.BlockSpec((count, width), lambda n, b: (0, 0), pipeline_mode=pl.Buffered(1))],
        [jax.ShapeDtypeStruct((count, depth), bf16)],
        [pl.BlockSpec((count, step), lambda n, b: (0, n))],
        block_index,
        "down_rows",
        2 * hidden.size * depth,
    )


def outer_kernel(*refs):
    pairs, out = refs[:-1], refs[-1]
    width = 0
    for left, right in zip(pairs[::2], pairs[1::2]):
        columns = right.shape[1]
        value = lax.dot_general(left[...], right[...], (((0,), (0,)), ((), ())), preferred_element_type=f32)
        out[:, width : width + columns] = value.astype(bf16)
        width += columns


def outer(*pairs):
    rows, depth = pairs[0][0].shape
    width = sum(right.shape[1] for _, right in pairs)
    step = depth // 2
    specs = []
    for _, right in pairs:
        specs.append(pl.BlockSpec((rows, step), lambda n: (0, n)))
        specs.append(pl.BlockSpec(right.shape, lambda n: (0, 0), pipeline_mode=pl.Buffered(1)))
    return pl.pallas_call(
        outer_kernel,
        grid=(depth // step,),
        in_specs=specs,
        out_specs=pl.BlockSpec((step, width), lambda n: (n, 0)),
        out_shape=jax.ShapeDtypeStruct((depth, width), bf16),
        compiler_params=pltpu.CompilerParams(vmem_limit_bytes=40 * 1024 * 1024),
        cost_estimate=pl.CostEstimate(
            flops=2 * rows * depth * width, bytes_accessed=2 * (rows * depth * len(pairs) + depth * width), transcendentals=0
        ),
        name="outer",
    )(*[x for pair in pairs for x in pair])


def normed_back_kernel(count, q_ref, wq_ref, kv_ref, wkv_ref, inverse_ref, *refs):
    hidden, (out_ref, scale_ref) = refs[:count], refs[count:]
    nt = (((1,), (1,)), ((), ()))
    total = lax.dot_general(q_ref[...], wq_ref[...], nt, preferred_element_type=f32)
    total += lax.dot_general(kv_ref[...], wkv_ref[...], nt, preferred_element_type=f32)
    out_ref[...] = total.astype(bf16)
    grad_scale, first = jnp.zeros((1, total.shape[1]), f32), 0
    for part in hidden:
        here = slice(first, first + part.shape[0])
        first += part.shape[0]
        unit = part[...].astype(f32) * inverse_ref[here, :]
        grad_scale += jnp.sum(total[here, :] * unit, axis=0, keepdims=True)
    scale_ref[...] = grad_scale


def normed_back(grad_query, query_weight, grad_kv, kv_weight, inverse, hidden):
    rows, width = grad_query.shape
    kv_width = grad_kv.shape[1]
    columns = query_weight.shape[0]
    step = 768 if columns % 768 == 0 else 256
    fixed = lambda n: (0, 0)
    once = pl.Buffered(1)
    return pl.pallas_call(
        functools.partial(normed_back_kernel, len(hidden)),
        grid=(columns // step,),
        in_specs=[
            pl.BlockSpec((rows, width), fixed, pipeline_mode=once),
            pl.BlockSpec((step, width), lambda n: (n, 0)),
            pl.BlockSpec((rows, kv_width), fixed, pipeline_mode=once),
            pl.BlockSpec((step, kv_width), lambda n: (n, 0)),
            pl.BlockSpec((rows, 1), fixed, pipeline_mode=once),
        ]
        + [pl.BlockSpec((part.shape[0], step), lambda n: (0, n)) for part in hidden],
        out_specs=[pl.BlockSpec((rows, step), lambda n: (0, n)), pl.BlockSpec((1, step), lambda n: (0, n))],
        out_shape=[jax.ShapeDtypeStruct((rows, columns), bf16), jax.ShapeDtypeStruct((1, columns), f32)],
        compiler_params=pltpu.CompilerParams(vmem_limit_bytes=40 * 1024 * 1024),
        cost_estimate=pl.CostEstimate(
            flops=2 * rows * columns * (width + kv_width), bytes_accessed=4 * rows * columns, transcendentals=0
        ),
        name="normed_back",
    )(grad_query, query_weight, grad_kv, kv_weight, inverse, *hidden)


def scores(query, key, score_scale):
    raw = lax.dot_general(query, key, (((1,), (1,)), ((), ())), preferred_element_type=f32)
    return jnp.tanh(raw * (score_scale / cap_value))


def load_pieces(step, pieces, kv_all, sems):
    copies = [pltpu.make_async_copy(piece, kv_all.at[at], sems.at[at]) for at, piece in enumerate(pieces)]

    @pl.when(step == 0)
    def _():
        for copy in copies:
            copy.start()

    for at, copy in enumerate(copies):

        @pl.when(step == 2 * at)
        def _():
            copy.wait()


def forward_kernel(group, span_len, tiles, spans_ref, q_ref, *refs):
    pieces, (mixed_ref, exact_ref, lse_ref, q_all, acc, total, kv_all, sems) = refs[: tiles // 2], refs[tiles // 2 :]
    step = pl.program_id(0)
    load_pieces(step, pieces, kv_all, sems)
    score_scale = 1.0 / math.sqrt(HD)
    rows = group * span_len

    @pl.when(step == 0)
    def _():
        for half in range(2):
            for g in range(group):
                q_all[half, g * span_len : (g + 1) * span_len, :] = q_ref[
                    half * span_len : (half + 1) * span_len, g * HD : (g + 1) * HD
                ]
        acc[...] = jnp.zeros_like(acc)
        total[...] = jnp.zeros_like(total)

    tile_span = spans_ref[step]
    here = pl.ds(pl.multiple_of((step % 2) * span_len, span_len), span_len)
    key = kv_all[step // 2, here, :HD]
    value = kv_all[step // 2, here, HD:]

    def visit(half, diagonal):
        weights = jnp.exp(cap_value * scores(q_all[half], key, score_scale))
        if diagonal:
            flip = spans_ref[tiles + 2]
            shape = (rows, span_len)
            q_pos = (lax.broadcasted_iota(jnp.int32, shape, 0) % span_len) ^ flip
            k_pos = lax.broadcasted_iota(jnp.int32, shape, 1) ^ flip
            weights = jnp.where(k_pos <= q_pos, weights, 0.0)
        part = weights[:, :128]
        for at in range(128, span_len, 128):
            part = part + weights[:, at : at + 128]
        total[half] += part
        acc[half] += jnp.dot(weights.astype(bf16), value, preferred_element_type=f32)

    for half in range(2):
        own = spans_ref[tiles + half]

        @pl.when(tile_span < own)
        def _():
            visit(half, False)

        @pl.when(tile_span == own)
        def _():
            visit(half, True)

    @pl.when(step == tiles - 1)
    def _():
        for half in range(2):
            sums = jnp.sum(total[half], axis=1, keepdims=True)
            exact = acc[half] / sums
            lse_ref[half] = jnp.log(jnp.sum(total[half].T, axis=0, keepdims=True))
            for g in range(group):
                piece = exact[g * span_len : (g + 1) * span_len]
                place = (slice(half * span_len, (half + 1) * span_len), slice(g * HD, (g + 1) * HD))
                exact_ref[place] = piece
                mixed_ref[place] = piece.astype(bf16)


def backward_kernel(group, span_len, tiles, spans_ref, q_ref, g_ref, exact_ref, lse_ref, cosine_ref, sine_ref, *refs):
    pieces, rest = refs[: tiles // 2], refs[tiles // 2 :]
    dq_ref, near_ref, far_ref, q_all, g_all, delta, dq_acc, kv_all, sems = rest
    step = pl.program_id(0)
    load_pieces(step, pieces, kv_all, sems)
    score_scale = 1.0 / math.sqrt(HD)
    rows = group * span_len

    @pl.when(step == 0)
    def _():
        for half in range(2):
            for g in range(group):
                place = (slice(half * span_len, (half + 1) * span_len), slice(g * HD, (g + 1) * HD))
                here = slice(g * span_len, (g + 1) * span_len)
                q_all[half, here, :] = q_ref[place]
                g_all[half, here, :] = g_ref[place]
                product = g_ref[place].astype(f32) * exact_ref[place]
                folded = product[:, :128] + product[:, 128:]
                delta[half, :, here] = jnp.sum(folded.T, axis=0, keepdims=True)
        dq_acc[...] = jnp.zeros_like(dq_acc)

    tile_span = spans_ref[step]
    here = pl.ds(pl.multiple_of((step % 2) * span_len, span_len), span_len)
    key = kv_all[step // 2, here, :HD]
    value = kv_all[step // 2, here, HD:]

    def visit(half, diagonal):
        query = q_all[half]
        grad = g_all[half]
        tangent = scores(key, query, score_scale)
        probability = jnp.exp(cap_value * tangent - lse_ref[half])
        if diagonal:
            flip = spans_ref[tiles + 2]
            shape = (span_len, rows)
            q_pos = (lax.broadcasted_iota(jnp.int32, shape, 1) % span_len) ^ flip
            k_pos = lax.broadcasted_iota(jnp.int32, shape, 0) ^ flip
            probability = jnp.where(k_pos <= q_pos, probability, 0.0)
        grad_prob = lax.dot_general(value, grad, (((1,), (1,)), ((), ())), preferred_element_type=f32)
        grad_raw = probability * (grad_prob - delta[half]) * ((1.0 - tangent * tangent) * score_scale)
        grad_raw = grad_raw.astype(bf16)
        dv = jnp.dot(probability.astype(bf16), grad, preferred_element_type=f32)
        dk = jnp.dot(grad_raw, query, preferred_element_type=f32)
        dq_acc[half] += lax.dot_general(grad_raw, key, (((0,), (0,)), ((), ())), preferred_element_type=f32)
        return dk, dv

    def put(dk, dv):
        @pl.when(step < tiles // 2)
        def _():
            near_ref[:, :HD] = dk.astype(bf16)
            near_ref[:, HD:] = dv.astype(bf16)

        @pl.when(step >= tiles // 2)
        def _():
            far_ref[:, :HD] = dk.astype(bf16)
            far_ref[:, HD:] = dv.astype(bf16)

    low, high = spans_ref[tiles], spans_ref[tiles + 1]
    first, second = tile_span <= low, tile_span <= high

    @pl.when(jnp.logical_not(jnp.logical_or(first, second)))
    def _():
        put(jnp.zeros((span_len, HD), f32), jnp.zeros((span_len, HD), f32))

    for half, own, other in ((0, low, high), (1, high, low)):
        for diagonal in (False, True):
            here = tile_span == own if diagonal else tile_span < own

            @pl.when(jnp.logical_and(here, tile_span > other))
            def _(half=half, diagonal=diagonal):
                put(*visit(half, diagonal))

    for half, own, other in ((0, low, high), (1, high, low)):
        for diagonal in (False, True):
            here = tile_span == own if diagonal else tile_span < own

            @pl.when(jnp.logical_and(here, own < other))
            def _(half=half, diagonal=diagonal):
                dk_low, dv_low = visit(half, diagonal)
                dk_high, dv_high = visit(1 - half, False)
                put(dk_low + dk_high, dv_low + dv_high)

    @pl.when(step == tiles - 1)
    def _():
        for half in range(2):
            for g in range(group):
                here = slice(half * span_len, (half + 1) * span_len)
                turned = rotated(
                    dq_acc[half, g * span_len : (g + 1) * span_len], cosine_ref[here, :], sine_ref[here, :], -1.0
                )
                dq_ref[here, g * HD : (g + 1) * HD] = turned.astype(bf16)


def attention_forward(spans, queries, pieces, span_len):
    tiles = 2 * len(pieces)
    kv_size = len(pieces) * pieces[0].size
    width = queries.shape[1]
    group = width // HD
    rows = group * span_len
    whole = lambda s, t: (0, 0)
    visits = tiles + 1
    return pl.pallas_call(
        functools.partial(forward_kernel, group, span_len, tiles),
        grid_spec=pltpu.PrefetchScalarGridSpec(
            num_scalar_prefetch=1,
            grid=(tiles,),
            in_specs=[
                pl.BlockSpec(queries.shape, whole),
            ]
            + [pl.BlockSpec(memory_space=pl.ANY)] * len(pieces),
            out_specs=[
                pl.BlockSpec(queries.shape, whole),
                pl.BlockSpec(queries.shape, whole),
                pl.BlockSpec((2, 1, rows), lambda s, t: (0, 0, 0)),
            ],
            scratch_shapes=[
                pltpu.VMEM((2, rows, HD), bf16),
                pltpu.VMEM((2, rows, HD), f32),
                pltpu.VMEM((2, rows, 128), f32),
                pltpu.VMEM((len(pieces),) + pieces[0].shape, bf16),
                pltpu.SemaphoreType.DMA((len(pieces),)),
            ],
        ),
        out_shape=[
            jax.ShapeDtypeStruct(queries.shape, bf16),
            jax.ShapeDtypeStruct(queries.shape, f32),
            jax.ShapeDtypeStruct((2, 1, rows), f32),
        ],
        compiler_params=pltpu.CompilerParams(vmem_limit_bytes=40 * 1024 * 1024),
        cost_estimate=pl.CostEstimate(
            flops=visits * rows * span_len * HD * 4,
            bytes_accessed=kv_size * 2 + queries.size * 12,
            transcendentals=visits * rows * span_len * 2,
        ),
        name="attention_forward",
    )(spans, queries, *pieces)


def attention_backward(spans, queries, grads, exact, lse, table, pieces, span_len):
    tiles = 2 * len(pieces)
    kv_size = len(pieces) * pieces[0].size
    width = queries.shape[1]
    group = width // HD
    rows = group * span_len
    whole = lambda s, t: (0, 0)
    visits = tiles + 1
    return pl.pallas_call(
        functools.partial(backward_kernel, group, span_len, tiles),
        grid_spec=pltpu.PrefetchScalarGridSpec(
            num_scalar_prefetch=1,
            grid=(tiles,),
            in_specs=[
                pl.BlockSpec(queries.shape, whole),
                pl.BlockSpec(queries.shape, whole),
                pl.BlockSpec(queries.shape, whole),
                pl.BlockSpec((2, 1, rows), lambda s, t: (0, 0, 0)),
                pl.BlockSpec(table[0].shape, whole),
                pl.BlockSpec(table[0].shape, whole),
            ]
            + [pl.BlockSpec(memory_space=pl.ANY)] * len(pieces),
            out_specs=[
                pl.BlockSpec(queries.shape, whole),
                pl.BlockSpec((span_len, 2 * HD), lambda s, t: (jnp.minimum(s, tiles // 2 - 1), 0)),
                pl.BlockSpec((span_len, 2 * HD), lambda s, t: (jnp.maximum(s - tiles // 2, 0), 0)),
            ],
            scratch_shapes=[
                pltpu.VMEM((2, rows, HD), bf16),
                pltpu.VMEM((2, rows, HD), bf16),
                pltpu.VMEM((2, 1, rows), f32),
                pltpu.VMEM((2, rows, HD), f32),
                pltpu.VMEM((len(pieces),) + pieces[0].shape, bf16),
                pltpu.SemaphoreType.DMA((len(pieces),)),
            ],
        ),
        out_shape=[
            jax.ShapeDtypeStruct(queries.shape, bf16),
            jax.ShapeDtypeStruct((tiles * span_len // 2, 2 * HD), bf16),
            jax.ShapeDtypeStruct((tiles * span_len // 2, 2 * HD), bf16),
        ],
        compiler_params=pltpu.CompilerParams(vmem_limit_bytes=40 * 1024 * 1024),
        cost_estimate=pl.CostEstimate(
            flops=visits * rows * span_len * HD * 10,
            bytes_accessed=kv_size * 4 + queries.size * 16,
            transcendentals=visits * rows * span_len * 2,
        ),
        name="attention_backward",
    )(spans, queries, grads, exact, lse, *table, *pieces)


def product(left, right, left_dim, right_dim, out=f32):
    result = lax.dot_general(left, right, (((left_dim,), (right_dim,)), ((), ())), preferred_element_type=f32)
    return result.astype(out)


def on_device(
    hidden_in,
    out_grad,
    span_order,
    w_query,
    w_key,
    w_value,
    w_output,
    w_gate,
    w_up,
    w_down,
    norm_scales,
):
    local_rows = hidden_in.shape[0]
    head_count = lax.axis_size("head")
    block_count = lax.axis_size("blk")
    block_index = lax.axis_index("blk")
    head_index = lax.axis_index("head")
    group_rows = local_rows * head_count
    span_len = group_rows // 2
    model_rows, query_width = w_query.shape
    model_width = hidden_in.shape[1]
    query_heads = query_width // HD
    half_units = w_gate.shape[1] // 2

    chip_masks = bits(block_count)[1:]
    pair, top = chip_masks[0], chip_masks[-1]
    far_masks = chip_masks[:0:-1]
    head_axes = [(0, mask) for mask in bits(head_count)]
    unit_axes = head_axes + [(pair, 0)]
    unit_side = (block_index // pair) % 2
    bit_count = len(chip_masks) + 1

    def side(mask):
        return (block_index // mask) % 2

    def send(value, mask, *after):
        return swap(tie(value, *after), (mask, 0))

    def segment(body, inputs, after=(), flying=()):
        inputs, after = lax.optimization_barrier((tuple(inputs), after))
        shapes = jax.eval_shape(body, *inputs)

        def nothing(*_):
            return jax.tree.map(lambda x: jnp.zeros(x.shape, x.dtype), shapes)

        results = lax.cond(span_order[0] >= 0, body, nothing, *inputs)
        return lax.optimization_barrier((results, flying))

    def far_spread(value, *after):
        held = {0: value}
        for mask in far_masks:
            for have in list(held):
                held[have ^ mask] = send(held[have], mask, *after)
        return held

    def near_spread(held, *after):
        return held | {have ^ pair: send(block, pair, *(after if have == 0 else ())) for have, block in held.items()}

    def split_dims(partial):
        return partial.reshape((2,) * bit_count + (-1, partial.shape[-1]))

    def halve(value, dim, mask, *after):
        moved = send(pick(value, dim, 1 - side(mask)), mask, *after)
        return plus(pick(value, dim, side(mask)), moved)

    slot = jnp.arange(head_count, dtype=jnp.int32) ^ head_index
    in_block = (slot[:, None] * local_rows + jnp.arange(local_rows, dtype=jnp.int32)[None, :]).reshape(-1)
    head_side = head_index // (head_count // 2)
    own_spans = jnp.stack([span_order[2 * block_index + head_side], span_order[2 * block_index + 1 - head_side]])
    row_spans = jnp.repeat(own_spans, span_len)
    position = row_spans * span_len + in_block % span_len
    even_masks = [0]
    for mask in chip_masks[::-1]:
        even_masks = even_masks + [have ^ mask for have in even_masks]
    slot_masks = even_masks + [mask ^ 1 for mask in even_masks]
    tile_blocks = jnp.array(slot_masks, jnp.int32) ^ block_index
    tile_slots = (2 * tile_blocks[:, None] + jnp.stack([head_side, 1 - head_side])[None, :]).reshape(-1)
    flip = (head_index % (head_count // 2)) * local_rows
    spans = jnp.concatenate([span_order[tile_slots], own_spans, flip[None]]).astype(jnp.int32)
    table = rotation(position)

    scale_count = norm_scales.shape[0]
    kv_at = head_index * query_heads // (H // KVH) * HD
    kv_local = jnp.concatenate(
        [
            lax.dynamic_slice_in_dim(w_key, kv_at, HD, 1),
            lax.dynamic_slice_in_dim(w_value, kv_at, HD, 1),
        ],
        1,
    )
    scale_local = jnp.pad(norm_scales, ((0, 16 - scale_count), (0, 2 * HD - model_rows)))
    kv_local = jnp.concatenate([kv_local, scale_local], 0)

    def half(local, index):
        return lax.dynamic_slice_in_dim(local, index * half_units, half_units, 1)

    def unit_slices():
        weights = (w_gate, w_up, w_down.T)
        return (
            half(w_gate, unit_side),
            jnp.concatenate([half(w, unit_side) for w in weights[1:]], 1),
            jnp.concatenate([half(w, 1 - unit_side) for w in weights[:2]], 1),
            half(weights[2], 1 - unit_side),
        )

    hidden_near = [swap(hidden_in, axis) for axis in head_axes]
    kv_chips = far_spread(kv_local)
    kv_chips.pop(0)
    kv_chips[pair] = send(kv_local, pair)
    (query_output_local, unit_local), (hidden_near, kv_chips) = segment(
        lambda w_query, w_output: (jnp.concatenate([w_query, w_output.T], 1), unit_slices()),
        (w_query, w_output),
        (table,),
        (hidden_near, kv_chips),
    )
    first_mine, second_mine, first_theirs, second_theirs = unit_local

    def first_rows(hidden_near, kv_chips):
        held = {0: kv_local} | kv_chips
        held |= {mask ^ pair: swap(block, (pair, 0)) for mask, block in kv_chips.items() if mask != pair}
        parts = {0: [hidden_in]} | {1 << at: [part] for at, part in enumerate(hidden_near)}
        for subset in range(1, head_count):
            if subset not in parts:
                ways = route(subset, len(head_axes), False)
                cuts = shares(local_rows, len(ways)) if len(ways) > 1 else [(0, local_rows)]
                parts[subset] = [
                    swap(parts[subset ^ (1 << way)][0][low:high], head_axes[way]) for way, (low, high) in zip(ways, cuts)
                ]
        def normed_keys(held, parts):
            came = ()
            for mask, block in list(held.items()):
                held[mask ^ 1] = swap(tie(block, *came), (1, 0))
                came = (held[mask ^ 1],)
            scale_blocks = place_scales(held, model_rows, block_index)
            scale_rows = scale_blocks.reshape(block_count, 16, 2 * HD)[:, :scale_count, :model_rows]
            scale_rows = scale_rows.transpose(1, 0, 2).reshape(scale_count, model_width).astype(f32)
            arrays = [part for slot in sorted(parts) for part in parts[slot]]
            normed_full, inverse_full = whole_call(
                functools.partial(norm_full_kernel, len(arrays)),
                [((group_rows, model_width), bf16), ((group_rows, 1), f32)],
                *arrays,
                scale_rows,
                name="norm_full",
            )
            kv_held = {mask: (block, 0) for mask, block in held.items()}
            kv_rows, kv_weight = project(normed_full, [kv_held], [2 * HD], table, 1, block_index, "key_rows")
            return kv_rows, kv_weight, scale_rows, normed_full, inverse_full

        held, parts = lax.optimization_barrier((held, parts))
        query_output = {mask: send(query_output_local, mask, held[pair ^ top]) for mask in (*far_masks, pair)}
        results, query_output = segment(normed_keys, (held, parts), (), query_output)
        return results, parts, query_output

    first_results, hidden_parts, query_output_chips = first_rows(hidden_near, kv_chips)
    kv_rows, kv_weight, scale_rows, normed_full, inverse_full = first_results
    hidden_slots = [part for slot in sorted(hidden_parts) for part in hidden_parts[slot]]
    row_shape = (local_rows, model_width)
    scale_shape = (1, model_width)

    if len(far_masks) > 1:
        query_output_chips = far_spread(query_output_local) | {pair: query_output_chips[pair]}
    query_output_chips[0] = query_output_local
    kv_far = far_spread(kv_rows)
    kv_far.pop(0)
    kv_near = send(kv_rows, pair)
    query_output_last = {
        mask ^ pair: send(block, pair, kv_rows) for mask, block in query_output_chips.items() if mask & ~pair
    }

    def beside_keys(kv_rows):
        cores, came = {}, ()
        for mask, block in ({-1: kv_rows} | query_output_chips).items():
            cores[mask] = swap(tie(block, *came), (1, 0))
            came = (cores[mask],)
        return cores

    cores, (kv_far, kv_near, query_output_last) = segment(
        beside_keys, (kv_rows,), (), (kv_far, kv_near, query_output_last)
    )

    def keys_and_queries(kv_far, kv_near, query_output_last):
        across = {mask ^ pair: swap(block, (pair, 0)) for mask, block in kv_far.items()}
        chips = query_output_chips | query_output_last
        held = query_output_last | {-1 - mask: piece for mask, piece in ({pair: kv_near} | kv_far | across).items()}
        came, others = (), dict(cores)
        for mask, block in held.items():
            others[mask] = swap(tie(block, *came), (1, 0))
            came = (others[mask],)
        pieces = {(-1 - mask) ^ 1: piece for mask, piece in others.items() if mask < 0}
        chips |= {mask ^ 1: block for mask, block in others.items() if mask >= 0}
        queries, query_weight, output_weight = project(
            normed_full,
            [{mask: (block, column) for mask, block in chips.items()} for column in (0, query_width)],
            [query_width, query_width],
            table,
            query_heads,
            block_index,
            "query_rows",
        )
        return across | pieces, query_weight, output_weight, queries

    first_near = far_spread(first_mine, kv_far[top])
    (kv_others, query_weight, output_weight, queries), first_near = segment(
        keys_and_queries, (kv_far, kv_near, query_output_last), (), first_near
    )
    kv_held = {0: kv_rows, pair: kv_near} | kv_far | kv_others
    kv_pieces = [kv_held[mask] for mask in slot_masks]

    def row_sum(partial, axes, light=False):
        shaped = partial.reshape(1 << len(axes), local_rows, model_width)
        return scatter_rows([shaped[i] for i in range(1 << len(axes))], axes, light)

    def attend(queries, first_near, second_mine):
        mixed, exact, lse = attention_forward(spans, queries, kv_pieces, span_len)
        cores = in_turn(first_near | {-1: second_mine})
        second_core = cores.pop(-1)
        first_core = {mask ^ 1: block for mask, block in cores.items()}
        mixed = tie(mixed, first_core, second_core)
        terms = row_sum(product(mixed, output_weight, 1, 1, bf16), head_axes)
        rows = whole_call(
            functools.partial(after_attention_kernel, len(terms)),
            [(row_shape, f32), (row_shape, f32), (row_shape, bf16)],
            *terms,
            hidden_in,
            scale_rows,
            name="after_attention",
        )
        return (mixed, exact, lse, *rows, first_core, second_core)

    second_near = far_spread(second_mine, queries)
    first_cross = send(first_theirs, pair, queries)
    (mixed, exact, lse, attn_out, resid, ffn_in, first_core, second_core), (second_near, first_cross) = segment(
        attend, (queries, first_near, second_mine), (), (second_near, first_cross)
    )
    second_far = {mask: block for mask, block in second_near.items() if mask}

    def join_units(ffn_in, first_cross, second_far):
        parts = {0: [ffn_in]}
        parts |= gather_hop(parts, unit_axes, True, hops(len(unit_axes), True)[0])

        def later_hops(parts):
            parts = gather_rows(None, unit_axes, True, parts)
            third = [part for t in parts if t.bit_count() > 1 and t != len(parts) - 1 for part in parts[t]]
            first_core = swap(tie(first_cross, *parts[len(parts) // 2]), (1, 0))
            second_cores = {
                mask ^ 1: swap(tie(block, *third, first_core), (1, 0)) for mask, block in second_far.items()
            }
            return join_rows(parts), first_core, second_cores

        second_cross = send(second_theirs, pair, parts)
        return segment(later_hops, (parts,), (), second_cross)

    first_across = far_spread(first_cross, ffn_in)
    ((ffn_full, cross_core, far_cores), second_cross), first_across = segment(
        join_units, (ffn_in, first_cross, second_far), (), first_across
    )
    second_held = second_near | {1: second_core} | far_cores

    def gate_and_up(ffn_full, first_across):
        cores = {1: cross_core} | {mask ^ 1: swap(block, (1, 0)) for mask, block in first_across.items() if mask}
        across = {mask ^ pair: block for mask, block in (first_across | cores).items()}
        gate_held = {mask: (block, 0) for mask, block in (first_near | first_core | across).items()}
        up_held = {mask: (block, 0) for mask, block in second_held.items()}
        up_held |= {mask: (block, half_units) for mask, block in across.items()}
        units = hidden_units(ffn_full, [gate_held, up_held], half_units, block_index)
        return units, swap(second_cross, (1, 0))

    second_across = far_spread(second_cross, ffn_full)
    ((hidden, active, slope, gate_weight, up_weight), second_cross_core), second_across = segment(
        gate_and_up, (ffn_full, first_across), (), second_across
    )
    down_held = {mask: (block, half_units) for mask, block in second_held.items()}
    down_held |= {mask ^ pair: (block, 0) for mask, block in second_across.items()}
    down_held |= {
        mask ^ pair ^ 1: (swap(block, (1, 0)) if mask else second_cross_core, 0)
        for mask, block in second_across.items()
    }
    ffn_part, down_weight = down_rows(hidden, down_held, block_index)
    ffn_terms = row_sum(ffn_part, unit_axes)
    layer_out, grad_ffn_out, scale_grad3 = whole_call(
        functools.partial(after_ffn_kernel, len(ffn_terms)),
        [(row_shape, bf16), (row_shape, bf16), (scale_shape, f32)],
        *ffn_terms,
        resid,
        out_grad,
        scale_rows,
        name="after_ffn",
    )

    def unit_core(partial):
        summed = halve(split_dims(partial), bit_count - 1, 1).astype(bf16)
        return pick(summed, 0, 1 - side(top)), pick(summed, 0, side(top))

    def unit_sides(kept, came):
        part = plus(kept, came).astype(bf16)
        for mask in far_masks[1:]:
            part = halve(part, 0, mask).astype(bf16)
        return pick(part, 0, 1 - unit_side), pick(part, 0, unit_side)

    def unit_whole(own, other):
        low = jnp.where(unit_side == 0, own, other)
        high = jnp.where(unit_side == 0, other, own)
        return jnp.concatenate([low, high], 1).astype(f32)

    def core_sum(partial):
        return halve(split_dims(partial), bit_count - 1, 1).astype(bf16)

    grad_ffn_full = join_rows(gather_rows(grad_ffn_out, unit_axes))
    grad_down = product(grad_ffn_full, hidden, 0, 0, bf16)
    grad_hidden = product(tie(grad_ffn_full, grad_down), down_weight, 1, 0)
    grad_gate_act = (grad_hidden * slope).astype(bf16)
    grad_up_act = (grad_hidden * active).astype(bf16)
    down_away, down_kept = unit_core(grad_down)
    down_came = send(down_away, top)

    def weight_back(act):
        return product(ffn_full, act, 0, 0, bf16)

    back_plan = scatter_plan(len(unit_axes), True)
    split_at = len(back_plan) - 2

    def beside_hops(bodies):
        results = []

        def beside(number):
            def run(moved):
                if number >= len(bodies):
                    return None, moved
                result, moved = segment(bodies[number], tuple(results[-1:]), (), moved)
                results.append(result)
                return result, moved

            return run

        return beside, results

    def ffn_back_first(grad_gate_act, grad_up_act):
        grad_ffn_part = two_products(grad_gate_act, gate_weight, grad_up_act, up_weight)
        shaped = grad_ffn_part.reshape(-1, local_rows, model_width)
        pieces, came = {t: [shaped[t]] for t in range(shaped.shape[0])}, ()
        beside, results = beside_hops([lambda: weight_back(tie(grad_gate_act, grad_ffn_part)), unit_core])
        for number, subsets in enumerate(back_plan[:split_at]):
            pieces, came, _ = scatter_hop(pieces, unit_axes, True, subsets, came, beside(number))
        return pieces, results[1]

    (ffn_pieces, (gate_away, gate_kept)), down_came = segment(
        ffn_back_first, (grad_gate_act, grad_up_act), (down_away, down_kept), down_came
    )

    def ffn_back_last(ffn_pieces, grad_up_act, down_came):
        pieces, came = ffn_pieces, ()
        beside, results = beside_hops(
            [lambda: weight_back(grad_up_act), lambda partial: (unit_core(partial), unit_sides(down_kept, down_came))]
        )
        for number, subsets in enumerate(back_plan[split_at:]):
            pieces, came, _ = scatter_hop(pieces, unit_axes, True, subsets, came, beside(number))
        rows = whole_call(
            functools.partial(after_ffn_back_kernel, len(pieces[0])),
            [(row_shape, f32), (row_shape, bf16), (scale_shape, f32), (scale_shape, f32)],
            *pieces[0],
            resid,
            attn_out,
            out_grad,
            scale_rows,
            name="after_ffn_back",
        )
        return (*rows, *results[1])

    gate_came = send(gate_away, top, down_came)
    (grad_resid, grad_attn, scale_grad2, scale_grad1, (up_away, up_kept), (down_far, down_own)), gate_came = segment(
        ffn_back_last, (ffn_pieces, grad_up_act, down_came), (gate_away, gate_kept), gate_came
    )

    def attend_back(grad_attn):
        grad_attn_full = join_rows(gather_rows(grad_attn, head_axes))
        grad_mixed = product(grad_attn_full, output_weight, 1, 0, bf16)
        grad_query_lin, kv_near, kv_far = attention_backward(
            spans, queries, grad_mixed, exact, lse, table, kv_pieces, span_len
        )
        kv_terms = plus(kv_near, swap(kv_far, (1, 0))).astype(bf16).reshape(-1, group_rows, 2 * HD)
        middle = kv_terms.shape[0] // 2
        return grad_attn_full, grad_query_lin, kv_terms[:middle], kv_terms[middle:]

    up_came = send(up_away, top, grad_attn)
    down_other = send(down_far, pair, grad_attn)
    (grad_attn_full, grad_query_lin, kv_kept, kv_away), (up_came, down_other) = segment(
        attend_back, (grad_attn,), (up_away, up_kept, down_far, down_own), (up_came, down_other)
    )

    def projections_back(grad_query_lin, gate_came):
        core = core_sum(outer((normed_full, grad_query_lin), (grad_attn_full, mixed)))
        away, kept = pick(core, bit_count - 2, 1 - unit_side), pick(core, bit_count - 2, unit_side)
        return away, kept, unit_sides(gate_kept, gate_came)

    kv_came = send(kv_away, pair)
    (query_output_away, query_output_kept, (gate_far, gate_own)), kv_came = segment(
        projections_back, (grad_query_lin, gate_came), (), kv_came
    )
    kv_terms = plus(kv_kept, kv_came).astype(bf16)
    for mask in chip_masks[1:-1]:
        middle = kv_terms.shape[0] // 2
        kv_terms = plus(kv_terms[:middle], swap(kv_terms[middle:], (mask, 0))).astype(bf16)

    def beside_last_keys(up_came, down_other):
        return unit_sides(up_kept, up_came), unit_whole(down_own, down_other).T

    kv_came = send(kv_terms[1], top)
    gate_other = send(gate_far, pair, kv_terms)
    ((up_far, up_own), out_down), (kv_came, gate_other) = segment(
        beside_last_keys, (up_came, down_other), (kv_terms,), (kv_came, gate_other)
    )

    def normed_rows_back(kv_kept, kv_came):
        (grad_kv_lin,) = whole_call(
            key_value_grad_kernel,
            [((group_rows, 2 * HD), bf16)],
            kv_kept,
            kv_came,
            *table,
            name="key_value_grad",
        )
        terms = core_sum(outer((normed_full, grad_kv_lin)))
        away, kept = pick(terms, bit_count - 2, 1 - unit_side), pick(terms, bit_count - 2, unit_side)

        def products_back(grad_kv_lin):
            grad_normed_part, scale_grad0 = normed_back(
                grad_query_lin, query_weight, grad_kv_lin, kv_weight, inverse_full, hidden_slots
            )
            scale_grad = jnp.concatenate([scale_grad0, scale_grad1, scale_grad2, scale_grad3], 0)
            scale_grad = scale_grad.reshape(scale_count, block_count, model_rows).transpose(1, 0, 2)
            scale_grad = scale_grad.reshape((2,) * bit_count + scale_grad.shape[1:])
            for at, mask in enumerate([1] + chip_masks[:-1]):
                scale_grad = halve(scale_grad, bit_count - 1 - at, mask)
            scale_grad = jnp.pad(scale_grad.astype(bf16), ((0, 0), (0, 16 - scale_count), (0, 2 * HD - model_rows)))
            return grad_normed_part, scale_grad

        wkv_came = send(away, pair)
        (grad_normed_part, scale_grad), wkv_came = segment(products_back, (grad_kv_lin,), (away, kept), wkv_came)
        wkv_terms = plus(kept, wkv_came).astype(bf16)
        for at, mask in list(enumerate(chip_masks))[1:-1]:
            wkv_terms = halve(wkv_terms, bit_count - 2 - at, mask).astype(bf16)

        def sums_back(grad_normed_part):
            terms = row_sum(grad_normed_part, head_axes)
            (grad_in,) = whole_call(
                functools.partial(after_all_kernel, len(terms)),
                [(row_shape, f32)],
                *terms,
                hidden_in,
                grad_resid,
                scale_rows,
                name="after_all",
            )
            return grad_in

        wkv_terms = jnp.concatenate([wkv_terms, scale_grad], 1)
        away, kept = lax.optimization_barrier((pick(wkv_terms, 0, 1 - side(top)), pick(wkv_terms, 0, side(top))))
        wkv_came = send(away, top)
        query_output_came = send(query_output_away, pair, away)
        grad_in, (wkv_came, query_output_came) = segment(
            sums_back, (grad_normed_part,), (away, kept), (wkv_came, query_output_came)
        )
        return (grad_in, plus(kept, wkv_came).astype(bf16)), query_output_came

    (grad_in, grad_wkv), query_output_came = segment(
        normed_rows_back, (kv_terms[0], kv_came), (up_far, up_own, out_down)
    )[0]
    query_output_terms = plus(query_output_kept, query_output_came).astype(bf16)
    for at, mask in list(enumerate(chip_masks))[1:-1]:
        query_output_terms = halve(query_output_terms, bit_count - 2 - at, mask).astype(bf16)
    query_output_away = pick(query_output_terms, 0, 1 - side(top))
    query_output_came = send(query_output_away, top)
    up_other = send(up_far, pair, grad_wkv)

    def head_rows(grad_wkv):
        parts = gather_rows(grad_wkv, head_axes)
        wkv_ordered = jnp.zeros((head_count,) + grad_wkv.shape, bf16)
        for mask, pieces in parts.items():
            first = 0
            for piece in pieces:
                wkv_ordered = lax.dynamic_update_slice(wkv_ordered, piece[None], (head_index ^ mask, first, 0))
                first += piece.shape[0]
        wkv_ordered = wkv_ordered.astype(f32)
        scale_total = wkv_ordered[:, model_rows : model_rows + scale_count, :model_rows].sum(0)
        wkv_ordered = wkv_ordered[:, :model_rows].reshape(KVH, head_count // KVH, model_rows, 2, HD).sum(1)
        out_key = wkv_ordered[:, :, 0].transpose(1, 0, 2).reshape(model_rows, KVH * HD)
        out_value = wkv_ordered[:, :, 1].transpose(1, 0, 2).reshape(model_rows, KVH * HD)
        return out_key, out_value, scale_total, unit_whole(gate_own, gate_other)

    (out_key, out_value, scale_total, out_gate), (query_output_came, up_other) = segment(
        head_rows, (grad_wkv,), (query_output_away,), (query_output_came, up_other)
    )
    out_query_output = plus(pick(query_output_terms, 0, side(top)), query_output_came)
    out_query = out_query_output[:, :query_width]
    out_output = out_query_output[:, query_width:].T
    out_up = unit_whole(up_own, up_other)

    return (
        layer_out,
        grad_in,
        out_query,
        out_key,
        out_value,
        out_output,
        out_gate,
        out_up,
        out_down,
        scale_total,
    )


def solution(mesh):
    placed = (
        P(("blk", "head"), None),
        P(("blk", "head"), None),
        P(),
        P("blk", "head"),
        P("blk", None),
        P("blk", None),
        P("head", "blk"),
        P("blk", "head"),
        P("blk", "head"),
        P("head", "blk"),
        P(None, "blk"),
    )
    return jax.shard_map(
        on_device,
        mesh=mesh,
        in_specs=placed,
        out_specs=(
            P(("blk", "head"), None),
            P(("blk", "head"), None),
            P("blk", "head"),
            P("blk", None),
            P("blk", None),
            P("head", "blk"),
            P("blk", "head"),
            P("blk", "head"),
            P("head", "blk"),
            P(None, "blk"),
        ),
        check_vma=False,
    )
```

time: 1020 us -> 823 us (0.81)
  waiting for transfers between devices: 572 us -> 397 us
  Pallas kernels: 23.7 us -> 131 us
  matrix products: 113 us -> 45.2 us
  starting transfers between devices: 119 us -> 86.9 us
  other arithmetic: 78.3 us -> 59.5 us
  local copies, waits for them, and re-layouts: 103 us -> 87.7 us
    ppermute x124 -> x63, waiting for transfers between devices: 470 us -> 237 us  [swap(): lax.ppermute(value, 'blk', [(i, i ^ blk_mask) for i in range(block_count)])]
    pallas_call x0 -> x18, Pallas kernels: none -> 102 us  [the longest x4 45.5 us: placed(): pl.pallas_call(functools.partial(placed_kernel, body, plans, counts, step...]
    dot_general x18 -> x6, matrix products: 113 us -> 45.2 us  [product(): lax.dot_general(left, right, (((left_dim,), (right_dim,)), ((), ())), pre...]
    ppermute x46 -> x48, waiting for transfers between devices: 102 us -> 160 us  [swap(): lax.ppermute(value, 'head', [(i, i ^ head_mask) for i in range(head_count)])]
    dynamic_update_slice x57 -> x5, local copies, waits for them, and re-layouts: 46.8 us -> 2.04 us  [head_rows(): lax.dynamic_update_slice(wkv_ordered, piece[None], (head_index ^ mask, fi...]
    ppermute x124 -> x63, starting transfers between devices: 78.8 us -> 42.3 us  [swap(): lax.ppermute(value, 'blk', [(i, i ^ blk_mask) for i in range(block_count)])]
    another operation x10 -> x1, other arithmetic: 17.6 us -> 1.38 us  [on_device(): jnp.stack([head_side, 1 - head_side])[None, :]]
    slice x30 -> x31, local copies, waits for them, and re-layouts: 5.25 us -> 21.4 us  [the longest x3 4.24 us: scatter_hop(): part = piece if len(ways) == 1 else piece[low:high]]
  transfers between devices with their start and end apart: 170 -> 111, of which waited for: 65 -> 77; matrix products, arithmetic and copies ran while one was open for 17% -> 18% of each run, Pallas kernels for 1% -> 14%
where the time goes in v2:
time: 823 us; the launch traced here: 812 us
  waiting for transfers between devices  397 us (48%)
  Pallas kernels  131 us (16%)
  local copies, waits for them, and re-layouts  87.7 us (11%)
  starting transfers between devices  86.9 us (11%)
  other arithmetic  59.5 us (7%)
  matrix products  45.2 us (5%)
    ppermute x63, waiting for transfers between devices, swap(): lax.ppermute(value, 'blk', [(i, i ^ blk_mask) for i in range(block_count)])  237 us
    ppermute x48, waiting for transfers between devices, swap(): lax.ppermute(value, 'head', [(i, i ^ head_mask) for i in range(head_count)])  160 us
    pallas_call x4, Pallas kernels, placed(): pl.pallas_call(functools.partial(placed_kernel, body, plans, counts, step...  45.5 us
    dot_general x6, matrix products, product(): lax.dot_general(left, right, (((left_dim,), (right_dim,)), ((), ())), pre...  45.2 us
    ppermute x48, starting transfers between devices, swap(): lax.ppermute(value, 'head', [(i, i ^ head_mask) for i in range(head_count)])  44.6 us
    ppermute x63, starting transfers between devices, swap(): lax.ppermute(value, 'blk', [(i, i ^ blk_mask) for i in range(block_count)])  42.3 us
    squeeze x15, local copies, waits for them, and re-layouts, pick(): return lax.dynamic_index_in_dim(value, index, dim, keepdims=False)  20.7 us
    pallas_call x6, Pallas kernels, whole_call(): pl.pallas_call(body, out_shape=[jax.ShapeDtypeStruct(shape, dtype) for sh...  17.3 us
  transfers between devices with their start and end apart: 111, of which 77 were waited for; matrix products, arithmetic and copies ran while one was open for 18% of the time, Pallas kernels for 14%

profile of v2, /device:TPU:0, one launch (start us, length us, event | category | flops | bytes accessed | tf_op | source)
XLA Modules:
  0.0 811.8 jit_solution(15113026884028694556)
XLA Ops:
  38.0 21.0 %collective-permute-done.69 = bf16[304,512]{1,0:T(8,128)(2,1)S(1)} collective-permute-done((bf16[304,512]{1,0:T(8,128)(2,1)}, bf16[304,512]{1,0:T(8,128)(2,1)S(1)}, u32[]{:S(2)}, u32[]{:S(2)}) %collective-permute-start.69) | collective-permute-done | bytes 311328 | tf_op jit(solution)/shard_map/ppermute | solution.py:60
  59.1 22.3 %conditional.22 = (bf16[512,512]{1,0:T(8,128)(2,1)}, bf16[2304,512]{1,0:T(8,128)(2,1)}, f32[4,2304]{1,0:T(4,128)}, bf16[512,2304]{1,0:T(8,128)(2,1)}, f32[512,1]{1,0:T(8,128)}) conditional(s32[]{:T(128)} %bitcast.56, () %tuple.268, (s32[]{:T(128)}, bf16[304,512]{1,0:T(8,128)(2,1)S(1)}, bf16[304,512]{1,0:T(8,128)(2,1)S(1)}, ...), branch_computations={%region_2.3_spmd, %region_3.4_spmd} | conditional | flops 1207968768 | bytes 22260080 | solution.py:927
  93.2 14.1 %collective-permute-done.74 = bf16[512,512]{1,0:T(8,128)(2,1)S(1)} collective-permute-done((bf16[512,512]{1,0:T(8,128)(2,1)}, bf16[512,512]{1,0:T(8,128)(2,1)S(1)}, u32[]{:S(2)}, u32[]{:S(2)}) %collective-permute-start.74) | collective-permute-done | bytes 524320 | tf_op jit(solution)/shard_map/ppermute | solution.py:60
  107.3 12.3 %collective-permute-done.75 = bf16[512,512]{1,0:T(8,128)(2,1)} collective-permute-done((bf16[512,512]{1,0:T(8,128)(2,1)}, bf16[512,512]{1,0:T(8,128)(2,1)}, u32[]{:S(2)}, u32[]{:S(2)}) %collective-permute-start.75) | collective-permute-done | bytes 524320 | tf_op jit(solution)/shard_map/ppermute | solution.py:60
  120.0 40.4 %conditional.24 = (bf16[512,512]{1,0:T(8,128)(2,1)S(1)}, bf16[512,512]{1,0:T(8,128)(2,1)}, bf16[512,512]{1,0:T(8,128)(2,1)}, bf16[512,512]{1,0:T(8,128)(2,1)}, b...) conditional(s32[]{:T(128)} %bitcast.56, () %tuple.266, ...), branch_computations={%region_6.7_spmd, %region_7.8_spmd} | conditional | flops 1207959552 | bytes 24772900 | solution.py:927
  125.3 26.2 %collective-permute-done.7 = bf16[512,512]{1,0:T(8,128)(2,1)} collective-permute-done((bf16[512,512]{1,0:T(8,128)(2,1)S(1)}, bf16[512,512]{1,0:T(8,128)(2,1)}, u32[]{:S(2)}, u32[]{:S(2)}) %collective-permute-start.7) | collective-permute-done | bytes 524320 | tf_op jit(solution)/shard_map/cond/branch_1_fun/ppermute | solution.py:60
  165.5 45.9 %conditional.25 = (bf16[512,512]{1,0:T(8,128)(2,1)S(1)}, f32[512,512]{1,0:T(8,128)S(1)}, f32[2,1,512]{2,1,0:T(1,128)S(1)}, f32[128,2304]{1,0:T(8,128)S(1)}, f32[...) conditional(s32[]{:T(128)} %bitcast.56, () %tuple.265, ...), branch_computations={%region_8.9_spmd, %region_9.10_spmd} | conditional | flops 3494379520 | bytes 57549292 | solution.py:927
  168.6 12.0 %attention_forward.1 = (bf16[512,512]{1,0:T(8,128)(2,1)S(1)}, f32[512,512]{1,0:T(8,128)S(1)}, f32[2,1,512]{2,1,0:T(1,128)S(1)}) custom-call(s32[19]{0:T(128)S(1)} %get-tuple-element.440.spans_ref, bf16[512,512]{1,0:T(8,128)(2,1)} %get-tuple-element.441.q_ref, bf16[512,512]{1,0:T(8,128)(2,1)} %get-tuple-element.442.refs_0_, ...), custom_call_target="tpu_custom_call" | custom-call | flops 2281701376 | bytes 7340032 | tf_op jit(solution)/shard_map/cond/branch_1_fun/attention_forward/pallas_call | solution.py:788
  196.4 12.3 %collective-permute-done.49.refs_1_ = bf16[128,2304]{1,0:T(8,128)(2,1)S(1)} collective-permute-done((bf16[128,2304]{1,0:T(8,128)(2,1)S(1)}, bf16[128,2304]{1,0:T(8,128)(2,1)S(1)}, u32[]{:S(2)}, u32[]{:S(2)}) %collective-permute-start.49) | collective-permute-done | bytes 589856 | tf_op jit(solution)/shard_map/cond/branch_1_fun/ppermute | solution.py:59
  221.3 83.3 %conditional.26 = (bf16[1024,2304]{1,0:T(8,128)(2,1)}, bf16[288,2304]{1,0:T(8,128)(2,1)}, bf16[288,2304]{1,0:T(8,128)(2,1)}, bf16[288,1152]{1,0:T(8,128)(2,1)}) conditional(s32[]{:T(128)} %bitcast.56, () %tuple.289, (s32[16]{0:T(128)S(1)}, bf16[128,2304]{1,0:T(8,128)(2,1)S(1)}, bf16[288,2304]{1,0:T(8,128)(2,1)}, bf16[288,2304]{1,0:T(8,128)(2,1)}, ...), branch_computations={%region_10.11_spmd, %region_11.14_spmd} | conditional | flops 2 | bytes 41583192 | solution.py:927
  224.9 11.3 %collective-permute-done.17 = bf16[128,2304]{1,0:T(8,128)(2,1)S(1)} collective-permute-done((bf16[128,2304]{1,0:T(8,128)(2,1)S(1)}, bf16[128,2304]{1,0:T(8,128)(2,1)S(1)}, u32[]{:S(2)}, u32[]{:S(2)}) %collective-permute-start.17) | collective-permute-done | bytes 589856 | tf_op jit(solution)/shard_map/cond/branch_1_fun/ppermute | solution.py:59
  236.4 26.1 %collective-permute-done.19 = bf16[128,2304]{1,0:T(8,128)(2,1)S(1)} collective-permute-done((bf16[128,2304]{1,0:T(8,128)(2,1)S(1)}, bf16[128,2304]{1,0:T(8,128)(2,1)S(1)}, u32[]{:S(2)}, u32[]{:S(2)}) %collective-permute-start.19) | collective-permute-done | bytes 589856 | tf_op jit(solution)/shard_map/cond/branch_1_fun/ppermute | solution.py:60
  265.0 39.6 %conditional = (bf16[1024,2304]{1,0:T(8,128)(2,1)}, bf16[288,2304]{1,0:T(8,128)(2,1)}, bf16[288,2304]{1,0:T(8,128)(2,1)}) conditional(s32[]{:T(128)} %bitcast.7, () %tuple.126, (bf16[128,2304]{1,0:T(8,128)(2,1)S(1)}, bf16[128,2304]{1,0:T(8,128)(2,1)S(1)}, bf16[128,2304]{1,0:T(8,128)(2,1)S(1)}, bf16[128,2304]{1,0:T(8,128)(2,1)S(1)}, ...), branch_computations={%region_12.12_spmd, %region_13.13_spmd} | conditional | bytes 31850840 | solution.py:927
  277.0 12.7 %collective-permute-done.11.refs_6_ = bf16[128,2304]{1,0:T(8,128)(2,1)S(1)} collective-permute-done((bf16[128,2304]{1,0:T(8,128)(2,1)S(1)}, bf16[128,2304]{1,0:T(8,128)(2,1)S(1)}, u32[]{:S(2)}, u32[]{:S(2)}) %collective-permute-start.11) | collective-permute-done | bytes 589856 | tf_op jit(solution)/shard_map/cond/branch_1_fun/cond/branch_1_fun/ppermute | solution.py:59
  305.6 28.1 %conditional.27 = (bf16[1024,1152]{1,0:T(8,128)(2,1)S(1)}, f32[1024,1152]{1,0:T(8,128)}, f32[1024,1152]{1,0:T(8,128)}, bf16[2304,1152]{1,0:T(8,128)(2,1)}, bf16[...) conditional(s32[]{:T(128)} %bitcast.56, () %tuple.288, (s32[]{:T(128)}, bf16[288,2304]{1,0:T(8,128)(2,1)}, ...), branch_computations={%region_14.15_spmd, %region_15.16_spmd} | conditional | flops 10871635968 | bytes 34504860 | solution.py:927
  310.9 22.4 %hidden_units.1 = (bf16[1024,1152]{1,0:T(8,128)(2,1)S(1)}, f32[1024,1152]{1,0:T(8,128)}, f32[1024,1152]{1,0:T(8,128)}, bf16[2304,1152]{1,0:T(8,128)(2,1)}, bf16[2304,1152]{1,0:T(8,128)(2,1)}) custom-call(s32[1]{0:T(128)} %bitcast.8.index_ref, bf16[288,1152]{1,0:T(8,128)(2,1)} %get-tuple-element.491.refs_0_, bf16[288,1152]{1,0:T(8,128)(2,1)} %get-tuple-element.492.refs_1_, ...), custom_call_target="tpu_custom_call" | custom-call | flops 10871635968 | bytes 21233664 | tf_op jit(solution)/shard_map/cond/branch_1_fun/hidden_units/pallas_call | solution.py:325
  469.9 52.2 %conditional.28 = (bf16[128,2304]{1,0:T(8,128)(2,1)S(1)}, bf16[128,2304]{1,0:T(8,128)(2,1)S(1)}, bf16[128,2304]{1,0:T(8,128)(2,1)S(1)}, bf16[128,2304]{1,0:T(8,1...) conditional(s32[]{:T(128)} %bitcast.56, () %tuple.307, ...), branch_computations={%region_16.17_spmd, %region_17.22_spmd} | conditional | flops 16321314816 | bytes 101155672 | solution.py:927
  470.1 15.5 %two_products.1 = bf16[1024,2304]{1,0:T(8,128)(2,1)S(1)} custom-call(bf16[1024,1152]{1,0:T(8,128)(2,1)S(1)} %get-tuple-element.513.a_ref, bf16[2304,1152]{1,0:T(8,128)(2,1)} %get-tuple-element.514.u_ref, bf16[1024,1152]{1,0:T(8,128)(2,1)S(1)} %get-tuple-element.515.b_ref, bf16[2304,1152]{1,0:T(8,128)(2,1)} %get-tuple-element.516.v_ref), custom_call_target="tpu_custom_call" | custom-call | flops 10871635968 | bytes 20054016 | tf_op jit(solution)/shard_map/cond/branch_1_fun/two_products/pallas_call | solution.py:170
  505.9 13.7 %conditional.2 = (bf16[2,288,1152]{2,1,0:T(8,128)(2,1)}, bf16[2,288,1152]{2,1,0:T(8,128)(2,1)}) conditional(s32[]{:T(128)} %bitcast.14, () %tuple.136, (bf16[2304,1152]{1,0:T(8,128)(2,1)}, s32[]{:T(128)}) %tuple.140), branch_computations={%region_20.20_spmd, %region_21.21_spmd} | conditional | flops 5308464 | bytes 29196844 | solution.py:927
  523.7 65.4 %conditional.29 = (f32[128,2304]{1,0:T(8,128)}, bf16[128,2304]{1,0:T(8,128)(2,1)}, f32[1,2304]{1,0:T(1,128)S(1)}, f32[1,2304]{1,0:T(1,128)}, bf16[2,288,1152]{2,...) conditional(s32[]{:T(128)} %bitcast.56, () %tuple.306, ...), branch_computations={%region_22.23_spmd, %region_23.28_spmd} | conditional | flops 5449973760 | bytes 99607608 | solution.py:927
  541.3 24.1 %collective-permute-done.57.refs_1_ = bf16[128,2304]{1,0:T(8,128)(2,1)S(1)} collective-permute-done((bf16[128,2304]{1,0:T(8,128)(2,1)}, bf16[128,2304]{1,0:T(8,128)(2,1)S(1)}, u32[]{:S(2)}, u32[]{:S(2)}) %collective-permute-start.57) | collective-permute-done | bytes 589856 | tf_op jit(solution)/shard_map/cond/branch_1_fun/ppermute | solution.py:60
  571.2 12.9 %conditional.4 = (bf16[2,288,1152]{2,1,0:T(8,128)(2,1)}, bf16[2,288,1152]{2,1,0:T(8,128)(2,1)}, bf16[288,1152]{1,0:T(8,128)(2,1)}, bf16[288,1152]{1,0:T(8,128)(2,1)}) conditional(s32[]{:T(128)} %bitcast.22, () %tuple.151, (bf16[2304,1152]{1,0:T(8,128)(2,1)}, s32[]{:T(128)}, bf16[2,288,1152]{2,1,0:T(8,128)(2,1)}, bf16[2,288,1152]{2,1,0:T(8,128)(2,1)}, ...), branch_computations={%region_26.26_spmd, %region_27.27_spmd} | conditional | flops 7962679 | bytes 57066156 | solution.py:927
  592.1 53.6 %conditional.30 = (bf16[512,2304]{1,0:T(8,128)(2,1)S(1)}, bf16[512,512]{1,0:T(8,128)(2,1)}, bf16[2,512,512]{2,1,0:T(8,128)(2,1)S(1)}, bf16[2,512,512]{2,1,0:T(8,128)(2,1)}) conditional(s32[]{:T(128)} %bitcast.56, () %tuple.305, (bf16[128,2304]{1,0:T(8,128)(2,1)}, bf16[2304,512]{1,0:T(8,128)(2,1)}, s32[19]{0:T(128)S(1)}, ...), branch_computations={%region_28.29_spmd, %region_29.30_spmd} | conditional | flops 6916669440 | bytes 79036816 | solution.py:927
  595.0 12.3 %collective-permute-done.61.refs_2_ = bf16[128,2304]{1,0:T(8,128)(2,1)S(1)} collective-permute-done((bf16[128,2304]{1,0:T(8,128)(2,1)}, bf16[128,2304]{1,0:T(8,128)(2,1)S(1)}, u32[]{:S(2)}, u32[]{:S(2)}) %collective-permute-start.61) | collective-permute-done | bytes 589856 | tf_op jit(solution)/shard_map/cond/branch_1_fun/ppermute | solution.py:59
  621.8 16.9 %attention_backward.1 = (bf16[512,512]{1,0:T(8,128)(2,1)}, bf16[2048,512]{1,0:T(8,128)(2,1)S(1)}, bf16[2048,512]{1,0:T(8,128)(2,1)S(1)}) custom-call(s32[19]{0:T(128)S(1)} %get-tuple-element.577.spans_ref, bf16[512,512]{1,0:T(8,128)(2,1)} %get-tuple-element.578.q_ref, bf16[512,512]{1,0:T(8,128)(2,1)S(1)} %convolution_convert_fusion.3.g_ref, ...), custom_call_target="tpu_custom_call" | custom-call | flops 5704253440 | bytes 12582912 | tf_op jit(solution)/shard_map/cond/branch_1_fun/attention_backward/pallas_call | solution.py:833
  650.1 15.1 %conditional.31 = (bf16[2,288,1024]{2,1,0:T(8,128)(2,1)}, bf16[2,288,1024]{2,1,0:T(8,128)(2,1)}, bf16[288,1152]{1,0:T(8,128)(2,1)}, bf16[288,1152]{1,0:T(8,128)(2,1)S(1)}) conditional(s32[]{:T(128)} %bitcast.56, () %tuple.327, (bf16[512,2304]{1,0:T(8,128)(2,1)}, bf16[512,512]{1,0:T(8,128)(2,1)}, bf16[512,2304]{1,0:T(8,128)(2,1)S(1)}, ...), branch_computations={%region_30.31_spmd, %region_31.32_spmd} | conditional | flops 2423291904 | bytes 79774112 | solution.py:927
  686.2 15.4 %collective-permute-done.107 = bf16[512,512]{1,0:T(8,128)(2,1)} collective-permute-done((bf16[512,512]{1,0:T(8,128)(2,1)}, bf16[512,512]{1,0:T(8,128)(2,1)}, u32[]{:S(2)}, u32[]{:S(2)}) %collective-permute-start.107) | collective-permute-done | bytes 524320 | tf_op jit(solution)/shard_map/ppermute | solution.py:60
  703.5 69.0 %conditional.33 = (f32[128,2304]{1,0:T(8,128)}, bf16[304,512]{1,0:T(8,128)(2,1)S(1)}, bf16[2,288,1024]{2,1,0:T(8,128)(2,1)}) conditional(s32[]{:T(128)} %bitcast.56, () %tuple.304, (s32[16]{0:T(128)S(1)}, bf16[512,512]{1,0:T(8,128)(2,1)}, bf16[512,512]{1,0:T(8,128)(2,1)}, f32[512,256]{1,0:T(8,128)S(1)}, f32[512,256]{1,0:T(8,128)S(1)}, ...), branch_computations={%region_34.35_spmd, %region_35.40_spmd} | conditional | flops 3632861184 | bytes 66155296 | solution.py:927
  715.2 18.9 %conditional.5 = (bf16[512,2304]{1,0:T(8,128)(2,1)S(1)}, bf16[2,16,512]{2,0,1:T(2,128)(2,1)S(1)}) conditional(s32[]{:T(128)} %bitcast.40, () %tuple.171, (bf16[512,512]{1,0:T(8,128)(2,1)}, bf16[2304,512]{1,0:T(8,128)(2,1)}, bf16[512,512]{1,0:T(8,128)(2,1)}, bf16[2304,512]{1,0:T(8,128)(2,1)}, f32[512,1]{1,0:T(8,128)}, ...), branch_computations={%region_36.36_spmd, %region_37.37_spmd} | conditional | flops 2415955968 | bytes 5443214 | solution.py:927
  740.4 25.2 %conditional.6 = (f32[128,2304]{1,0:T(8,128)}) conditional(s32[]{:T(128)} %bitcast.40, () %tuple.170, (bf16[512,2304]{1,0:T(8,128)(2,1)S(1)}, bf16[128,2304]{1,0:T(8,128)(2,1)S(1)}, f32[128,2304]{1,0:T(8,128)}, f32[4,2304]{1,0:T(4,128)}) %tuple.463), branch_computations={%region_38.38_spmd, %region_39.39_spmd} | conditional | flops 3538944 | bytes 21897384 | solution.py:927
  750.3 11.9 %collective-permute-done.34.refs_1_ = bf16[128,2304]{1,0:T(8,128)(2,1)S(1)} collective-permute-done((bf16[128,2304]{1,0:T(8,128)(2,1)S(1)}, bf16[128,2304]{1,0:T(8,128)(2,1)S(1)}, u32[]{:S(2)}, u32[]{:S(2)}) %collective-permute-start.34) | collective-permute-done | bytes 589856 | tf_op jit(solution)/shard_map/cond/branch_1_fun/cond/branch_1_fun/ppermute | solution.py:59
  778.5 26.7 %conditional.34 = (f32[288,1024]{1,0:T(8,128)S(1)}, f32[288,1024]{1,0:T(8,128)S(1)}, f32[4,288]{1,0:T(4,128)S(1)}, f32[288,2304]{1,0:T(8,128)}) conditional(s32[]{:T(128)} %bitcast.56, () %tuple.338, (bf16[304,512]{1,0:T(8,128)(2,1)S(1)}, s32[]{:T(128)}, s32[]{:T(128)}, bf16[288,1152]{1,0:T(8,128)(2,1)S(1)}, bf16[288,1152]{1,0:T(8,128)(2,1)}) %tuple.469), branch_computations={%region_40.41_spmd, %region_41.43_spmd} | conditional | flops 3943824 | bytes 42081160 | solution.py:927
  (526 shorter events, 584.1 us)
Async XLA Ops:
  0.7 23.9 %collective-permute-start.65 = (bf16[128,2304]{1,0:T(8,128)(2,1)}, bf16[128,2304]{1,0:T(8,128)(2,1)}, u32[]{:S(2)}, u32[]{:S(2)}) collective-permute-start(bf16[128,2304]{1,0:T(8,128)(2,1)} %param.54), channel_id=1, source_target_pairs={{0,1},{1,0},{2,3},{3,2},{4,5},{5,4},{6,7},{7,6},{8,9},{9,8},{10,11... | collective-permute-start | bytes 1769480 | tf_op jit(solution)/shard_map/ppermute | solution.py:59
  3.7 20.9 %collective-permute-start.66 = (bf16[128,2304]{1,0:T(8,128)(2,1)}, bf16[128,2304]{1,0:T(8,128)(2,1)}, u32[]{:S(2)}, u32[]{:S(2)}) collective-permute-start(bf16[128,2304]{1,0:T(8,128)(2,1)} %param.54), channel_id=1, source_target_pairs={{0,2},{1,3},{2,0},{3,1},{4,6},{5,7},{6,4},{7,5},{8,10},{9,11},{10,... | collective-permute-start | bytes 1769480 | tf_op jit(solution)/shard_map/ppermute | solution.py:59
  25.6 55.8 %collective-permute-start.72 = (bf16[288,1024]{1,0:T(8,128)(2,1)}, bf16[288,1024]{1,0:T(8,128)(2,1)}, u32[]{:S(2)}, u32[]{:S(2)}) collective-permute-start(bf16[288,1024]{1,0:T(8,128)(2,1)} %copy.59), channel_id=1, source_target_pairs={{0,8},{4,12},{8,0},{12,4},{16,24},{20,28},{24,16},{28,20},{1,9},{5... | collective-permute-start | bytes 1769480 | tf_op jit(solution)/shard_map/ppermute | solution.py:60
  26.1 55.3 %collective-permute-start.73 = (bf16[288,1024]{1,0:T(8,128)(2,1)}, bf16[288,1024]{1,0:T(8,128)(2,1)}, u32[]{:S(2)}, u32[]{:S(2)}) collective-permute-start(bf16[288,1024]{1,0:T(8,128)(2,1)} %copy.59), channel_id=1, source_target_pairs={{0,16},{4,20},{8,24},{12,28},{16,0},{20,4},{24,8},{28,12},{1,17},{... | collective-permute-start | bytes 1769480 | tf_op jit(solution)/shard_map/ppermute | solution.py:60
  28.7 30.4 %collective-permute-start.69 = (bf16[304,512]{1,0:T(8,128)(2,1)}, bf16[304,512]{1,0:T(8,128)(2,1)S(1)}, u32[]{:S(2)}, u32[]{:S(2)}) collective-permute-start(bf16[304,512]{1,0:T(8,128)(2,1)} %collective-permute-done.68), channel_id=1, source_target_pairs={{0,8},{4,12},{8,0},{12,4},{16,24},{20,28},{24,16},{28,20},{1,9},{5... | collective-permute-start | bytes 933896 | tf_op jit(solution)/shard_map/ppermute | solution.py:60
  81.4 38.2 %collective-permute-start.76 = (bf16[288,1024]{1,0:T(8,128)(2,1)}, bf16[288,1024]{1,0:T(8,128)(2,1)S(1)}, u32[]{:S(2)}, u32[]{:S(2)}) collective-permute-start(bf16[288,1024]{1,0:T(8,128)(2,1)} %collective-permute-done.73), channel_id=1, source_target_pairs={{0,8},{4,12},{8,0},{12,4},{16,24},{20,28},{24,16},{28,20},{1,9},{5... | collective-permute-start | bytes 1769480 | tf_op jit(solution)/shard_map/ppermute | solution.py:60
  82.0 25.2 %collective-permute-start.74 = (bf16[512,512]{1,0:T(8,128)(2,1)}, bf16[512,512]{1,0:T(8,128)(2,1)S(1)}, u32[]{:S(2)}, u32[]{:S(2)}) collective-permute-start(bf16[512,512]{1,0:T(8,128)(2,1)} %get-tuple-element.957), channel_id=1, source_target_pairs={{0,16},{4,20},{8,24},{12,28},{16,0},{20,4},{24,8},{28,12},{1,17},{... | collective-permute-start | bytes 1572872 | tf_op jit(solution)/shard_map/ppermute | solution.py:60
  82.4 37.3 %collective-permute-start.75 = (bf16[512,512]{1,0:T(8,128)(2,1)}, bf16[512,512]{1,0:T(8,128)(2,1)}, u32[]{:S(2)}, u32[]{:S(2)}) collective-permute-start(bf16[512,512]{1,0:T(8,128)(2,1)} %get-tuple-element.957), channel_id=1, source_target_pairs={{0,8},{4,12},{8,0},{12,4},{16,24},{20,28},{24,16},{28,20},{1,9},{5... | collective-permute-start | bytes 1572872 | tf_op jit(solution)/shard_map/ppermute | solution.py:60
  119.6 40.8 %collective-permute-start.77 = (bf16[288,1152]{1,0:T(8,128)(2,1)}, bf16[288,1152]{1,0:T(8,128)(2,1)}, u32[]{:S(2)}, u32[]{:S(2)}) collective-permute-start(bf16[288,1152]{1,0:T(8,128)(2,1)} %get-tuple-element.996), channel_id=1, source_target_pairs={{0,16},{4,20},{8,24},{12,28},{16,0},{20,4},{24,8},{28,12},{1,17},{... | collective-permute-start | bytes 1990664 | tf_op jit(solution)/shard_map/ppermute | solution.py:60
  123.1 28.4 %collective-permute-start.7 = (bf16[512,512]{1,0:T(8,128)(2,1)S(1)}, bf16[512,512]{1,0:T(8,128)(2,1)}, u32[]{:S(2)}, u32[]{:S(2)}) collective-permute-start(bf16[512,512]{1,0:T(8,128)(2,1)S(1)} %get-tuple-element.425), channel_id=1, source_target_pairs={{0,8},{4,12},{8,0},{12,4},{16,24},{20,28},{24,16},{28,20},{1,9},{5... | collective-permute-start | bytes 1572872 | tf_op jit(solution)/shard_map/cond/branch_1_fun/ppermute | solution.py:60
  125.2 26.3 %collective-permute-start.6 = (bf16[512,512]{1,0:T(8,128)(2,1)S(1)}, bf16[512,512]{1,0:T(8,128)(2,1)}, u32[]{:S(2)}, u32[]{:S(2)}) collective-permute-start(bf16[512,512]{1,0:T(8,128)(2,1)S(1)} %get-tuple-element.425), channel_id=1, source_target_pairs={{0,4},{4,0},{8,12},{12,8},{16,20},{20,16},{24,28},{28,24},{1,5},{5... | collective-permute-start | bytes 1572872 | tf_op jit(solution)/shard_map/cond/branch_1_fun/ppermute | solution.py:60
  160.4 60.3 %collective-permute-start.78 = (bf16[288,2304]{1,0:T(8,128)(2,1)}, bf16[288,2304]{1,0:T(8,128)(2,1)}, u32[]{:S(2)}, u32[]{:S(2)}) collective-permute-start(bf16[288,2304]{1,0:T(8,128)(2,1)} %get-tuple-element.1013.refs_0_), channel_id=1, source_target_pairs={{0,16},{4,20},{8,24},{12,28},{16,0},{20,4},{24,8},{28,12},{1,17},{... | collective-permute-start | bytes 3981320 | tf_op jit(solution)/shard_map/ppermute | solution.py:60
  160.5 60.4 %collective-permute-start.79 = (bf16[288,2304]{1,0:T(8,128)(2,1)}, bf16[288,2304]{1,0:T(8,128)(2,1)}, u32[]{:S(2)}, u32[]{:S(2)}) collective-permute-start(bf16[288,2304]{1,0:T(8,128)(2,1)} %get-tuple-element.1012), channel_id=1, source_target_pairs={{0,8},{4,12},{8,0},{12,4},{16,24},{20,28},{24,16},{28,20},{1,9},{5... | collective-permute-start | bytes 3981320 | tf_op jit(solution)/shard_map/ppermute | solution.py:60
  220.9 83.7 %collective-permute-start.80 = (bf16[288,2304]{1,0:T(8,128)(2,1)}, bf16[288,2304]{1,0:T(8,128)(2,1)}, u32[]{:S(2)}, u32[]{:S(2)}) collective-permute-start(bf16[288,2304]{1,0:T(8,128)(2,1)} %collective-permute-done.79), channel_id=1, source_target_pairs={{0,16},{4,20},{8,24},{12,28},{16,0},{20,4},{24,8},{28,12},{1,17},{... | collective-permute-start | bytes 3981320 | tf_op jit(solution)/shard_map/ppermute | solution.py:60
  222.4 40.1 %collective-permute-start.19 = (bf16[128,2304]{1,0:T(8,128)(2,1)S(1)}, bf16[128,2304]{1,0:T(8,128)(2,1)S(1)}, u32[]{:S(2)}, u32[]{:S(2)}) collective-permute-start(bf16[128,2304]{1,0:T(8,128)(2,1)S(1)} %get-tuple-element.482), channel_id=1, source_target_pairs={{0,8},{4,12},{8,0},{12,4},{16,24},{20,28},{24,16},{28,20},{1,9},{5... | collective-permute-start | bytes 1769480 | tf_op jit(solution)/shard_map/cond/branch_1_fun/ppermute | solution.py:60
  262.5 42.1 %collective-permute-start.20 = (bf16[288,1152]{1,0:T(8,128)(2,1)}, bf16[288,1152]{1,0:T(8,128)(2,1)}, u32[]{:S(2)}, u32[]{:S(2)}) collective-permute-start(bf16[288,1152]{1,0:T(8,128)(2,1)} %get-tuple-element.489), channel_id=1, source_target_pairs={{0,8},{4,12},{8,0},{12,4},{16,24},{20,28},{24,16},{28,20},{1,9},{5... | collective-permute-start | bytes 1990664 | tf_op jit(solution)/shard_map/cond/branch_1_fun/ppermute | solution.py:60
  265.1 25.9 %collective-permute-start.15 = (bf16[288,2304]{1,0:T(8,128)(2,1)}, bf16[288,2304]{1,0:T(8,128)(2,1)}, u32[]{:S(2)}, u32[]{:S(2)}) collective-permute-start(bf16[288,2304]{1,0:T(8,128)(2,1)} %get-tuple-element.474), channel_id=1, source_target_pairs={{0,4},{4,0},{8,12},{12,8},{16,20},{20,16},{24,28},{28,24},{1,5},{5... | collective-permute-start | bytes 3981320 | tf_op jit(solution)/shard_map/cond/branch_1_fun/cond/branch_1_fun/ppermute | solution.py:60
  304.6 31.4 %collective-permute-start.81 = (bf16[288,1152]{1,0:T(8,128)(2,1)}, bf16[288,1152]{1,0:T(8,128)(2,1)}, u32[]{:S(2)}, u32[]{:S(2)}) collective-permute-start(bf16[288,1152]{1,0:T(8,128)(2,1)} %get-tuple-element.1045.refs_2_), channel_id=1, source_target_pairs={{0,16},{4,20},{8,24},{12,28},{16,0},{20,4},{24,8},{28,12},{1,17},{... | collective-permute-start | bytes 1990664 | tf_op jit(solution)/shard_map/ppermute | solution.py:60
  305.6 27.7 %collective-permute-start.22 = (bf16[288,1152]{1,0:T(8,128)(2,1)}, bf16[288,1152]{1,0:T(8,128)(2,1)}, u32[]{:S(2)}, u32[]{:S(2)}) collective-permute-start(bf16[288,1152]{1,0:T(8,128)(2,1)} %get-tuple-element.508), channel_id=1, source_target_pairs={{0,4},{4,0},{8,12},{12,8},{16,20},{20,16},{24,28},{28,24},{1,5},{5... | collective-permute-start | bytes 1990664 | tf_op jit(solution)/shard_map/cond/branch_1_fun/ppermute | solution.py:60
  456.8 65.3 %collective-permute-start.102 = (bf16[2,288,1152]{2,1,0:T(8,128)(2,1)}, bf16[2,288,1152]{2,1,0:T(8,128)(2,1)}, u32[]{:S(2)}, u32[]{:S(2)}) collective-permute-start(bf16[2,288,1152]{2,1,0:T(8,128)(2,1)} %get-tuple-element.1337), channel_id=1, source_target_pairs={{0,16},{4,20},{8,24},{12,28},{16,0},{20,4},{24,8},{28,12},{1,17},{... | collective-permute-start | bytes 3981320 | tf_op jit(solution)/shard_map/ppermute | solution.py:60
  522.1 67.1 %collective-permute-start.103 = (bf16[2,288,1152]{2,1,0:T(8,128)(2,1)}, bf16[2,288,1152]{2,1,0:T(8,128)(2,1)}, u32[]{:S(2)}, u32[]{:S(2)}) collective-permute-start(bf16[2,288,1152]{2,1,0:T(8,128)(2,1)} %get-tuple-element.1104), channel_id=1, source_target_pairs={{0,16},{4,20},{8,24},{12,28},{16,0},{20,4},{24,8},{28,12},{1,17},{... | collective-permute-start | bytes 3981320 | tf_op jit(solution)/shard_map/ppermute | solution.py:60
  524.6 40.8 %collective-permute-start.57 = (bf16[128,2304]{1,0:T(8,128)(2,1)}, bf16[128,2304]{1,0:T(8,128)(2,1)S(1)}, u32[]{:S(2)}, u32[]{:S(2)}) collective-permute-start(bf16[128,2304]{1,0:T(8,128)(2,1)} %get-tuple-element.543), channel_id=1, source_target_pairs={{0,8},{4,12},{8,0},{12,4},{16,24},{20,28},{24,16},{28,20},{1,9},{5... | collective-permute-start | bytes 1769480 | tf_op jit(solution)/shard_map/cond/branch_1_fun/ppermute | solution.py:60
  589.2 60.9 %collective-permute-start.104 = (bf16[2,288,1152]{2,1,0:T(8,128)(2,1)}, bf16[2,288,1152]{2,1,0:T(8,128)(2,1)}, u32[]{:S(2)}, u32[]{:S(2)}) collective-permute-start(bf16[2,288,1152]{2,1,0:T(8,128)(2,1)} %get-tuple-element.1117), channel_id=1, source_target_pairs={{0,16},{4,20},{8,24},{12,28},{16,0},{20,4},{24,8},{28,12},{1,17},{... | collective-permute-start | bytes 3981320 | tf_op jit(solution)/shard_map/ppermute | solution.py:60
  592.1 53.6 %collective-permute-start.105 = (bf16[288,1152]{1,0:T(8,128)(2,1)}, bf16[288,1152]{1,0:T(8,128)(2,1)}, u32[]{:S(2)}, u32[]{:S(2)}) collective-permute-start(bf16[288,1152]{1,0:T(8,128)(2,1)} %get-tuple-element.1118), channel_id=1, source_target_pairs={{0,8},{4,12},{8,0},{12,4},{16,24},{20,28},{24,16},{28,20},{1,9},{5... | collective-permute-start | bytes 1990664 | tf_op jit(solution)/shard_map/ppermute | solution.py:60
  650.1 24.7 %collective-permute-start.106 = (bf16[2,512,512]{2,1,0:T(8,128)(2,1)}, bf16[2,512,512]{2,1,0:T(8,128)(2,1)}, u32[]{:S(2)}, u32[]{:S(2)}) collective-permute-start(bf16[2,512,512]{2,1,0:T(8,128)(2,1)} %get-tuple-element.1130), channel_id=1, source_target_pairs={{0,8},{4,12},{8,0},{12,4},{16,24},{20,28},{24,16},{28,20},{1,9},{5... | collective-permute-start | bytes 3145736 | tf_op jit(solution)/shard_map/ppermute | solution.py:60
  676.6 26.8 %collective-permute-start.108 = (bf16[288,1152]{1,0:T(8,128)(2,1)}, bf16[288,1152]{1,0:T(8,128)(2,1)}, u32[]{:S(2)}, u32[]{:S(2)}) collective-permute-start(bf16[288,1152]{1,0:T(8,128)(2,1)} %get-tuple-element.1140), channel_id=1, source_target_pairs={{0,8},{4,12},{8,0},{12,4},{16,24},{20,28},{24,16},{28,20},{1,9},{5... | collective-permute-start | bytes 1990664 | tf_op jit(solution)/shard_map/ppermute | solution.py:60
  678.0 23.5 %collective-permute-start.107 = (bf16[512,512]{1,0:T(8,128)(2,1)}, bf16[512,512]{1,0:T(8,128)(2,1)}, u32[]{:S(2)}, u32[]{:S(2)}) collective-permute-start(bf16[512,512]{1,0:T(8,128)(2,1)} %get-tuple-element.1342), channel_id=1, source_target_pairs={{0,16},{4,20},{8,24},{12,28},{16,0},{20,4},{24,8},{28,12},{1,17},{... | collective-permute-start | bytes 1572872 | tf_op jit(solution)/shard_map/ppermute | solution.py:60
  714.5 19.7 %collective-permute-start.37 = (bf16[2,288,512]{2,1,0:T(8,128)(2,1)}, bf16[2,288,512]{2,1,0:T(8,128)(2,1)}, u32[]{:S(2)}, u32[]{:S(2)}) collective-permute-start(bf16[2,288,512]{2,1,0:T(8,128)(2,1)} %get-tuple-element.1315), channel_id=1, source_target_pairs={{0,8},{4,12},{8,0},{12,4},{16,24},{20,28},{24,16},{28,20},{1,9},{5... | collective-permute-start | bytes 1769480 | tf_op jit(solution)/shard_map/cond/branch_1_fun/ppermute | solution.py:60
  737.5 33.9 %collective-permute-start.39 = (bf16[2,288,1024]{2,1,0:T(8,128)(2,1)}, bf16[2,288,1024]{2,1,0:T(8,128)(2,1)}, u32[]{:S(2)}, u32[]{:S(2)}) collective-permute-start(bf16[2,288,1024]{2,1,0:T(8,128)(2,1)} %get-tuple-element.663), channel_id=1, source_target_pairs={{0,8},{4,12},{8,0},{12,4},{16,24},{20,28},{24,16},{28,20},{1,9},{5... | collective-permute-start | bytes 3538952 | tf_op jit(solution)/shard_map/cond/branch_1_fun/ppermute | solution.py:60
  738.9 31.4 %collective-permute-start.38 = (bf16[304,512]{1,0:T(8,128)(2,1)}, bf16[304,512]{1,0:T(8,128)(2,1)}, u32[]{:S(2)}, u32[]{:S(2)}) collective-permute-start(bf16[304,512]{1,0:T(8,128)(2,1)} %get-tuple-element.656), channel_id=1, source_target_pairs={{0,16},{4,20},{8,24},{12,28},{16,0},{20,4},{24,8},{28,12},{1,17},{... | collective-permute-start | bytes 933896 | tf_op jit(solution)/shard_map/cond/branch_1_fun/ppermute | solution.py:60
  772.5 32.8 %collective-permute-start.110 = (bf16[288,1152]{1,0:T(8,128)(2,1)}, bf16[288,1152]{1,0:T(8,128)(2,1)}, u32[]{:S(2)}, u32[]{:S(2)}) collective-permute-start(bf16[288,1152]{1,0:T(8,128)(2,1)} %get-tuple-element.1171), channel_id=1, source_target_pairs={{0,8},{4,12},{8,0},{12,4},{16,24},{20,28},{24,16},{28,20},{1,9},{5... | collective-permute-start | bytes 1990664 | tf_op jit(solution)/shard_map/ppermute | solution.py:60
  777.0 28.2 %collective-permute-start.109 = (bf16[288,1024]{1,0:T(8,128)(2,1)}, bf16[288,1024]{1,0:T(8,128)(2,1)}, u32[]{:S(2)}, u32[]{:S(2)}) collective-permute-start(bf16[288,1024]{1,0:T(8,128)(2,1)} %dynamic-slice_bitcast_fusion.24), channel_id=1, source_target_pairs={{0,16},{4,20},{8,24},{12,28},{16,0},{20,4},{24,8},{28,12},{1,17},{... | collective-permute-start | bytes 1769480 | tf_op jit(solution)/shard_map/ppermute | solution.py:60
  (155 other events, 1931.4 us)

commit v3 on v2

--- a/solution.py
+++ b/solution.py
@@ -113,7 +113,7 @@
     last = 1 << (len(axes) - 1)
     parts, before = parts or {0: [value]}, ()
     for subsets in hops(len(axes), light):
-        if subsets[0] in parts:
+        if all(t in parts for t in subsets):
             continue
         if light and last in parts:
             before = [x for x in before if x is not parts[last][0]]
@@ -149,20 +149,26 @@
         in_specs=[pl.BlockSpec(a.shape, lambda m: (0, 0), pipeline_mode=pl.Buffered(1)) for a in arrays],
         out_specs=pl.BlockSpec((rows, columns), lambda m: (m, 0)),
         out_shape=jax.ShapeDtypeStruct((len(parts) * rows, columns), arrays[0].dtype),
-        compiler_params=pltpu.CompilerParams(vmem_limit_bytes=32 * 1024 * 1024),
+        compiler_params=pltpu.CompilerParams(vmem_limit_bytes=16 * 1024 * 1024),
         cost_estimate=pl.CostEstimate(flops=0, bytes_accessed=4 * len(parts) * rows * columns, transcendentals=0),
         name="join_rows",
     )(*arrays)
 
 
-def two_products_kernel(a_ref, u_ref, b_ref, v_ref, out_ref):
+def two_products_kernel(a_ref, u_ref, b_ref, v_ref, *outs):
     nt = (((1,), (1,)), ((), ()))
     total = lax.dot_general(a_ref[...], u_ref[...], nt, preferred_element_type=f32)
     total += lax.dot_general(b_ref[...], v_ref[...], nt, preferred_element_type=f32)
-    out_ref[...] = total.astype(out_ref.dtype)
-
-
-def two_products(a, u, b, v):
+    put_pieces(outs, total)
+
+
+def put_pieces(outs, value):
+    rows = outs[0].shape[0]
+    for at, out in enumerate(outs):
+        out[...] = value[at * rows : (at + 1) * rows].astype(out.dtype)
+
+
+def two_products(a, u, b, v, count):
     rows, depth = a.shape
     columns = u.shape[0]
     step = 256
@@ -171,9 +177,9 @@
         two_products_kernel,
         grid=(columns // step,),
         in_specs=[resident, pl.BlockSpec((step, depth), lambda n: (n, 0))] * 2,
-        out_specs=pl.BlockSpec((rows, step), lambda n: (0, n)),
-        out_shape=jax.ShapeDtypeStruct((rows, columns), bf16),
-        compiler_params=pltpu.CompilerParams(vmem_limit_bytes=40 * 1024 * 1024),
+        out_specs=[pl.BlockSpec((rows // count, step), lambda n: (0, n))] * count,
+        out_shape=[jax.ShapeDtypeStruct((rows // count, columns), bf16)] * count,
+        compiler_params=pltpu.CompilerParams(vmem_limit_bytes=20 * 1024 * 1024),
         cost_estimate=pl.CostEstimate(
             flops=4 * rows * columns * depth,
             bytes_accessed=4 * (rows * depth + columns * depth) + 2 * rows * columns,
@@ -267,10 +273,14 @@
 
 def placed_kernel(body, plans, counts, steps, index_ref, *refs):
     refs = list(refs)
-    arrays, inputs, outs, wholes, weights = [[refs.pop(0) for _ in range(count)] for count in counts]
+    arrays, loads, inputs, outs, wholes, weights, loaded = [[refs.pop(0) for _ in range(count)] for count in counts]
     in_sems, out_sems = refs
     step = pl.program_id(0)
     came, at = [], 0
+    for source, target in zip(loads, loaded):
+        came.append([pltpu.make_async_copy(source, target, in_sems.at[at])])
+        at += 1
+    gone = [None] * len(loads)
     for weight, plan in zip(weights, plans):
         copies = []
         rows = weight.shape[0] // len(plan)
@@ -282,7 +292,7 @@
             copies.append(pltpu.make_async_copy(block, weight.at[pl.ds(row, rows)], in_sems.at[at]))
             at += 1
         came.append(copies)
-    gone = [
+    gone += [
         pltpu.make_async_copy(weight, whole, out_sems.at[n]) for n, (weight, whole) in enumerate(zip(weights, wholes))
     ]
 
@@ -294,17 +304,18 @@
         for copies, copy_out in zip(came, gone):
             for copy in copies:
                 copy.wait()
-            copy_out.start()
-
-    body(step, inputs, outs, weights)
+            if copy_out is not None:
+                copy_out.start()
+
+    body(step, loaded + inputs, outs, weights)
 
     @pl.when(step == steps - 1)
     def _():
-        for copy_out in gone:
+        for copy_out in gone[len(loads) :]:
             copy_out.wait()
 
 
-def placed(body, steps, held, columns, inputs, in_specs, outs, out_specs, block_index, name, flops):
+def placed(body, steps, held, columns, loads, inputs, in_specs, outs, out_specs, block_index, name, flops, vmem):
     arrays, plans = [], []
     for blocks, width in zip(held, columns):
         plan = []
@@ -320,28 +331,29 @@
     rows = min(array.shape[0] for array in arrays) // 16 * 16
     rows = rows - (16 if name == "key_rows" else 0)
     shapes = [(len(plan) * rows, width) for plan, width in zip(plans, columns)]
-    anywhere = pl.BlockSpec(memory_space=pl.ANY)
-    counts = (len(arrays), len(inputs), len(outs), len(plans), len(plans))
+    anywhere = pl.BlockSpec(memory_space=pltpu.HBM)
+    counts = (len(arrays), len(loads), len(inputs), len(outs), len(plans), len(plans), len(loads))
     return pl.pallas_call(
         functools.partial(placed_kernel, body, plans, counts, steps),
         grid_spec=pltpu.PrefetchScalarGridSpec(
             num_scalar_prefetch=1,
             grid=(steps,),
-            in_specs=[anywhere] * len(arrays) + in_specs,
+            in_specs=[anywhere] * (len(arrays) + len(loads)) + in_specs,
             out_specs=out_specs + [anywhere] * len(plans),
             scratch_shapes=[pltpu.VMEM(shape, bf16) for shape in shapes]
+            + [pltpu.VMEM(array.shape, array.dtype) for array in loads]
             + [
-                pltpu.SemaphoreType.DMA((sum(len(plan) for plan in plans),)),
+                pltpu.SemaphoreType.DMA((sum(len(plan) for plan in plans) + len(loads),)),
                 pltpu.SemaphoreType.DMA((len(plans),)),
             ],
         ),
         out_shape=outs + [jax.ShapeDtypeStruct(shape, bf16) for shape in shapes],
-        compiler_params=pltpu.CompilerParams(vmem_limit_bytes=56 * 1024 * 1024),
+        compiler_params=pltpu.CompilerParams(vmem_limit_bytes=vmem * 1024 * 1024),
         cost_estimate=pl.CostEstimate(
             flops=flops, bytes_accessed=4 * sum(h * w for h, w in shapes), transcendentals=0
         ),
         name=name,
-    )(block_index[None].astype(jnp.int32), *arrays, *inputs)
+    )(block_index[None].astype(jnp.int32), *arrays, *loads, *inputs)
 
 
 def in_turn(held):
@@ -368,7 +380,7 @@
     return pl.pallas_call(
         body,
         out_shape=[jax.ShapeDtypeStruct(shape, dtype) for shape, dtype in outs],
-        compiler_params=pltpu.CompilerParams(vmem_limit_bytes=40 * 1024 * 1024),
+        compiler_params=pltpu.CompilerParams(vmem_limit_bytes=28 * 1024 * 1024),
         cost_estimate=pl.CostEstimate(flops=0, bytes_accessed=2 * size, transcendentals=0),
         name=name,
     )(*inputs)
@@ -456,9 +468,9 @@
         heads,
         held,
         columns,
-        [rows, *table],
+        [rows],
+        list(table),
         [
-            pl.BlockSpec((count, depth), fixed, pipeline_mode=once),
             pl.BlockSpec((count, HD), fixed, pipeline_mode=once),
             pl.BlockSpec((count, HD), fixed, pipeline_mode=once),
         ],
@@ -467,6 +479,7 @@
         block_index,
         name,
         2 * rows.size * columns[0],
+        20,
     )
 
 
@@ -493,6 +506,7 @@
         count // step,
         held,
         [width, width],
+        [],
         [rows],
         [pl.BlockSpec((step, depth), lambda n, b: (n, 0))],
         [jax.ShapeDtypeStruct((count, width), dtype) for dtype in (bf16, f32, f32)],
@@ -500,10 +514,11 @@
         block_index,
         "hidden_units",
         4 * rows.size * width,
-    )
-
-
-def down_rows(hidden, held, block_index):
+        40,
+    )
+
+
+def down_rows(hidden, held, block_index, pieces):
     count, width = hidden.shape
     depth = len(held) * held[0][0].shape[0]
     step = 768 if depth % 768 == 0 else 256
@@ -513,7 +528,7 @@
         value = lax.dot_general(
             inputs[0][...], weights[0][here, :], (((1,), (1,)), ((), ())), preferred_element_type=f32
         )
-        outs[0][...] = value.astype(bf16)
+        put_pieces(outs, value)
 
     return placed(
         body,
@@ -521,12 +536,14 @@
         [held],
         [width],
         [hidden],
-        [pl.BlockSpec((count, width), lambda n, b: (0, 0), pipeline_mode=pl.Buffered(1))],
-        [jax.ShapeDtypeStruct((count, depth), bf16)],
-        [pl.BlockSpec((count, step), lambda n, b: (0, n))],
+        [],
+        [],
+        [jax.ShapeDtypeStruct((count // pieces, depth), bf16)] * pieces,
+        [pl.BlockSpec((count // pieces, step), lambda n, b: (0, n))] * pieces,
         block_index,
         "down_rows",
         2 * hidden.size * depth,
+        24,
     )
 
 
@@ -554,7 +571,7 @@
         in_specs=specs,
         out_specs=pl.BlockSpec((step, width), lambda n: (n, 0)),
         out_shape=jax.ShapeDtypeStruct((depth, width), bf16),
-        compiler_params=pltpu.CompilerParams(vmem_limit_bytes=40 * 1024 * 1024),
+        compiler_params=pltpu.CompilerParams(vmem_limit_bytes=24 * 1024 * 1024),
         cost_estimate=pl.CostEstimate(
             flops=2 * rows * depth * width, bytes_accessed=2 * (rows * depth * len(pairs) + depth * width), transcendentals=0
         ),
@@ -563,11 +580,11 @@
 
 
 def normed_back_kernel(count, q_ref, wq_ref, kv_ref, wkv_ref, inverse_ref, *refs):
-    hidden, (out_ref, scale_ref) = refs[:count], refs[count:]
+    hidden, (*outs, scale_ref) = refs[:count], refs[count:]
     nt = (((1,), (1,)), ((), ()))
     total = lax.dot_general(q_ref[...], wq_ref[...], nt, preferred_element_type=f32)
     total += lax.dot_general(kv_ref[...], wkv_ref[...], nt, preferred_element_type=f32)
-    out_ref[...] = total.astype(bf16)
+    put_pieces(outs, total)
     grad_scale, first = jnp.zeros((1, total.shape[1]), f32), 0
     for part in hidden:
         here = slice(first, first + part.shape[0])
@@ -577,7 +594,7 @@
     scale_ref[...] = grad_scale
 
 
-def normed_back(grad_query, query_weight, grad_kv, kv_weight, inverse, hidden):
+def normed_back(grad_query, query_weight, grad_kv, kv_weight, inverse, hidden, pieces):
     rows, width = grad_query.shape
     kv_width = grad_kv.shape[1]
     columns = query_weight.shape[0]
@@ -595,9 +612,11 @@
             pl.BlockSpec((rows, 1), fixed, pipeline_mode=once),
         ]
         + [pl.BlockSpec((part.shape[0], step), lambda n: (0, n)) for part in hidden],
-        out_specs=[pl.BlockSpec((rows, step), lambda n: (0, n)), pl.BlockSpec((1, step), lambda n: (0, n))],
-        out_shape=[jax.ShapeDtypeStruct((rows, columns), bf16), jax.ShapeDtypeStruct((1, columns), f32)],
-        compiler_params=pltpu.CompilerParams(vmem_limit_bytes=40 * 1024 * 1024),
+        out_specs=[pl.BlockSpec((rows // pieces, step), lambda n: (0, n))] * pieces
+        + [pl.BlockSpec((1, step), lambda n: (0, n))],
+        out_shape=[jax.ShapeDtypeStruct((rows // pieces, columns), bf16)] * pieces
+        + [jax.ShapeDtypeStruct((1, columns), f32)],
+        compiler_params=pltpu.CompilerParams(vmem_limit_bytes=20 * 1024 * 1024),
         cost_estimate=pl.CostEstimate(
             flops=2 * rows * columns * (width + kv_width), bytes_accessed=4 * rows * columns, transcendentals=0
         ),
@@ -793,7 +812,7 @@
             in_specs=[
                 pl.BlockSpec(queries.shape, whole),
             ]
-            + [pl.BlockSpec(memory_space=pl.ANY)] * len(pieces),
+            + [pl.BlockSpec(memory_space=pltpu.HBM)] * len(pieces),
             out_specs=[
                 pl.BlockSpec(queries.shape, whole),
                 pl.BlockSpec(queries.shape, whole),
@@ -812,7 +831,7 @@
             jax.ShapeDtypeStruct(queries.shape, f32),
             jax.ShapeDtypeStruct((2, 1, rows), f32),
         ],
-        compiler_params=pltpu.CompilerParams(vmem_limit_bytes=40 * 1024 * 1024),
+        compiler_params=pltpu.CompilerParams(vmem_limit_bytes=14 * 1024 * 1024 + 2 * kv_size),
         cost_estimate=pl.CostEstimate(
             flops=visits * rows * span_len * HD * 4,
             bytes_accessed=kv_size * 2 + queries.size * 12,
@@ -843,7 +862,7 @@
                 pl.BlockSpec(table[0].shape, whole),
                 pl.BlockSpec(table[0].shape, whole),
             ]
-            + [pl.BlockSpec(memory_space=pl.ANY)] * len(pieces),
+            + [pl.BlockSpec(memory_space=pltpu.HBM)] * len(pieces),
             out_specs=[
                 pl.BlockSpec(queries.shape, whole),
                 pl.BlockSpec((span_len, 2 * HD), lambda s, t: (jnp.minimum(s, tiles // 2 - 1), 0)),
@@ -863,7 +882,7 @@
             jax.ShapeDtypeStruct((tiles * span_len // 2, 2 * HD), bf16),
             jax.ShapeDtypeStruct((tiles * span_len // 2, 2 * HD), bf16),
         ],
-        compiler_params=pltpu.CompilerParams(vmem_limit_bytes=40 * 1024 * 1024),
+        compiler_params=pltpu.CompilerParams(vmem_limit_bytes=18 * 1024 * 1024 + 2 * kv_size),
         cost_estimate=pl.CostEstimate(
             flops=visits * rows * span_len * HD * 10,
             bytes_accessed=kv_size * 4 + queries.size * 16,
@@ -1027,8 +1046,8 @@
             kv_rows, kv_weight = project(normed_full, [kv_held], [2 * HD], table, 1, block_index, "key_rows")
             return kv_rows, kv_weight, scale_rows, normed_full, inverse_full
 
-        held, parts = lax.optimization_barrier((held, parts))
-        query_output = {mask: send(query_output_local, mask, held[pair ^ top]) for mask in (*far_masks, pair)}
+        first = held[pair ^ top], *[part for slot, pieces in parts.items() if slot.bit_count() > 1 for part in pieces]
+        query_output = {mask: send(query_output_local, mask, *first) for mask in (*far_masks, pair)}
         results, query_output = segment(normed_keys, (held, parts), (), query_output)
         return results, parts, query_output
 
@@ -1062,12 +1081,11 @@
     def keys_and_queries(kv_far, kv_near, query_output_last):
         across = {mask ^ pair: swap(block, (pair, 0)) for mask, block in kv_far.items()}
         chips = query_output_chips | query_output_last
-        held = query_output_last | {-1 - mask: piece for mask, piece in ({pair: kv_near} | kv_far | across).items()}
+        held = query_output_last | {-1 - mask: piece for mask, piece in ({pair: kv_near} | kv_far).items()}
         came, others = (), dict(cores)
         for mask, block in held.items():
             others[mask] = swap(tie(block, *came), (1, 0))
             came = (others[mask],)
-        pieces = {(-1 - mask) ^ 1: piece for mask, piece in others.items() if mask < 0}
         chips |= {mask ^ 1: block for mask, block in others.items() if mask >= 0}
         queries, query_weight, output_weight = project(
             normed_full,
@@ -1078,6 +1096,11 @@
             block_index,
             "query_rows",
         )
+        came += (queries,)
+        for mask, block in across.items():
+            others[-1 - mask] = swap(tie(block, *came), (1, 0))
+            came = (others[-1 - mask],)
+        pieces = {(-1 - mask) ^ 1: piece for mask, piece in others.items() if mask < 0}
         return across | pieces, query_weight, output_weight, queries
 
     first_near = far_spread(first_mine, kv_far[top])
@@ -1117,7 +1140,10 @@
 
     def join_units(ffn_in, first_cross, second_far):
         parts = {0: [ffn_in]}
-        parts |= gather_hop(parts, unit_axes, True, hops(len(unit_axes), True)[0])
+        plan = hops(len(unit_axes), True)
+        parts |= gather_hop(parts, unit_axes, True, plan[0])
+        flat = [part for t in plan[0][:-1] for part in parts[t]]
+        parts |= gather_hop(parts, unit_axes, True, plan[1], flat)
 
         def later_hops(parts):
             parts = gather_rows(None, unit_axes, True, parts)
@@ -1156,8 +1182,8 @@
         mask ^ pair ^ 1: (swap(block, (1, 0)) if mask else second_cross_core, 0)
         for mask, block in second_across.items()
     }
-    ffn_part, down_weight = down_rows(hidden, down_held, block_index)
-    ffn_terms = row_sum(ffn_part, unit_axes)
+    *ffn_parts, down_weight = down_rows(hidden, down_held, block_index, 1 << len(unit_axes))
+    ffn_terms = scatter_rows(ffn_parts, unit_axes)
     layer_out, grad_ffn_out, scale_grad3 = whole_call(
         functools.partial(after_ffn_kernel, len(ffn_terms)),
         [(row_shape, bf16), (row_shape, bf16), (scale_shape, f32)],
@@ -1198,7 +1224,7 @@
         return product(ffn_full, act, 0, 0, bf16)
 
     back_plan = scatter_plan(len(unit_axes), True)
-    split_at = len(back_plan) - 2
+    split_at = next(i for i, hop in enumerate(back_plan) if 1 << (len(unit_axes) - 1) in hop)
 
     def beside_hops(bodies):
         results = []
@@ -1216,10 +1242,9 @@
         return beside, results
 
     def ffn_back_first(grad_gate_act, grad_up_act):
-        grad_ffn_part = two_products(grad_gate_act, gate_weight, grad_up_act, up_weight)
-        shaped = grad_ffn_part.reshape(-1, local_rows, model_width)
-        pieces, came = {t: [shaped[t]] for t in range(shaped.shape[0])}, ()
-        beside, results = beside_hops([lambda: weight_back(tie(grad_gate_act, grad_ffn_part)), unit_core])
+        parts = two_products(grad_gate_act, gate_weight, grad_up_act, up_weight, 1 << len(unit_axes))
+        pieces, came = {t: [part] for t, part in enumerate(parts)}, ()
+        beside, results = beside_hops([lambda: weight_back(tie(grad_gate_act, *parts)), unit_core])
         for number, subsets in enumerate(back_plan[:split_at]):
             pieces, came, _ = scatter_hop(pieces, unit_axes, True, subsets, came, beside(number))
         return pieces, results[1]
@@ -1229,27 +1254,37 @@
     )
 
     def ffn_back_last(ffn_pieces, grad_up_act, down_came):
-        pieces, came = ffn_pieces, ()
-        beside, results = beside_hops(
-            [lambda: weight_back(grad_up_act), lambda partial: (unit_core(partial), unit_sides(down_kept, down_came))]
-        )
-        for number, subsets in enumerate(back_plan[split_at:]):
-            pieces, came, _ = scatter_hop(pieces, unit_axes, True, subsets, came, beside(number))
+        last = 1 << (len(unit_axes) - 1)
+
+        def over_head(pieces, grad_up_act):
+            came = ()
+            beside, results = beside_hops(
+                [lambda: weight_back(grad_up_act), lambda partial: (unit_core(partial), unit_sides(down_kept, down_came))]
+            )
+            for number, subsets in enumerate(back_plan[split_at:]):
+                subsets = [t for t in subsets if t != last]
+                pieces, came, _ = scatter_hop(pieces, unit_axes, True, subsets, came, beside(number))
+            return pieces[0], results[1]
+
+        pieces = dict(ffn_pieces)
+        across = swap(pieces.pop(last)[0], unit_axes[-1])
+        (terms, results), across = segment(over_head, (pieces, grad_up_act), (), across)
         rows = whole_call(
-            functools.partial(after_ffn_back_kernel, len(pieces[0])),
+            functools.partial(after_ffn_back_kernel, len(terms) + 1),
             [(row_shape, f32), (row_shape, bf16), (scale_shape, f32), (scale_shape, f32)],
-            *pieces[0],
+            *terms,
+            across,
             resid,
             attn_out,
             out_grad,
             scale_rows,
             name="after_ffn_back",
         )
-        return (*rows, *results[1])
-
-    gate_came = send(gate_away, top, down_came)
-    (grad_resid, grad_attn, scale_grad2, scale_grad1, (up_away, up_kept), (down_far, down_own)), gate_came = segment(
-        ffn_back_last, (ffn_pieces, grad_up_act, down_came), (gate_away, gate_kept), gate_came
+        return (*rows, *results)
+
+    gate_came = [send(gate_away[0], top, down_came), None]
+    (grad_resid, grad_attn, scale_grad2, scale_grad1, (up_away, up_kept), (down_far, down_own)), gate_came[0] = segment(
+        ffn_back_last, (ffn_pieces, grad_up_act, down_came), (gate_away, gate_kept), gate_came[0]
     )
 
     def attend_back(grad_attn):
@@ -1262,16 +1297,17 @@
         middle = kv_terms.shape[0] // 2
         return grad_attn_full, grad_query_lin, kv_terms[:middle], kv_terms[middle:]
 
-    up_came = send(up_away, top, grad_attn)
+    gate_came[1] = send(gate_away[1], top, grad_attn)
+    up_came = [send(up_away[0], top, grad_attn), None]
     down_other = send(down_far, pair, grad_attn)
-    (grad_attn_full, grad_query_lin, kv_kept, kv_away), (up_came, down_other) = segment(
-        attend_back, (grad_attn,), (up_away, up_kept, down_far, down_own), (up_came, down_other)
+    (grad_attn_full, grad_query_lin, kv_kept, kv_away), (gate_came[1], up_came[0], down_other) = segment(
+        attend_back, (grad_attn,), (up_away, up_kept, down_far, down_own), (gate_came[1], up_came[0], down_other)
     )
 
     def projections_back(grad_query_lin, gate_came):
         core = core_sum(outer((normed_full, grad_query_lin), (grad_attn_full, mixed)))
         away, kept = pick(core, bit_count - 2, 1 - unit_side), pick(core, bit_count - 2, unit_side)
-        return away, kept, unit_sides(gate_kept, gate_came)
+        return (away[0], away[1]), kept, unit_sides(gate_kept, jnp.stack(gate_came))
 
     kv_came = send(kv_away, pair)
     (query_output_away, query_output_kept, (gate_far, gate_own)), kv_came = segment(
@@ -1282,51 +1318,55 @@
         middle = kv_terms.shape[0] // 2
         kv_terms = plus(kv_terms[:middle], swap(kv_terms[middle:], (mask, 0))).astype(bf16)
 
-    def beside_last_keys(up_came, down_other):
-        return unit_sides(up_kept, up_came), unit_whole(down_own, down_other).T
+    def beside_last_keys(down_other):
+        return unit_whole(down_own, down_other).T
 
     kv_came = send(kv_terms[1], top)
     gate_other = send(gate_far, pair, kv_terms)
-    ((up_far, up_own), out_down), (kv_came, gate_other) = segment(
-        beside_last_keys, (up_came, down_other), (kv_terms,), (kv_came, gate_other)
-    )
+    out_down, (kv_came, gate_other) = segment(beside_last_keys, (down_other,), (kv_terms,), (kv_came, gate_other))
 
     def normed_rows_back(kv_kept, kv_came):
-        (grad_kv_lin,) = whole_call(
-            key_value_grad_kernel,
-            [((group_rows, 2 * HD), bf16)],
-            kv_kept,
-            kv_came,
-            *table,
-            name="key_value_grad",
-        )
-        terms = core_sum(outer((normed_full, grad_kv_lin)))
-        away, kept = pick(terms, bit_count - 2, 1 - unit_side), pick(terms, bit_count - 2, unit_side)
-
-        def products_back(grad_kv_lin):
-            grad_normed_part, scale_grad0 = normed_back(
-                grad_query_lin, query_weight, grad_kv_lin, kv_weight, inverse_full, hidden_slots
+        normed_plan = scatter_plan(len(head_axes), False)
+
+        def first_sums_back(kv_kept, kv_came):
+            (grad_kv_lin,) = whole_call(
+                key_value_grad_kernel,
+                [((group_rows, 2 * HD), bf16)],
+                kv_kept,
+                kv_came,
+                *table,
+                name="key_value_grad",
             )
-            scale_grad = jnp.concatenate([scale_grad0, scale_grad1, scale_grad2, scale_grad3], 0)
-            scale_grad = scale_grad.reshape(scale_count, block_count, model_rows).transpose(1, 0, 2)
-            scale_grad = scale_grad.reshape((2,) * bit_count + scale_grad.shape[1:])
-            for at, mask in enumerate([1] + chip_masks[:-1]):
-                scale_grad = halve(scale_grad, bit_count - 1 - at, mask)
-            scale_grad = jnp.pad(scale_grad.astype(bf16), ((0, 0), (0, 16 - scale_count), (0, 2 * HD - model_rows)))
-            return grad_normed_part, scale_grad
-
-        wkv_came = send(away, pair)
-        (grad_normed_part, scale_grad), wkv_came = segment(products_back, (grad_kv_lin,), (away, kept), wkv_came)
-        wkv_terms = plus(kept, wkv_came).astype(bf16)
-        for at, mask in list(enumerate(chip_masks))[1:-1]:
-            wkv_terms = halve(wkv_terms, bit_count - 2 - at, mask).astype(bf16)
-
-        def sums_back(grad_normed_part):
-            terms = row_sum(grad_normed_part, head_axes)
+            *parts, scale_grad0 = normed_back(
+                grad_query_lin, query_weight, grad_kv_lin, kv_weight, inverse_full, hidden_slots, head_count
+            )
+
+            def key_weights_back(grad_kv_lin, scale_grad0):
+                scale_grad = jnp.concatenate([scale_grad0, scale_grad1, scale_grad2, scale_grad3], 0).astype(bf16)
+                scale_grad = scale_grad.reshape(scale_count, block_count, model_rows).transpose(1, 0, 2)
+                scale_grad = jnp.pad(scale_grad, ((0, 0), (0, 16 - scale_count), (0, 2 * HD - model_rows)))
+                partial = outer((normed_full, grad_kv_lin)).reshape(block_count, model_rows, 2 * HD)
+                terms = core_sum(jnp.concatenate([partial, scale_grad], 1).reshape(-1, 2 * HD))
+                return pick(terms, bit_count - 2, 1 - unit_side), pick(terms, bit_count - 2, unit_side)
+
+            def beside(moved):
+                return segment(key_weights_back, (grad_kv_lin, scale_grad0), (), moved)
+
+            pieces = {t: [part] for t, part in enumerate(parts)}
+            pieces, _, terms = scatter_hop(pieces, head_axes, False, normed_plan[0], (), beside)
+            return pieces, terms
+
+        query_output_came = send(query_output_away[0], pair, kv_came)
+        (pieces, (away, kept)), query_output_came = segment(first_sums_back, (kv_kept, kv_came), (), query_output_came)
+
+        def sums_back(pieces):
+            came = ()
+            for subsets in normed_plan[1:]:
+                pieces, came, _ = scatter_hop(pieces, head_axes, False, subsets, came)
             (grad_in,) = whole_call(
-                functools.partial(after_all_kernel, len(terms)),
+                functools.partial(after_all_kernel, len(pieces[0])),
                 [(row_shape, f32)],
-                *terms,
+                *pieces[0],
                 hidden_in,
                 grad_resid,
                 scale_rows,
@@ -1334,19 +1374,29 @@
             )
             return grad_in
 
-        wkv_terms = jnp.concatenate([wkv_terms, scale_grad], 1)
-        away, kept = lax.optimization_barrier((pick(wkv_terms, 0, 1 - side(top)), pick(wkv_terms, 0, side(top))))
-        wkv_came = send(away, top)
-        query_output_came = send(query_output_away, pair, away)
-        grad_in, (wkv_came, query_output_came) = segment(
-            sums_back, (grad_normed_part,), (away, kept), (wkv_came, query_output_came)
-        )
-        return (grad_in, plus(kept, wkv_came).astype(bf16)), query_output_came
-
-    (grad_in, grad_wkv), query_output_came = segment(
-        normed_rows_back, (kv_terms[0], kv_came), (up_far, up_own, out_down)
-    )[0]
-    query_output_terms = plus(query_output_kept, query_output_came).astype(bf16)
+        wkv_came = send(away, pair)
+        grad_in, wkv_came = segment(sums_back, (pieces,), (away, kept), wkv_came)
+        wkv_terms = plus(kept, wkv_came).astype(bf16)
+        for at, mask in list(enumerate(chip_masks))[1:-1]:
+            wkv_terms = halve(wkv_terms, bit_count - 2 - at, mask).astype(bf16)
+        return grad_in, pick(wkv_terms, 0, 1 - side(top)), pick(wkv_terms, 0, side(top)), query_output_came
+
+    up_came[1] = send(up_away[1], top, kv_came)
+    query_output_came = [None, None]
+    (grad_in, wkv_away, wkv_kept, query_output_came[0]), up_came[1] = segment(
+        normed_rows_back, (kv_terms[0], kv_came), (out_down, *query_output_away), up_came[1]
+    )
+    wkv_came = send(wkv_away, top)
+    query_output_came[1] = send(query_output_away[1], pair, wkv_away)
+
+    def beside_key_weights(up_came, gate_other):
+        return unit_sides(up_kept, jnp.stack(up_came)), unit_whole(gate_own, gate_other)
+
+    ((up_far, up_own), out_gate), (wkv_came, query_output_came[1]) = segment(
+        beside_key_weights, (up_came, gate_other), (wkv_away, wkv_kept), (wkv_came, query_output_came[1])
+    )
+    grad_wkv = plus(wkv_kept, wkv_came).astype(bf16)
+    query_output_terms = plus(query_output_kept, jnp.stack(query_output_came)).astype(bf16)
     for at, mask in list(enumerate(chip_masks))[1:-1]:
         query_output_terms = halve(query_output_terms, bit_count - 2 - at, mask).astype(bf16)
     query_output_away = pick(query_output_terms, 0, 1 - side(top))
@@ -1366,10 +1416,10 @@
         wkv_ordered = wkv_ordered[:, :model_rows].reshape(KVH, head_count // KVH, model_rows, 2, HD).sum(1)
         out_key = wkv_ordered[:, :, 0].transpose(1, 0, 2).reshape(model_rows, KVH * HD)
         out_value = wkv_ordered[:, :, 1].transpose(1, 0, 2).reshape(model_rows, KVH * HD)
-        return out_key, out_value, scale_total, unit_whole(gate_own, gate_other)
-
-    (out_key, out_value, scale_total, out_gate), (query_output_came, up_other) = segment(
-        head_rows, (grad_wkv,), (query_output_away,), (query_output_came, up_other)
+        return out_key, out_value, scale_total
+
+    (out_key, out_value, scale_total), (query_output_came, up_other) = segment(
+        head_rows, (grad_wkv,), (query_output_away, up_far), (query_output_came, up_other)
     )
     out_query_output = plus(pick(query_output_terms, 0, side(top)), query_output_came)
     out_query = out_query_output[:, :query_width]

time: 823 us -> 765 us (0.930)
  waiting for transfers between devices: 397 us -> 339 us
    ppermute x63 -> x64, waiting for transfers between devices: 237 us -> 199 us  [swap(): lax.ppermute(value, 'blk', [(i, i ^ blk_mask) for i in range(block_count)])]
    ppermute x48, waiting for transfers between devices: 160 us -> 140 us  [swap(): lax.ppermute(value, 'head', [(i, i ^ head_mask) for i in range(head_count)])]
    ppermute x63 -> x64, starting transfers between devices: 42.3 us -> 48.6 us  [swap(): lax.ppermute(value, 'blk', [(i, i ^ blk_mask) for i in range(block_count)])]
    squeeze x15 -> x14, local copies, waits for them, and re-layouts: 20.7 us -> 20.9 us  [pick(): return lax.dynamic_index_in_dim(value, index, dim, keepdims=False)]
  transfers between devices with their start and end apart: 111 -> 112, of which waited for: 77 -> 71; matrix products, arithmetic and copies ran while one was open for 18% -> 19% of each run, Pallas kernels for 14% -> 15%
where the time goes in v3:
time: 765 us; the launch traced here: 755 us
  waiting for transfers between devices  339 us (44%)
  Pallas kernels  129 us (17%)
  starting transfers between devices  95 us (12%)
  local copies, waits for them, and re-layouts  80.1 us (10%)
  other arithmetic  57.8 us (8%)
  matrix products  45.8 us (6%)
    ppermute x64, waiting for transfers between devices, swap(): lax.ppermute(value, 'blk', [(i, i ^ blk_mask) for i in range(block_count)])  199 us
    ppermute x48, waiting for transfers between devices, swap(): lax.ppermute(value, 'head', [(i, i ^ head_mask) for i in range(head_count)])  140 us
    ppermute x64, starting transfers between devices, swap(): lax.ppermute(value, 'blk', [(i, i ^ blk_mask) for i in range(block_count)])  48.6 us
    ppermute x48, starting transfers between devices, swap(): lax.ppermute(value, 'head', [(i, i ^ head_mask) for i in range(head_count)])  46.4 us
    dot_general x6, matrix products, product(): lax.dot_general(left, right, (((left_dim,), (right_dim,)), ((), ())), pre...  45.8 us
    pallas_call x4, Pallas kernels, placed(): pl.pallas_call(functools.partial(placed_kernel, body, plans, counts, step...  41.7 us
    squeeze x14, local copies, waits for them, and re-layouts, pick(): return lax.dynamic_index_in_dim(value, index, dim, keepdims=False)  20.9 us
    pallas_call x6, Pallas kernels, whole_call(): pl.pallas_call(body, out_shape=[jax.ShapeDtypeStruct(shape, dtype) for sh...  18.5 us
  transfers between devices with their start and end apart: 112, of which 71 were waited for; matrix products, arithmetic and copies ran while one was open for 19% of the time, Pallas kernels for 15%

profile of v3, /device:TPU:0, one launch (start us, length us, event | category | flops | bytes accessed | tf_op | source)
XLA Modules:
  0.0 755.1 jit_solution(16084553173542701940)
XLA Ops:
  38.2 21.7 %conditional.25 = (bf16[512,512]{1,0:T(8,128)(2,1)}, bf16[2304,512]{1,0:T(8,128)(2,1)}, f32[4,2304]{1,0:T(4,128)}, bf16[512,2304]{1,0:T(8,128)(2,1)}, f32[512,1]{1,0:T(8,128)}) conditional(s32[]{:T(128)} %bitcast.60, () %tuple.299, (s32[]{:T(128)}, bf16[304,512]{1,0:T(8,128)(2,1)S(1)}, bf16[304,512]{1,0:T(8,128)(2,1)S(1)}, ...), branch_computations={%region_2.3_spmd, %region_3.4_spmd} | conditional | flops 1207968768 | bytes 29862424 | solution.py:946
  75.1 14.0 %collective-permute-done.71 = bf16[512,512]{1,0:T(8,128)(2,1)} collective-permute-done((bf16[512,512]{1,0:T(8,128)(2,1)}, bf16[512,512]{1,0:T(8,128)(2,1)}, u32[]{:S(2)}, u32[]{:S(2)}) %collective-permute-start.71) | collective-permute-done | bytes 524320 | tf_op jit(solution)/shard_map/ppermute | solution.py:60
  100.5 33.0 %conditional.27 = (bf16[512,512]{1,0:T(8,128)(2,1)}, bf16[512,512]{1,0:T(8,128)(2,1)}, bf16[512,512]{1,0:T(8,128)(2,1)}, bf16[512,512]{1,0:T(8,128)(2,1)}, bf16[...) conditional(s32[]{:T(128)} %bitcast.60, () %tuple.297, ...), branch_computations={%region_6.7_spmd, %region_7.8_spmd} | conditional | flops 1207959552 | bytes 24772900 | solution.py:946
  111.0 20.3 %collective-permute-done.7 = bf16[512,512]{1,0:T(8,128)(2,1)} collective-permute-done((bf16[512,512]{1,0:T(8,128)(2,1)}, bf16[512,512]{1,0:T(8,128)(2,1)}, u32[]{:S(2)}, u32[]{:S(2)}) %collective-permute-start.7) | collective-permute-done | bytes 524320 | tf_op jit(solution)/shard_map/cond/branch_1_fun/ppermute | solution.py:60
  138.7 46.3 %conditional.28 = (bf16[512,512]{1,0:T(8,128)(2,1)S(1)}, f32[512,512]{1,0:T(8,128)S(1)}, f32[2,1,512]{2,1,0:T(1,128)S(1)}, f32[128,2304]{1,0:T(8,128)S(1)}, f32[...) conditional(s32[]{:T(128)} %bitcast.60, () %tuple.296, ...), branch_computations={%region_8.9_spmd, %region_9.10_spmd} | conditional | flops 3494379520 | bytes 57549292 | solution.py:946
  141.8 12.1 %attention_forward.1 = (bf16[512,512]{1,0:T(8,128)(2,1)S(1)}, f32[512,512]{1,0:T(8,128)S(1)}, f32[2,1,512]{2,1,0:T(1,128)S(1)}) custom-call(s32[19]{0:T(128)S(1)} %get-tuple-element.510.spans_ref, bf16[512,512]{1,0:T(8,128)(2,1)} %get-tuple-element.511.q_ref, bf16[512,512]{1,0:T(8,128)(2,1)} %get-tuple-element.512.refs_0_, ...), custom_call_target="tpu_custom_call" | custom-call | flops 2281701376 | bytes 7340032 | tf_op jit(solution)/shard_map/cond/branch_1_fun/attention_forward/pallas_call | solution.py:807
  169.7 13.1 %collective-permute-done.46.refs_1_ = bf16[128,2304]{1,0:T(8,128)(2,1)S(1)} collective-permute-done((bf16[128,2304]{1,0:T(8,128)(2,1)S(1)}, bf16[128,2304]{1,0:T(8,128)(2,1)S(1)}, u32[]{:S(2)}, u32[]{:S(2)}) %collective-permute-start.46) | collective-permute-done | bytes 589856 | tf_op jit(solution)/shard_map/cond/branch_1_fun/ppermute | solution.py:59
  194.0 74.4 %conditional.29 = (bf16[1024,2304]{1,0:T(8,128)(2,1)}, bf16[288,2304]{1,0:T(8,128)(2,1)}, bf16[288,2304]{1,0:T(8,128)(2,1)}, bf16[288,1152]{1,0:T(8,128)(2,1)}) conditional(s32[]{:T(128)} %bitcast.60, () %tuple.321, (s32[16]{0:T(128)S(1)}, bf16[128,2304]{1,0:T(8,128)(2,1)S(1)}, bf16[288,2304]{1,0:T(8,128)(2,1)}, bf16[288,2304]{1,0:T(8,128)(2,1)}, ...), branch_computations={%region_10.11_spmd, %region_11.14_spmd} | conditional | flops 2 | bytes 41583208 | solution.py:946
  212.2 23.0 %collective-permute-done.19 = bf16[128,2304]{1,0:T(8,128)(2,1)S(1)} collective-permute-done((bf16[128,2304]{1,0:T(8,128)(2,1)S(1)}, bf16[128,2304]{1,0:T(8,128)(2,1)S(1)}, u32[]{:S(2)}, u32[]{:S(2)}) %collective-permute-start.19) | collective-permute-done | bytes 589856 | tf_op jit(solution)/shard_map/cond/branch_1_fun/ppermute | solution.py:60
  237.8 30.7 %conditional = (bf16[1024,2304]{1,0:T(8,128)(2,1)}, bf16[288,2304]{1,0:T(8,128)(2,1)}, bf16[288,2304]{1,0:T(8,128)(2,1)}) conditional(s32[]{:T(128)} %bitcast.7, () %tuple.137, (bf16[128,2304]{1,0:T(8,128)(2,1)S(1)}, bf16[128,2304]{1,0:T(8,128)(2,1)S(1)}, bf16[128,2304]{1,0:T(8,128)(2,1)S(1)}, bf16[128,2304]{1,0:T(8,128)(2,1)S(1)}, ...), branch_computations={%region_12.12_spmd, %region_13.13_spmd} | conditional | bytes 28311816 | solution.py:946
  239.9 13.7 %collective-permute-done.9.refs_6_ = bf16[128,2304]{1,0:T(8,128)(2,1)S(1)} collective-permute-done((bf16[128,2304]{1,0:T(8,128)(2,1)S(1)}, bf16[128,2304]{1,0:T(8,128)(2,1)S(1)}, u32[]{:S(2)}, u32[]{:S(2)}) %collective-permute-start.9) | collective-permute-done | bytes 589856 | tf_op jit(solution)/shard_map/cond/branch_1_fun/cond/branch_1_fun/ppermute | solution.py:59
  269.2 26.2 %conditional.30 = (bf16[1024,1152]{1,0:T(8,128)(2,1)S(1)}, f32[1024,1152]{1,0:T(8,128)}, f32[1024,1152]{1,0:T(8,128)}, bf16[2304,1152]{1,0:T(8,128)(2,1)}, bf16[...) conditional(s32[]{:T(128)} %bitcast.60, () %tuple.320, (s32[]{:T(128)}, bf16[288,2304]{1,0:T(8,128)(2,1)}, ...), branch_computations={%region_14.15_spmd, %region_15.16_spmd} | conditional | flops 10871635968 | bytes 29196416 | solution.py:946
  273.5 21.6 %hidden_units.1 = (bf16[1024,1152]{1,0:T(8,128)(2,1)S(1)}, f32[1024,1152]{1,0:T(8,128)}, f32[1024,1152]{1,0:T(8,128)}, bf16[2304,1152]{1,0:T(8,128)(2,1)}, bf16[2304,1152]{1,0:T(8,128)(2,1)}) custom-call(s32[1]{0:T(128)} %bitcast.8.index_ref, bf16[288,1152]{1,0:T(8,128)(2,1)} %get-tuple-element.567.refs_0_, bf16[288,1152]{1,0:T(8,128)(2,1)} %get-tuple-element.568.refs_1_, ...), custom_call_target="tpu_custom_call" | custom-call | flops 10871635968 | bytes 21233664 | tf_op jit(solution)/shard_map/cond/branch_1_fun/hidden_units/pallas_call | solution.py:336
  325.9 11.7 %collective-permute-done.83 = bf16[128,2304]{1,0:T(8,128)(2,1)S(1)} collective-permute-done((bf16[128,2304]{1,0:T(8,128)(2,1)S(1)}, bf16[128,2304]{1,0:T(8,128)(2,1)S(1)}, u32[]{:S(2)}, u32[]{:S(2)}) %collective-permute-start.83) | collective-permute-done | bytes 589856 | tf_op jit(solution)/shard_map/ppermute | solution.py:60
  430.2 47.9 %conditional.31 = (bf16[128,2304]{1,0:T(8,128)(2,1)}, bf16[128,2304]{1,0:T(8,128)(2,1)}, bf16[128,2304]{1,0:T(8,128)(2,1)}, bf16[128,2304]{1,0:T(8,128)(2,1)}, b...) conditional(s32[]{:T(128)} %bitcast.60, () %tuple.339, ...), branch_computations={%region_16.17_spmd, %region_17.22_spmd} | conditional | flops 16321314816 | bytes 78742360 | solution.py:946
  430.2 14.8 %two_products.1 = (bf16[128,2304]{1,0:T(8,128)(2,1)}, bf16[128,2304]{1,0:T(8,128)(2,1)}, bf16[128,2304]{1,0:T(8,128)(2,1)}, bf16[128,2304]{1,0:T(8,128)(2,1)}, b...) custom-call(bf16[1024,1152]{1,0:T(8,128)(2,1)S(1)} %get-tuple-elemen, ...), custom_call_target="tpu_custom_call" | custom-call | flops 10871635968 | bytes 20054016 | tf_op jit(solution)/shard_map/cond/branch_1_fun/two_products/pallas_call | solution.py:176
  462.1 13.6 %conditional.2 = (bf16[2,288,1152]{2,1,0:T(8,128)(2,1)}, bf16[2,288,1152]{2,1,0:T(8,128)(2,1)}) conditional(s32[]{:T(128)} %bitcast.14, () %tuple.149, (bf16[2304,1152]{1,0:T(8,128)(2,1)}, s32[]{:T(128)}) %tuple.153), branch_computations={%region_20.20_spmd, %region_21.21_spmd} | conditional | flops 5308464 | bytes 29196844 | solution.py:946
  482.2 45.5 %conditional.32 = (f32[128,2304]{1,0:T(8,128)}, bf16[128,2304]{1,0:T(8,128)(2,1)}, f32[1,2304]{1,0:T(1,128)S(1)}, f32[1,2304]{1,0:T(1,128)S(1)}, bf16[2,288,1152...) conditional(s32[]{:T(128)} %bitcast.60, () %tuple.338, ...), branch_computations={%region_22.23_spmd, %region_23.30_spmd} | conditional | flops 5449973760 | bytes 97248448 | solution.py:946
  483.3 36.3 %conditional.5 = (bf16[128,2304]{1,0:T(8,128)(2,1)}, bf16[128,2304]{1,0:T(8,128)(2,1)}, bf16[128,2304]{1,0:T(8,128)(2,1)}, bf16[2,288,1152]{2,1,0:T(8,128)(2,1)}...) conditional(s32[]{:T(128)} %bitcast.23, () %tuple.171, ...), branch_computations={%region_24.24_spmd, %region_25.29_spmd} | conditional | flops 5449973760 | bytes 84198384 | solution.py:946
  489.2 11.0 %conditional.3 = (bf16[2304,1152]{1,0:T(8,128)(2,1)}) conditional(s32[]{:T(128)} %bitcast.22, () %tuple.163, (bf16[1024,2304]{1,0:T(8,128)(2,1)}, bf16[1024,1152]{1,0:T(8,128)(2,1)}) %tuple.164), branch_computations={%region_26.25_spmd, %region_27.26_spmd} | conditional | flops 5438472192 | bytes 12386312 | solution.py:946
  506.1 12.9 %conditional.4 = (bf16[2,288,1152]{2,1,0:T(8,128)(2,1)}, bf16[2,288,1152]{2,1,0:T(8,128)(2,1)}, bf16[288,1152]{1,0:T(8,128)(2,1)}, bf16[288,1152]{1,0:T(8,128)(2,1)}) conditional(s32[]{:T(128)} %bitcast.22, () %tuple.162, (bf16[2304,1152]{1,0:T(8,128)(2,1)}, s32[]{:T(128)}, bf16[2,288,1152]{2,1,0:T(8,128)(2,1)S(1)}, ...), branch_computations={%region_28.27_spmd, %region_29.28_spmd} | conditional | flops 7962679 | bytes 57066156 | solution.py:946
  534.4 51.7 %conditional.33 = (bf16[512,2304]{1,0:T(8,128)(2,1)S(1)}, bf16[512,512]{1,0:T(8,128)(2,1)}, bf16[2,512,512]{2,1,0:T(8,128)(2,1)S(1)}, bf16[2,512,512]{2,1,0:T(8,128)(2,1)}) conditional(s32[]{:T(128)} %bitcast.60, () %tuple.337, (bf16[128,2304]{1,0:T(8,128)(2,1)}, bf16[2304,512]{1,0:T(8,128)(2,1)}, s32[19]{0:T(128)S(1)}, ...), branch_computations={%region_30.31_spmd, %region_31.32_spmd} | conditional | flops 6916669440 | bytes 68550944 | solution.py:946
  535.6 13.1 %collective-permute-done.58.refs_2_ = bf16[128,2304]{1,0:T(8,128)(2,1)S(1)} collective-permute-done((bf16[128,2304]{1,0:T(8,128)(2,1)}, bf16[128,2304]{1,0:T(8,128)(2,1)S(1)}, u32[]{:S(2)}, u32[]{:S(2)}) %collective-permute-start.58) | collective-permute-done | bytes 589856 | tf_op jit(solution)/shard_map/cond/branch_1_fun/ppermute | solution.py:59
  562.0 17.2 %attention_backward.1 = (bf16[512,512]{1,0:T(8,128)(2,1)}, bf16[2048,512]{1,0:T(8,128)(2,1)S(1)}, bf16[2048,512]{1,0:T(8,128)(2,1)S(1)}) custom-call(s32[19]{0:T(128)S(1)} %get-tuple-element.691.spans_ref, bf16[512,512]{1,0:T(8,128)(2,1)} %get-tuple-element.692.q_ref, bf16[512,512]{1,0:T(8,128)(2,1)S(1)} %convolution_convert_fusion.3.g_ref, ...), custom_call_target="tpu_custom_call" | custom-call | flops 5704253440 | bytes 12582912 | tf_op jit(solution)/shard_map/cond/branch_1_fun/attention_backward/pallas_call | solution.py:852
  588.4 15.7 %conditional.34 = (bf16[288,1024]{1,0:T(8,128)(2,1)}, bf16[288,1024]{1,0:T(8,128)(2,1)}, bf16[2,288,1024]{2,1,0:T(8,128)(2,1)}, bf16[288,1152]{1,0:T(8,128)(2,1)}, bf16[288,1152]{1,0:T(8,128)(2,1)}) conditional(s32[]{:T(128)} %bitcast.60, () %tuple.360, (bf16[512,2304]{1,0:T(8,128)(2,1)}, bf16[512,512]{1,0:T(8,128)(2,1)}, ...), branch_computations={%region_32.33_spmd, %region_33.34_spmd} | conditional | flops 2423955456 | bytes 79774144 | solution.py:946
  621.5 18.7 %collective-permute-done.105 = bf16[512,512]{1,0:T(8,128)(2,1)S(1)} collective-permute-done((bf16[512,512]{1,0:T(8,128)(2,1)}, bf16[512,512]{1,0:T(8,128)(2,1)S(1)}, u32[]{:S(2)}, u32[]{:S(2)}) %collective-permute-start.105) | collective-permute-done | bytes 524320 | tf_op jit(solution)/shard_map/ppermute | solution.py:60
  643.6 51.2 %conditional.36 = (f32[128,2304]{1,0:T(8,128)}, bf16[304,512]{1,0:T(8,128)(2,1)}, bf16[304,512]{1,0:T(8,128)(2,1)S(1)}, bf16[288,1024]{1,0:T(8,128)(2,1)}) conditional(s32[]{:T(128)} %bitcast.60, () %tuple.336, (s32[16]{0:T(128)S(1)}, bf16[512,512]{1,0:T(8,128)(2,1)S(1)}, bf16[512,512]{1,0:T(8,128)(2,1)S(1)}, f32[512,256]{1,0:T(8,128)S(1)}, ...), branch_computations={%region_36.37_spmd, %region_37.44_spmd} | conditional | flops 3636170752 | bytes 65967540 | solution.py:946
  644.5 27.5 %conditional.7 = (bf16[128,2304]{1,0:T(8,128)(2,1)}, bf16[128,2304]{1,0:T(8,128)(2,1)}, bf16[128,2304]{1,0:T(8,128)(2,1)}, bf16[2,304,512]{2,1,0:T(8,128)(2,1)}, bf16[2,304,512]{2,1,0:T(8,128)(2,1)}) conditional(s32[]{:T(128)} %bitcast.45, () %tuple.192, (bf16[512,512]{1,0:T(8,128)(2,1)S(1)}, bf16[512,512]{1,0:T(8,128)(2,1)S(1)}, ...), branch_computations={%region_38.38_spmd, %region_39.41_spmd} | conditional | flops 3634925568 | bytes 46133952 | solution.py:946
  657.3 11.5 %conditional.6 = (bf16[2,304,512]{2,1,0:T(8,128)(2,1)}, bf16[2,304,512]{2,1,0:T(8,128)(2,1)}) conditional(s32[]{:T(128)} %bitcast.44, () %tuple.186, (bf16[512,2304]{1,0:T(8,128)(2,1)}, bf16[512,512]{1,0:T(8,128)(2,1)S(1)}, f32[1,2304]{1,0:T(1,128)S(1)}, f32[1,2304]{1,0:T(1,128)S(1)}, f32[1,2304]{1,0:T(1,128)S(1)}, ...), branch_computations={%region_40.39_spmd, %region_41.40_spmd} | conditional | flops 1215467520 | bytes 23916968 | solution.py:946
  673.7 19.1 %conditional.8 = (f32[128,2304]{1,0:T(8,128)}) conditional(s32[]{:T(128)} %bitcast.45, () %tuple.191, (bf16[128,2304]{1,0:T(8,128)(2,1)}, bf16[128,2304]{1,0:T(8,128)(2,1)}, bf16[128,2304]{1,0:T(8,128)(2,1)}, bf16[128,2304]{1,0:T(8,128)(2,1)}, f32[128,2304]{1,0:T(8,128)}, /*index=5*/f32[4,2304]{1,0:T(4,128)}) %tuple.198), branch_computations={%region_42.42_spmd, %region_43.43_spmd} | conditional | bytes 11870296 | solution.py:946
  675.6 13.4 %collective-permute-done.23.refs_1_ = bf16[128,2304]{1,0:T(8,128)(2,1)S(1)} collective-permute-done((bf16[128,2304]{1,0:T(8,128)(2,1)}, bf16[128,2304]{1,0:T(8,128)(2,1)S(1)}, u32[]{:S(2)}, u32[]{:S(2)}) %collective-permute-start.23) | collective-permute-done | bytes 589856 | tf_op jit(solution)/shard_map/cond/branch_1_fun/cond/branch_1_fun/ppermute | solution.py:59
  722.6 26.8 %conditional.38 = (f32[288,1024]{1,0:T(8,128)}, f32[288,1024]{1,0:T(8,128)}, f32[4,288]{1,0:T(4,128)S(1)}) conditional(s32[]{:T(128)} %bitcast.60, () %tuple.378, (bf16[304,512]{1,0:T(8,128)(2,1)S(1)}, s32[]{:T(128)}) %tuple.380), branch_computations={%region_46.47_spmd, %region_47.49_spmd} | conditional | flops 626063 | bytes 35445624 | solution.py:946
  (537 shorter events, 576.3 us)
Async XLA Ops:
  0.7 24.0 %collective-permute-start.62 = (bf16[128,2304]{1,0:T(8,128)(2,1)}, bf16[128,2304]{1,0:T(8,128)(2,1)}, u32[]{:S(2)}, u32[]{:S(2)}) collective-permute-start(bf16[128,2304]{1,0:T(8,128)(2,1)} %param.60), channel_id=1, source_target_pairs={{0,1},{1,0},{2,3},{3,2},{4,5},{5,4},{6,7},{7,6},{8,9},{9,8},{10,11... | collective-permute-start | bytes 1769480 | tf_op jit(solution)/shard_map/ppermute | solution.py:59
  3.7 21.0 %collective-permute-start.63 = (bf16[128,2304]{1,0:T(8,128)(2,1)}, bf16[128,2304]{1,0:T(8,128)(2,1)}, u32[]{:S(2)}, u32[]{:S(2)}) collective-permute-start(bf16[128,2304]{1,0:T(8,128)(2,1)} %param.60), channel_id=1, source_target_pairs={{0,2},{1,3},{2,0},{3,1},{4,6},{5,7},{6,4},{7,5},{8,10},{9,11},{10,... | collective-permute-start | bytes 1769480 | tf_op jit(solution)/shard_map/ppermute | solution.py:59
  36.1 23.7 %collective-permute-start.69 = (bf16[288,1024]{1,0:T(8,128)(2,1)}, bf16[288,1024]{1,0:T(8,128)(2,1)}, u32[]{:S(2)}, u32[]{:S(2)}) collective-permute-start(bf16[288,1024]{1,0:T(8,128)(2,1)} %copy.56), channel_id=1, source_target_pairs={{0,8},{4,12},{8,0},{12,4},{16,24},{20,28},{24,16},{28,20},{1,9},{5... | collective-permute-start | bytes 1769480 | tf_op jit(solution)/shard_map/ppermute | solution.py:60
  37.6 26.1 %collective-permute-start.70 = (bf16[288,1024]{1,0:T(8,128)(2,1)}, bf16[288,1024]{1,0:T(8,128)(2,1)}, u32[]{:S(2)}, u32[]{:S(2)}) collective-permute-start(bf16[288,1024]{1,0:T(8,128)(2,1)} %copy.56), channel_id=1, source_target_pairs={{0,16},{4,20},{8,24},{12,28},{16,0},{20,4},{24,8},{28,12},{1,17},{... | collective-permute-start | bytes 1769480 | tf_op jit(solution)/shard_map/ppermute | solution.py:60
  63.8 35.1 %collective-permute-start.73 = (bf16[288,1024]{1,0:T(8,128)(2,1)}, bf16[288,1024]{1,0:T(8,128)(2,1)S(1)}, u32[]{:S(2)}, u32[]{:S(2)}) collective-permute-start(bf16[288,1024]{1,0:T(8,128)(2,1)} %collective-permute-done.70), channel_id=1, source_target_pairs={{0,8},{4,12},{8,0},{12,4},{16,24},{20,28},{24,16},{28,20},{1,9},{5... | collective-permute-start | bytes 1769480 | tf_op jit(solution)/shard_map/ppermute | solution.py:60
  63.8 25.3 %collective-permute-start.71 = (bf16[512,512]{1,0:T(8,128)(2,1)}, bf16[512,512]{1,0:T(8,128)(2,1)}, u32[]{:S(2)}, u32[]{:S(2)}) collective-permute-start(bf16[512,512]{1,0:T(8,128)(2,1)} %get-tuple-element.1123), channel_id=1, source_target_pairs={{0,16},{4,20},{8,24},{12,28},{16,0},{20,4},{24,8},{28,12},{1,17},{... | collective-permute-start | bytes 1572872 | tf_op jit(solution)/shard_map/ppermute | solution.py:60
  64.0 34.9 %collective-permute-start.72 = (bf16[512,512]{1,0:T(8,128)(2,1)}, bf16[512,512]{1,0:T(8,128)(2,1)}, u32[]{:S(2)}, u32[]{:S(2)}) collective-permute-start(bf16[512,512]{1,0:T(8,128)(2,1)} %get-tuple-element.1123), channel_id=1, source_target_pairs={{0,8},{4,12},{8,0},{12,4},{16,24},{20,28},{24,16},{28,20},{1,9},{5... | collective-permute-start | bytes 1572872 | tf_op jit(solution)/shard_map/ppermute | solution.py:60
  98.8 34.7 %collective-permute-start.74 = (bf16[288,1152]{1,0:T(8,128)(2,1)}, bf16[288,1152]{1,0:T(8,128)(2,1)}, u32[]{:S(2)}, u32[]{:S(2)}) collective-permute-start(bf16[288,1152]{1,0:T(8,128)(2,1)} %get-tuple-element.1162), channel_id=1, source_target_pairs={{0,16},{4,20},{8,24},{12,28},{16,0},{20,4},{24,8},{28,12},{1,17},{... | collective-permute-start | bytes 1990664 | tf_op jit(solution)/shard_map/ppermute | solution.py:60
  102.8 28.5 %collective-permute-start.7 = (bf16[512,512]{1,0:T(8,128)(2,1)}, bf16[512,512]{1,0:T(8,128)(2,1)}, u32[]{:S(2)}, u32[]{:S(2)}) collective-permute-start(bf16[512,512]{1,0:T(8,128)(2,1)} %get-tuple-element.495), channel_id=1, source_target_pairs={{0,8},{4,12},{8,0},{12,4},{16,24},{20,28},{24,16},{28,20},{1,9},{5... | collective-permute-start | bytes 1572872 | tf_op jit(solution)/shard_map/cond/branch_1_fun/ppermute | solution.py:60
  104.9 26.4 %collective-permute-start.6 = (bf16[512,512]{1,0:T(8,128)(2,1)}, bf16[512,512]{1,0:T(8,128)(2,1)}, u32[]{:S(2)}, u32[]{:S(2)}) collective-permute-start(bf16[512,512]{1,0:T(8,128)(2,1)} %get-tuple-element.495), channel_id=1, source_target_pairs={{0,4},{4,0},{8,12},{12,8},{16,20},{20,16},{24,28},{28,24},{1,5},{5... | collective-permute-start | bytes 1572872 | tf_op jit(solution)/shard_map/cond/branch_1_fun/ppermute | solution.py:60
  133.6 59.9 %collective-permute-start.75 = (bf16[288,2304]{1,0:T(8,128)(2,1)}, bf16[288,2304]{1,0:T(8,128)(2,1)}, u32[]{:S(2)}, u32[]{:S(2)}) collective-permute-start(bf16[288,2304]{1,0:T(8,128)(2,1)} %get-tuple-element.1179.refs_0_), channel_id=1, source_target_pairs={{0,16},{4,20},{8,24},{12,28},{16,0},{20,4},{24,8},{28,12},{1,17},{... | collective-permute-start | bytes 3981320 | tf_op jit(solution)/shard_map/ppermute | solution.py:60
  133.6 60.1 %collective-permute-start.76 = (bf16[288,2304]{1,0:T(8,128)(2,1)}, bf16[288,2304]{1,0:T(8,128)(2,1)}, u32[]{:S(2)}, u32[]{:S(2)}) collective-permute-start(bf16[288,2304]{1,0:T(8,128)(2,1)} %get-tuple-element.1178), channel_id=1, source_target_pairs={{0,8},{4,12},{8,0},{12,4},{16,24},{20,28},{24,16},{28,20},{1,9},{5... | collective-permute-start | bytes 3981320 | tf_op jit(solution)/shard_map/ppermute | solution.py:60
  193.7 74.8 %collective-permute-start.77 = (bf16[288,2304]{1,0:T(8,128)(2,1)}, bf16[288,2304]{1,0:T(8,128)(2,1)}, u32[]{:S(2)}, u32[]{:S(2)}) collective-permute-start(bf16[288,2304]{1,0:T(8,128)(2,1)} %collective-permute-done.76), channel_id=1, source_target_pairs={{0,16},{4,20},{8,24},{12,28},{16,0},{20,4},{24,8},{28,12},{1,17},{... | collective-permute-start | bytes 3981320 | tf_op jit(solution)/shard_map/ppermute | solution.py:60
  196.1 39.1 %collective-permute-start.19 = (bf16[128,2304]{1,0:T(8,128)(2,1)S(1)}, bf16[128,2304]{1,0:T(8,128)(2,1)S(1)}, u32[]{:S(2)}, u32[]{:S(2)}) collective-permute-start(bf16[128,2304]{1,0:T(8,128)(2,1)S(1)} %get-tuple-element.554), channel_id=1, source_target_pairs={{0,8},{4,12},{8,0},{12,4},{16,24},{20,28},{24,16},{28,20},{1,9},{5... | collective-permute-start | bytes 1769480 | tf_op jit(solution)/shard_map/cond/branch_1_fun/ppermute | solution.py:60
  209.1 26.1 %collective-permute-start.17 = (bf16[64,2304]{1,0:T(8,128)(2,1)S(1)}, bf16[64,2304]{1,0:T(8,128)(2,1)S(1)}, u32[]{:S(2)}, u32[]{:S(2)}) collective-permute-start(bf16[64,2304]{1,0:T(8,128)(2,1)S(1)} %slice.293), channel_id=1, source_target_pairs={{0,1},{1,0},{2,3},{3,2},{4,5},{5,4},{6,7},{7,6},{8,9},{9,8},{10,11... | collective-permute-start | bytes 884744 | tf_op jit(solution)/shard_map/cond/branch_1_fun/ppermute | solution.py:59
  210.6 24.6 %collective-permute-start.18 = (bf16[64,2304]{1,0:T(8,128)(2,1)S(1)}, bf16[64,2304]{1,0:T(8,128)(2,1)S(1)}, u32[]{:S(2)}, u32[]{:S(2)}) collective-permute-start(bf16[64,2304]{1,0:T(8,128)(2,1)S(1)} %slice.294), channel_id=1, source_target_pairs={{0,2},{1,3},{2,0},{3,1},{4,6},{5,7},{6,4},{7,5},{8,10},{9,11},{10,... | collective-permute-start | bytes 884744 | tf_op jit(solution)/shard_map/cond/branch_1_fun/ppermute | solution.py:59
  235.2 33.2 %collective-permute-start.20 = (bf16[288,1152]{1,0:T(8,128)(2,1)}, bf16[288,1152]{1,0:T(8,128)(2,1)}, u32[]{:S(2)}, u32[]{:S(2)}) collective-permute-start(bf16[288,1152]{1,0:T(8,128)(2,1)} %get-tuple-element.565), channel_id=1, source_target_pairs={{0,8},{4,12},{8,0},{12,4},{16,24},{20,28},{24,16},{28,20},{1,9},{5... | collective-permute-start | bytes 1990664 | tf_op jit(solution)/shard_map/cond/branch_1_fun/ppermute | solution.py:60
  268.5 31.3 %collective-permute-start.78 = (bf16[288,1152]{1,0:T(8,128)(2,1)}, bf16[288,1152]{1,0:T(8,128)(2,1)S(1)}, u32[]{:S(2)}, u32[]{:S(2)}) collective-permute-start(bf16[288,1152]{1,0:T(8,128)(2,1)} %get-tuple-element.1211.refs_2_), channel_id=1, source_target_pairs={{0,16},{4,20},{8,24},{12,28},{16,0},{20,4},{24,8},{28,12},{1,17},{... | collective-permute-start | bytes 1990664 | tf_op jit(solution)/shard_map/ppermute | solution.py:60
  269.2 25.8 %collective-permute-start.22 = (bf16[288,1152]{1,0:T(8,128)(2,1)}, bf16[288,1152]{1,0:T(8,128)(2,1)}, u32[]{:S(2)}, u32[]{:S(2)}) collective-permute-start(bf16[288,1152]{1,0:T(8,128)(2,1)} %get-tuple-element.584), channel_id=1, source_target_pairs={{0,4},{4,0},{8,12},{12,8},{16,20},{20,16},{24,28},{28,24},{1,5},{5... | collective-permute-start | bytes 1990664 | tf_op jit(solution)/shard_map/cond/branch_1_fun/ppermute | solution.py:60
  416.6 61.5 %collective-permute-start.99 = (bf16[2,288,1152]{2,1,0:T(8,128)(2,1)}, bf16[2,288,1152]{2,1,0:T(8,128)(2,1)}, u32[]{:S(2)}, u32[]{:S(2)}) collective-permute-start(bf16[2,288,1152]{2,1,0:T(8,128)(2,1)} %get-tuple-element.1501), channel_id=1, source_target_pairs={{0,16},{4,20},{8,24},{12,28},{16,0},{20,4},{24,8},{28,12},{1,17},{... | collective-permute-start | bytes 3981320 | tf_op jit(solution)/shard_map/ppermute | solution.py:60
  480.7 47.1 %collective-permute-start.100 = (bf16[288,1152]{1,0:T(8,128)(2,1)}, bf16[288,1152]{1,0:T(8,128)(2,1)}, u32[]{:S(2)}, u32[]{:S(2)}) collective-permute-start(bf16[288,1152]{1,0:T(8,128)(2,1)} %get-tuple-element.1277), channel_id=1, source_target_pairs={{0,16},{4,20},{8,24},{12,28},{16,0},{20,4},{24,8},{28,12},{1,17},{... | collective-permute-start | bytes 1990664 | tf_op jit(solution)/shard_map/ppermute | solution.py:60
  482.2 37.4 %collective-permute-start.56 = (bf16[128,2304]{1,0:T(8,128)(2,1)}, bf16[128,2304]{1,0:T(8,128)(2,1)S(1)}, u32[]{:S(2)}, u32[]{:S(2)}) collective-permute-start(bf16[128,2304]{1,0:T(8,128)(2,1)} %get-tuple-element.671), channel_id=1, source_target_pairs={{0,8},{4,12},{8,0},{12,4},{16,24},{20,28},{24,16},{28,20},{1,9},{5... | collective-permute-start | bytes 1769480 | tf_op jit(solution)/shard_map/cond/branch_1_fun/ppermute | solution.py:60
  527.8 58.4 %collective-permute-start.101 = (bf16[288,1152]{1,0:T(8,128)(2,1)}, bf16[288,1152]{1,0:T(8,128)(2,1)}, u32[]{:S(2)}, u32[]{:S(2)}) collective-permute-start(bf16[288,1152]{1,0:T(8,128)(2,1)} %get-tuple-element.1290), channel_id=1, source_target_pairs={{0,16},{4,20},{8,24},{12,28},{16,0},{20,4},{24,8},{28,12},{1,17},{... | collective-permute-start | bytes 1990664 | tf_op jit(solution)/shard_map/ppermute | solution.py:60
  531.9 56.4 %collective-permute-start.102 = (bf16[288,1152]{1,0:T(8,128)(2,1)}, bf16[288,1152]{1,0:T(8,128)(2,1)}, u32[]{:S(2)}, u32[]{:S(2)}) collective-permute-start(bf16[288,1152]{1,0:T(8,128)(2,1)} %get-tuple-element.1291), channel_id=1, source_target_pairs={{0,16},{4,20},{8,24},{12,28},{16,0},{20,4},{24,8},{28,12},{1,17},{... | collective-permute-start | bytes 1990664 | tf_op jit(solution)/shard_map/ppermute | solution.py:60
  533.2 55.1 %collective-permute-start.103 = (bf16[288,1152]{1,0:T(8,128)(2,1)}, bf16[288,1152]{1,0:T(8,128)(2,1)}, u32[]{:S(2)}, u32[]{:S(2)}) collective-permute-start(bf16[288,1152]{1,0:T(8,128)(2,1)} %get-tuple-element.1292), channel_id=1, source_target_pairs={{0,8},{4,12},{8,0},{12,4},{16,24},{20,28},{24,16},{28,20},{1,9},{5... | collective-permute-start | bytes 1990664 | tf_op jit(solution)/shard_map/ppermute | solution.py:60
  588.4 24.9 %collective-permute-start.104 = (bf16[2,512,512]{2,1,0:T(8,128)(2,1)}, bf16[2,512,512]{2,1,0:T(8,128)(2,1)}, u32[]{:S(2)}, u32[]{:S(2)}) collective-permute-start(bf16[2,512,512]{2,1,0:T(8,128)(2,1)} %get-tuple-element.1307), channel_id=1, source_target_pairs={{0,8},{4,12},{8,0},{12,4},{16,24},{20,28},{24,16},{28,20},{1,9},{5... | collective-permute-start | bytes 3145736 | tf_op jit(solution)/shard_map/ppermute | solution.py:60
  615.1 27.0 %collective-permute-start.106 = (bf16[288,1152]{1,0:T(8,128)(2,1)}, bf16[288,1152]{1,0:T(8,128)(2,1)S(1)}, u32[]{:S(2)}, u32[]{:S(2)}) collective-permute-start(bf16[288,1152]{1,0:T(8,128)(2,1)} %get-tuple-element.1312), channel_id=1, source_target_pairs={{0,8},{4,12},{8,0},{12,4},{16,24},{20,28},{24,16},{28,20},{1,9},{5... | collective-permute-start | bytes 1990664 | tf_op jit(solution)/shard_map/ppermute | solution.py:60
  616.3 24.0 %collective-permute-start.105 = (bf16[512,512]{1,0:T(8,128)(2,1)}, bf16[512,512]{1,0:T(8,128)(2,1)S(1)}, u32[]{:S(2)}, u32[]{:S(2)}) collective-permute-start(bf16[512,512]{1,0:T(8,128)(2,1)} %get-tuple-element.1510), channel_id=1, source_target_pairs={{0,16},{4,20},{8,24},{12,28},{16,0},{20,4},{24,8},{28,12},{1,17},{... | collective-permute-start | bytes 1572872 | tf_op jit(solution)/shard_map/ppermute | solution.py:60
  642.1 52.7 %collective-permute-start.107 = (bf16[288,1152]{1,0:T(8,128)(2,1)}, bf16[288,1152]{1,0:T(8,128)(2,1)}, u32[]{:S(2)}, u32[]{:S(2)}) collective-permute-start(bf16[288,1152]{1,0:T(8,128)(2,1)} %get-tuple-element.1330), channel_id=1, source_target_pairs={{0,16},{4,20},{8,24},{12,28},{16,0},{20,4},{24,8},{28,12},{1,17},{... | collective-permute-start | bytes 1990664 | tf_op jit(solution)/shard_map/ppermute | solution.py:60
  643.6 28.3 %collective-permute-start.39 = (bf16[288,1024]{1,0:T(8,128)(2,1)}, bf16[288,1024]{1,0:T(8,128)(2,1)}, u32[]{:S(2)}, u32[]{:S(2)}) collective-permute-start(bf16[288,1024]{1,0:T(8,128)(2,1)} %get-tuple-element.796), channel_id=1, source_target_pairs={{0,8},{4,12},{8,0},{12,4},{16,24},{20,28},{24,16},{28,20},{1,9},{5... | collective-permute-start | bytes 1769480 | tf_op jit(solution)/shard_map/cond/branch_1_fun/ppermute | solution.py:60
  717.0 32.4 %collective-permute-start.111 = (bf16[288,1152]{1,0:T(8,128)(2,1)}, bf16[288,1152]{1,0:T(8,128)(2,1)}, u32[]{:S(2)}, u32[]{:S(2)}) collective-permute-start(bf16[288,1152]{1,0:T(8,128)(2,1)} %get-tuple-element.1354), channel_id=1, source_target_pairs={{0,8},{4,12},{8,0},{12,4},{16,24},{20,28},{24,16},{28,20},{1,9},{5... | collective-permute-start | bytes 1990664 | tf_op jit(solution)/shard_map/ppermute | solution.py:60
  721.5 27.9 %collective-permute-start.110 = (bf16[288,1024]{1,0:T(8,128)(2,1)}, bf16[288,1024]{1,0:T(8,128)(2,1)}, u32[]{:S(2)}, u32[]{:S(2)}) collective-permute-start(bf16[288,1024]{1,0:T(8,128)(2,1)} %dynamic-slice_bitcast_fusion.25), channel_id=1, source_target_pairs={{0,16},{4,20},{8,24},{12,28},{16,0},{20,4},{24,8},{28,12},{1,17},{... | collective-permute-start | bytes 1769480 | tf_op jit(solution)/shard_map/ppermute | solution.py:60
  (153 other events, 1597.1 us)

commit v4 on v3

--- a/solution.py
+++ b/solution.py
@@ -246,12 +246,9 @@
 
 
 def scale_kernel(count, index_ref, *refs):
-    step = pl.program_id(0)
-    for at in range(count):
-
-        @pl.when(step == at)
-        def _():
-            refs[count][...] = refs[at][...]
+    for mask in range(count):
+        row = pl.multiple_of((index_ref[0] ^ mask) * 16, 16)
+        refs[count][pl.ds(row, 16), :] = refs[mask][...]
 
 
 def place_scales(held, rows, block_index):
@@ -261,14 +258,60 @@
         functools.partial(scale_kernel, count),
         grid_spec=pltpu.PrefetchScalarGridSpec(
             num_scalar_prefetch=1,
-            grid=(count,),
-            in_specs=[pl.BlockSpec(shape, lambda m, b: (rows // 16, 0), pipeline_mode=pl.Buffered(1))] * count,
-            out_specs=pl.BlockSpec(shape, lambda m, b: (b[0] ^ m, 0)),
+            grid=(1,),
+            in_specs=[pl.BlockSpec(shape, lambda n, b: (rows // 16, 0))] * count,
+            out_specs=pl.BlockSpec((count * 16, shape[1]), lambda n, b: (0, 0)),
         ),
         out_shape=jax.ShapeDtypeStruct((count * 16, shape[1]), bf16),
         cost_estimate=pl.CostEstimate(flops=0, bytes_accessed=4 * count * 16 * shape[1], transcendentals=0),
         name="place_scales",
     )(block_index[None].astype(jnp.int32), *[held[mask] for mask in range(count)])
+
+
+def head_kernel(plan, rows, scale_count, index_ref, *refs):
+    parts, (key_ref, value_ref, scale_ref) = refs[: len(plan)], refs[len(plan) :]
+    step = pl.program_id(0)
+
+    @pl.when(step == 0)
+    def _():
+        scale_ref[...] = jnp.zeros_like(scale_ref)
+
+    for part, (slot, first) in zip(parts, plan):
+        count = part.shape[0]
+
+        @pl.when(step == slot)
+        def _():
+            last = min(first + count, rows)
+            here, taken = slice(first, last), slice(0, last - first)
+            key_ref[here, :] = part[taken, :HD].astype(f32)
+            value_ref[here, :] = part[taken, HD:].astype(f32)
+            if first + count > rows:
+                scale_ref[...] += part[rows - first : rows - first + scale_count, :].astype(f32)
+
+
+def place_heads(parts, rows, scale_count, head_index):
+    plan, arrays = [], []
+    for slot in sorted(parts):
+        first = 0
+        for array in parts[slot]:
+            plan.append((slot, first))
+            arrays.append(array)
+            first += array.shape[0]
+    columns = pl.BlockSpec((rows, HD), lambda m, h: (0, h[0] ^ m))
+    fixed = lambda m, h: (0, 0)
+    return pl.pallas_call(
+        functools.partial(head_kernel, plan, rows, scale_count),
+        grid_spec=pltpu.PrefetchScalarGridSpec(
+            num_scalar_prefetch=1,
+            grid=(len(parts),),
+            in_specs=[pl.BlockSpec(a.shape, fixed, pipeline_mode=pl.Buffered(1)) for a in arrays],
+            out_specs=[columns, columns, pl.BlockSpec((scale_count, 2 * HD), fixed)],
+        ),
+        out_shape=[jax.ShapeDtypeStruct((rows, len(parts) * HD), f32)] * 2
+        + [jax.ShapeDtypeStruct((scale_count, 2 * HD), f32)],
+        cost_estimate=pl.CostEstimate(flops=0, bytes_accessed=8 * len(parts) * rows * HD, transcendentals=0),
+        name="place_heads",
+    )(head_index[None].astype(jnp.int32), *arrays)
 
 
 def placed_kernel(body, plans, counts, steps, index_ref, *refs):
@@ -1307,10 +1350,11 @@
     def projections_back(grad_query_lin, gate_came):
         core = core_sum(outer((normed_full, grad_query_lin), (grad_attn_full, mixed)))
         away, kept = pick(core, bit_count - 2, 1 - unit_side), pick(core, bit_count - 2, unit_side)
-        return (away[0], away[1]), kept, unit_sides(gate_kept, jnp.stack(gate_came))
+        parts = [(pick(away, 0, index), pick(kept, 0, index)) for index in (1 - side(top), side(top))]
+        return parts, unit_sides(gate_kept, jnp.stack(gate_came))
 
     kv_came = send(kv_away, pair)
-    (query_output_away, query_output_kept, (gate_far, gate_own)), kv_came = segment(
+    (((onward_away, onward_kept), (staying_away, staying_kept)), (gate_far, gate_own)), kv_came = segment(
         projections_back, (grad_query_lin, gate_came), (), kv_came
     )
     kv_terms = plus(kv_kept, kv_came).astype(bf16)
@@ -1356,8 +1400,12 @@
             pieces, _, terms = scatter_hop(pieces, head_axes, False, normed_plan[0], (), beside)
             return pieces, terms
 
-        query_output_came = send(query_output_away[0], pair, kv_came)
-        (pieces, (away, kept)), query_output_came = segment(first_sums_back, (kv_kept, kv_came), (), query_output_came)
+        onward_came = send(onward_away, pair, kv_came)
+        (pieces, (away, kept)), onward_came = segment(first_sums_back, (kv_kept, kv_came), (), onward_came)
+        onward = plus(onward_kept, onward_came).astype(bf16)
+        for at, mask in list(enumerate(chip_masks))[1:-1]:
+            onward = halve(onward, bit_count - 3 - at, mask).astype(bf16)
+        onward_query, onward_output = lax.optimization_barrier((onward[:, :query_width], onward[:, query_width:]))
 
         def sums_back(pieces):
             came = ()
@@ -1375,36 +1423,40 @@
             return grad_in
 
         wkv_came = send(away, pair)
-        grad_in, wkv_came = segment(sums_back, (pieces,), (away, kept), wkv_came)
+        query_came = send(onward_query, top)
+        grad_in, (wkv_came, query_came) = segment(sums_back, (pieces,), (away, kept), (wkv_came, query_came))
         wkv_terms = plus(kept, wkv_came).astype(bf16)
         for at, mask in list(enumerate(chip_masks))[1:-1]:
             wkv_terms = halve(wkv_terms, bit_count - 2 - at, mask).astype(bf16)
-        return grad_in, pick(wkv_terms, 0, 1 - side(top)), pick(wkv_terms, 0, side(top)), query_output_came
+        return grad_in, pick(wkv_terms, 0, 1 - side(top)), pick(wkv_terms, 0, side(top)), query_came, onward_output
 
     up_came[1] = send(up_away[1], top, kv_came)
-    query_output_came = [None, None]
-    (grad_in, wkv_away, wkv_kept, query_output_came[0]), up_came[1] = segment(
-        normed_rows_back, (kv_terms[0], kv_came), (out_down, *query_output_away), up_came[1]
+    (grad_in, wkv_away, wkv_kept, query_came, onward_output), up_came[1] = segment(
+        normed_rows_back, (kv_terms[0], kv_came), (out_down, onward_away), up_came[1]
     )
     wkv_came = send(wkv_away, top)
-    query_output_came[1] = send(query_output_away[1], pair, wkv_away)
+    staying_came = send(staying_away, pair, wkv_away)
 
     def beside_key_weights(up_came, gate_other):
         return unit_sides(up_kept, jnp.stack(up_came)), unit_whole(gate_own, gate_other)
 
-    ((up_far, up_own), out_gate), (wkv_came, query_output_came[1]) = segment(
-        beside_key_weights, (up_came, gate_other), (wkv_away, wkv_kept), (wkv_came, query_output_came[1])
+    ((up_far, up_own), out_gate), (wkv_came, staying_came) = segment(
+        beside_key_weights, (up_came, gate_other), (wkv_away, wkv_kept), (wkv_came, staying_came)
     )
     grad_wkv = plus(wkv_kept, wkv_came).astype(bf16)
-    query_output_terms = plus(query_output_kept, jnp.stack(query_output_came)).astype(bf16)
-    for at, mask in list(enumerate(chip_masks))[1:-1]:
-        query_output_terms = halve(query_output_terms, bit_count - 2 - at, mask).astype(bf16)
-    query_output_away = pick(query_output_terms, 0, 1 - side(top))
-    query_output_came = send(query_output_away, top)
+    output_came = send(onward_output, top, grad_wkv)
     up_other = send(up_far, pair, grad_wkv)
 
-    def head_rows(grad_wkv):
+    def head_rows(grad_wkv, staying_kept, staying_came, query_came):
+        staying = plus(staying_kept, staying_came).astype(bf16)
+        for at, mask in list(enumerate(chip_masks))[1:-1]:
+            staying = halve(staying, bit_count - 3 - at, mask).astype(bf16)
+        out_query = plus(staying[:, :query_width], query_came)
+        staying_output = staying[:, query_width:]
         parts = gather_rows(grad_wkv, head_axes)
+        if head_count == KVH:
+            out_key, out_value, scale_total = place_heads(parts, model_rows, scale_count, head_index)
+            return out_key, out_value, scale_total[:, :model_rows], out_query, staying_output
         wkv_ordered = jnp.zeros((head_count,) + grad_wkv.shape, bf16)
         for mask, pieces in parts.items():
             first = 0
@@ -1416,14 +1468,12 @@
         wkv_ordered = wkv_ordered[:, :model_rows].reshape(KVH, head_count // KVH, model_rows, 2, HD).sum(1)
         out_key = wkv_ordered[:, :, 0].transpose(1, 0, 2).reshape(model_rows, KVH * HD)
         out_value = wkv_ordered[:, :, 1].transpose(1, 0, 2).reshape(model_rows, KVH * HD)
-        return out_key, out_value, scale_total
-
-    (out_key, out_value, scale_total), (query_output_came, up_other) = segment(
-        head_rows, (grad_wkv,), (query_output_away, up_far), (query_output_came, up_other)
-    )
-    out_query_output = plus(pick(query_output_terms, 0, side(top)), query_output_came)
-    out_query = out_query_output[:, :query_width]
-    out_output = out_query_output[:, query_width:].T
+        return out_key, out_value, scale_total, out_query, staying_output
+
+    (out_key, out_value, scale_total, out_query, staying_output), (output_came, up_other) = segment(
+        head_rows, (grad_wkv, staying_kept, staying_came, query_came), (onward_output, up_far), (output_came, up_other)
+    )
+    out_output = plus(staying_output, output_came).T
     out_up = unit_whole(up_own, up_other)
 
     return (

time: 765 us -> 756 us (0.988)
  local copies, waits for them, and re-layouts: 80.1 us -> 67.4 us
    ppermute x64 -> x65, waiting for transfers between devices: 199 us -> 202 us  [swap(): lax.ppermute(value, 'blk', [(i, i ^ blk_mask) for i in range(block_count)])]
    squeeze x14 -> x13, local copies, waits for them, and re-layouts: 20.9 us -> 19.6 us  [pick(): return lax.dynamic_index_in_dim(value, index, dim, keepdims=False)]
    ppermute x64 -> x65, starting transfers between devices: 48.6 us -> 47.6 us  [swap(): lax.ppermute(value, 'blk', [(i, i ^ blk_mask) for i in range(block_count)])]
  transfers between devices with their start and end apart: 112 -> 113, of which waited for: 71 -> 73; matrix products, arithmetic and copies ran while one was open for 19% -> 19% of each run, Pallas kernels for 15% -> 15%
where the time goes in v4:
time: 756 us; the launch traced here: 746 us
  waiting for transfers between devices  340 us (45%)
  Pallas kernels  129 us (17%)
  starting transfers between devices  94.8 us (13%)
  local copies, waits for them, and re-layouts  67.4 us (9%)
  other arithmetic  59.9 us (8%)
  matrix products  46 us (6%)
    ppermute x65, waiting for transfers between devices, swap(): lax.ppermute(value, 'blk', [(i, i ^ blk_mask) for i in range(block_count)])  202 us
    ppermute x48, waiting for transfers between devices, swap(): lax.ppermute(value, 'head', [(i, i ^ head_mask) for i in range(head_count)])  138 us
    ppermute x65, starting transfers between devices, swap(): lax.ppermute(value, 'blk', [(i, i ^ blk_mask) for i in range(block_count)])  47.6 us
    ppermute x48, starting transfers between devices, swap(): lax.ppermute(value, 'head', [(i, i ^ head_mask) for i in range(head_count)])  47.3 us
    dot_general x6, matrix products, product(): lax.dot_general(left, right, (((left_dim,), (right_dim,)), ((), ())), pre...  46 us
    pallas_call x4, Pallas kernels, placed(): pl.pallas_call(functools.partial(placed_kernel, body, plans, counts, step...  41.7 us
    squeeze x13, local copies, waits for them, and re-layouts, pick(): return lax.dynamic_index_in_dim(value, index, dim, keepdims=False)  19.6 us
    pallas_call x6, Pallas kernels, whole_call(): pl.pallas_call(body, out_shape=[jax.ShapeDtypeStruct(shape, dtype) for sh...  18.3 us
  transfers between devices with their start and end apart: 113, of which 73 were waited for; matrix products, arithmetic and copies ran while one was open for 19% of the time, Pallas kernels for 15%

profile of v4, /device:TPU:0, one launch (start us, length us, event | category | flops | bytes accessed | tf_op | source)
XLA Modules:
  0.0 745.8 jit_solution(878271761741418470)
XLA Ops:
  38.2 19.9 %conditional.25 = (bf16[512,512]{1,0:T(8,128)(2,1)}, bf16[2304,512]{1,0:T(8,128)(2,1)}, f32[4,2304]{1,0:T(4,128)}, bf16[512,2304]{1,0:T(8,128)(2,1)}, f32[512,1]{1,0:T(8,128)}) conditional(s32[]{:T(128)} %bitcast.55, () %tuple.301, (s32[]{:T(128)}, bf16[304,512]{1,0:T(8,128)(2,1)S(1)}, bf16[304,512]{1,0:T(8,128)(2,1)S(1)}, ...), branch_computations={%region_2.3_spmd, %region_3.4_spmd} | conditional | flops 1207968768 | bytes 29862424 | solution.py:989
  75.0 14.1 %collective-permute-done.72 = bf16[512,512]{1,0:T(8,128)(2,1)S(1)} collective-permute-done((bf16[512,512]{1,0:T(8,128)(2,1)}, bf16[512,512]{1,0:T(8,128)(2,1)S(1)}, u32[]{:S(2)}, u32[]{:S(2)}) %collective-permute-start.72) | collective-permute-done | bytes 524320 | tf_op jit(solution)/shard_map/ppermute | solution.py:60
  98.8 28.1 %conditional.27 = (bf16[512,512]{1,0:T(8,128)(2,1)S(1)}, bf16[512,512]{1,0:T(8,128)(2,1)}, bf16[512,512]{1,0:T(8,128)(2,1)}, bf16[512,512]{1,0:T(8,128)(2,1)}, b...) conditional(s32[]{:T(128)} %bitcast.55, () %tuple.299, ...), branch_computations={%region_6.7_spmd, %region_7.8_spmd} | conditional | flops 1207959552 | bytes 24772900 | solution.py:989
  109.2 15.4 %collective-permute-done.7 = bf16[512,512]{1,0:T(8,128)(2,1)} collective-permute-done((bf16[512,512]{1,0:T(8,128)(2,1)S(1)}, bf16[512,512]{1,0:T(8,128)(2,1)}, u32[]{:S(2)}, u32[]{:S(2)}) %collective-permute-start.7) | collective-permute-done | bytes 524320 | tf_op jit(solution)/shard_map/cond/branch_1_fun/ppermute | solution.py:60
  135.7 46.3 %conditional.28 = (bf16[512,512]{1,0:T(8,128)(2,1)S(1)}, f32[512,512]{1,0:T(8,128)S(1)}, f32[2,1,512]{2,1,0:T(1,128)S(1)}, f32[128,2304]{1,0:T(8,128)S(1)}, f32[...) conditional(s32[]{:T(128)} %bitcast.55, () %tuple.298, ...), branch_computations={%region_8.9_spmd, %region_9.10_spmd} | conditional | flops 3494379520 | bytes 57549292 | solution.py:989
  138.8 12.0 %attention_forward.1 = (bf16[512,512]{1,0:T(8,128)(2,1)S(1)}, f32[512,512]{1,0:T(8,128)S(1)}, f32[2,1,512]{2,1,0:T(1,128)S(1)}) custom-call(s32[19]{0:T(128)S(1)} %get-tuple-element.518.spans_ref, bf16[512,512]{1,0:T(8,128)(2,1)} %get-tuple-element.519.q_ref, bf16[512,512]{1,0:T(8,128)(2,1)} %get-tuple-element.520.refs_0_, ...), custom_call_target="tpu_custom_call" | custom-call | flops 2281701376 | bytes 7340032 | tf_op jit(solution)/shard_map/cond/branch_1_fun/attention_forward/pallas_call | solution.py:850
  166.7 13.2 %collective-permute-done.47.refs_1_ = bf16[128,2304]{1,0:T(8,128)(2,1)S(1)} collective-permute-done((bf16[128,2304]{1,0:T(8,128)(2,1)S(1)}, bf16[128,2304]{1,0:T(8,128)(2,1)S(1)}, u32[]{:S(2)}, u32[]{:S(2)}) %collective-permute-start.47) | collective-permute-done | bytes 589856 | tf_op jit(solution)/shard_map/cond/branch_1_fun/ppermute | solution.py:59
  191.2 74.3 %conditional.29 = (bf16[1024,2304]{1,0:T(8,128)(2,1)}, bf16[288,2304]{1,0:T(8,128)(2,1)}, bf16[288,2304]{1,0:T(8,128)(2,1)}, bf16[288,1152]{1,0:T(8,128)(2,1)}) conditional(s32[]{:T(128)} %bitcast.55, () %tuple.323, (s32[16]{0:T(128)S(1)}, bf16[128,2304]{1,0:T(8,128)(2,1)S(1)}, bf16[288,2304]{1,0:T(8,128)(2,1)}, bf16[288,2304]{1,0:T(8,128)(2,1)}, ...), branch_computations={%region_10.11_spmd, %region_11.14_spmd} | conditional | flops 2 | bytes 41583208 | solution.py:989
  209.2 23.1 %collective-permute-done.19 = bf16[128,2304]{1,0:T(8,128)(2,1)S(1)} collective-permute-done((bf16[128,2304]{1,0:T(8,128)(2,1)S(1)}, bf16[128,2304]{1,0:T(8,128)(2,1)S(1)}, u32[]{:S(2)}, u32[]{:S(2)}) %collective-permute-start.19) | collective-permute-done | bytes 589856 | tf_op jit(solution)/shard_map/cond/branch_1_fun/ppermute | solution.py:60
  234.8 30.7 %conditional = (bf16[1024,2304]{1,0:T(8,128)(2,1)}, bf16[288,2304]{1,0:T(8,128)(2,1)}, bf16[288,2304]{1,0:T(8,128)(2,1)}) conditional(s32[]{:T(128)} %bitcast.7, () %tuple.137, (bf16[128,2304]{1,0:T(8,128)(2,1)S(1)}, bf16[128,2304]{1,0:T(8,128)(2,1)S(1)}, bf16[128,2304]{1,0:T(8,128)(2,1)S(1)}, bf16[128,2304]{1,0:T(8,128)(2,1)S(1)}, ...), branch_computations={%region_12.12_spmd, %region_13.13_spmd} | conditional | bytes 28311816 | solution.py:989
  237.0 13.7 %collective-permute-done.9.refs_6_ = bf16[128,2304]{1,0:T(8,128)(2,1)S(1)} collective-permute-done((bf16[128,2304]{1,0:T(8,128)(2,1)S(1)}, bf16[128,2304]{1,0:T(8,128)(2,1)S(1)}, u32[]{:S(2)}, u32[]{:S(2)}) %collective-permute-start.9) | collective-permute-done | bytes 589856 | tf_op jit(solution)/shard_map/cond/branch_1_fun/cond/branch_1_fun/ppermute | solution.py:59
  265.6 26.3 %conditional.30 = (bf16[1024,1152]{1,0:T(8,128)(2,1)S(1)}, f32[1024,1152]{1,0:T(8,128)}, f32[1024,1152]{1,0:T(8,128)}, bf16[2304,1152]{1,0:T(8,128)(2,1)}, bf16[...) conditional(s32[]{:T(128)} %bitcast.55, () %tuple.322, (s32[]{:T(128)}, bf16[288,2304]{1,0:T(8,128)(2,1)}, ...), branch_computations={%region_14.15_spmd, %region_15.16_spmd} | conditional | flops 10871635968 | bytes 29196416 | solution.py:989
  269.9 21.6 %hidden_units.1 = (bf16[1024,1152]{1,0:T(8,128)(2,1)S(1)}, f32[1024,1152]{1,0:T(8,128)}, f32[1024,1152]{1,0:T(8,128)}, bf16[2304,1152]{1,0:T(8,128)(2,1)}, bf16[2304,1152]{1,0:T(8,128)(2,1)}) custom-call(s32[1]{0:T(128)} %bitcast.8.index_ref, bf16[288,1152]{1,0:T(8,128)(2,1)} %get-tuple-element.575.refs_0_, bf16[288,1152]{1,0:T(8,128)(2,1)} %get-tuple-element.576.refs_1_, ...), custom_call_target="tpu_custom_call" | custom-call | flops 10871635968 | bytes 21233664 | tf_op jit(solution)/shard_map/cond/branch_1_fun/hidden_units/pallas_call | solution.py:379
  322.7 11.7 %collective-permute-done.84 = bf16[128,2304]{1,0:T(8,128)(2,1)S(1)} collective-permute-done((bf16[128,2304]{1,0:T(8,128)(2,1)S(1)}, bf16[128,2304]{1,0:T(8,128)(2,1)S(1)}, u32[]{:S(2)}, u32[]{:S(2)}) %collective-permute-start.84) | collective-permute-done | bytes 589856 | tf_op jit(solution)/shard_map/ppermute | solution.py:60
  427.1 48.8 %conditional.31 = (bf16[128,2304]{1,0:T(8,128)(2,1)}, bf16[128,2304]{1,0:T(8,128)(2,1)}, bf16[128,2304]{1,0:T(8,128)(2,1)}, bf16[128,2304]{1,0:T(8,128)(2,1)}, b...) conditional(s32[]{:T(128)} %bitcast.55, () %tuple.341, ...), branch_computations={%region_16.17_spmd, %region_17.22_spmd} | conditional | flops 16321314816 | bytes 77562680 | solution.py:989
  427.1 14.8 %two_products.1 = (bf16[128,2304]{1,0:T(8,128)(2,1)}, bf16[128,2304]{1,0:T(8,128)(2,1)}, bf16[128,2304]{1,0:T(8,128)(2,1)}, bf16[128,2304]{1,0:T(8,128)(2,1)}, b...) custom-call(bf16[1024,1152]{1,0:T(8,128)(2,1)S(1)} %get-tuple-elemen, ...), custom_call_target="tpu_custom_call" | custom-call | flops 10871635968 | bytes 20054016 | tf_op jit(solution)/shard_map/cond/branch_1_fun/two_products/pallas_call | solution.py:176
  460.0 13.6 %conditional.2 = (bf16[2,288,1152]{2,1,0:T(8,128)(2,1)}, bf16[2,288,1152]{2,1,0:T(8,128)(2,1)}) conditional(s32[]{:T(128)} %bitcast.14, () %tuple.149, (bf16[2304,1152]{1,0:T(8,128)(2,1)}, s32[]{:T(128)}) %tuple.153), branch_computations={%region_20.20_spmd, %region_21.21_spmd} | conditional | flops 5308464 | bytes 29196844 | solution.py:989
  480.0 46.5 %conditional.32 = (f32[128,2304]{1,0:T(8,128)}, bf16[128,2304]{1,0:T(8,128)(2,1)}, f32[1,2304]{1,0:T(1,128)S(1)}, f32[1,2304]{1,0:T(1,128)S(1)}, bf16[2,288,1152...) conditional(s32[]{:T(128)} %bitcast.55, () %tuple.340, ...), branch_computations={%region_22.23_spmd, %region_23.30_spmd} | conditional | flops 5449973760 | bytes 96068768 | solution.py:989
  481.0 37.4 %conditional.5 = (bf16[128,2304]{1,0:T(8,128)(2,1)}, bf16[128,2304]{1,0:T(8,128)(2,1)}, bf16[128,2304]{1,0:T(8,128)(2,1)}, bf16[2,288,1152]{2,1,0:T(8,128)(2,1)}...) conditional(s32[]{:T(128)} %bitcast.23, () %tuple.171, ...), branch_computations={%region_24.24_spmd, %region_25.29_spmd} | conditional | flops 5449973760 | bytes 83018704 | solution.py:989
  504.8 12.9 %conditional.4 = (bf16[2,288,1152]{2,1,0:T(8,128)(2,1)}, bf16[2,288,1152]{2,1,0:T(8,128)(2,1)}, bf16[288,1152]{1,0:T(8,128)(2,1)}, bf16[288,1152]{1,0:T(8,128)(2,1)}) conditional(s32[]{:T(128)} %bitcast.22, () %tuple.162, (bf16[2304,1152]{1,0:T(8,128)(2,1)}, s32[]{:T(128)}, bf16[2,288,1152]{2,1,0:T(8,128)(2,1)S(1)}, ...), branch_computations={%region_28.27_spmd, %region_29.28_spmd} | conditional | flops 7962679 | bytes 57066156 | solution.py:989
  533.2 51.3 %conditional.33 = (bf16[512,2304]{1,0:T(8,128)(2,1)S(1)}, bf16[512,512]{1,0:T(8,128)(2,1)}, bf16[2,512,512]{2,1,0:T(8,128)(2,1)S(1)}, bf16[2,512,512]{2,1,0:T(8,128)(2,1)}) conditional(s32[]{:T(128)} %bitcast.55, () %tuple.339, (bf16[128,2304]{1,0:T(8,128)(2,1)}, bf16[2304,512]{1,0:T(8,128)(2,1)}, s32[19]{0:T(128)S(1)}, ...), branch_computations={%region_30.31_spmd, %region_31.32_spmd} | conditional | flops 6916669440 | bytes 70648128 | solution.py:989
  534.4 13.2 %collective-permute-done.59.refs_2_ = bf16[128,2304]{1,0:T(8,128)(2,1)S(1)} collective-permute-done((bf16[128,2304]{1,0:T(8,128)(2,1)}, bf16[128,2304]{1,0:T(8,128)(2,1)S(1)}, u32[]{:S(2)}, u32[]{:S(2)}) %collective-permute-start.59) | collective-permute-done | bytes 589856 | tf_op jit(solution)/shard_map/cond/branch_1_fun/ppermute | solution.py:59
  560.8 16.7 %attention_backward.1 = (bf16[512,512]{1,0:T(8,128)(2,1)}, bf16[2048,512]{1,0:T(8,128)(2,1)S(1)}, bf16[2048,512]{1,0:T(8,128)(2,1)S(1)}) custom-call(s32[19]{0:T(128)S(1)} %get-tuple-element.699.spans_ref, bf16[512,512]{1,0:T(8,128)(2,1)} %get-tuple-element.700.q_ref, bf16[512,512]{1,0:T(8,128)(2,1)S(1)} %convolution_convert_fusion.3.g_ref, ...), custom_call_target="tpu_custom_call" | custom-call | flops 5704253440 | bytes 12582912 | tf_op jit(solution)/shard_map/cond/branch_1_fun/attention_backward/pallas_call | solution.py:895
  587.1 14.9 %conditional.34 = (bf16[288,1024]{1,0:T(8,128)(2,1)}, bf16[288,1024]{1,0:T(8,128)(2,1)}, bf16[288,1024]{1,0:T(8,128)(2,1)}, bf16[288,1024]{1,0:T(8,128)(2,1)}, b...) conditional(s32[]{:T(128)} %bitcast.55, () %tuple.362, (bf16[512,2304]{1,0:T(8,128)(2,1)}, ...), branch_computations={%region_32.33_spmd, %region_33.34_spmd} | conditional | flops 2423955456 | bytes 79774520 | solution.py:989
  619.7 19.0 %collective-permute-done.106 = bf16[512,512]{1,0:T(8,128)(2,1)S(1)} collective-permute-done((bf16[512,512]{1,0:T(8,128)(2,1)S(1)}, bf16[512,512]{1,0:T(8,128)(2,1)S(1)}, u32[]{:S(2)}, u32[]{:S(2)}) %collective-permute-start.106) | collective-permute-done | bytes 524320 | tf_op jit(solution)/shard_map/ppermute | solution.py:60
  642.1 55.8 %conditional.36 = (f32[128,2304]{1,0:T(8,128)}, bf16[304,512]{1,0:T(8,128)(2,1)}, bf16[304,512]{1,0:T(8,128)(2,1)}, bf16[288,512]{1,0:T(8,128)(2,1)}, bf16[288,512]{1,0:T(8,128)(2,1)}) conditional(s32[]{:T(128)} %bitcast.55, () %tuple.338, (s32[16]{0:T(128)S(1)}, bf16[512,512]{1,0:T(8,128)(2,1)S(1)}, bf16[512,512]{1,0:T(8,128)(2,1)S(1)}, ...), branch_computations={%region_36.37_spmd, %region_37.44_spmd} | conditional | flops 3637350400 | bytes 64722316 | solution.py:989
  643.5 28.0 %conditional.7 = (bf16[128,2304]{1,0:T(8,128)(2,1)}, bf16[128,2304]{1,0:T(8,128)(2,1)}, bf16[128,2304]{1,0:T(8,128)(2,1)}, bf16[2,304,512]{2,1,0:T(8,128)(2,1)}, bf16[2,304,512]{2,1,0:T(8,128)(2,1)}) conditional(s32[]{:T(128)} %bitcast.46, () %tuple.192, (bf16[512,512]{1,0:T(8,128)(2,1)S(1)}, bf16[512,512]{1,0:T(8,128)(2,1)S(1)}, ...), branch_computations={%region_38.38_spmd, %region_39.41_spmd} | conditional | flops 3634925568 | bytes 40759916 | solution.py:989
  655.3 12.2 %conditional.6 = (bf16[2,304,512]{2,1,0:T(8,128)(2,1)}, bf16[2,304,512]{2,1,0:T(8,128)(2,1)}) conditional(s32[]{:T(128)} %bitcast.45, () %tuple.186, (bf16[512,2304]{1,0:T(8,128)(2,1)}, bf16[512,512]{1,0:T(8,128)(2,1)}, f32[1,2304]{1,0:T(1,128)S(1)}, f32[1,2304]{1,0:T(1,128)S(1)}, f32[1,2304]{1,0:T(1,128)S(1)}, ...), branch_computations={%region_40.39_spmd, %region_41.40_spmd} | conditional | flops 1215467520 | bytes 21819788 | solution.py:989
  675.9 19.8 %conditional.8 = (f32[128,2304]{1,0:T(8,128)}) conditional(s32[]{:T(128)} %bitcast.46, () %tuple.191, (bf16[128,2304]{1,0:T(8,128)(2,1)}, bf16[128,2304]{1,0:T(8,128)(2,1)}, bf16[128,2304]{1,0:T(8,128)(2,1)}, bf16[128,2304]{1,0:T(8,128)(2,1)}, f32[128,2304]{1,0:T(8,128)}, /*index=5*/f32[4,2304]{1,0:T(4,128)}) %tuple.198), branch_computations={%region_42.42_spmd, %region_43.43_spmd} | conditional | bytes 11870296 | solution.py:989
  678.3 12.8 %collective-permute-done.23.refs_1_ = bf16[128,2304]{1,0:T(8,128)(2,1)S(1)} collective-permute-done((bf16[128,2304]{1,0:T(8,128)(2,1)}, bf16[128,2304]{1,0:T(8,128)(2,1)S(1)}, u32[]{:S(2)}, u32[]{:S(2)}) %collective-permute-start.23) | collective-permute-done | bytes 589856 | tf_op jit(solution)/shard_map/cond/branch_1_fun/cond/branch_1_fun/ppermute | solution.py:59
  705.2 12.3 %collective-permute-done.109 = bf16[304,512]{1,0:T(8,128)(2,1)} collective-permute-done((bf16[304,512]{1,0:T(8,128)(2,1)}, bf16[304,512]{1,0:T(8,128)(2,1)}, u32[]{:S(2)}, u32[]{:S(2)}) %collective-permute-start.109) | collective-permute-done | bytes 311328 | tf_op jit(solution)/shard_map/ppermute | solution.py:60
  722.2 19.7 %conditional.38 = (f32[288,1024]{1,0:T(8,128)}, f32[288,1024]{1,0:T(8,128)}, f32[4,288]{1,0:T(4,128)S(1)}, f32[288,512]{1,0:T(8,128)}, bf16[288,512]{1,0:T(8,128)(2,1)S(1)}) conditional(s32[]{:T(128)} %bitcast.55, () %tuple.375, (s32[]{:T(128)}, bf16[304,512]{1,0:T(8,128)(2,1)S(1)}, bf16[288,1024]{1,0:T(8,128)(2,1)}, bf16[288,1024]{1,0:T(8,128)(2,1)}, ...), branch_computations={%region_46.47_spmd, %region_47.48_spmd} | conditional | flops 1622016 | bytes 14001464 | solution.py:989
  (526 shorter events, 570.3 us)
Async XLA Ops:
  0.7 23.9 %collective-permute-start.63 = (bf16[128,2304]{1,0:T(8,128)(2,1)}, bf16[128,2304]{1,0:T(8,128)(2,1)}, u32[]{:S(2)}, u32[]{:S(2)}) collective-permute-start(bf16[128,2304]{1,0:T(8,128)(2,1)} %param.60), channel_id=1, source_target_pairs={{0,1},{1,0},{2,3},{3,2},{4,5},{5,4},{6,7},{7,6},{8,9},{9,8},{10,11... | collective-permute-start | bytes 1769480 | tf_op jit(solution)/shard_map/ppermute | solution.py:59
  3.7 20.9 %collective-permute-start.64 = (bf16[128,2304]{1,0:T(8,128)(2,1)}, bf16[128,2304]{1,0:T(8,128)(2,1)}, u32[]{:S(2)}, u32[]{:S(2)}) collective-permute-start(bf16[128,2304]{1,0:T(8,128)(2,1)} %param.60), channel_id=1, source_target_pairs={{0,2},{1,3},{2,0},{3,1},{4,6},{5,7},{6,4},{7,5},{8,10},{9,11},{10,... | collective-permute-start | bytes 1769480 | tf_op jit(solution)/shard_map/ppermute | solution.py:59
  36.0 22.7 %collective-permute-start.70 = (bf16[288,1024]{1,0:T(8,128)(2,1)}, bf16[288,1024]{1,0:T(8,128)(2,1)}, u32[]{:S(2)}, u32[]{:S(2)}) collective-permute-start(bf16[288,1024]{1,0:T(8,128)(2,1)} %copy.41), channel_id=1, source_target_pairs={{0,8},{4,12},{8,0},{12,4},{16,24},{20,28},{24,16},{28,20},{1,9},{5... | collective-permute-start | bytes 1769480 | tf_op jit(solution)/shard_map/ppermute | solution.py:60
  37.5 26.2 %collective-permute-start.71 = (bf16[288,1024]{1,0:T(8,128)(2,1)}, bf16[288,1024]{1,0:T(8,128)(2,1)}, u32[]{:S(2)}, u32[]{:S(2)}) collective-permute-start(bf16[288,1024]{1,0:T(8,128)(2,1)} %copy.41), channel_id=1, source_target_pairs={{0,16},{4,20},{8,24},{12,28},{16,0},{20,4},{24,8},{28,12},{1,17},{... | collective-permute-start | bytes 1769480 | tf_op jit(solution)/shard_map/ppermute | solution.py:60
  63.7 35.0 %collective-permute-start.74 = (bf16[288,1024]{1,0:T(8,128)(2,1)}, bf16[288,1024]{1,0:T(8,128)(2,1)S(1)}, u32[]{:S(2)}, u32[]{:S(2)}) collective-permute-start(bf16[288,1024]{1,0:T(8,128)(2,1)} %collective-permute-done.71), channel_id=1, source_target_pairs={{0,8},{4,12},{8,0},{12,4},{16,24},{20,28},{24,16},{28,20},{1,9},{5... | collective-permute-start | bytes 1769480 | tf_op jit(solution)/shard_map/ppermute | solution.py:60
  63.7 25.3 %collective-permute-start.72 = (bf16[512,512]{1,0:T(8,128)(2,1)}, bf16[512,512]{1,0:T(8,128)(2,1)S(1)}, u32[]{:S(2)}, u32[]{:S(2)}) collective-permute-start(bf16[512,512]{1,0:T(8,128)(2,1)} %get-tuple-element.1153), channel_id=1, source_target_pairs={{0,16},{4,20},{8,24},{12,28},{16,0},{20,4},{24,8},{28,12},{1,17},{... | collective-permute-start | bytes 1572872 | tf_op jit(solution)/shard_map/ppermute | solution.py:60
  63.9 34.9 %collective-permute-start.73 = (bf16[512,512]{1,0:T(8,128)(2,1)}, bf16[512,512]{1,0:T(8,128)(2,1)}, u32[]{:S(2)}, u32[]{:S(2)}) collective-permute-start(bf16[512,512]{1,0:T(8,128)(2,1)} %get-tuple-element.1153), channel_id=1, source_target_pairs={{0,8},{4,12},{8,0},{12,4},{16,24},{20,28},{24,16},{28,20},{1,9},{5... | collective-permute-start | bytes 1572872 | tf_op jit(solution)/shard_map/ppermute | solution.py:60
  98.7 31.0 %collective-permute-start.75 = (bf16[288,1152]{1,0:T(8,128)(2,1)}, bf16[288,1152]{1,0:T(8,128)(2,1)}, u32[]{:S(2)}, u32[]{:S(2)}) collective-permute-start(bf16[288,1152]{1,0:T(8,128)(2,1)} %get-tuple-element.1192), channel_id=1, source_target_pairs={{0,16},{4,20},{8,24},{12,28},{16,0},{20,4},{24,8},{28,12},{1,17},{... | collective-permute-start | bytes 1990664 | tf_op jit(solution)/shard_map/ppermute | solution.py:60
  101.0 23.6 %collective-permute-start.7 = (bf16[512,512]{1,0:T(8,128)(2,1)S(1)}, bf16[512,512]{1,0:T(8,128)(2,1)}, u32[]{:S(2)}, u32[]{:S(2)}) collective-permute-start(bf16[512,512]{1,0:T(8,128)(2,1)S(1)} %get-tuple-element.503), channel_id=1, source_target_pairs={{0,8},{4,12},{8,0},{12,4},{16,24},{20,28},{24,16},{28,20},{1,9},{5... | collective-permute-start | bytes 1572872 | tf_op jit(solution)/shard_map/cond/branch_1_fun/ppermute | solution.py:60
  103.1 21.5 %collective-permute-start.6 = (bf16[512,512]{1,0:T(8,128)(2,1)S(1)}, bf16[512,512]{1,0:T(8,128)(2,1)}, u32[]{:S(2)}, u32[]{:S(2)}) collective-permute-start(bf16[512,512]{1,0:T(8,128)(2,1)S(1)} %get-tuple-element.503), channel_id=1, source_target_pairs={{0,4},{4,0},{8,12},{12,8},{16,20},{20,16},{24,28},{28,24},{1,5},{5... | collective-permute-start | bytes 1572872 | tf_op jit(solution)/shard_map/cond/branch_1_fun/ppermute | solution.py:60
  129.8 60.8 %collective-permute-start.76 = (bf16[288,2304]{1,0:T(8,128)(2,1)}, bf16[288,2304]{1,0:T(8,128)(2,1)}, u32[]{:S(2)}, u32[]{:S(2)}) collective-permute-start(bf16[288,2304]{1,0:T(8,128)(2,1)} %get-tuple-element.1209.refs_0_), channel_id=1, source_target_pairs={{0,16},{4,20},{8,24},{12,28},{16,0},{20,4},{24,8},{28,12},{1,17},{... | collective-permute-start | bytes 3981320 | tf_op jit(solution)/shard_map/ppermute | solution.py:60
  129.8 60.9 %collective-permute-start.77 = (bf16[288,2304]{1,0:T(8,128)(2,1)}, bf16[288,2304]{1,0:T(8,128)(2,1)}, u32[]{:S(2)}, u32[]{:S(2)}) collective-permute-start(bf16[288,2304]{1,0:T(8,128)(2,1)} %get-tuple-element.1208), channel_id=1, source_target_pairs={{0,8},{4,12},{8,0},{12,4},{16,24},{20,28},{24,16},{28,20},{1,9},{5... | collective-permute-start | bytes 3981320 | tf_op jit(solution)/shard_map/ppermute | solution.py:60
  190.6 74.9 %collective-permute-start.78 = (bf16[288,2304]{1,0:T(8,128)(2,1)}, bf16[288,2304]{1,0:T(8,128)(2,1)}, u32[]{:S(2)}, u32[]{:S(2)}) collective-permute-start(bf16[288,2304]{1,0:T(8,128)(2,1)} %collective-permute-done.77), channel_id=1, source_target_pairs={{0,16},{4,20},{8,24},{12,28},{16,0},{20,4},{24,8},{28,12},{1,17},{... | collective-permute-start | bytes 3981320 | tf_op jit(solution)/shard_map/ppermute | solution.py:60
  193.3 39.0 %collective-permute-start.19 = (bf16[128,2304]{1,0:T(8,128)(2,1)S(1)}, bf16[128,2304]{1,0:T(8,128)(2,1)S(1)}, u32[]{:S(2)}, u32[]{:S(2)}) collective-permute-start(bf16[128,2304]{1,0:T(8,128)(2,1)S(1)} %get-tuple-element.562), channel_id=1, source_target_pairs={{0,8},{4,12},{8,0},{12,4},{16,24},{20,28},{24,16},{28,20},{1,9},{5... | collective-permute-start | bytes 1769480 | tf_op jit(solution)/shard_map/cond/branch_1_fun/ppermute | solution.py:60
  206.1 26.2 %collective-permute-start.17 = (bf16[64,2304]{1,0:T(8,128)(2,1)S(1)}, bf16[64,2304]{1,0:T(8,128)(2,1)S(1)}, u32[]{:S(2)}, u32[]{:S(2)}) collective-permute-start(bf16[64,2304]{1,0:T(8,128)(2,1)S(1)} %slice.280), channel_id=1, source_target_pairs={{0,1},{1,0},{2,3},{3,2},{4,5},{5,4},{6,7},{7,6},{8,9},{9,8},{10,11... | collective-permute-start | bytes 884744 | tf_op jit(solution)/shard_map/cond/branch_1_fun/ppermute | solution.py:59
  207.6 24.7 %collective-permute-start.18 = (bf16[64,2304]{1,0:T(8,128)(2,1)S(1)}, bf16[64,2304]{1,0:T(8,128)(2,1)S(1)}, u32[]{:S(2)}, u32[]{:S(2)}) collective-permute-start(bf16[64,2304]{1,0:T(8,128)(2,1)S(1)} %slice.281), channel_id=1, source_target_pairs={{0,2},{1,3},{2,0},{3,1},{4,6},{5,7},{6,4},{7,5},{8,10},{9,11},{10,... | collective-permute-start | bytes 884744 | tf_op jit(solution)/shard_map/cond/branch_1_fun/ppermute | solution.py:59
  232.3 33.2 %collective-permute-start.20 = (bf16[288,1152]{1,0:T(8,128)(2,1)}, bf16[288,1152]{1,0:T(8,128)(2,1)}, u32[]{:S(2)}, u32[]{:S(2)}) collective-permute-start(bf16[288,1152]{1,0:T(8,128)(2,1)} %get-tuple-element.573), channel_id=1, source_target_pairs={{0,8},{4,12},{8,0},{12,4},{16,24},{20,28},{24,16},{28,20},{1,9},{5... | collective-permute-start | bytes 1990664 | tf_op jit(solution)/shard_map/cond/branch_1_fun/ppermute | solution.py:60
  265.5 31.1 %collective-permute-start.79 = (bf16[288,1152]{1,0:T(8,128)(2,1)}, bf16[288,1152]{1,0:T(8,128)(2,1)S(1)}, u32[]{:S(2)}, u32[]{:S(2)}) collective-permute-start(bf16[288,1152]{1,0:T(8,128)(2,1)} %get-tuple-element.1241.refs_2_), channel_id=1, source_target_pairs={{0,16},{4,20},{8,24},{12,28},{16,0},{20,4},{24,8},{28,12},{1,17},{... | collective-permute-start | bytes 1990664 | tf_op jit(solution)/shard_map/ppermute | solution.py:60
  265.7 25.8 %collective-permute-start.22 = (bf16[288,1152]{1,0:T(8,128)(2,1)}, bf16[288,1152]{1,0:T(8,128)(2,1)}, u32[]{:S(2)}, u32[]{:S(2)}) collective-permute-start(bf16[288,1152]{1,0:T(8,128)(2,1)} %get-tuple-element.592), channel_id=1, source_target_pairs={{0,4},{4,0},{8,12},{12,8},{16,20},{20,16},{24,28},{28,24},{1,5},{5... | collective-permute-start | bytes 1990664 | tf_op jit(solution)/shard_map/cond/branch_1_fun/ppermute | solution.py:60
  413.6 62.4 %collective-permute-start.100 = (bf16[2,288,1152]{2,1,0:T(8,128)(2,1)}, bf16[2,288,1152]{2,1,0:T(8,128)(2,1)}, u32[]{:S(2)}, u32[]{:S(2)}) collective-permute-start(bf16[2,288,1152]{2,1,0:T(8,128)(2,1)} %get-tuple-element.1519), channel_id=1, source_target_pairs={{0,16},{4,20},{8,24},{12,28},{16,0},{20,4},{24,8},{28,12},{1,17},{... | collective-permute-start | bytes 3981320 | tf_op jit(solution)/shard_map/ppermute | solution.py:60
  478.6 48.1 %collective-permute-start.101 = (bf16[288,1152]{1,0:T(8,128)(2,1)}, bf16[288,1152]{1,0:T(8,128)(2,1)}, u32[]{:S(2)}, u32[]{:S(2)}) collective-permute-start(bf16[288,1152]{1,0:T(8,128)(2,1)} %get-tuple-element.1307), channel_id=1, source_target_pairs={{0,16},{4,20},{8,24},{12,28},{16,0},{20,4},{24,8},{28,12},{1,17},{... | collective-permute-start | bytes 1990664 | tf_op jit(solution)/shard_map/ppermute | solution.py:60
  480.0 38.4 %collective-permute-start.57 = (bf16[128,2304]{1,0:T(8,128)(2,1)}, bf16[128,2304]{1,0:T(8,128)(2,1)S(1)}, u32[]{:S(2)}, u32[]{:S(2)}) collective-permute-start(bf16[128,2304]{1,0:T(8,128)(2,1)} %get-tuple-element.679), channel_id=1, source_target_pairs={{0,8},{4,12},{8,0},{12,4},{16,24},{20,28},{24,16},{28,20},{1,9},{5... | collective-permute-start | bytes 1769480 | tf_op jit(solution)/shard_map/cond/branch_1_fun/ppermute | solution.py:60
  526.6 57.8 %collective-permute-start.102 = (bf16[288,1152]{1,0:T(8,128)(2,1)}, bf16[288,1152]{1,0:T(8,128)(2,1)}, u32[]{:S(2)}, u32[]{:S(2)}) collective-permute-start(bf16[288,1152]{1,0:T(8,128)(2,1)} %get-tuple-element.1320), channel_id=1, source_target_pairs={{0,16},{4,20},{8,24},{12,28},{16,0},{20,4},{24,8},{28,12},{1,17},{... | collective-permute-start | bytes 1990664 | tf_op jit(solution)/shard_map/ppermute | solution.py:60
  530.8 56.3 %collective-permute-start.103 = (bf16[288,1152]{1,0:T(8,128)(2,1)}, bf16[288,1152]{1,0:T(8,128)(2,1)}, u32[]{:S(2)}, u32[]{:S(2)}) collective-permute-start(bf16[288,1152]{1,0:T(8,128)(2,1)} %get-tuple-element.1321), channel_id=1, source_target_pairs={{0,16},{4,20},{8,24},{12,28},{16,0},{20,4},{24,8},{28,12},{1,17},{... | collective-permute-start | bytes 1990664 | tf_op jit(solution)/shard_map/ppermute | solution.py:60
  532.1 55.0 %collective-permute-start.104 = (bf16[288,1152]{1,0:T(8,128)(2,1)}, bf16[288,1152]{1,0:T(8,128)(2,1)}, u32[]{:S(2)}, u32[]{:S(2)}) collective-permute-start(bf16[288,1152]{1,0:T(8,128)(2,1)} %get-tuple-element.1322), channel_id=1, source_target_pairs={{0,8},{4,12},{8,0},{12,4},{16,24},{20,28},{24,16},{28,20},{1,9},{5... | collective-permute-start | bytes 1990664 | tf_op jit(solution)/shard_map/ppermute | solution.py:60
  587.1 24.8 %collective-permute-start.105 = (bf16[2,512,512]{2,1,0:T(8,128)(2,1)}, bf16[2,512,512]{2,1,0:T(8,128)(2,1)}, u32[]{:S(2)}, u32[]{:S(2)}) collective-permute-start(bf16[2,512,512]{2,1,0:T(8,128)(2,1)} %get-tuple-element.1338), channel_id=1, source_target_pairs={{0,8},{4,12},{8,0},{12,4},{16,24},{20,28},{24,16},{28,20},{1,9},{5... | collective-permute-start | bytes 3145736 | tf_op jit(solution)/shard_map/ppermute | solution.py:60
  613.8 26.9 %collective-permute-start.107 = (bf16[288,1152]{1,0:T(8,128)(2,1)}, bf16[288,1152]{1,0:T(8,128)(2,1)S(1)}, u32[]{:S(2)}, u32[]{:S(2)}) collective-permute-start(bf16[288,1152]{1,0:T(8,128)(2,1)} %get-tuple-element.1343), channel_id=1, source_target_pairs={{0,8},{4,12},{8,0},{12,4},{16,24},{20,28},{24,16},{28,20},{1,9},{5... | collective-permute-start | bytes 1990664 | tf_op jit(solution)/shard_map/ppermute | solution.py:60
  614.2 24.5 %collective-permute-start.106 = (bf16[512,512]{1,0:T(8,128)(2,1)S(1)}, bf16[512,512]{1,0:T(8,128)(2,1)S(1)}, u32[]{:S(2)}, u32[]{:S(2)}) collective-permute-start(bf16[512,512]{1,0:T(8,128)(2,1)S(1)} %get-tuple-element.1526), channel_id=1, source_target_pairs={{0,16},{4,20},{8,24},{12,28},{16,0},{20,4},{24,8},{28,12},{1,17},{... | collective-permute-start | bytes 1572872 | tf_op jit(solution)/shard_map/ppermute | solution.py:60
  640.6 57.3 %collective-permute-start.108 = (bf16[288,1152]{1,0:T(8,128)(2,1)}, bf16[288,1152]{1,0:T(8,128)(2,1)}, u32[]{:S(2)}, u32[]{:S(2)}) collective-permute-start(bf16[288,1152]{1,0:T(8,128)(2,1)} %get-tuple-element.1362), channel_id=1, source_target_pairs={{0,16},{4,20},{8,24},{12,28},{16,0},{20,4},{24,8},{28,12},{1,17},{... | collective-permute-start | bytes 1990664 | tf_op jit(solution)/shard_map/ppermute | solution.py:60
  642.1 29.3 %collective-permute-start.39 = (bf16[288,1024]{1,0:T(8,128)(2,1)}, bf16[288,1024]{1,0:T(8,128)(2,1)}, u32[]{:S(2)}, u32[]{:S(2)}) collective-permute-start(bf16[288,1024]{1,0:T(8,128)(2,1)} %get-tuple-element.804), channel_id=1, source_target_pairs={{0,8},{4,12},{8,0},{12,4},{16,24},{20,28},{24,16},{28,20},{1,9},{5... | collective-permute-start | bytes 1769480 | tf_op jit(solution)/shard_map/cond/branch_1_fun/ppermute | solution.py:60
  671.5 24.2 %collective-permute-start.40 = (bf16[2,304,512]{2,1,0:T(8,128)(2,1)}, bf16[2,304,512]{2,1,0:T(8,128)(2,1)S(1)}, u32[]{:S(2)}, u32[]{:S(2)}) collective-permute-start(bf16[2,304,512]{2,1,0:T(8,128)(2,1)} %get-tuple-element.808), channel_id=1, source_target_pairs={{0,8},{4,12},{8,0},{12,4},{16,24},{20,28},{24,16},{28,20},{1,9},{5... | collective-permute-start | bytes 1867784 | tf_op jit(solution)/shard_map/cond/branch_1_fun/ppermute | solution.py:60
  719.6 22.3 %collective-permute-start.112 = (bf16[288,1152]{1,0:T(8,128)(2,1)S(1)}, bf16[288,1152]{1,0:T(8,128)(2,1)S(1)}, u32[]{:S(2)}, u32[]{:S(2)}) collective-permute-start(bf16[288,1152]{1,0:T(8,128)(2,1)S(1)} %get-tuple-element.1394), channel_id=1, source_target_pairs={{0,8},{4,12},{8,0},{12,4},{16,24},{20,28},{24,16},{28,20},{1,9},{5... | collective-permute-start | bytes 1990664 | tf_op jit(solution)/shard_map/ppermute | solution.py:60
  (153 other events, 1635.5 us)

commit v5 on v4

--- a/solution.py
+++ b/solution.py
@@ -286,7 +286,7 @@
             key_ref[here, :] = part[taken, :HD].astype(f32)
             value_ref[here, :] = part[taken, HD:].astype(f32)
             if first + count > rows:
-                scale_ref[...] += part[rows - first : rows - first + scale_count, :].astype(f32)
+                scale_ref[...] += part[rows - first : rows - first + 16, :].astype(f32)[:scale_count]
 
 
 def place_heads(parts, rows, scale_count, head_index):
@@ -1423,15 +1423,15 @@
             return grad_in
 
         wkv_came = send(away, pair)
-        query_came = send(onward_query, top)
-        grad_in, (wkv_came, query_came) = segment(sums_back, (pieces,), (away, kept), (wkv_came, query_came))
+        output_came = send(onward_output, top)
+        grad_in, (wkv_came, output_came) = segment(sums_back, (pieces,), (away, kept), (wkv_came, output_came))
         wkv_terms = plus(kept, wkv_came).astype(bf16)
         for at, mask in list(enumerate(chip_masks))[1:-1]:
             wkv_terms = halve(wkv_terms, bit_count - 2 - at, mask).astype(bf16)
-        return grad_in, pick(wkv_terms, 0, 1 - side(top)), pick(wkv_terms, 0, side(top)), query_came, onward_output
+        return grad_in, pick(wkv_terms, 0, 1 - side(top)), pick(wkv_terms, 0, side(top)), output_came, onward_query
 
     up_came[1] = send(up_away[1], top, kv_came)
-    (grad_in, wkv_away, wkv_kept, query_came, onward_output), up_came[1] = segment(
+    (grad_in, wkv_away, wkv_kept, output_came, onward_query), up_came[1] = segment(
         normed_rows_back, (kv_terms[0], kv_came), (out_down, onward_away), up_came[1]
     )
     wkv_came = send(wkv_away, top)
@@ -1444,19 +1444,19 @@
         beside_key_weights, (up_came, gate_other), (wkv_away, wkv_kept), (wkv_came, staying_came)
     )
     grad_wkv = plus(wkv_kept, wkv_came).astype(bf16)
-    output_came = send(onward_output, top, grad_wkv)
+    query_came = send(onward_query, top, grad_wkv)
     up_other = send(up_far, pair, grad_wkv)
 
-    def head_rows(grad_wkv, staying_kept, staying_came, query_came):
+    def head_rows(grad_wkv, staying_kept, staying_came, output_came):
         staying = plus(staying_kept, staying_came).astype(bf16)
         for at, mask in list(enumerate(chip_masks))[1:-1]:
             staying = halve(staying, bit_count - 3 - at, mask).astype(bf16)
-        out_query = plus(staying[:, :query_width], query_came)
-        staying_output = staying[:, query_width:]
+        out_output = plus(staying[:, query_width:], output_came).T
+        staying_query = staying[:, :query_width]
         parts = gather_rows(grad_wkv, head_axes)
         if head_count == KVH:
             out_key, out_value, scale_total = place_heads(parts, model_rows, scale_count, head_index)
-            return out_key, out_value, scale_total[:, :model_rows], out_query, staying_output
+            return out_key, out_value, scale_total[:, :model_rows], out_output, staying_query
         wkv_ordered = jnp.zeros((head_count,) + grad_wkv.shape, bf16)
         for mask, pieces in parts.items():
             first = 0
@@ -1468,12 +1468,12 @@
         wkv_ordered = wkv_ordered[:, :model_rows].reshape(KVH, head_count // KVH, model_rows, 2, HD).sum(1)
         out_key = wkv_ordered[:, :, 0].transpose(1, 0, 2).reshape(model_rows, KVH * HD)
         out_value = wkv_ordered[:, :, 1].transpose(1, 0, 2).reshape(model_rows, KVH * HD)
-        return out_key, out_value, scale_total, out_query, staying_output
-
-    (out_key, out_value, scale_total, out_query, staying_output), (output_came, up_other) = segment(
-        head_rows, (grad_wkv, staying_kept, staying_came, query_came), (onward_output, up_far), (output_came, up_other)
-    )
-    out_output = plus(staying_output, output_came).T
+        return out_key, out_value, scale_total, out_output, staying_query
+
+    (out_key, out_value, scale_total, out_output, staying_query), (query_came, up_other) = segment(
+        head_rows, (grad_wkv, staying_kept, staying_came, output_came), (onward_query, up_far), (query_came, up_other)
+    )
+    out_query = plus(staying_query, query_came)
     out_up = unit_whole(up_own, up_other)
 
     return (

time: 756 us -> 756 us (level)
  no operation moved by 1% of the time
where the time goes in v5:
time: 756 us; the launch traced here: 746 us
  waiting for transfers between devices  340 us (45%)
  Pallas kernels  130 us (17%)
  starting transfers between devices  95 us (13%)
  local copies, waits for them, and re-layouts  67.4 us (9%)
  other arithmetic  59.9 us (8%)
  matrix products  46 us (6%)
    ppermute x65, waiting for transfers between devices, swap(): lax.ppermute(value, 'blk', [(i, i ^ blk_mask) for i in range(block_count)])  202 us
    ppermute x48, waiting for transfers between devices, swap(): lax.ppermute(value, 'head', [(i, i ^ head_mask) for i in range(head_count)])  138 us
    ppermute x65, starting transfers between devices, swap(): lax.ppermute(value, 'blk', [(i, i ^ blk_mask) for i in range(block_count)])  47.7 us
    ppermute x48, starting transfers between devices, swap(): lax.ppermute(value, 'head', [(i, i ^ head_mask) for i in range(head_count)])  47.3 us
    dot_general x6, matrix products, product(): lax.dot_general(left, right, (((left_dim,), (right_dim,)), ((), ())), pre...  46 us
    pallas_call x4, Pallas kernels, placed(): pl.pallas_call(functools.partial(placed_kernel, body, plans, counts, step...  41.7 us
    squeeze x13, local copies, waits for them, and re-layouts, pick(): return lax.dynamic_index_in_dim(value, index, dim, keepdims=False)  19.6 us
    pallas_call x6, Pallas kernels, whole_call(): pl.pallas_call(body, out_shape=[jax.ShapeDtypeStruct(shape, dtype) for sh...  18.3 us
  transfers between devices with their start and end apart: 113, of which 73 were waited for; matrix products, arithmetic and copies ran while one was open for 19% of the time, Pallas kernels for 15%

profile of v5, /device:TPU:0, one launch (start us, length us, event | category | flops | bytes accessed | tf_op | source)
XLA Modules:
  0.0 746.1 jit_solution(6016599618932449303)
XLA Ops:
  38.2 19.9 %conditional.25 = (bf16[512,512]{1,0:T(8,128)(2,1)}, bf16[2304,512]{1,0:T(8,128)(2,1)}, f32[4,2304]{1,0:T(4,128)}, bf16[512,2304]{1,0:T(8,128)(2,1)}, f32[512,1]{1,0:T(8,128)}) conditional(s32[]{:T(128)} %bitcast.56, () %tuple.301, (s32[]{:T(128)}, bf16[304,512]{1,0:T(8,128)(2,1)S(1)}, bf16[304,512]{1,0:T(8,128)(2,1)S(1)}, ...), branch_computations={%region_2.3_spmd, %region_3.4_spmd} | conditional | flops 1207968768 | bytes 29862424 | solution.py:989
  75.0 14.1 %collective-permute-done.72 = bf16[512,512]{1,0:T(8,128)(2,1)S(1)} collective-permute-done((bf16[512,512]{1,0:T(8,128)(2,1)}, bf16[512,512]{1,0:T(8,128)(2,1)S(1)}, u32[]{:S(2)}, u32[]{:S(2)}) %collective-permute-start.72) | collective-permute-done | bytes 524320 | tf_op jit(solution)/shard_map/ppermute | solution.py:60
  98.8 28.1 %conditional.27 = (bf16[512,512]{1,0:T(8,128)(2,1)S(1)}, bf16[512,512]{1,0:T(8,128)(2,1)}, bf16[512,512]{1,0:T(8,128)(2,1)}, bf16[512,512]{1,0:T(8,128)(2,1)}, b...) conditional(s32[]{:T(128)} %bitcast.56, () %tuple.299, ...), branch_computations={%region_6.7_spmd, %region_7.8_spmd} | conditional | flops 1207959552 | bytes 24772900 | solution.py:989
  109.2 15.4 %collective-permute-done.7 = bf16[512,512]{1,0:T(8,128)(2,1)} collective-permute-done((bf16[512,512]{1,0:T(8,128)(2,1)S(1)}, bf16[512,512]{1,0:T(8,128)(2,1)}, u32[]{:S(2)}, u32[]{:S(2)}) %collective-permute-start.7) | collective-permute-done | bytes 524320 | tf_op jit(solution)/shard_map/cond/branch_1_fun/ppermute | solution.py:60
  135.7 46.4 %conditional.28 = (bf16[512,512]{1,0:T(8,128)(2,1)S(1)}, f32[512,512]{1,0:T(8,128)S(1)}, f32[2,1,512]{2,1,0:T(1,128)S(1)}, f32[128,2304]{1,0:T(8,128)S(1)}, f32[...) conditional(s32[]{:T(128)} %bitcast.56, () %tuple.298, ...), branch_computations={%region_8.9_spmd, %region_9.10_spmd} | conditional | flops 3494379520 | bytes 57549292 | solution.py:989
  138.8 12.0 %attention_forward.1 = (bf16[512,512]{1,0:T(8,128)(2,1)S(1)}, f32[512,512]{1,0:T(8,128)S(1)}, f32[2,1,512]{2,1,0:T(1,128)S(1)}) custom-call(s32[19]{0:T(128)S(1)} %get-tuple-element.518.spans_ref, bf16[512,512]{1,0:T(8,128)(2,1)} %get-tuple-element.519.q_ref, bf16[512,512]{1,0:T(8,128)(2,1)} %get-tuple-element.520.refs_0_, ...), custom_call_target="tpu_custom_call" | custom-call | flops 2281701376 | bytes 7340032 | tf_op jit(solution)/shard_map/cond/branch_1_fun/attention_forward/pallas_call | solution.py:850
  166.7 13.2 %collective-permute-done.47.refs_1_ = bf16[128,2304]{1,0:T(8,128)(2,1)S(1)} collective-permute-done((bf16[128,2304]{1,0:T(8,128)(2,1)S(1)}, bf16[128,2304]{1,0:T(8,128)(2,1)S(1)}, u32[]{:S(2)}, u32[]{:S(2)}) %collective-permute-start.47) | collective-permute-done | bytes 589856 | tf_op jit(solution)/shard_map/cond/branch_1_fun/ppermute | solution.py:59
  191.2 74.3 %conditional.29 = (bf16[1024,2304]{1,0:T(8,128)(2,1)}, bf16[288,2304]{1,0:T(8,128)(2,1)}, bf16[288,2304]{1,0:T(8,128)(2,1)}, bf16[288,1152]{1,0:T(8,128)(2,1)}) conditional(s32[]{:T(128)} %bitcast.56, () %tuple.323, (s32[16]{0:T(128)S(1)}, bf16[128,2304]{1,0:T(8,128)(2,1)S(1)}, bf16[288,2304]{1,0:T(8,128)(2,1)}, bf16[288,2304]{1,0:T(8,128)(2,1)}, ...), branch_computations={%region_10.11_spmd, %region_11.14_spmd} | conditional | flops 2 | bytes 41583208 | solution.py:989
  209.2 23.1 %collective-permute-done.19 = bf16[128,2304]{1,0:T(8,128)(2,1)S(1)} collective-permute-done((bf16[128,2304]{1,0:T(8,128)(2,1)S(1)}, bf16[128,2304]{1,0:T(8,128)(2,1)S(1)}, u32[]{:S(2)}, u32[]{:S(2)}) %collective-permute-start.19) | collective-permute-done | bytes 589856 | tf_op jit(solution)/shard_map/cond/branch_1_fun/ppermute | solution.py:60
  234.8 30.7 %conditional = (bf16[1024,2304]{1,0:T(8,128)(2,1)}, bf16[288,2304]{1,0:T(8,128)(2,1)}, bf16[288,2304]{1,0:T(8,128)(2,1)}) conditional(s32[]{:T(128)} %bitcast.7, () %tuple.137, (bf16[128,2304]{1,0:T(8,128)(2,1)S(1)}, bf16[128,2304]{1,0:T(8,128)(2,1)S(1)}, bf16[128,2304]{1,0:T(8,128)(2,1)S(1)}, bf16[128,2304]{1,0:T(8,128)(2,1)S(1)}, ...), branch_computations={%region_12.12_spmd, %region_13.13_spmd} | conditional | bytes 28311816 | solution.py:989
  237.0 13.7 %collective-permute-done.9.refs_6_ = bf16[128,2304]{1,0:T(8,128)(2,1)S(1)} collective-permute-done((bf16[128,2304]{1,0:T(8,128)(2,1)S(1)}, bf16[128,2304]{1,0:T(8,128)(2,1)S(1)}, u32[]{:S(2)}, u32[]{:S(2)}) %collective-permute-start.9) | collective-permute-done | bytes 589856 | tf_op jit(solution)/shard_map/cond/branch_1_fun/cond/branch_1_fun/ppermute | solution.py:59
  265.6 26.3 %conditional.30 = (bf16[1024,1152]{1,0:T(8,128)(2,1)S(1)}, f32[1024,1152]{1,0:T(8,128)}, f32[1024,1152]{1,0:T(8,128)}, bf16[2304,1152]{1,0:T(8,128)(2,1)}, bf16[...) conditional(s32[]{:T(128)} %bitcast.56, () %tuple.322, (s32[]{:T(128)}, bf16[288,2304]{1,0:T(8,128)(2,1)}, ...), branch_computations={%region_14.15_spmd, %region_15.16_spmd} | conditional | flops 10871635968 | bytes 29196416 | solution.py:989
  269.9 21.6 %hidden_units.1 = (bf16[1024,1152]{1,0:T(8,128)(2,1)S(1)}, f32[1024,1152]{1,0:T(8,128)}, f32[1024,1152]{1,0:T(8,128)}, bf16[2304,1152]{1,0:T(8,128)(2,1)}, bf16[2304,1152]{1,0:T(8,128)(2,1)}) custom-call(s32[1]{0:T(128)} %bitcast.8.index_ref, bf16[288,1152]{1,0:T(8,128)(2,1)} %get-tuple-element.575.refs_0_, bf16[288,1152]{1,0:T(8,128)(2,1)} %get-tuple-element.576.refs_1_, ...), custom_call_target="tpu_custom_call" | custom-call | flops 10871635968 | bytes 21233664 | tf_op jit(solution)/shard_map/cond/branch_1_fun/hidden_units/pallas_call | solution.py:379
  322.7 11.7 %collective-permute-done.84 = bf16[128,2304]{1,0:T(8,128)(2,1)S(1)} collective-permute-done((bf16[128,2304]{1,0:T(8,128)(2,1)S(1)}, bf16[128,2304]{1,0:T(8,128)(2,1)S(1)}, u32[]{:S(2)}, u32[]{:S(2)}) %collective-permute-start.84) | collective-permute-done | bytes 589856 | tf_op jit(solution)/shard_map/ppermute | solution.py:60
  427.1 48.8 %conditional.31 = (bf16[128,2304]{1,0:T(8,128)(2,1)}, bf16[128,2304]{1,0:T(8,128)(2,1)}, bf16[128,2304]{1,0:T(8,128)(2,1)}, bf16[128,2304]{1,0:T(8,128)(2,1)}, b...) conditional(s32[]{:T(128)} %bitcast.56, () %tuple.341, ...), branch_computations={%region_16.17_spmd, %region_17.22_spmd} | conditional | flops 16321314816 | bytes 77562680 | solution.py:989
  427.1 14.8 %two_products.1 = (bf16[128,2304]{1,0:T(8,128)(2,1)}, bf16[128,2304]{1,0:T(8,128)(2,1)}, bf16[128,2304]{1,0:T(8,128)(2,1)}, bf16[128,2304]{1,0:T(8,128)(2,1)}, b...) custom-call(bf16[1024,1152]{1,0:T(8,128)(2,1)S(1)} %get-tuple-elemen, ...), custom_call_target="tpu_custom_call" | custom-call | flops 10871635968 | bytes 20054016 | tf_op jit(solution)/shard_map/cond/branch_1_fun/two_products/pallas_call | solution.py:176
  460.0 13.6 %conditional.2 = (bf16[2,288,1152]{2,1,0:T(8,128)(2,1)}, bf16[2,288,1152]{2,1,0:T(8,128)(2,1)}) conditional(s32[]{:T(128)} %bitcast.14, () %tuple.149, (bf16[2304,1152]{1,0:T(8,128)(2,1)}, s32[]{:T(128)}) %tuple.153), branch_computations={%region_20.20_spmd, %region_21.21_spmd} | conditional | flops 5308464 | bytes 29196844 | solution.py:989
  480.0 46.5 %conditional.32 = (f32[128,2304]{1,0:T(8,128)}, bf16[128,2304]{1,0:T(8,128)(2,1)}, f32[1,2304]{1,0:T(1,128)S(1)}, f32[1,2304]{1,0:T(1,128)S(1)}, bf16[2,288,1152...) conditional(s32[]{:T(128)} %bitcast.56, () %tuple.340, ...), branch_computations={%region_22.23_spmd, %region_23.30_spmd} | conditional | flops 5449973760 | bytes 96068768 | solution.py:989
  481.0 37.4 %conditional.5 = (bf16[128,2304]{1,0:T(8,128)(2,1)}, bf16[128,2304]{1,0:T(8,128)(2,1)}, bf16[128,2304]{1,0:T(8,128)(2,1)}, bf16[2,288,1152]{2,1,0:T(8,128)(2,1)}...) conditional(s32[]{:T(128)} %bitcast.23, () %tuple.171, ...), branch_computations={%region_24.24_spmd, %region_25.29_spmd} | conditional | flops 5449973760 | bytes 83018704 | solution.py:989
  504.8 12.9 %conditional.4 = (bf16[2,288,1152]{2,1,0:T(8,128)(2,1)}, bf16[2,288,1152]{2,1,0:T(8,128)(2,1)}, bf16[288,1152]{1,0:T(8,128)(2,1)}, bf16[288,1152]{1,0:T(8,128)(2,1)}) conditional(s32[]{:T(128)} %bitcast.22, () %tuple.162, (bf16[2304,1152]{1,0:T(8,128)(2,1)}, s32[]{:T(128)}, bf16[2,288,1152]{2,1,0:T(8,128)(2,1)S(1)}, ...), branch_computations={%region_28.27_spmd, %region_29.28_spmd} | conditional | flops 7962679 | bytes 57066156 | solution.py:989
  533.2 52.0 %conditional.33 = (bf16[512,2304]{1,0:T(8,128)(2,1)S(1)}, bf16[512,512]{1,0:T(8,128)(2,1)}, bf16[2,512,512]{2,1,0:T(8,128)(2,1)S(1)}, bf16[2,512,512]{2,1,0:T(8,128)(2,1)}) conditional(s32[]{:T(128)} %bitcast.56, () %tuple.339, (bf16[128,2304]{1,0:T(8,128)(2,1)}, bf16[2304,512]{1,0:T(8,128)(2,1)}, s32[19]{0:T(128)S(1)}, ...), branch_computations={%region_30.31_spmd, %region_31.32_spmd} | conditional | flops 6916669440 | bytes 70648128 | solution.py:989
  534.4 13.2 %collective-permute-done.59.refs_2_ = bf16[128,2304]{1,0:T(8,128)(2,1)S(1)} collective-permute-done((bf16[128,2304]{1,0:T(8,128)(2,1)}, bf16[128,2304]{1,0:T(8,128)(2,1)S(1)}, u32[]{:S(2)}, u32[]{:S(2)}) %collective-permute-start.59) | collective-permute-done | bytes 589856 | tf_op jit(solution)/shard_map/cond/branch_1_fun/ppermute | solution.py:59
  560.8 17.4 %attention_backward.1 = (bf16[512,512]{1,0:T(8,128)(2,1)}, bf16[2048,512]{1,0:T(8,128)(2,1)S(1)}, bf16[2048,512]{1,0:T(8,128)(2,1)S(1)}) custom-call(s32[19]{0:T(128)S(1)} %get-tuple-element.699.spans_ref, bf16[512,512]{1,0:T(8,128)(2,1)} %get-tuple-element.700.q_ref, bf16[512,512]{1,0:T(8,128)(2,1)S(1)} %convolution_convert_fusion.3.g_ref, ...), custom_call_target="tpu_custom_call" | custom-call | flops 5704253440 | bytes 12582912 | tf_op jit(solution)/shard_map/cond/branch_1_fun/attention_backward/pallas_call | solution.py:895
  587.1 14.9 %conditional.34 = (bf16[288,1024]{1,0:T(8,128)(2,1)}, bf16[288,1024]{1,0:T(8,128)(2,1)}, bf16[288,1024]{1,0:T(8,128)(2,1)}, bf16[288,1024]{1,0:T(8,128)(2,1)}, b...) conditional(s32[]{:T(128)} %bitcast.56, () %tuple.362, (bf16[512,2304]{1,0:T(8,128)(2,1)}, ...), branch_computations={%region_32.33_spmd, %region_33.34_spmd} | conditional | flops 2423955456 | bytes 79774520 | solution.py:989
  619.7 19.0 %collective-permute-done.106 = bf16[512,512]{1,0:T(8,128)(2,1)S(1)} collective-permute-done((bf16[512,512]{1,0:T(8,128)(2,1)S(1)}, bf16[512,512]{1,0:T(8,128)(2,1)S(1)}, u32[]{:S(2)}, u32[]{:S(2)}) %collective-permute-start.106) | collective-permute-done | bytes 524320 | tf_op jit(solution)/shard_map/ppermute | solution.py:60
  642.1 55.8 %conditional.36 = (f32[128,2304]{1,0:T(8,128)}, bf16[304,512]{1,0:T(8,128)(2,1)}, bf16[304,512]{1,0:T(8,128)(2,1)}, bf16[288,512]{1,0:T(8,128)(2,1)}, bf16[288,512]{1,0:T(8,128)(2,1)}) conditional(s32[]{:T(128)} %bitcast.56, () %tuple.338, (s32[16]{0:T(128)S(1)}, bf16[512,512]{1,0:T(8,128)(2,1)S(1)}, bf16[512,512]{1,0:T(8,128)(2,1)S(1)}, ...), branch_computations={%region_36.37_spmd, %region_37.44_spmd} | conditional | flops 3637350400 | bytes 64722316 | solution.py:989
  643.5 28.3 %conditional.7 = (bf16[128,2304]{1,0:T(8,128)(2,1)}, bf16[128,2304]{1,0:T(8,128)(2,1)}, bf16[128,2304]{1,0:T(8,128)(2,1)}, bf16[2,304,512]{2,1,0:T(8,128)(2,1)}, bf16[2,304,512]{2,1,0:T(8,128)(2,1)}) conditional(s32[]{:T(128)} %bitcast.46, () %tuple.192, (bf16[512,512]{1,0:T(8,128)(2,1)S(1)}, bf16[512,512]{1,0:T(8,128)(2,1)S(1)}, ...), branch_computations={%region_38.38_spmd, %region_39.41_spmd} | conditional | flops 3634925568 | bytes 40759916 | solution.py:989
  655.6 12.2 %conditional.6 = (bf16[2,304,512]{2,1,0:T(8,128)(2,1)}, bf16[2,304,512]{2,1,0:T(8,128)(2,1)}) conditional(s32[]{:T(128)} %bitcast.45, () %tuple.186, (bf16[512,2304]{1,0:T(8,128)(2,1)}, bf16[512,512]{1,0:T(8,128)(2,1)}, f32[1,2304]{1,0:T(1,128)S(1)}, f32[1,2304]{1,0:T(1,128)S(1)}, f32[1,2304]{1,0:T(1,128)S(1)}, ...), branch_computations={%region_40.39_spmd, %region_41.40_spmd} | conditional | flops 1215467520 | bytes 21819788 | solution.py:989
  676.2 19.5 %conditional.8 = (f32[128,2304]{1,0:T(8,128)}) conditional(s32[]{:T(128)} %bitcast.46, () %tuple.191, (bf16[128,2304]{1,0:T(8,128)(2,1)}, bf16[128,2304]{1,0:T(8,128)(2,1)}, bf16[128,2304]{1,0:T(8,128)(2,1)}, bf16[128,2304]{1,0:T(8,128)(2,1)}, f32[128,2304]{1,0:T(8,128)}, /*index=5*/f32[4,2304]{1,0:T(4,128)}) %tuple.198), branch_computations={%region_42.42_spmd, %region_43.43_spmd} | conditional | bytes 11870296 | solution.py:989
  678.3 13.2 %collective-permute-done.23.refs_1_ = bf16[128,2304]{1,0:T(8,128)(2,1)S(1)} collective-permute-done((bf16[128,2304]{1,0:T(8,128)(2,1)}, bf16[128,2304]{1,0:T(8,128)(2,1)S(1)}, u32[]{:S(2)}, u32[]{:S(2)}) %collective-permute-start.23) | collective-permute-done | bytes 589856 | tf_op jit(solution)/shard_map/cond/branch_1_fun/cond/branch_1_fun/ppermute | solution.py:59
  705.2 12.6 %collective-permute-done.109 = bf16[304,512]{1,0:T(8,128)(2,1)} collective-permute-done((bf16[304,512]{1,0:T(8,128)(2,1)}, bf16[304,512]{1,0:T(8,128)(2,1)}, u32[]{:S(2)}, u32[]{:S(2)}) %collective-permute-start.109) | collective-permute-done | bytes 311328 | tf_op jit(solution)/shard_map/ppermute | solution.py:60
  722.5 19.7 %conditional.38 = (f32[288,1024]{1,0:T(8,128)}, f32[288,1024]{1,0:T(8,128)}, f32[4,288]{1,0:T(4,128)S(1)}, f32[512,288]{0,1:T(8,128)}, bf16[288,512]{1,0:T(8,128)(2,1)S(1)}) conditional(s32[]{:T(128)} %bitcast.56, () %tuple.375, (s32[]{:T(128)}, bf16[304,512]{1,0:T(8,128)(2,1)S(1)}, bf16[288,1024]{1,0:T(8,128)(2,1)}, bf16[288,1024]{1,0:T(8,128)(2,1)}, ...), branch_computations={%region_46.47_spmd, %region_47.48_spmd} | conditional | flops 1622016 | bytes 14001464 | solution.py:989
  (526 shorter events, 569.2 us)
Async XLA Ops:
  0.7 23.9 %collective-permute-start.63 = (bf16[128,2304]{1,0:T(8,128)(2,1)}, bf16[128,2304]{1,0:T(8,128)(2,1)}, u32[]{:S(2)}, u32[]{:S(2)}) collective-permute-start(bf16[128,2304]{1,0:T(8,128)(2,1)} %param.60), channel_id=1, source_target_pairs={{0,1},{1,0},{2,3},{3,2},{4,5},{5,4},{6,7},{7,6},{8,9},{9,8},{10,11... | collective-permute-start | bytes 1769480 | tf_op jit(solution)/shard_map/ppermute | solution.py:59
  36.0 22.7 %collective-permute-start.70 = (bf16[288,1024]{1,0:T(8,128)(2,1)}, bf16[288,1024]{1,0:T(8,128)(2,1)}, u32[]{:S(2)}, u32[]{:S(2)}) collective-permute-start(bf16[288,1024]{1,0:T(8,128)(2,1)} %copy.41), channel_id=1, source_target_pairs={{0,8},{4,12},{8,0},{12,4},{16,24},{20,28},{24,16},{28,20},{1,9},{5... | collective-permute-start | bytes 1769480 | tf_op jit(solution)/shard_map/ppermute | solution.py:60
  37.5 26.2 %collective-permute-start.71 = (bf16[288,1024]{1,0:T(8,128)(2,1)}, bf16[288,1024]{1,0:T(8,128)(2,1)}, u32[]{:S(2)}, u32[]{:S(2)}) collective-permute-start(bf16[288,1024]{1,0:T(8,128)(2,1)} %copy.41), channel_id=1, source_target_pairs={{0,16},{4,20},{8,24},{12,28},{16,0},{20,4},{24,8},{28,12},{1,17},{... | collective-permute-start | bytes 1769480 | tf_op jit(solution)/shard_map/ppermute | solution.py:60
  63.7 35.0 %collective-permute-start.74 = (bf16[288,1024]{1,0:T(8,128)(2,1)}, bf16[288,1024]{1,0:T(8,128)(2,1)S(1)}, u32[]{:S(2)}, u32[]{:S(2)}) collective-permute-start(bf16[288,1024]{1,0:T(8,128)(2,1)} %collective-permute-done.71), channel_id=1, source_target_pairs={{0,8},{4,12},{8,0},{12,4},{16,24},{20,28},{24,16},{28,20},{1,9},{5... | collective-permute-start | bytes 1769480 | tf_op jit(solution)/shard_map/ppermute | solution.py:60
  63.7 25.3 %collective-permute-start.72 = (bf16[512,512]{1,0:T(8,128)(2,1)}, bf16[512,512]{1,0:T(8,128)(2,1)S(1)}, u32[]{:S(2)}, u32[]{:S(2)}) collective-permute-start(bf16[512,512]{1,0:T(8,128)(2,1)} %get-tuple-element.1153), channel_id=1, source_target_pairs={{0,16},{4,20},{8,24},{12,28},{16,0},{20,4},{24,8},{28,12},{1,17},{... | collective-permute-start | bytes 1572872 | tf_op jit(solution)/shard_map/ppermute | solution.py:60
  63.9 34.9 %collective-permute-start.73 = (bf16[512,512]{1,0:T(8,128)(2,1)}, bf16[512,512]{1,0:T(8,128)(2,1)}, u32[]{:S(2)}, u32[]{:S(2)}) collective-permute-start(bf16[512,512]{1,0:T(8,128)(2,1)} %get-tuple-element.1153), channel_id=1, source_target_pairs={{0,8},{4,12},{8,0},{12,4},{16,24},{20,28},{24,16},{28,20},{1,9},{5... | collective-permute-start | bytes 1572872 | tf_op jit(solution)/shard_map/ppermute | solution.py:60
  98.7 31.0 %collective-permute-start.75 = (bf16[288,1152]{1,0:T(8,128)(2,1)}, bf16[288,1152]{1,0:T(8,128)(2,1)}, u32[]{:S(2)}, u32[]{:S(2)}) collective-permute-start(bf16[288,1152]{1,0:T(8,128)(2,1)} %get-tuple-element.1192), channel_id=1, source_target_pairs={{0,16},{4,20},{8,24},{12,28},{16,0},{20,4},{24,8},{28,12},{1,17},{... | collective-permute-start | bytes 1990664 | tf_op jit(solution)/shard_map/ppermute | solution.py:60
  101.0 23.6 %collective-permute-start.7 = (bf16[512,512]{1,0:T(8,128)(2,1)S(1)}, bf16[512,512]{1,0:T(8,128)(2,1)}, u32[]{:S(2)}, u32[]{:S(2)}) collective-permute-start(bf16[512,512]{1,0:T(8,128)(2,1)S(1)} %get-tuple-element.503), channel_id=1, source_target_pairs={{0,8},{4,12},{8,0},{12,4},{16,24},{20,28},{24,16},{28,20},{1,9},{5... | collective-permute-start | bytes 1572872 | tf_op jit(solution)/shard_map/cond/branch_1_fun/ppermute | solution.py:60
  103.1 21.5 %collective-permute-start.6 = (bf16[512,512]{1,0:T(8,128)(2,1)S(1)}, bf16[512,512]{1,0:T(8,128)(2,1)}, u32[]{:S(2)}, u32[]{:S(2)}) collective-permute-start(bf16[512,512]{1,0:T(8,128)(2,1)S(1)} %get-tuple-element.503), channel_id=1, source_target_pairs={{0,4},{4,0},{8,12},{12,8},{16,20},{20,16},{24,28},{28,24},{1,5},{5... | collective-permute-start | bytes 1572872 | tf_op jit(solution)/shard_map/cond/branch_1_fun/ppermute | solution.py:60
  129.8 60.8 %collective-permute-start.76 = (bf16[288,2304]{1,0:T(8,128)(2,1)}, bf16[288,2304]{1,0:T(8,128)(2,1)}, u32[]{:S(2)}, u32[]{:S(2)}) collective-permute-start(bf16[288,2304]{1,0:T(8,128)(2,1)} %get-tuple-element.1209.refs_0_), channel_id=1, source_target_pairs={{0,16},{4,20},{8,24},{12,28},{16,0},{20,4},{24,8},{28,12},{1,17},{... | collective-permute-start | bytes 3981320 | tf_op jit(solution)/shard_map/ppermute | solution.py:60
  129.8 60.9 %collective-permute-start.77 = (bf16[288,2304]{1,0:T(8,128)(2,1)}, bf16[288,2304]{1,0:T(8,128)(2,1)}, u32[]{:S(2)}, u32[]{:S(2)}) collective-permute-start(bf16[288,2304]{1,0:T(8,128)(2,1)} %get-tuple-element.1208), channel_id=1, source_target_pairs={{0,8},{4,12},{8,0},{12,4},{16,24},{20,28},{24,16},{28,20},{1,9},{5... | collective-permute-start | bytes 3981320 | tf_op jit(solution)/shard_map/ppermute | solution.py:60
  190.6 74.9 %collective-permute-start.78 = (bf16[288,2304]{1,0:T(8,128)(2,1)}, bf16[288,2304]{1,0:T(8,128)(2,1)}, u32[]{:S(2)}, u32[]{:S(2)}) collective-permute-start(bf16[288,2304]{1,0:T(8,128)(2,1)} %collective-permute-done.77), channel_id=1, source_target_pairs={{0,16},{4,20},{8,24},{12,28},{16,0},{20,4},{24,8},{28,12},{1,17},{... | collective-permute-start | bytes 3981320 | tf_op jit(solution)/shard_map/ppermute | solution.py:60
  193.3 39.0 %collective-permute-start.19 = (bf16[128,2304]{1,0:T(8,128)(2,1)S(1)}, bf16[128,2304]{1,0:T(8,128)(2,1)S(1)}, u32[]{:S(2)}, u32[]{:S(2)}) collective-permute-start(bf16[128,2304]{1,0:T(8,128)(2,1)S(1)} %get-tuple-element.562), channel_id=1, source_target_pairs={{0,8},{4,12},{8,0},{12,4},{16,24},{20,28},{24,16},{28,20},{1,9},{5... | collective-permute-start | bytes 1769480 | tf_op jit(solution)/shard_map/cond/branch_1_fun/ppermute | solution.py:60
  206.1 26.2 %collective-permute-start.17 = (bf16[64,2304]{1,0:T(8,128)(2,1)S(1)}, bf16[64,2304]{1,0:T(8,128)(2,1)S(1)}, u32[]{:S(2)}, u32[]{:S(2)}) collective-permute-start(bf16[64,2304]{1,0:T(8,128)(2,1)S(1)} %slice.280), channel_id=1, source_target_pairs={{0,1},{1,0},{2,3},{3,2},{4,5},{5,4},{6,7},{7,6},{8,9},{9,8},{10,11... | collective-permute-start | bytes 884744 | tf_op jit(solution)/shard_map/cond/branch_1_fun/ppermute | solution.py:59
  207.6 24.7 %collective-permute-start.18 = (bf16[64,2304]{1,0:T(8,128)(2,1)S(1)}, bf16[64,2304]{1,0:T(8,128)(2,1)S(1)}, u32[]{:S(2)}, u32[]{:S(2)}) collective-permute-start(bf16[64,2304]{1,0:T(8,128)(2,1)S(1)} %slice.281), channel_id=1, source_target_pairs={{0,2},{1,3},{2,0},{3,1},{4,6},{5,7},{6,4},{7,5},{8,10},{9,11},{10,... | collective-permute-start | bytes 884744 | tf_op jit(solution)/shard_map/cond/branch_1_fun/ppermute | solution.py:59
  232.3 33.2 %collective-permute-start.20 = (bf16[288,1152]{1,0:T(8,128)(2,1)}, bf16[288,1152]{1,0:T(8,128)(2,1)}, u32[]{:S(2)}, u32[]{:S(2)}) collective-permute-start(bf16[288,1152]{1,0:T(8,128)(2,1)} %get-tuple-element.573), channel_id=1, source_target_pairs={{0,8},{4,12},{8,0},{12,4},{16,24},{20,28},{24,16},{28,20},{1,9},{5... | collective-permute-start | bytes 1990664 | tf_op jit(solution)/shard_map/cond/branch_1_fun/ppermute | solution.py:60
  265.5 31.1 %collective-permute-start.79 = (bf16[288,1152]{1,0:T(8,128)(2,1)}, bf16[288,1152]{1,0:T(8,128)(2,1)S(1)}, u32[]{:S(2)}, u32[]{:S(2)}) collective-permute-start(bf16[288,1152]{1,0:T(8,128)(2,1)} %get-tuple-element.1241.refs_2_), channel_id=1, source_target_pairs={{0,16},{4,20},{8,24},{12,28},{16,0},{20,4},{24,8},{28,12},{1,17},{... | collective-permute-start | bytes 1990664 | tf_op jit(solution)/shard_map/ppermute | solution.py:60
  265.7 25.8 %collective-permute-start.22 = (bf16[288,1152]{1,0:T(8,128)(2,1)}, bf16[288,1152]{1,0:T(8,128)(2,1)}, u32[]{:S(2)}, u32[]{:S(2)}) collective-permute-start(bf16[288,1152]{1,0:T(8,128)(2,1)} %get-tuple-element.592), channel_id=1, source_target_pairs={{0,4},{4,0},{8,12},{12,8},{16,20},{20,16},{24,28},{28,24},{1,5},{5... | collective-permute-start | bytes 1990664 | tf_op jit(solution)/shard_map/cond/branch_1_fun/ppermute | solution.py:60
  413.6 62.4 %collective-permute-start.100 = (bf16[2,288,1152]{2,1,0:T(8,128)(2,1)}, bf16[2,288,1152]{2,1,0:T(8,128)(2,1)}, u32[]{:S(2)}, u32[]{:S(2)}) collective-permute-start(bf16[2,288,1152]{2,1,0:T(8,128)(2,1)} %get-tuple-element.1519), channel_id=1, source_target_pairs={{0,16},{4,20},{8,24},{12,28},{16,0},{20,4},{24,8},{28,12},{1,17},{... | collective-permute-start | bytes 3981320 | tf_op jit(solution)/shard_map/ppermute | solution.py:60
  478.6 48.1 %collective-permute-start.101 = (bf16[288,1152]{1,0:T(8,128)(2,1)}, bf16[288,1152]{1,0:T(8,128)(2,1)}, u32[]{:S(2)}, u32[]{:S(2)}) collective-permute-start(bf16[288,1152]{1,0:T(8,128)(2,1)} %get-tuple-element.1307), channel_id=1, source_target_pairs={{0,16},{4,20},{8,24},{12,28},{16,0},{20,4},{24,8},{28,12},{1,17},{... | collective-permute-start | bytes 1990664 | tf_op jit(solution)/shard_map/ppermute | solution.py:60
  480.0 38.4 %collective-permute-start.57 = (bf16[128,2304]{1,0:T(8,128)(2,1)}, bf16[128,2304]{1,0:T(8,128)(2,1)S(1)}, u32[]{:S(2)}, u32[]{:S(2)}) collective-permute-start(bf16[128,2304]{1,0:T(8,128)(2,1)} %get-tuple-element.679), channel_id=1, source_target_pairs={{0,8},{4,12},{8,0},{12,4},{16,24},{20,28},{24,16},{28,20},{1,9},{5... | collective-permute-start | bytes 1769480 | tf_op jit(solution)/shard_map/cond/branch_1_fun/ppermute | solution.py:60
  526.6 58.6 %collective-permute-start.102 = (bf16[288,1152]{1,0:T(8,128)(2,1)}, bf16[288,1152]{1,0:T(8,128)(2,1)}, u32[]{:S(2)}, u32[]{:S(2)}) collective-permute-start(bf16[288,1152]{1,0:T(8,128)(2,1)} %get-tuple-element.1320), channel_id=1, source_target_pairs={{0,16},{4,20},{8,24},{12,28},{16,0},{20,4},{24,8},{28,12},{1,17},{... | collective-permute-start | bytes 1990664 | tf_op jit(solution)/shard_map/ppermute | solution.py:60
  530.8 56.3 %collective-permute-start.103 = (bf16[288,1152]{1,0:T(8,128)(2,1)}, bf16[288,1152]{1,0:T(8,128)(2,1)}, u32[]{:S(2)}, u32[]{:S(2)}) collective-permute-start(bf16[288,1152]{1,0:T(8,128)(2,1)} %get-tuple-element.1321), channel_id=1, source_target_pairs={{0,16},{4,20},{8,24},{12,28},{16,0},{20,4},{24,8},{28,12},{1,17},{... | collective-permute-start | bytes 1990664 | tf_op jit(solution)/shard_map/ppermute | solution.py:60
  532.1 55.0 %collective-permute-start.104 = (bf16[288,1152]{1,0:T(8,128)(2,1)}, bf16[288,1152]{1,0:T(8,128)(2,1)}, u32[]{:S(2)}, u32[]{:S(2)}) collective-permute-start(bf16[288,1152]{1,0:T(8,128)(2,1)} %get-tuple-element.1322), channel_id=1, source_target_pairs={{0,8},{4,12},{8,0},{12,4},{16,24},{20,28},{24,16},{28,20},{1,9},{5... | collective-permute-start | bytes 1990664 | tf_op jit(solution)/shard_map/ppermute | solution.py:60
  587.1 24.8 %collective-permute-start.105 = (bf16[2,512,512]{2,1,0:T(8,128)(2,1)}, bf16[2,512,512]{2,1,0:T(8,128)(2,1)}, u32[]{:S(2)}, u32[]{:S(2)}) collective-permute-start(bf16[2,512,512]{2,1,0:T(8,128)(2,1)} %get-tuple-element.1338), channel_id=1, source_target_pairs={{0,8},{4,12},{8,0},{12,4},{16,24},{20,28},{24,16},{28,20},{1,9},{5... | collective-permute-start | bytes 3145736 | tf_op jit(solution)/shard_map/ppermute | solution.py:60
  613.8 26.9 %collective-permute-start.107 = (bf16[288,1152]{1,0:T(8,128)(2,1)}, bf16[288,1152]{1,0:T(8,128)(2,1)S(1)}, u32[]{:S(2)}, u32[]{:S(2)}) collective-permute-start(bf16[288,1152]{1,0:T(8,128)(2,1)} %get-tuple-element.1343), channel_id=1, source_target_pairs={{0,8},{4,12},{8,0},{12,4},{16,24},{20,28},{24,16},{28,20},{1,9},{5... | collective-permute-start | bytes 1990664 | tf_op jit(solution)/shard_map/ppermute | solution.py:60
  614.2 24.5 %collective-permute-start.106 = (bf16[512,512]{1,0:T(8,128)(2,1)S(1)}, bf16[512,512]{1,0:T(8,128)(2,1)S(1)}, u32[]{:S(2)}, u32[]{:S(2)}) collective-permute-start(bf16[512,512]{1,0:T(8,128)(2,1)S(1)} %get-tuple-element.1526), channel_id=1, source_target_pairs={{0,16},{4,20},{8,24},{12,28},{16,0},{20,4},{24,8},{28,12},{1,17},{... | collective-permute-start | bytes 1572872 | tf_op jit(solution)/shard_map/ppermute | solution.py:60
  640.6 57.3 %collective-permute-start.108 = (bf16[288,1152]{1,0:T(8,128)(2,1)}, bf16[288,1152]{1,0:T(8,128)(2,1)}, u32[]{:S(2)}, u32[]{:S(2)}) collective-permute-start(bf16[288,1152]{1,0:T(8,128)(2,1)} %get-tuple-element.1362), channel_id=1, source_target_pairs={{0,16},{4,20},{8,24},{12,28},{16,0},{20,4},{24,8},{28,12},{1,17},{... | collective-permute-start | bytes 1990664 | tf_op jit(solution)/shard_map/ppermute | solution.py:60
  642.1 29.7 %collective-permute-start.39 = (bf16[288,1024]{1,0:T(8,128)(2,1)}, bf16[288,1024]{1,0:T(8,128)(2,1)}, u32[]{:S(2)}, u32[]{:S(2)}) collective-permute-start(bf16[288,1024]{1,0:T(8,128)(2,1)} %get-tuple-element.804), channel_id=1, source_target_pairs={{0,8},{4,12},{8,0},{12,4},{16,24},{20,28},{24,16},{28,20},{1,9},{5... | collective-permute-start | bytes 1769480 | tf_op jit(solution)/shard_map/cond/branch_1_fun/ppermute | solution.py:60
  671.8 23.9 %collective-permute-start.40 = (bf16[2,304,512]{2,1,0:T(8,128)(2,1)}, bf16[2,304,512]{2,1,0:T(8,128)(2,1)S(1)}, u32[]{:S(2)}, u32[]{:S(2)}) collective-permute-start(bf16[2,304,512]{2,1,0:T(8,128)(2,1)} %get-tuple-element.808), channel_id=1, source_target_pairs={{0,8},{4,12},{8,0},{12,4},{16,24},{20,28},{24,16},{28,20},{1,9},{5... | collective-permute-start | bytes 1867784 | tf_op jit(solution)/shard_map/cond/branch_1_fun/ppermute | solution.py:60
  719.7 22.5 %collective-permute-start.112 = (bf16[288,1152]{1,0:T(8,128)(2,1)S(1)}, bf16[288,1152]{1,0:T(8,128)(2,1)S(1)}, u32[]{:S(2)}, u32[]{:S(2)}) collective-permute-start(bf16[288,1152]{1,0:T(8,128)(2,1)S(1)} %get-tuple-element.1394), channel_id=1, source_target_pairs={{0,8},{4,12},{8,0},{12,4},{16,24},{20,28},{24,16},{28,20},{1,9},{5... | collective-permute-start | bytes 1990664 | tf_op jit(solution)/shard_map/ppermute | solution.py:60
  721.3 20.9 %collective-permute-start.111 = (bf16[288,512]{1,0:T(8,128)(2,1)}, bf16[288,512]{1,0:T(8,128)(2,1)}, u32[]{:S(2)}, u32[]{:S(2)}) collective-permute-start(bf16[288,512]{1,0:T(8,128)(2,1)} %get-tuple-element.1393), channel_id=1, source_target_pairs={{0,16},{4,20},{8,24},{12,28},{16,0},{20,4},{24,8},{28,12},{1,17},{... | collective-permute-start | bytes 884744 | tf_op jit(solution)/shard_map/ppermute | solution.py:60
  (153 other events, 1635.9 us)

commit v6 on v5

--- a/solution.py
+++ b/solution.py
@@ -1257,11 +1257,21 @@
 
     grad_ffn_full = join_rows(gather_rows(grad_ffn_out, unit_axes))
     grad_down = product(grad_ffn_full, hidden, 0, 0, bf16)
-    grad_hidden = product(tie(grad_ffn_full, grad_down), down_weight, 1, 0)
-    grad_gate_act = (grad_hidden * slope).astype(bf16)
-    grad_up_act = (grad_hidden * active).astype(bf16)
-    down_away, down_kept = unit_core(grad_down)
+    down_dims = split_dims(grad_down)
+
+    def down_half(far, core):
+        return pick(pick(down_dims, bit_count - 1, core), 0, far)
+
+    down_away = down_half(1 - side(top), 1 - side(1))
+    down_away = plus(down_half(1 - side(top), side(1)), send(down_away, 1)).astype(bf16)
     down_came = send(down_away, top)
+    down_other = send(down_half(side(top), 1 - side(1)), 1, down_away)
+
+    def hidden_back(rows):
+        grad_hidden = product(rows, down_weight, 1, 0)
+        return (grad_hidden * slope).astype(bf16), (grad_hidden * active).astype(bf16)
+
+    (grad_gate_act, grad_up_act), down_other = segment(hidden_back, (grad_ffn_full,), (down_away,), down_other)
 
     def weight_back(act):
         return product(ffn_full, act, 0, 0, bf16)
@@ -1293,7 +1303,7 @@
         return pieces, results[1]
 
     (ffn_pieces, (gate_away, gate_kept)), down_came = segment(
-        ffn_back_first, (grad_gate_act, grad_up_act), (down_away, down_kept), down_came
+        ffn_back_first, (grad_gate_act, grad_up_act), (down_away,), down_came
     )
 
     def ffn_back_last(ffn_pieces, grad_up_act, down_came):
@@ -1302,7 +1312,7 @@
         def over_head(pieces, grad_up_act):
             came = ()
             beside, results = beside_hops(
-                [lambda: weight_back(grad_up_act), lambda partial: (unit_core(partial), unit_sides(down_kept, down_came))]
+                [lambda: weight_back(grad_up_act), lambda partial: (unit_core(partial), unit_sides(plus(down_half(side(top), side(1)), down_other), down_came))]
             )
             for number, subsets in enumerate(back_plan[split_at:]):
                 subsets = [t for t in subsets if t != last]

time: 756 us -> 753 us (level)
    ppermute x65 -> x66, waiting for transfers between devices: 202 us -> 198 us  [swap(): lax.ppermute(value, 'blk', [(i, i ^ blk_mask) for i in range(block_count)])]
    squeeze x13 -> x12, local copies, waits for them, and re-layouts: 19.6 us -> 16.8 us  [pick(): return lax.dynamic_index_in_dim(value, index, dim, keepdims=False)]
    ppermute x65 -> x66, starting transfers between devices: 47.7 us -> 48.9 us  [swap(): lax.ppermute(value, 'blk', [(i, i ^ blk_mask) for i in range(block_count)])]
  transfers between devices with their start and end apart: 113 -> 114, of which waited for: 73 -> 74; matrix products, arithmetic and copies ran while one was open for 19% -> 19% of each run, Pallas kernels for 15% -> 16%
where the time goes in v6:
time: 753 us; the launch traced here: 742 us
  waiting for transfers between devices  338 us (45%)
  Pallas kernels  130 us (17%)
  starting transfers between devices  95.2 us (13%)
  local copies, waits for them, and re-layouts  62.9 us (8%)
  other arithmetic  60.7 us (8%)
  matrix products  46.7 us (6%)
    ppermute x66, waiting for transfers between devices, swap(): lax.ppermute(value, 'blk', [(i, i ^ blk_mask) for i in range(block_count)])  198 us
    ppermute x48, waiting for transfers between devices, swap(): lax.ppermute(value, 'head', [(i, i ^ head_mask) for i in range(head_count)])  140 us
    ppermute x66, starting transfers between devices, swap(): lax.ppermute(value, 'blk', [(i, i ^ blk_mask) for i in range(block_count)])  48.9 us
    dot_general x6, matrix products, product(): lax.dot_general(left, right, (((left_dim,), (right_dim,)), ((), ())), pre...  46.7 us
    ppermute x48, starting transfers between devices, swap(): lax.ppermute(value, 'head', [(i, i ^ head_mask) for i in range(head_count)])  46.3 us
    pallas_call x4, Pallas kernels, placed(): pl.pallas_call(functools.partial(placed_kernel, body, plans, counts, step...  41.2 us
    pallas_call x6, Pallas kernels, whole_call(): pl.pallas_call(body, out_shape=[jax.ShapeDtypeStruct(shape, dtype) for sh...  17.6 us
    pallas_call x1, Pallas kernels, attention_backward(): pl.pallas_call(functools.partial(backward_kernel, group, span_len, tiles)...  17.3 us
  transfers between devices with their start and end apart: 114, of which 74 were waited for; matrix products, arithmetic and copies ran while one was open for 19% of the time, Pallas kernels for 16%

profile of v6, /device:TPU:0, one launch (start us, length us, event | category | flops | bytes accessed | tf_op | source)
XLA Modules:
  0.0 742.1 jit_solution(4090051878359931019)
XLA Ops:
  38.2 19.9 %conditional.26 = (bf16[512,512]{1,0:T(8,128)(2,1)}, bf16[2304,512]{1,0:T(8,128)(2,1)}, f32[4,2304]{1,0:T(4,128)}, bf16[512,2304]{1,0:T(8,128)(2,1)}, f32[512,1]{1,0:T(8,128)}) conditional(s32[]{:T(128)} %bitcast.57, () %tuple.311, (s32[]{:T(128)}, bf16[304,512]{1,0:T(8,128)(2,1)S(1)}, bf16[304,512]{1,0:T(8,128)(2,1)S(1)}, ...), branch_computations={%region_2.3_spmd, %region_3.4_spmd} | conditional | flops 1207968768 | bytes 29862424 | solution.py:989
  74.7 14.1 %collective-permute-done.72 = bf16[512,512]{1,0:T(8,128)(2,1)S(1)} collective-permute-done((bf16[512,512]{1,0:T(8,128)(2,1)}, bf16[512,512]{1,0:T(8,128)(2,1)S(1)}, u32[]{:S(2)}, u32[]{:S(2)}) %collective-permute-start.72) | collective-permute-done | bytes 524320 | tf_op jit(solution)/shard_map/ppermute | solution.py:60
  98.5 27.7 %conditional.28 = (bf16[512,512]{1,0:T(8,128)(2,1)S(1)}, bf16[512,512]{1,0:T(8,128)(2,1)}, bf16[512,512]{1,0:T(8,128)(2,1)}, bf16[512,512]{1,0:T(8,128)(2,1)}, b...) conditional(s32[]{:T(128)} %bitcast.57, () %tuple.309, ...), branch_computations={%region_6.7_spmd, %region_7.8_spmd} | conditional | flops 1207959552 | bytes 24772900 | solution.py:989
  109.0 15.0 %collective-permute-done.7 = bf16[512,512]{1,0:T(8,128)(2,1)} collective-permute-done((bf16[512,512]{1,0:T(8,128)(2,1)S(1)}, bf16[512,512]{1,0:T(8,128)(2,1)}, u32[]{:S(2)}, u32[]{:S(2)}) %collective-permute-start.7) | collective-permute-done | bytes 524320 | tf_op jit(solution)/shard_map/cond/branch_1_fun/ppermute | solution.py:60
  135.4 46.4 %conditional.29 = (bf16[512,512]{1,0:T(8,128)(2,1)S(1)}, f32[512,512]{1,0:T(8,128)S(1)}, f32[2,1,512]{2,1,0:T(1,128)S(1)}, f32[128,2304]{1,0:T(8,128)S(1)}, f32[...) conditional(s32[]{:T(128)} %bitcast.57, () %tuple.308, ...), branch_computations={%region_8.9_spmd, %region_9.10_spmd} | conditional | flops 3494379520 | bytes 57549292 | solution.py:989
  138.5 12.0 %attention_forward.1 = (bf16[512,512]{1,0:T(8,128)(2,1)S(1)}, f32[512,512]{1,0:T(8,128)S(1)}, f32[2,1,512]{2,1,0:T(1,128)S(1)}) custom-call(s32[19]{0:T(128)S(1)} %get-tuple-element.532.spans_ref, bf16[512,512]{1,0:T(8,128)(2,1)} %get-tuple-element.533.q_ref, bf16[512,512]{1,0:T(8,128)(2,1)} %get-tuple-element.534.refs_0_, ...), custom_call_target="tpu_custom_call" | custom-call | flops 2281701376 | bytes 7340032 | tf_op jit(solution)/shard_map/cond/branch_1_fun/attention_forward/pallas_call | solution.py:850
  166.4 13.2 %collective-permute-done.46.refs_1_ = bf16[128,2304]{1,0:T(8,128)(2,1)S(1)} collective-permute-done((bf16[128,2304]{1,0:T(8,128)(2,1)S(1)}, bf16[128,2304]{1,0:T(8,128)(2,1)S(1)}, u32[]{:S(2)}, u32[]{:S(2)}) %collective-permute-start.46) | collective-permute-done | bytes 589856 | tf_op jit(solution)/shard_map/cond/branch_1_fun/ppermute | solution.py:59
  191.0 74.3 %conditional.30 = (bf16[1024,2304]{1,0:T(8,128)(2,1)}, bf16[288,2304]{1,0:T(8,128)(2,1)}, bf16[288,2304]{1,0:T(8,128)(2,1)}, bf16[288,1152]{1,0:T(8,128)(2,1)}) conditional(s32[]{:T(128)} %bitcast.57, () %tuple.333, (s32[16]{0:T(128)S(1)}, bf16[128,2304]{1,0:T(8,128)(2,1)S(1)}, bf16[288,2304]{1,0:T(8,128)(2,1)}, bf16[288,2304]{1,0:T(8,128)(2,1)}, ...), branch_computations={%region_10.11_spmd, %region_11.14_spmd} | conditional | flops 2 | bytes 41583208 | solution.py:989
  209.0 23.1 %collective-permute-done.19 = bf16[128,2304]{1,0:T(8,128)(2,1)S(1)} collective-permute-done((bf16[128,2304]{1,0:T(8,128)(2,1)S(1)}, bf16[128,2304]{1,0:T(8,128)(2,1)S(1)}, u32[]{:S(2)}, u32[]{:S(2)}) %collective-permute-start.19) | collective-permute-done | bytes 589856 | tf_op jit(solution)/shard_map/cond/branch_1_fun/ppermute | solution.py:60
  234.6 30.7 %conditional = (bf16[1024,2304]{1,0:T(8,128)(2,1)}, bf16[288,2304]{1,0:T(8,128)(2,1)}, bf16[288,2304]{1,0:T(8,128)(2,1)}) conditional(s32[]{:T(128)} %bitcast.7, () %tuple.141, (bf16[128,2304]{1,0:T(8,128)(2,1)S(1)}, bf16[128,2304]{1,0:T(8,128)(2,1)S(1)}, bf16[128,2304]{1,0:T(8,128)(2,1)S(1)}, bf16[128,2304]{1,0:T(8,128)(2,1)S(1)}, ...), branch_computations={%region_12.12_spmd, %region_13.13_spmd} | conditional | bytes 28311816 | solution.py:989
  236.8 13.7 %collective-permute-done.9.refs_6_ = bf16[128,2304]{1,0:T(8,128)(2,1)S(1)} collective-permute-done((bf16[128,2304]{1,0:T(8,128)(2,1)S(1)}, bf16[128,2304]{1,0:T(8,128)(2,1)S(1)}, u32[]{:S(2)}, u32[]{:S(2)}) %collective-permute-start.9) | collective-permute-done | bytes 589856 | tf_op jit(solution)/shard_map/cond/branch_1_fun/cond/branch_1_fun/ppermute | solution.py:59
  265.6 26.2 %conditional.31 = (bf16[1024,1152]{1,0:T(8,128)(2,1)S(1)}, f32[1024,1152]{1,0:T(8,128)}, f32[1024,1152]{1,0:T(8,128)}, bf16[2304,1152]{1,0:T(8,128)(2,1)}, bf16[...) conditional(s32[]{:T(128)} %bitcast.57, () %tuple.332, (s32[]{:T(128)}, bf16[288,2304]{1,0:T(8,128)(2,1)}, ...), branch_computations={%region_14.15_spmd, %region_15.16_spmd} | conditional | flops 10871635968 | bytes 29196416 | solution.py:989
  269.8 21.6 %hidden_units.1 = (bf16[1024,1152]{1,0:T(8,128)(2,1)S(1)}, f32[1024,1152]{1,0:T(8,128)}, f32[1024,1152]{1,0:T(8,128)}, bf16[2304,1152]{1,0:T(8,128)(2,1)}, bf16[2304,1152]{1,0:T(8,128)(2,1)}) custom-call(s32[1]{0:T(128)} %bitcast.8.index_ref, bf16[288,1152]{1,0:T(8,128)(2,1)} %get-tuple-element.589.refs_0_, bf16[288,1152]{1,0:T(8,128)(2,1)} %get-tuple-element.590.refs_1_, ...), custom_call_target="tpu_custom_call" | custom-call | flops 10871635968 | bytes 21233664 | tf_op jit(solution)/shard_map/cond/branch_1_fun/hidden_units/pallas_call | solution.py:379
  408.8 11.9 %conditional.32 = (bf16[1024,1152]{1,0:T(8,128)(2,1)S(1)}, bf16[1024,1152]{1,0:T(8,128)(2,1)S(1)}) conditional(s32[]{:T(128)} %bitcast.57, () %tuple.352, (bf16[1024,2304]{1,0:T(8,128)(2,1)}, bf16[2304,1152]{1,0:T(8,128)(2,1)}, f32[1024,1152]{1,0:T(8,128)}, f32[1024,1152]{1,0:T(8,128)}) %tuple.512), branch_computations={%region_16.17_spmd, %region_17.18_spmd} | conditional | flops 5440536576 | bytes 24182800 | solution.py:989
  408.9 11.8 %multiply_convert_fusion = (bf16[1024,1152]{1,0:T(8,128)(2,1)S(1)}, bf16[1024,1152]{1,0:T(8,128)(2,1)S(1)}) fusion(f32[1024,1152]{1,0:T(8,128)} %get-tuple-element.610, f32[1024,1152]{1,0:T(8,128)} %get-tuple-element.609, bf16[1024,2304]{1,0:T(8,128)(2,1)} %get-tuple-element.607, bf16[2304,1152]{1,0:T(8,128)(2,1)} %get-tuple-element.608), kind=kOutput, calls=%fused_computation.16 | convolution fusion | flops 5440536576 | bytes 24182784 | tf_op jit(solution)/shard_map/cond/branch_1_fun/dot_general | solution.py:939
  422.6 48.6 %conditional.33 = (bf16[128,2304]{1,0:T(8,128)(2,1)}, bf16[128,2304]{1,0:T(8,128)(2,1)}, bf16[128,2304]{1,0:T(8,128)(2,1)}, bf16[128,2304]{1,0:T(8,128)(2,1)}, b...) conditional(s32[]{:T(128)} %bitcast.57, () %tuple.351, ...), branch_computations={%region_18.19_spmd, %region_19.24_spmd} | conditional | flops 16321314816 | bytes 77562680 | solution.py:989
  422.6 16.2 %two_products.1 = (bf16[128,2304]{1,0:T(8,128)(2,1)}, bf16[128,2304]{1,0:T(8,128)(2,1)}, bf16[128,2304]{1,0:T(8,128)(2,1)}, bf16[128,2304]{1,0:T(8,128)(2,1)}, b...) custom-call(bf16[1024,1152]{1,0:T(8,128)(2,1)S(1)} %get-tuple-elemen, ...), custom_call_target="tpu_custom_call" | custom-call | flops 10871635968 | bytes 20054016 | tf_op jit(solution)/shard_map/cond/branch_1_fun/two_products/pallas_call | solution.py:176
  454.8 12.0 %conditional.2 = (bf16[2,288,1152]{2,1,0:T(8,128)(2,1)}, bf16[2,288,1152]{2,1,0:T(8,128)(2,1)}) conditional(s32[]{:T(128)} %bitcast.14, () %tuple.155, (bf16[2304,1152]{1,0:T(8,128)(2,1)}, s32[]{:T(128)}) %tuple.159), branch_computations={%region_22.22_spmd, %region_23.23_spmd} | conditional | flops 5308464 | bytes 29196844 | solution.py:989
  475.0 46.8 %conditional.34 = (f32[128,2304]{1,0:T(8,128)}, bf16[128,2304]{1,0:T(8,128)(2,1)}, f32[1,2304]{1,0:T(1,128)S(1)}, f32[1,2304]{1,0:T(1,128)}, bf16[2,288,1152]{2,...) conditional(s32[]{:T(128)} %bitcast.57, () %tuple.350, ...), branch_computations={%region_24.25_spmd, %region_25.32_spmd} | conditional | flops 5451300864 | bytes 100934936 | solution.py:989
  476.3 37.4 %conditional.5 = (bf16[128,2304]{1,0:T(8,128)(2,1)}, bf16[128,2304]{1,0:T(8,128)(2,1)}, bf16[128,2304]{1,0:T(8,128)(2,1)}, bf16[2,288,1152]{2,1,0:T(8,128)(2,1)}...) conditional(s32[]{:T(128)} %bitcast.24, () %tuple.177, ...), branch_computations={%region_26.26_spmd, %region_27.31_spmd} | conditional | flops 5451300864 | bytes 85525536 | solution.py:989
  500.6 12.9 %conditional.4 = (bf16[2,288,1152]{2,1,0:T(8,128)(2,1)}, bf16[2,288,1152]{2,1,0:T(8,128)(2,1)}, bf16[288,1152]{1,0:T(8,128)(2,1)}, bf16[288,1152]{1,0:T(8,128)(2,1)}) conditional(s32[]{:T(128)} %bitcast.23, () %tuple.168, (bf16[2304,1152]{1,0:T(8,128)(2,1)}, s32[]{:T(128)}, bf16[2,2,2,288,1152]{4,3,2,1,0:T(8,128)(2,1)}, ...), branch_computations={%region_30.29_spmd, %region_31.30_spmd} | conditional | flops 9289785 | bytes 58393300 | solution.py:989
  528.1 52.7 %conditional.35 = (bf16[512,2304]{1,0:T(8,128)(2,1)S(1)}, bf16[512,512]{1,0:T(8,128)(2,1)}, bf16[2,512,512]{2,1,0:T(8,128)(2,1)S(1)}, bf16[2,512,512]{2,1,0:T(8,128)(2,1)}) conditional(s32[]{:T(128)} %bitcast.57, () %tuple.349, (bf16[128,2304]{1,0:T(8,128)(2,1)}, bf16[2304,512]{1,0:T(8,128)(2,1)}, s32[19]{0:T(128)S(1)}, ...), branch_computations={%region_32.33_spmd, %region_33.34_spmd} | conditional | flops 6916669440 | bytes 70648128 | solution.py:989
  529.7 13.2 %collective-permute-done.53.refs_2_ = bf16[128,2304]{1,0:T(8,128)(2,1)S(1)} collective-permute-done((bf16[128,2304]{1,0:T(8,128)(2,1)}, bf16[128,2304]{1,0:T(8,128)(2,1)S(1)}, u32[]{:S(2)}, u32[]{:S(2)}) %collective-permute-start.53) | collective-permute-done | bytes 589856 | tf_op jit(solution)/shard_map/cond/branch_1_fun/ppermute | solution.py:59
  556.4 17.3 %attention_backward.1 = (bf16[512,512]{1,0:T(8,128)(2,1)}, bf16[2048,512]{1,0:T(8,128)(2,1)S(1)}, bf16[2048,512]{1,0:T(8,128)(2,1)S(1)}) custom-call(s32[19]{0:T(128)S(1)} %get-tuple-element.720.spans_ref, bf16[512,512]{1,0:T(8,128)(2,1)} %get-tuple-element.721.q_ref, bf16[512,512]{1,0:T(8,128)(2,1)S(1)} %convolution_convert_fusion.3.g_ref, ...), custom_call_target="tpu_custom_call" | custom-call | flops 5704253440 | bytes 12582912 | tf_op jit(solution)/shard_map/cond/branch_1_fun/attention_backward/pallas_call | solution.py:895
  582.8 14.9 %conditional.36 = (bf16[288,1024]{1,0:T(8,128)(2,1)}, bf16[288,1024]{1,0:T(8,128)(2,1)}, bf16[288,1024]{1,0:T(8,128)(2,1)}, bf16[288,1024]{1,0:T(8,128)(2,1)}, b...) conditional(s32[]{:T(128)} %bitcast.57, () %tuple.376, (bf16[512,2304]{1,0:T(8,128)(2,1)}, ...), branch_computations={%region_34.35_spmd, %region_35.36_spmd} | conditional | flops 2423955456 | bytes 79774520 | solution.py:989
  615.6 19.7 %collective-permute-done.107 = bf16[512,512]{1,0:T(8,128)(2,1)S(1)} collective-permute-done((bf16[512,512]{1,0:T(8,128)(2,1)S(1)}, bf16[512,512]{1,0:T(8,128)(2,1)S(1)}, u32[]{:S(2)}, u32[]{:S(2)}) %collective-permute-start.107) | collective-permute-done | bytes 524320 | tf_op jit(solution)/shard_map/ppermute | solution.py:60
  638.7 55.5 %conditional.38 = (f32[128,2304]{1,0:T(8,128)}, bf16[304,512]{1,0:T(8,128)(2,1)}, bf16[304,512]{1,0:T(8,128)(2,1)}, bf16[288,512]{1,0:T(8,128)(2,1)}, bf16[288,512]{1,0:T(8,128)(2,1)}) conditional(s32[]{:T(128)} %bitcast.57, () %tuple.348, (s32[16]{0:T(128)S(1)}, bf16[512,512]{1,0:T(8,128)(2,1)S(1)}, bf16[512,512]{1,0:T(8,128)(2,1)S(1)}, ...), branch_computations={%region_38.39_spmd, %region_39.46_spmd} | conditional | flops 3637350400 | bytes 64722316 | solution.py:989
  639.7 27.8 %conditional.7 = (bf16[128,2304]{1,0:T(8,128)(2,1)}, bf16[128,2304]{1,0:T(8,128)(2,1)}, bf16[128,2304]{1,0:T(8,128)(2,1)}, bf16[2,304,512]{2,1,0:T(8,128)(2,1)}, bf16[2,304,512]{2,1,0:T(8,128)(2,1)}) conditional(s32[]{:T(128)} %bitcast.47, () %tuple.198, (bf16[512,512]{1,0:T(8,128)(2,1)S(1)}, bf16[512,512]{1,0:T(8,128)(2,1)S(1)}, ...), branch_computations={%region_40.40_spmd, %region_41.43_spmd} | conditional | flops 3634925568 | bytes 40759916 | solution.py:989
  650.6 12.9 %conditional.6 = (bf16[2,304,512]{2,1,0:T(8,128)(2,1)}, bf16[2,304,512]{2,1,0:T(8,128)(2,1)}) conditional(s32[]{:T(128)} %bitcast.46, () %tuple.192, (bf16[512,2304]{1,0:T(8,128)(2,1)}, bf16[512,512]{1,0:T(8,128)(2,1)}, f32[1,2304]{1,0:T(1,128)S(1)}, f32[1,2304]{1,0:T(1,128)}, f32[1,2304]{1,0:T(1,128)S(1)}, /*index=5*/f32[1,2304]{1,0:T(1,128)S(1)}, ...), branch_computations={%region_42.41_spmd, %region_43.42_spmd} | conditional | flops 1215467520 | bytes 21819788 | solution.py:989
  672.6 19.4 %conditional.8 = (f32[128,2304]{1,0:T(8,128)}) conditional(s32[]{:T(128)} %bitcast.47, () %tuple.197, (bf16[128,2304]{1,0:T(8,128)(2,1)}, bf16[128,2304]{1,0:T(8,128)(2,1)}, bf16[128,2304]{1,0:T(8,128)(2,1)}, bf16[128,2304]{1,0:T(8,128)(2,1)}, f32[128,2304]{1,0:T(8,128)}, /*index=5*/f32[4,2304]{1,0:T(4,128)}) %tuple.204), branch_computations={%region_44.44_spmd, %region_45.45_spmd} | conditional | bytes 11870296 | solution.py:989
  675.5 12.1 %collective-permute-done.23.refs_1_ = bf16[128,2304]{1,0:T(8,128)(2,1)S(1)} collective-permute-done((bf16[128,2304]{1,0:T(8,128)(2,1)}, bf16[128,2304]{1,0:T(8,128)(2,1)S(1)}, u32[]{:S(2)}, u32[]{:S(2)}) %collective-permute-start.23) | collective-permute-done | bytes 589856 | tf_op jit(solution)/shard_map/cond/branch_1_fun/cond/branch_1_fun/ppermute | solution.py:59
  718.6 19.5 %conditional.40 = (f32[288,1024]{1,0:T(8,128)}, f32[288,1024]{1,0:T(8,128)}, f32[4,288]{1,0:T(4,128)S(1)}, f32[512,288]{0,1:T(8,128)}, bf16[288,512]{1,0:T(8,128)(2,1)S(1)}) conditional(s32[]{:T(128)} %bitcast.57, () %tuple.389, (s32[]{:T(128)}, bf16[304,512]{1,0:T(8,128)(2,1)S(1)}, bf16[288,1024]{1,0:T(8,128)(2,1)}, bf16[288,1024]{1,0:T(8,128)(2,1)}, ...), branch_computations={%region_48.49_spmd, %region_49.50_spmd} | conditional | flops 1622016 | bytes 14001464 | solution.py:989
  (519 shorter events, 577.0 us)
Async XLA Ops:
  0.7 23.9 %collective-permute-start.63 = (bf16[128,2304]{1,0:T(8,128)(2,1)}, bf16[128,2304]{1,0:T(8,128)(2,1)}, u32[]{:S(2)}, u32[]{:S(2)}) collective-permute-start(bf16[128,2304]{1,0:T(8,128)(2,1)} %param.62), channel_id=1, source_target_pairs={{0,1},{1,0},{2,3},{3,2},{4,5},{5,4},{6,7},{7,6},{8,9},{9,8},{10,11... | collective-permute-start | bytes 1769480 | tf_op jit(solution)/shard_map/ppermute | solution.py:59
  3.7 20.9 %collective-permute-start.64 = (bf16[128,2304]{1,0:T(8,128)(2,1)}, bf16[128,2304]{1,0:T(8,128)(2,1)}, u32[]{:S(2)}, u32[]{:S(2)}) collective-permute-start(bf16[128,2304]{1,0:T(8,128)(2,1)} %param.62), channel_id=1, source_target_pairs={{0,2},{1,3},{2,0},{3,1},{4,6},{5,7},{6,4},{7,5},{8,10},{9,11},{10,... | collective-permute-start | bytes 1769480 | tf_op jit(solution)/shard_map/ppermute | solution.py:59
  35.8 23.0 %collective-permute-start.70 = (bf16[288,1024]{1,0:T(8,128)(2,1)}, bf16[288,1024]{1,0:T(8,128)(2,1)}, u32[]{:S(2)}, u32[]{:S(2)}) collective-permute-start(bf16[288,1024]{1,0:T(8,128)(2,1)} %copy.44), channel_id=1, source_target_pairs={{0,8},{4,12},{8,0},{12,4},{16,24},{20,28},{24,16},{28,20},{1,9},{5... | collective-permute-start | bytes 1769480 | tf_op jit(solution)/shard_map/ppermute | solution.py:60
  37.4 26.1 %collective-permute-start.71 = (bf16[288,1024]{1,0:T(8,128)(2,1)}, bf16[288,1024]{1,0:T(8,128)(2,1)}, u32[]{:S(2)}, u32[]{:S(2)}) collective-permute-start(bf16[288,1024]{1,0:T(8,128)(2,1)} %copy.44), channel_id=1, source_target_pairs={{0,16},{4,20},{8,24},{12,28},{16,0},{20,4},{24,8},{28,12},{1,17},{... | collective-permute-start | bytes 1769480 | tf_op jit(solution)/shard_map/ppermute | solution.py:60
  63.4 35.0 %collective-permute-start.74 = (bf16[288,1024]{1,0:T(8,128)(2,1)}, bf16[288,1024]{1,0:T(8,128)(2,1)S(1)}, u32[]{:S(2)}, u32[]{:S(2)}) collective-permute-start(bf16[288,1024]{1,0:T(8,128)(2,1)} %collective-permute-done.71), channel_id=1, source_target_pairs={{0,8},{4,12},{8,0},{12,4},{16,24},{20,28},{24,16},{28,20},{1,9},{5... | collective-permute-start | bytes 1769480 | tf_op jit(solution)/shard_map/ppermute | solution.py:60
  63.4 25.3 %collective-permute-start.72 = (bf16[512,512]{1,0:T(8,128)(2,1)}, bf16[512,512]{1,0:T(8,128)(2,1)S(1)}, u32[]{:S(2)}, u32[]{:S(2)}) collective-permute-start(bf16[512,512]{1,0:T(8,128)(2,1)} %get-tuple-element.1180), channel_id=1, source_target_pairs={{0,16},{4,20},{8,24},{12,28},{16,0},{20,4},{24,8},{28,12},{1,17},{... | collective-permute-start | bytes 1572872 | tf_op jit(solution)/shard_map/ppermute | solution.py:60
  63.6 34.9 %collective-permute-start.73 = (bf16[512,512]{1,0:T(8,128)(2,1)}, bf16[512,512]{1,0:T(8,128)(2,1)}, u32[]{:S(2)}, u32[]{:S(2)}) collective-permute-start(bf16[512,512]{1,0:T(8,128)(2,1)} %get-tuple-element.1180), channel_id=1, source_target_pairs={{0,8},{4,12},{8,0},{12,4},{16,24},{20,28},{24,16},{28,20},{1,9},{5... | collective-permute-start | bytes 1572872 | tf_op jit(solution)/shard_map/ppermute | solution.py:60
  98.4 30.7 %collective-permute-start.75 = (bf16[288,1152]{1,0:T(8,128)(2,1)}, bf16[288,1152]{1,0:T(8,128)(2,1)}, u32[]{:S(2)}, u32[]{:S(2)}) collective-permute-start(bf16[288,1152]{1,0:T(8,128)(2,1)} %get-tuple-element.1219), channel_id=1, source_target_pairs={{0,16},{4,20},{8,24},{12,28},{16,0},{20,4},{24,8},{28,12},{1,17},{... | collective-permute-start | bytes 1990664 | tf_op jit(solution)/shard_map/ppermute | solution.py:60
  100.7 23.2 %collective-permute-start.7 = (bf16[512,512]{1,0:T(8,128)(2,1)S(1)}, bf16[512,512]{1,0:T(8,128)(2,1)}, u32[]{:S(2)}, u32[]{:S(2)}) collective-permute-start(bf16[512,512]{1,0:T(8,128)(2,1)S(1)} %get-tuple-element.517), channel_id=1, source_target_pairs={{0,8},{4,12},{8,0},{12,4},{16,24},{20,28},{24,16},{28,20},{1,9},{5... | collective-permute-start | bytes 1572872 | tf_op jit(solution)/shard_map/cond/branch_1_fun/ppermute | solution.py:60
  102.9 21.1 %collective-permute-start.6 = (bf16[512,512]{1,0:T(8,128)(2,1)S(1)}, bf16[512,512]{1,0:T(8,128)(2,1)}, u32[]{:S(2)}, u32[]{:S(2)}) collective-permute-start(bf16[512,512]{1,0:T(8,128)(2,1)S(1)} %get-tuple-element.517), channel_id=1, source_target_pairs={{0,4},{4,0},{8,12},{12,8},{16,20},{20,16},{24,28},{28,24},{1,5},{5... | collective-permute-start | bytes 1572872 | tf_op jit(solution)/shard_map/cond/branch_1_fun/ppermute | solution.py:60
  129.2 60.8 %collective-permute-start.76 = (bf16[288,2304]{1,0:T(8,128)(2,1)}, bf16[288,2304]{1,0:T(8,128)(2,1)}, u32[]{:S(2)}, u32[]{:S(2)}) collective-permute-start(bf16[288,2304]{1,0:T(8,128)(2,1)} %get-tuple-element.1236.refs_0_), channel_id=1, source_target_pairs={{0,16},{4,20},{8,24},{12,28},{16,0},{20,4},{24,8},{28,12},{1,17},{... | collective-permute-start | bytes 3981320 | tf_op jit(solution)/shard_map/ppermute | solution.py:60
  130.2 59.8 %collective-permute-start.77 = (bf16[288,2304]{1,0:T(8,128)(2,1)}, bf16[288,2304]{1,0:T(8,128)(2,1)}, u32[]{:S(2)}, u32[]{:S(2)}) collective-permute-start(bf16[288,2304]{1,0:T(8,128)(2,1)} %get-tuple-element.1235), channel_id=1, source_target_pairs={{0,8},{4,12},{8,0},{12,4},{16,24},{20,28},{24,16},{28,20},{1,9},{5... | collective-permute-start | bytes 3981320 | tf_op jit(solution)/shard_map/ppermute | solution.py:60
  190.0 75.3 %collective-permute-start.78 = (bf16[288,2304]{1,0:T(8,128)(2,1)}, bf16[288,2304]{1,0:T(8,128)(2,1)}, u32[]{:S(2)}, u32[]{:S(2)}) collective-permute-start(bf16[288,2304]{1,0:T(8,128)(2,1)} %collective-permute-done.77), channel_id=1, source_target_pairs={{0,16},{4,20},{8,24},{12,28},{16,0},{20,4},{24,8},{28,12},{1,17},{... | collective-permute-start | bytes 3981320 | tf_op jit(solution)/shard_map/ppermute | solution.py:60
  193.1 39.0 %collective-permute-start.19 = (bf16[128,2304]{1,0:T(8,128)(2,1)S(1)}, bf16[128,2304]{1,0:T(8,128)(2,1)S(1)}, u32[]{:S(2)}, u32[]{:S(2)}) collective-permute-start(bf16[128,2304]{1,0:T(8,128)(2,1)S(1)} %get-tuple-element.576), channel_id=1, source_target_pairs={{0,8},{4,12},{8,0},{12,4},{16,24},{20,28},{24,16},{28,20},{1,9},{5... | collective-permute-start | bytes 1769480 | tf_op jit(solution)/shard_map/cond/branch_1_fun/ppermute | solution.py:60
  205.9 26.2 %collective-permute-start.17 = (bf16[64,2304]{1,0:T(8,128)(2,1)S(1)}, bf16[64,2304]{1,0:T(8,128)(2,1)S(1)}, u32[]{:S(2)}, u32[]{:S(2)}) collective-permute-start(bf16[64,2304]{1,0:T(8,128)(2,1)S(1)} %slice.281), channel_id=1, source_target_pairs={{0,1},{1,0},{2,3},{3,2},{4,5},{5,4},{6,7},{7,6},{8,9},{9,8},{10,11... | collective-permute-start | bytes 884744 | tf_op jit(solution)/shard_map/cond/branch_1_fun/ppermute | solution.py:59
  207.4 24.7 %collective-permute-start.18 = (bf16[64,2304]{1,0:T(8,128)(2,1)S(1)}, bf16[64,2304]{1,0:T(8,128)(2,1)S(1)}, u32[]{:S(2)}, u32[]{:S(2)}) collective-permute-start(bf16[64,2304]{1,0:T(8,128)(2,1)S(1)} %slice.282), channel_id=1, source_target_pairs={{0,2},{1,3},{2,0},{3,1},{4,6},{5,7},{6,4},{7,5},{8,10},{9,11},{10,... | collective-permute-start | bytes 884744 | tf_op jit(solution)/shard_map/cond/branch_1_fun/ppermute | solution.py:59
  232.1 33.2 %collective-permute-start.20 = (bf16[288,1152]{1,0:T(8,128)(2,1)}, bf16[288,1152]{1,0:T(8,128)(2,1)}, u32[]{:S(2)}, u32[]{:S(2)}) collective-permute-start(bf16[288,1152]{1,0:T(8,128)(2,1)} %get-tuple-element.587), channel_id=1, source_target_pairs={{0,8},{4,12},{8,0},{12,4},{16,24},{20,28},{24,16},{28,20},{1,9},{5... | collective-permute-start | bytes 1990664 | tf_op jit(solution)/shard_map/cond/branch_1_fun/ppermute | solution.py:60
  265.3 31.1 %collective-permute-start.79 = (bf16[288,1152]{1,0:T(8,128)(2,1)}, bf16[288,1152]{1,0:T(8,128)(2,1)S(1)}, u32[]{:S(2)}, u32[]{:S(2)}) collective-permute-start(bf16[288,1152]{1,0:T(8,128)(2,1)} %get-tuple-element.1268.refs_2_), channel_id=1, source_target_pairs={{0,16},{4,20},{8,24},{12,28},{16,0},{20,4},{24,8},{28,12},{1,17},{... | collective-permute-start | bytes 1990664 | tf_op jit(solution)/shard_map/ppermute | solution.py:60
  265.6 25.8 %collective-permute-start.22 = (bf16[288,1152]{1,0:T(8,128)(2,1)}, bf16[288,1152]{1,0:T(8,128)(2,1)}, u32[]{:S(2)}, u32[]{:S(2)}) collective-permute-start(bf16[288,1152]{1,0:T(8,128)(2,1)} %get-tuple-element.606), channel_id=1, source_target_pairs={{0,4},{4,0},{8,12},{12,8},{16,20},{20,16},{24,28},{28,24},{1,5},{5... | collective-permute-start | bytes 1990664 | tf_op jit(solution)/shard_map/cond/branch_1_fun/ppermute | solution.py:60
  407.4 63.7 %collective-permute-start.101 = (bf16[2,288,1152]{2,1,0:T(8,128)(2,1)}, bf16[2,288,1152]{2,1,0:T(8,128)(2,1)}, u32[]{:S(2)}, u32[]{:S(2)}) collective-permute-start(bf16[2,288,1152]{2,1,0:T(8,128)(2,1)} %fusion.10), channel_id=1, source_target_pairs={{0,16},{4,20},{8,24},{12,28},{16,0},{20,4},{24,8},{28,12},{1,17},{... | collective-permute-start | bytes 3981320 | tf_op jit(solution)/shard_map/ppermute | solution.py:60
  473.7 48.1 %collective-permute-start.102 = (bf16[288,1152]{1,0:T(8,128)(2,1)}, bf16[288,1152]{1,0:T(8,128)(2,1)}, u32[]{:S(2)}, u32[]{:S(2)}) collective-permute-start(bf16[288,1152]{1,0:T(8,128)(2,1)} %get-tuple-element.1340), channel_id=1, source_target_pairs={{0,16},{4,20},{8,24},{12,28},{16,0},{20,4},{24,8},{28,12},{1,17},{... | collective-permute-start | bytes 1990664 | tf_op jit(solution)/shard_map/ppermute | solution.py:60
  475.0 38.7 %collective-permute-start.62 = (bf16[128,2304]{1,0:T(8,128)(2,1)}, bf16[128,2304]{1,0:T(8,128)(2,1)S(1)}, u32[]{:S(2)}, u32[]{:S(2)}) collective-permute-start(bf16[128,2304]{1,0:T(8,128)(2,1)} %get-tuple-element.700), channel_id=1, source_target_pairs={{0,8},{4,12},{8,0},{12,4},{16,24},{20,28},{24,16},{28,20},{1,9},{5... | collective-permute-start | bytes 1769480 | tf_op jit(solution)/shard_map/cond/branch_1_fun/ppermute | solution.py:60
  521.9 58.8 %collective-permute-start.103 = (bf16[288,1152]{1,0:T(8,128)(2,1)}, bf16[288,1152]{1,0:T(8,128)(2,1)}, u32[]{:S(2)}, u32[]{:S(2)}) collective-permute-start(bf16[288,1152]{1,0:T(8,128)(2,1)} %get-tuple-element.1353), channel_id=1, source_target_pairs={{0,16},{4,20},{8,24},{12,28},{16,0},{20,4},{24,8},{28,12},{1,17},{... | collective-permute-start | bytes 1990664 | tf_op jit(solution)/shard_map/ppermute | solution.py:60
  525.5 57.3 %collective-permute-start.104 = (bf16[288,1152]{1,0:T(8,128)(2,1)}, bf16[288,1152]{1,0:T(8,128)(2,1)}, u32[]{:S(2)}, u32[]{:S(2)}) collective-permute-start(bf16[288,1152]{1,0:T(8,128)(2,1)} %get-tuple-element.1354), channel_id=1, source_target_pairs={{0,16},{4,20},{8,24},{12,28},{16,0},{20,4},{24,8},{28,12},{1,17},{... | collective-permute-start | bytes 1990664 | tf_op jit(solution)/shard_map/ppermute | solution.py:60
  527.3 55.5 %collective-permute-start.105 = (bf16[288,1152]{1,0:T(8,128)(2,1)}, bf16[288,1152]{1,0:T(8,128)(2,1)}, u32[]{:S(2)}, u32[]{:S(2)}) collective-permute-start(bf16[288,1152]{1,0:T(8,128)(2,1)} %get-tuple-element.1355), channel_id=1, source_target_pairs={{0,8},{4,12},{8,0},{12,4},{16,24},{20,28},{24,16},{28,20},{1,9},{5... | collective-permute-start | bytes 1990664 | tf_op jit(solution)/shard_map/ppermute | solution.py:60
  582.8 25.2 %collective-permute-start.106 = (bf16[2,512,512]{2,1,0:T(8,128)(2,1)}, bf16[2,512,512]{2,1,0:T(8,128)(2,1)}, u32[]{:S(2)}, u32[]{:S(2)}) collective-permute-start(bf16[2,512,512]{2,1,0:T(8,128)(2,1)} %get-tuple-element.1371), channel_id=1, source_target_pairs={{0,8},{4,12},{8,0},{12,4},{16,24},{20,28},{24,16},{28,20},{1,9},{5... | collective-permute-start | bytes 3145736 | tf_op jit(solution)/shard_map/ppermute | solution.py:60
  609.9 27.3 %collective-permute-start.108 = (bf16[288,1152]{1,0:T(8,128)(2,1)}, bf16[288,1152]{1,0:T(8,128)(2,1)S(1)}, u32[]{:S(2)}, u32[]{:S(2)}) collective-permute-start(bf16[288,1152]{1,0:T(8,128)(2,1)} %get-tuple-element.1376), channel_id=1, source_target_pairs={{0,8},{4,12},{8,0},{12,4},{16,24},{20,28},{24,16},{28,20},{1,9},{5... | collective-permute-start | bytes 1990664 | tf_op jit(solution)/shard_map/ppermute | solution.py:60
  610.3 25.0 %collective-permute-start.107 = (bf16[512,512]{1,0:T(8,128)(2,1)S(1)}, bf16[512,512]{1,0:T(8,128)(2,1)S(1)}, u32[]{:S(2)}, u32[]{:S(2)}) collective-permute-start(bf16[512,512]{1,0:T(8,128)(2,1)S(1)} %get-tuple-element.1559), channel_id=1, source_target_pairs={{0,16},{4,20},{8,24},{12,28},{16,0},{20,4},{24,8},{28,12},{1,17},{... | collective-permute-start | bytes 1572872 | tf_op jit(solution)/shard_map/ppermute | solution.py:60
  637.2 57.0 %collective-permute-start.109 = (bf16[288,1152]{1,0:T(8,128)(2,1)}, bf16[288,1152]{1,0:T(8,128)(2,1)}, u32[]{:S(2)}, u32[]{:S(2)}) collective-permute-start(bf16[288,1152]{1,0:T(8,128)(2,1)} %get-tuple-element.1395), channel_id=1, source_target_pairs={{0,16},{4,20},{8,24},{12,28},{16,0},{20,4},{24,8},{28,12},{1,17},{... | collective-permute-start | bytes 1990664 | tf_op jit(solution)/shard_map/ppermute | solution.py:60
  638.7 28.8 %collective-permute-start.38 = (bf16[288,1024]{1,0:T(8,128)(2,1)}, bf16[288,1024]{1,0:T(8,128)(2,1)}, u32[]{:S(2)}, u32[]{:S(2)}) collective-permute-start(bf16[288,1024]{1,0:T(8,128)(2,1)} %get-tuple-element.825), channel_id=1, source_target_pairs={{0,8},{4,12},{8,0},{12,4},{16,24},{20,28},{24,16},{28,20},{1,9},{5... | collective-permute-start | bytes 1769480 | tf_op jit(solution)/shard_map/cond/branch_1_fun/ppermute | solution.py:60
  667.5 24.5 %collective-permute-start.39 = (bf16[2,304,512]{2,1,0:T(8,128)(2,1)}, bf16[2,304,512]{2,1,0:T(8,128)(2,1)S(1)}, u32[]{:S(2)}, u32[]{:S(2)}) collective-permute-start(bf16[2,304,512]{2,1,0:T(8,128)(2,1)} %get-tuple-element.829), channel_id=1, source_target_pairs={{0,8},{4,12},{8,0},{12,4},{16,24},{20,28},{24,16},{28,20},{1,9},{5... | collective-permute-start | bytes 1867784 | tf_op jit(solution)/shard_map/cond/branch_1_fun/ppermute | solution.py:60
  716.2 21.9 %collective-permute-start.113 = (bf16[288,1152]{1,0:T(8,128)(2,1)S(1)}, bf16[288,1152]{1,0:T(8,128)(2,1)S(1)}, u32[]{:S(2)}, u32[]{:S(2)}) collective-permute-start(bf16[288,1152]{1,0:T(8,128)(2,1)S(1)} %get-tuple-element.1427), channel_id=1, source_target_pairs={{0,8},{4,12},{8,0},{12,4},{16,24},{20,28},{24,16},{28,20},{1,9},{5... | collective-permute-start | bytes 1990664 | tf_op jit(solution)/shard_map/ppermute | solution.py:60
  (151 other events, 1608.9 us)

commit v7 on v6

--- a/solution.py
+++ b/solution.py
@@ -541,8 +541,8 @@
         active = gate * share
         slope = share + (0.5 * inner) * gate * (1.0 - tangent * tangent) * (1.0 + (3 * 0.044715) * square)
         hidden_ref[...] = (active * up).astype(bf16)
-        active_ref[...] = active
-        slope_ref[...] = slope * up
+        active_ref[...] = active.astype(bf16)
+        slope_ref[...] = (slope * up).astype(bf16)
 
     return placed(
         body,
@@ -552,7 +552,7 @@
         [],
         [rows],
         [pl.BlockSpec((step, depth), lambda n, b: (n, 0))],
-        [jax.ShapeDtypeStruct((count, width), dtype) for dtype in (bf16, f32, f32)],
+        [jax.ShapeDtypeStruct((count, width), bf16)] * 3,
         [pl.BlockSpec((step, width), lambda n, b: (n, 0))] * 3,
         block_index,
         "hidden_units",

time: 753 us -> 751 us (level)
  transfers between devices with their start and end apart: 114 -> 114, of which waited for: 74 -> 72; matrix products, arithmetic and copies ran while one was open for 19% -> 18% of each run, Pallas kernels for 16% -> 15%
where the time goes in v7:
time: 751 us; the launch traced here: 741 us
  waiting for transfers between devices  343 us (46%)
  Pallas kernels  129 us (17%)
  starting transfers between devices  91.1 us (12%)
  local copies, waits for them, and re-layouts  62.4 us (8%)
  other arithmetic  61.2 us (8%)
  matrix products  45.1 us (6%)
    ppermute x66, waiting for transfers between devices, swap(): lax.ppermute(value, 'blk', [(i, i ^ blk_mask) for i in range(block_count)])  202 us
    ppermute x48, waiting for transfers between devices, swap(): lax.ppermute(value, 'head', [(i, i ^ head_mask) for i in range(head_count)])  141 us
    ppermute x48, starting transfers between devices, swap(): lax.ppermute(value, 'head', [(i, i ^ head_mask) for i in range(head_count)])  47.3 us
    dot_general x6, matrix products, product(): lax.dot_general(left, right, (((left_dim,), (right_dim,)), ((), ())), pre...  45.1 us
    ppermute x66, starting transfers between devices, swap(): lax.ppermute(value, 'blk', [(i, i ^ blk_mask) for i in range(block_count)])  43.9 us
    pallas_call x4, Pallas kernels, placed(): pl.pallas_call(functools.partial(placed_kernel, body, plans, counts, step...  40.8 us
    squeeze x12, local copies, waits for them, and re-layouts, pick(): return lax.dynamic_index_in_dim(value, index, dim, keepdims=False)  18.5 us
    pallas_call x6, Pallas kernels, whole_call(): pl.pallas_call(body, out_shape=[jax.ShapeDtypeStruct(shape, dtype) for sh...  17.7 us
  transfers between devices with their start and end apart: 114, of which 72 were waited for; matrix products, arithmetic and copies ran while one was open for 18% of the time, Pallas kernels for 15%

profile of v7, /device:TPU:0, one launch (start us, length us, event | category | flops | bytes accessed | tf_op | source)
XLA Modules:
  0.0 740.9 jit_solution(8698103107765114923)
XLA Ops:
  38.2 19.9 %conditional.26 = (bf16[512,512]{1,0:T(8,128)(2,1)}, bf16[2304,512]{1,0:T(8,128)(2,1)}, f32[4,2304]{1,0:T(4,128)}, bf16[512,2304]{1,0:T(8,128)(2,1)}, f32[512,1]{1,0:T(8,128)}) conditional(s32[]{:T(128)} %bitcast.57, () %tuple.311, (s32[]{:T(128)}, bf16[304,512]{1,0:T(8,128)(2,1)S(1)}, bf16[304,512]{1,0:T(8,128)(2,1)S(1)}, ...), branch_computations={%region_2.3_spmd, %region_3.4_spmd} | conditional | flops 1207968768 | bytes 29862424 | solution.py:989
  75.1 14.1 %collective-permute-done.72 = bf16[512,512]{1,0:T(8,128)(2,1)S(1)} collective-permute-done((bf16[512,512]{1,0:T(8,128)(2,1)}, bf16[512,512]{1,0:T(8,128)(2,1)S(1)}, u32[]{:S(2)}, u32[]{:S(2)}) %collective-permute-start.72) | collective-permute-done | bytes 524320 | tf_op jit(solution)/shard_map/ppermute | solution.py:60
  98.9 28.3 %conditional.28 = (bf16[512,512]{1,0:T(8,128)(2,1)S(1)}, bf16[512,512]{1,0:T(8,128)(2,1)}, bf16[512,512]{1,0:T(8,128)(2,1)}, bf16[512,512]{1,0:T(8,128)(2,1)}, b...) conditional(s32[]{:T(128)} %bitcast.57, () %tuple.309, ...), branch_computations={%region_6.7_spmd, %region_7.8_spmd} | conditional | flops 1207959552 | bytes 24772900 | solution.py:989
  109.4 15.6 %collective-permute-done.7 = bf16[512,512]{1,0:T(8,128)(2,1)} collective-permute-done((bf16[512,512]{1,0:T(8,128)(2,1)S(1)}, bf16[512,512]{1,0:T(8,128)(2,1)}, u32[]{:S(2)}, u32[]{:S(2)}) %collective-permute-start.7) | collective-permute-done | bytes 524320 | tf_op jit(solution)/shard_map/cond/branch_1_fun/ppermute | solution.py:60
  133.7 46.3 %conditional.29 = (bf16[512,512]{1,0:T(8,128)(2,1)S(1)}, f32[512,512]{1,0:T(8,128)S(1)}, f32[2,1,512]{2,1,0:T(1,128)S(1)}, f32[128,2304]{1,0:T(8,128)S(1)}, f32[...) conditional(s32[]{:T(128)} %bitcast.57, () %tuple.308, ...), branch_computations={%region_8.9_spmd, %region_9.10_spmd} | conditional | flops 3494379520 | bytes 57549292 | solution.py:989
  136.8 12.0 %attention_forward.1 = (bf16[512,512]{1,0:T(8,128)(2,1)S(1)}, f32[512,512]{1,0:T(8,128)S(1)}, f32[2,1,512]{2,1,0:T(1,128)S(1)}) custom-call(s32[19]{0:T(128)S(1)} %get-tuple-element.532.spans_ref, bf16[512,512]{1,0:T(8,128)(2,1)} %get-tuple-element.533.q_ref, bf16[512,512]{1,0:T(8,128)(2,1)} %get-tuple-element.534.refs_0_, ...), custom_call_target="tpu_custom_call" | custom-call | flops 2281701376 | bytes 7340032 | tf_op jit(solution)/shard_map/cond/branch_1_fun/attention_forward/pallas_call | solution.py:850
  164.7 13.2 %collective-permute-done.46.refs_1_ = bf16[128,2304]{1,0:T(8,128)(2,1)S(1)} collective-permute-done((bf16[128,2304]{1,0:T(8,128)(2,1)S(1)}, bf16[128,2304]{1,0:T(8,128)(2,1)S(1)}, u32[]{:S(2)}, u32[]{:S(2)}) %collective-permute-start.46) | collective-permute-done | bytes 589856 | tf_op jit(solution)/shard_map/cond/branch_1_fun/ppermute | solution.py:59
  190.7 74.3 %conditional.30 = (bf16[1024,2304]{1,0:T(8,128)(2,1)}, bf16[288,2304]{1,0:T(8,128)(2,1)}, bf16[288,2304]{1,0:T(8,128)(2,1)}, bf16[288,1152]{1,0:T(8,128)(2,1)}) conditional(s32[]{:T(128)} %bitcast.57, () %tuple.333, (s32[16]{0:T(128)S(1)}, bf16[128,2304]{1,0:T(8,128)(2,1)S(1)}, bf16[288,2304]{1,0:T(8,128)(2,1)}, bf16[288,2304]{1,0:T(8,128)(2,1)}, ...), branch_computations={%region_10.11_spmd, %region_11.14_spmd} | conditional | flops 2 | bytes 41583208 | solution.py:989
  193.2 12.3 %collective-permute-done.16 = bf16[128,2304]{1,0:T(8,128)(2,1)S(1)} collective-permute-done((bf16[128,2304]{1,0:T(8,128)(2,1)S(1)}, bf16[128,2304]{1,0:T(8,128)(2,1)S(1)}, u32[]{:S(2)}, u32[]{:S(2)}) %collective-permute-start.16) | collective-permute-done | bytes 589856 | tf_op jit(solution)/shard_map/cond/branch_1_fun/ppermute | solution.py:59
  208.8 23.0 %collective-permute-done.19 = bf16[128,2304]{1,0:T(8,128)(2,1)S(1)} collective-permute-done((bf16[128,2304]{1,0:T(8,128)(2,1)S(1)}, bf16[128,2304]{1,0:T(8,128)(2,1)S(1)}, u32[]{:S(2)}, u32[]{:S(2)}) %collective-permute-start.19) | collective-permute-done | bytes 589856 | tf_op jit(solution)/shard_map/cond/branch_1_fun/ppermute | solution.py:60
  234.4 30.7 %conditional = (bf16[1024,2304]{1,0:T(8,128)(2,1)}, bf16[288,2304]{1,0:T(8,128)(2,1)}, bf16[288,2304]{1,0:T(8,128)(2,1)}) conditional(s32[]{:T(128)} %bitcast.7, () %tuple.141, (bf16[128,2304]{1,0:T(8,128)(2,1)S(1)}, bf16[128,2304]{1,0:T(8,128)(2,1)S(1)}, bf16[128,2304]{1,0:T(8,128)(2,1)S(1)}, bf16[128,2304]{1,0:T(8,128)(2,1)S(1)}, ...), branch_computations={%region_12.12_spmd, %region_13.13_spmd} | conditional | bytes 28311816 | solution.py:989
  236.5 13.7 %collective-permute-done.9.refs_6_ = bf16[128,2304]{1,0:T(8,128)(2,1)S(1)} collective-permute-done((bf16[128,2304]{1,0:T(8,128)(2,1)S(1)}, bf16[128,2304]{1,0:T(8,128)(2,1)S(1)}, u32[]{:S(2)}, u32[]{:S(2)}) %collective-permute-start.9) | collective-permute-done | bytes 589856 | tf_op jit(solution)/shard_map/cond/branch_1_fun/cond/branch_1_fun/ppermute | solution.py:59
  265.3 25.7 %conditional.31 = (bf16[1024,1152]{1,0:T(8,128)(2,1)S(1)}, bf16[1024,1152]{1,0:T(8,128)(2,1)}, bf16[1024,1152]{1,0:T(8,128)(2,1)}, bf16[2304,1152]{1,0:T(8,128)(...) conditional(s32[]{:T(128)} %bitcast.57, () %tuple.332, (s32[]{:T(128)}, ...), branch_computations={%region_14.15_spmd, %region_15.16_spmd} | conditional | flops 10871635968 | bytes 29196416 | solution.py:989
  269.5 21.1 %hidden_units.1 = (bf16[1024,1152]{1,0:T(8,128)(2,1)S(1)}, bf16[1024,1152]{1,0:T(8,128)(2,1)}, bf16[1024,1152]{1,0:T(8,128)(2,1)}, bf16[2304,1152]{1,0:T(8,128)(2,1)}, bf16[2304,1152]{1,0:T(8,128)(2,1)}) custom-call(s32[1]{0:T(128)} %bitcast.8.index_ref, bf16[288,1152]{1,0:T(8,128)(2,1)} %get-tuple-element.589.refs_0_, ...), custom_call_target="tpu_custom_call" | custom-call | flops 10871635968 | bytes 21233664 | tf_op jit(solution)/shard_map/cond/branch_1_fun/hidden_units/pallas_call | solution.py:379
  421.3 48.4 %conditional.33 = (bf16[128,2304]{1,0:T(8,128)(2,1)}, bf16[128,2304]{1,0:T(8,128)(2,1)}, bf16[128,2304]{1,0:T(8,128)(2,1)}, bf16[128,2304]{1,0:T(8,128)(2,1)}, b...) conditional(s32[]{:T(128)} %bitcast.57, () %tuple.351, ...), branch_computations={%region_18.19_spmd, %region_19.24_spmd} | conditional | flops 16321314816 | bytes 77562680 | solution.py:989
  421.3 16.1 %two_products.1 = (bf16[128,2304]{1,0:T(8,128)(2,1)}, bf16[128,2304]{1,0:T(8,128)(2,1)}, bf16[128,2304]{1,0:T(8,128)(2,1)}, bf16[128,2304]{1,0:T(8,128)(2,1)}, b...) custom-call(bf16[1024,1152]{1,0:T(8,128)(2,1)S(1)} %get-tuple-elemen, ...), custom_call_target="tpu_custom_call" | custom-call | flops 10871635968 | bytes 20054016 | tf_op jit(solution)/shard_map/cond/branch_1_fun/two_products/pallas_call | solution.py:176
  453.5 12.0 %conditional.2 = (bf16[2,288,1152]{2,1,0:T(8,128)(2,1)}, bf16[2,288,1152]{2,1,0:T(8,128)(2,1)}) conditional(s32[]{:T(128)} %bitcast.14, () %tuple.155, (bf16[2304,1152]{1,0:T(8,128)(2,1)}, s32[]{:T(128)}) %tuple.159), branch_computations={%region_22.22_spmd, %region_23.23_spmd} | conditional | flops 5308464 | bytes 29196844 | solution.py:989
  473.6 46.8 %conditional.34 = (f32[128,2304]{1,0:T(8,128)}, bf16[128,2304]{1,0:T(8,128)(2,1)}, f32[1,2304]{1,0:T(1,128)S(1)}, f32[1,2304]{1,0:T(1,128)}, bf16[2,288,1152]{2,...) conditional(s32[]{:T(128)} %bitcast.57, () %tuple.350, ...), branch_computations={%region_24.25_spmd, %region_25.32_spmd} | conditional | flops 5451300864 | bytes 100934936 | solution.py:989
  475.0 37.4 %conditional.5 = (bf16[128,2304]{1,0:T(8,128)(2,1)}, bf16[128,2304]{1,0:T(8,128)(2,1)}, bf16[128,2304]{1,0:T(8,128)(2,1)}, bf16[2,288,1152]{2,1,0:T(8,128)(2,1)}...) conditional(s32[]{:T(128)} %bitcast.24, () %tuple.177, ...), branch_computations={%region_26.26_spmd, %region_27.31_spmd} | conditional | flops 5451300864 | bytes 85525536 | solution.py:989
  499.2 12.9 %conditional.4 = (bf16[2,288,1152]{2,1,0:T(8,128)(2,1)}, bf16[2,288,1152]{2,1,0:T(8,128)(2,1)}, bf16[288,1152]{1,0:T(8,128)(2,1)}, bf16[288,1152]{1,0:T(8,128)(2,1)}) conditional(s32[]{:T(128)} %bitcast.23, () %tuple.168, (bf16[2304,1152]{1,0:T(8,128)(2,1)}, s32[]{:T(128)}, bf16[2,2,2,288,1152]{4,3,2,1,0:T(8,128)(2,1)}, ...), branch_computations={%region_30.29_spmd, %region_31.30_spmd} | conditional | flops 9289785 | bytes 58393300 | solution.py:989
  526.8 52.4 %conditional.35 = (bf16[512,2304]{1,0:T(8,128)(2,1)S(1)}, bf16[512,512]{1,0:T(8,128)(2,1)}, bf16[2,512,512]{2,1,0:T(8,128)(2,1)S(1)}, bf16[2,512,512]{2,1,0:T(8,128)(2,1)}) conditional(s32[]{:T(128)} %bitcast.57, () %tuple.349, (bf16[128,2304]{1,0:T(8,128)(2,1)}, bf16[2304,512]{1,0:T(8,128)(2,1)}, s32[19]{0:T(128)S(1)}, ...), branch_computations={%region_32.33_spmd, %region_33.34_spmd} | conditional | flops 6916669440 | bytes 70648128 | solution.py:989
  528.4 13.2 %collective-permute-done.53.refs_2_ = bf16[128,2304]{1,0:T(8,128)(2,1)S(1)} collective-permute-done((bf16[128,2304]{1,0:T(8,128)(2,1)}, bf16[128,2304]{1,0:T(8,128)(2,1)S(1)}, u32[]{:S(2)}, u32[]{:S(2)}) %collective-permute-start.53) | collective-permute-done | bytes 589856 | tf_op jit(solution)/shard_map/cond/branch_1_fun/ppermute | solution.py:59
  555.1 17.1 %attention_backward.1 = (bf16[512,512]{1,0:T(8,128)(2,1)}, bf16[2048,512]{1,0:T(8,128)(2,1)S(1)}, bf16[2048,512]{1,0:T(8,128)(2,1)S(1)}) custom-call(s32[19]{0:T(128)S(1)} %get-tuple-element.720.spans_ref, bf16[512,512]{1,0:T(8,128)(2,1)} %get-tuple-element.721.q_ref, bf16[512,512]{1,0:T(8,128)(2,1)S(1)} %convolution_convert_fusion.3.g_ref, ...), custom_call_target="tpu_custom_call" | custom-call | flops 5704253440 | bytes 12582912 | tf_op jit(solution)/shard_map/cond/branch_1_fun/attention_backward/pallas_call | solution.py:895
  581.5 14.9 %conditional.36 = (bf16[288,1024]{1,0:T(8,128)(2,1)}, bf16[288,1024]{1,0:T(8,128)(2,1)}, bf16[288,1024]{1,0:T(8,128)(2,1)}, bf16[288,1024]{1,0:T(8,128)(2,1)}, b...) conditional(s32[]{:T(128)} %bitcast.57, () %tuple.376, (bf16[512,2304]{1,0:T(8,128)(2,1)}, ...), branch_computations={%region_34.35_spmd, %region_35.36_spmd} | conditional | flops 2423955456 | bytes 79774520 | solution.py:989
  614.2 19.7 %collective-permute-done.107 = bf16[512,512]{1,0:T(8,128)(2,1)S(1)} collective-permute-done((bf16[512,512]{1,0:T(8,128)(2,1)S(1)}, bf16[512,512]{1,0:T(8,128)(2,1)S(1)}, u32[]{:S(2)}, u32[]{:S(2)}) %collective-permute-start.107) | collective-permute-done | bytes 524320 | tf_op jit(solution)/shard_map/ppermute | solution.py:60
  637.4 55.5 %conditional.38 = (f32[128,2304]{1,0:T(8,128)}, bf16[304,512]{1,0:T(8,128)(2,1)}, bf16[304,512]{1,0:T(8,128)(2,1)}, bf16[288,512]{1,0:T(8,128)(2,1)}, bf16[288,512]{1,0:T(8,128)(2,1)}) conditional(s32[]{:T(128)} %bitcast.57, () %tuple.348, (s32[16]{0:T(128)S(1)}, bf16[512,512]{1,0:T(8,128)(2,1)S(1)}, bf16[512,512]{1,0:T(8,128)(2,1)S(1)}, ...), branch_computations={%region_38.39_spmd, %region_39.46_spmd} | conditional | flops 3637350400 | bytes 64722316 | solution.py:989
  638.3 28.3 %conditional.7 = (bf16[128,2304]{1,0:T(8,128)(2,1)}, bf16[128,2304]{1,0:T(8,128)(2,1)}, bf16[128,2304]{1,0:T(8,128)(2,1)}, bf16[2,304,512]{2,1,0:T(8,128)(2,1)}, bf16[2,304,512]{2,1,0:T(8,128)(2,1)}) conditional(s32[]{:T(128)} %bitcast.47, () %tuple.198, (bf16[512,512]{1,0:T(8,128)(2,1)S(1)}, bf16[512,512]{1,0:T(8,128)(2,1)S(1)}, ...), branch_computations={%region_40.40_spmd, %region_41.43_spmd} | conditional | flops 3634925568 | bytes 40759916 | solution.py:989
  649.8 12.8 %conditional.6 = (bf16[2,304,512]{2,1,0:T(8,128)(2,1)}, bf16[2,304,512]{2,1,0:T(8,128)(2,1)}) conditional(s32[]{:T(128)} %bitcast.46, () %tuple.192, (bf16[512,2304]{1,0:T(8,128)(2,1)}, bf16[512,512]{1,0:T(8,128)(2,1)}, f32[1,2304]{1,0:T(1,128)S(1)}, f32[1,2304]{1,0:T(1,128)}, f32[1,2304]{1,0:T(1,128)S(1)}, /*index=5*/f32[1,2304]{1,0:T(1,128)S(1)}, ...), branch_computations={%region_42.41_spmd, %region_43.42_spmd} | conditional | flops 1215467520 | bytes 21819788 | solution.py:989
  671.5 19.2 %conditional.8 = (f32[128,2304]{1,0:T(8,128)}) conditional(s32[]{:T(128)} %bitcast.47, () %tuple.197, (bf16[128,2304]{1,0:T(8,128)(2,1)}, bf16[128,2304]{1,0:T(8,128)(2,1)}, bf16[128,2304]{1,0:T(8,128)(2,1)}, bf16[128,2304]{1,0:T(8,128)(2,1)}, f32[128,2304]{1,0:T(8,128)}, /*index=5*/f32[4,2304]{1,0:T(4,128)}) %tuple.204), branch_computations={%region_44.44_spmd, %region_45.45_spmd} | conditional | bytes 11870296 | solution.py:989
  674.2 12.3 %collective-permute-done.23.refs_1_ = bf16[128,2304]{1,0:T(8,128)(2,1)S(1)} collective-permute-done((bf16[128,2304]{1,0:T(8,128)(2,1)}, bf16[128,2304]{1,0:T(8,128)(2,1)S(1)}, u32[]{:S(2)}, u32[]{:S(2)}) %collective-permute-start.23) | collective-permute-done | bytes 589856 | tf_op jit(solution)/shard_map/cond/branch_1_fun/cond/branch_1_fun/ppermute | solution.py:59
  700.4 12.2 %collective-permute-done.110 = bf16[304,512]{1,0:T(8,128)(2,1)} collective-permute-done((bf16[304,512]{1,0:T(8,128)(2,1)}, bf16[304,512]{1,0:T(8,128)(2,1)}, u32[]{:S(2)}, u32[]{:S(2)}) %collective-permute-start.110) | collective-permute-done | bytes 311328 | tf_op jit(solution)/shard_map/ppermute | solution.py:60
  717.3 19.7 %conditional.40 = (f32[288,1024]{1,0:T(8,128)}, f32[288,1024]{1,0:T(8,128)}, f32[4,288]{1,0:T(4,128)S(1)}, f32[512,288]{0,1:T(8,128)}, bf16[288,512]{1,0:T(8,128)(2,1)S(1)}) conditional(s32[]{:T(128)} %bitcast.57, () %tuple.389, (s32[]{:T(128)}, bf16[304,512]{1,0:T(8,128)(2,1)S(1)}, bf16[288,1024]{1,0:T(8,128)(2,1)}, bf16[288,1024]{1,0:T(8,128)(2,1)}, ...), branch_computations={%region_48.49_spmd, %region_49.50_spmd} | conditional | flops 1622016 | bytes 14001464 | solution.py:989
  (519 shorter events, 572.6 us)
Async XLA Ops:
  0.7 24.0 %collective-permute-start.63 = (bf16[128,2304]{1,0:T(8,128)(2,1)}, bf16[128,2304]{1,0:T(8,128)(2,1)}, u32[]{:S(2)}, u32[]{:S(2)}) collective-permute-start(bf16[128,2304]{1,0:T(8,128)(2,1)} %param.62), channel_id=1, source_target_pairs={{0,1},{1,0},{2,3},{3,2},{4,5},{5,4},{6,7},{7,6},{8,9},{9,8},{10,11... | collective-permute-start | bytes 1769480 | tf_op jit(solution)/shard_map/ppermute | solution.py:59
  3.7 21.0 %collective-permute-start.64 = (bf16[128,2304]{1,0:T(8,128)(2,1)}, bf16[128,2304]{1,0:T(8,128)(2,1)}, u32[]{:S(2)}, u32[]{:S(2)}) collective-permute-start(bf16[128,2304]{1,0:T(8,128)(2,1)} %param.62), channel_id=1, source_target_pairs={{0,2},{1,3},{2,0},{3,1},{4,6},{5,7},{6,4},{7,5},{8,10},{9,11},{10,... | collective-permute-start | bytes 1769480 | tf_op jit(solution)/shard_map/ppermute | solution.py:59
  36.2 22.7 %collective-permute-start.70 = (bf16[288,1024]{1,0:T(8,128)(2,1)}, bf16[288,1024]{1,0:T(8,128)(2,1)}, u32[]{:S(2)}, u32[]{:S(2)}) collective-permute-start(bf16[288,1024]{1,0:T(8,128)(2,1)} %copy.44), channel_id=1, source_target_pairs={{0,8},{4,12},{8,0},{12,4},{16,24},{20,28},{24,16},{28,20},{1,9},{5... | collective-permute-start | bytes 1769480 | tf_op jit(solution)/shard_map/ppermute | solution.py:60
  37.7 26.2 %collective-permute-start.71 = (bf16[288,1024]{1,0:T(8,128)(2,1)}, bf16[288,1024]{1,0:T(8,128)(2,1)}, u32[]{:S(2)}, u32[]{:S(2)}) collective-permute-start(bf16[288,1024]{1,0:T(8,128)(2,1)} %copy.44), channel_id=1, source_target_pairs={{0,16},{4,20},{8,24},{12,28},{16,0},{20,4},{24,8},{28,12},{1,17},{... | collective-permute-start | bytes 1769480 | tf_op jit(solution)/shard_map/ppermute | solution.py:60
  63.9 35.0 %collective-permute-start.74 = (bf16[288,1024]{1,0:T(8,128)(2,1)}, bf16[288,1024]{1,0:T(8,128)(2,1)S(1)}, u32[]{:S(2)}, u32[]{:S(2)}) collective-permute-start(bf16[288,1024]{1,0:T(8,128)(2,1)} %collective-permute-done.71), channel_id=1, source_target_pairs={{0,8},{4,12},{8,0},{12,4},{16,24},{20,28},{24,16},{28,20},{1,9},{5... | collective-permute-start | bytes 1769480 | tf_op jit(solution)/shard_map/ppermute | solution.py:60
  63.9 25.3 %collective-permute-start.72 = (bf16[512,512]{1,0:T(8,128)(2,1)}, bf16[512,512]{1,0:T(8,128)(2,1)S(1)}, u32[]{:S(2)}, u32[]{:S(2)}) collective-permute-start(bf16[512,512]{1,0:T(8,128)(2,1)} %get-tuple-element.1180), channel_id=1, source_target_pairs={{0,16},{4,20},{8,24},{12,28},{16,0},{20,4},{24,8},{28,12},{1,17},{... | collective-permute-start | bytes 1572872 | tf_op jit(solution)/shard_map/ppermute | solution.py:60
  64.0 34.9 %collective-permute-start.73 = (bf16[512,512]{1,0:T(8,128)(2,1)}, bf16[512,512]{1,0:T(8,128)(2,1)}, u32[]{:S(2)}, u32[]{:S(2)}) collective-permute-start(bf16[512,512]{1,0:T(8,128)(2,1)} %get-tuple-element.1180), channel_id=1, source_target_pairs={{0,8},{4,12},{8,0},{12,4},{16,24},{20,28},{24,16},{28,20},{1,9},{5... | collective-permute-start | bytes 1572872 | tf_op jit(solution)/shard_map/ppermute | solution.py:60
  98.9 31.2 %collective-permute-start.75 = (bf16[288,1152]{1,0:T(8,128)(2,1)}, bf16[288,1152]{1,0:T(8,128)(2,1)}, u32[]{:S(2)}, u32[]{:S(2)}) collective-permute-start(bf16[288,1152]{1,0:T(8,128)(2,1)} %get-tuple-element.1219), channel_id=1, source_target_pairs={{0,16},{4,20},{8,24},{12,28},{16,0},{20,4},{24,8},{28,12},{1,17},{... | collective-permute-start | bytes 1990664 | tf_op jit(solution)/shard_map/ppermute | solution.py:60
  101.2 23.8 %collective-permute-start.7 = (bf16[512,512]{1,0:T(8,128)(2,1)S(1)}, bf16[512,512]{1,0:T(8,128)(2,1)}, u32[]{:S(2)}, u32[]{:S(2)}) collective-permute-start(bf16[512,512]{1,0:T(8,128)(2,1)S(1)} %get-tuple-element.517), channel_id=1, source_target_pairs={{0,8},{4,12},{8,0},{12,4},{16,24},{20,28},{24,16},{28,20},{1,9},{5... | collective-permute-start | bytes 1572872 | tf_op jit(solution)/shard_map/cond/branch_1_fun/ppermute | solution.py:60
  103.3 21.7 %collective-permute-start.6 = (bf16[512,512]{1,0:T(8,128)(2,1)S(1)}, bf16[512,512]{1,0:T(8,128)(2,1)}, u32[]{:S(2)}, u32[]{:S(2)}) collective-permute-start(bf16[512,512]{1,0:T(8,128)(2,1)S(1)} %get-tuple-element.517), channel_id=1, source_target_pairs={{0,4},{4,0},{8,12},{12,8},{16,20},{20,16},{24,28},{28,24},{1,5},{5... | collective-permute-start | bytes 1572872 | tf_op jit(solution)/shard_map/cond/branch_1_fun/ppermute | solution.py:60
  130.1 60.0 %collective-permute-start.76 = (bf16[288,2304]{1,0:T(8,128)(2,1)}, bf16[288,2304]{1,0:T(8,128)(2,1)}, u32[]{:S(2)}, u32[]{:S(2)}) collective-permute-start(bf16[288,2304]{1,0:T(8,128)(2,1)} %get-tuple-element.1236.refs_0_), channel_id=1, source_target_pairs={{0,16},{4,20},{8,24},{12,28},{16,0},{20,4},{24,8},{28,12},{1,17},{... | collective-permute-start | bytes 3981320 | tf_op jit(solution)/shard_map/ppermute | solution.py:60
  130.1 60.0 %collective-permute-start.77 = (bf16[288,2304]{1,0:T(8,128)(2,1)}, bf16[288,2304]{1,0:T(8,128)(2,1)}, u32[]{:S(2)}, u32[]{:S(2)}) collective-permute-start(bf16[288,2304]{1,0:T(8,128)(2,1)} %get-tuple-element.1235), channel_id=1, source_target_pairs={{0,8},{4,12},{8,0},{12,4},{16,24},{20,28},{24,16},{28,20},{1,9},{5... | collective-permute-start | bytes 3981320 | tf_op jit(solution)/shard_map/ppermute | solution.py:60
  190.1 75.0 %collective-permute-start.78 = (bf16[288,2304]{1,0:T(8,128)(2,1)}, bf16[288,2304]{1,0:T(8,128)(2,1)}, u32[]{:S(2)}, u32[]{:S(2)}) collective-permute-start(bf16[288,2304]{1,0:T(8,128)(2,1)} %collective-permute-done.77), channel_id=1, source_target_pairs={{0,16},{4,20},{8,24},{12,28},{16,0},{20,4},{24,8},{28,12},{1,17},{... | collective-permute-start | bytes 3981320 | tf_op jit(solution)/shard_map/ppermute | solution.py:60
  192.8 39.1 %collective-permute-start.19 = (bf16[128,2304]{1,0:T(8,128)(2,1)S(1)}, bf16[128,2304]{1,0:T(8,128)(2,1)S(1)}, u32[]{:S(2)}, u32[]{:S(2)}) collective-permute-start(bf16[128,2304]{1,0:T(8,128)(2,1)S(1)} %get-tuple-element.576), channel_id=1, source_target_pairs={{0,8},{4,12},{8,0},{12,4},{16,24},{20,28},{24,16},{28,20},{1,9},{5... | collective-permute-start | bytes 1769480 | tf_op jit(solution)/shard_map/cond/branch_1_fun/ppermute | solution.py:60
  205.7 26.2 %collective-permute-start.17 = (bf16[64,2304]{1,0:T(8,128)(2,1)S(1)}, bf16[64,2304]{1,0:T(8,128)(2,1)S(1)}, u32[]{:S(2)}, u32[]{:S(2)}) collective-permute-start(bf16[64,2304]{1,0:T(8,128)(2,1)S(1)} %slice.281), channel_id=1, source_target_pairs={{0,1},{1,0},{2,3},{3,2},{4,5},{5,4},{6,7},{7,6},{8,9},{9,8},{10,11... | collective-permute-start | bytes 884744 | tf_op jit(solution)/shard_map/cond/branch_1_fun/ppermute | solution.py:59
  207.2 24.6 %collective-permute-start.18 = (bf16[64,2304]{1,0:T(8,128)(2,1)S(1)}, bf16[64,2304]{1,0:T(8,128)(2,1)S(1)}, u32[]{:S(2)}, u32[]{:S(2)}) collective-permute-start(bf16[64,2304]{1,0:T(8,128)(2,1)S(1)} %slice.282), channel_id=1, source_target_pairs={{0,2},{1,3},{2,0},{3,1},{4,6},{5,7},{6,4},{7,5},{8,10},{9,11},{10,... | collective-permute-start | bytes 884744 | tf_op jit(solution)/shard_map/cond/branch_1_fun/ppermute | solution.py:59
  231.8 33.2 %collective-permute-start.20 = (bf16[288,1152]{1,0:T(8,128)(2,1)}, bf16[288,1152]{1,0:T(8,128)(2,1)}, u32[]{:S(2)}, u32[]{:S(2)}) collective-permute-start(bf16[288,1152]{1,0:T(8,128)(2,1)} %get-tuple-element.587), channel_id=1, source_target_pairs={{0,8},{4,12},{8,0},{12,4},{16,24},{20,28},{24,16},{28,20},{1,9},{5... | collective-permute-start | bytes 1990664 | tf_op jit(solution)/shard_map/cond/branch_1_fun/ppermute | solution.py:60
  265.0 31.1 %collective-permute-start.79 = (bf16[288,1152]{1,0:T(8,128)(2,1)}, bf16[288,1152]{1,0:T(8,128)(2,1)S(1)}, u32[]{:S(2)}, u32[]{:S(2)}) collective-permute-start(bf16[288,1152]{1,0:T(8,128)(2,1)} %get-tuple-element.1268.refs_2_), channel_id=1, source_target_pairs={{0,16},{4,20},{8,24},{12,28},{16,0},{20,4},{24,8},{28,12},{1,17},{... | collective-permute-start | bytes 1990664 | tf_op jit(solution)/shard_map/ppermute | solution.py:60
  265.3 25.3 %collective-permute-start.22 = (bf16[288,1152]{1,0:T(8,128)(2,1)}, bf16[288,1152]{1,0:T(8,128)(2,1)}, u32[]{:S(2)}, u32[]{:S(2)}) collective-permute-start(bf16[288,1152]{1,0:T(8,128)(2,1)} %get-tuple-element.606), channel_id=1, source_target_pairs={{0,4},{4,0},{8,12},{12,8},{16,20},{20,16},{24,28},{28,24},{1,5},{5... | collective-permute-start | bytes 1990664 | tf_op jit(solution)/shard_map/cond/branch_1_fun/ppermute | solution.py:60
  408.1 61.6 %collective-permute-start.101 = (bf16[2,288,1152]{2,1,0:T(8,128)(2,1)}, bf16[2,288,1152]{2,1,0:T(8,128)(2,1)}, u32[]{:S(2)}, u32[]{:S(2)}) collective-permute-start(bf16[2,288,1152]{2,1,0:T(8,128)(2,1)} %fusion.10), channel_id=1, source_target_pairs={{0,16},{4,20},{8,24},{12,28},{16,0},{20,4},{24,8},{28,12},{1,17},{... | collective-permute-start | bytes 3981320 | tf_op jit(solution)/shard_map/ppermute | solution.py:60
  472.4 48.1 %collective-permute-start.102 = (bf16[288,1152]{1,0:T(8,128)(2,1)}, bf16[288,1152]{1,0:T(8,128)(2,1)}, u32[]{:S(2)}, u32[]{:S(2)}) collective-permute-start(bf16[288,1152]{1,0:T(8,128)(2,1)} %get-tuple-element.1340), channel_id=1, source_target_pairs={{0,16},{4,20},{8,24},{12,28},{16,0},{20,4},{24,8},{28,12},{1,17},{... | collective-permute-start | bytes 1990664 | tf_op jit(solution)/shard_map/ppermute | solution.py:60
  473.6 38.7 %collective-permute-start.62 = (bf16[128,2304]{1,0:T(8,128)(2,1)}, bf16[128,2304]{1,0:T(8,128)(2,1)S(1)}, u32[]{:S(2)}, u32[]{:S(2)}) collective-permute-start(bf16[128,2304]{1,0:T(8,128)(2,1)} %get-tuple-element.700), channel_id=1, source_target_pairs={{0,8},{4,12},{8,0},{12,4},{16,24},{20,28},{24,16},{28,20},{1,9},{5... | collective-permute-start | bytes 1769480 | tf_op jit(solution)/shard_map/cond/branch_1_fun/ppermute | solution.py:60
  520.5 58.7 %collective-permute-start.103 = (bf16[288,1152]{1,0:T(8,128)(2,1)}, bf16[288,1152]{1,0:T(8,128)(2,1)}, u32[]{:S(2)}, u32[]{:S(2)}) collective-permute-start(bf16[288,1152]{1,0:T(8,128)(2,1)} %get-tuple-element.1353), channel_id=1, source_target_pairs={{0,16},{4,20},{8,24},{12,28},{16,0},{20,4},{24,8},{28,12},{1,17},{... | collective-permute-start | bytes 1990664 | tf_op jit(solution)/shard_map/ppermute | solution.py:60
  524.2 57.3 %collective-permute-start.104 = (bf16[288,1152]{1,0:T(8,128)(2,1)}, bf16[288,1152]{1,0:T(8,128)(2,1)}, u32[]{:S(2)}, u32[]{:S(2)}) collective-permute-start(bf16[288,1152]{1,0:T(8,128)(2,1)} %get-tuple-element.1354), channel_id=1, source_target_pairs={{0,16},{4,20},{8,24},{12,28},{16,0},{20,4},{24,8},{28,12},{1,17},{... | collective-permute-start | bytes 1990664 | tf_op jit(solution)/shard_map/ppermute | solution.py:60
  526.0 55.4 %collective-permute-start.105 = (bf16[288,1152]{1,0:T(8,128)(2,1)}, bf16[288,1152]{1,0:T(8,128)(2,1)}, u32[]{:S(2)}, u32[]{:S(2)}) collective-permute-start(bf16[288,1152]{1,0:T(8,128)(2,1)} %get-tuple-element.1355), channel_id=1, source_target_pairs={{0,8},{4,12},{8,0},{12,4},{16,24},{20,28},{24,16},{28,20},{1,9},{5... | collective-permute-start | bytes 1990664 | tf_op jit(solution)/shard_map/ppermute | solution.py:60
  581.4 25.2 %collective-permute-start.106 = (bf16[2,512,512]{2,1,0:T(8,128)(2,1)}, bf16[2,512,512]{2,1,0:T(8,128)(2,1)}, u32[]{:S(2)}, u32[]{:S(2)}) collective-permute-start(bf16[2,512,512]{2,1,0:T(8,128)(2,1)} %get-tuple-element.1371), channel_id=1, source_target_pairs={{0,8},{4,12},{8,0},{12,4},{16,24},{20,28},{24,16},{28,20},{1,9},{5... | collective-permute-start | bytes 3145736 | tf_op jit(solution)/shard_map/ppermute | solution.py:60
  608.5 27.3 %collective-permute-start.108 = (bf16[288,1152]{1,0:T(8,128)(2,1)}, bf16[288,1152]{1,0:T(8,128)(2,1)S(1)}, u32[]{:S(2)}, u32[]{:S(2)}) collective-permute-start(bf16[288,1152]{1,0:T(8,128)(2,1)} %get-tuple-element.1376), channel_id=1, source_target_pairs={{0,8},{4,12},{8,0},{12,4},{16,24},{20,28},{24,16},{28,20},{1,9},{5... | collective-permute-start | bytes 1990664 | tf_op jit(solution)/shard_map/ppermute | solution.py:60
  608.9 25.0 %collective-permute-start.107 = (bf16[512,512]{1,0:T(8,128)(2,1)S(1)}, bf16[512,512]{1,0:T(8,128)(2,1)S(1)}, u32[]{:S(2)}, u32[]{:S(2)}) collective-permute-start(bf16[512,512]{1,0:T(8,128)(2,1)S(1)} %get-tuple-element.1559), channel_id=1, source_target_pairs={{0,16},{4,20},{8,24},{12,28},{16,0},{20,4},{24,8},{28,12},{1,17},{... | collective-permute-start | bytes 1572872 | tf_op jit(solution)/shard_map/ppermute | solution.py:60
  635.9 57.0 %collective-permute-start.109 = (bf16[288,1152]{1,0:T(8,128)(2,1)}, bf16[288,1152]{1,0:T(8,128)(2,1)}, u32[]{:S(2)}, u32[]{:S(2)}) collective-permute-start(bf16[288,1152]{1,0:T(8,128)(2,1)} %get-tuple-element.1395), channel_id=1, source_target_pairs={{0,16},{4,20},{8,24},{12,28},{16,0},{20,4},{24,8},{28,12},{1,17},{... | collective-permute-start | bytes 1990664 | tf_op jit(solution)/shard_map/ppermute | solution.py:60
  637.4 29.3 %collective-permute-start.38 = (bf16[288,1024]{1,0:T(8,128)(2,1)}, bf16[288,1024]{1,0:T(8,128)(2,1)}, u32[]{:S(2)}, u32[]{:S(2)}) collective-permute-start(bf16[288,1024]{1,0:T(8,128)(2,1)} %get-tuple-element.825), channel_id=1, source_target_pairs={{0,8},{4,12},{8,0},{12,4},{16,24},{20,28},{24,16},{28,20},{1,9},{5... | collective-permute-start | bytes 1769480 | tf_op jit(solution)/shard_map/cond/branch_1_fun/ppermute | solution.py:60
  666.6 24.1 %collective-permute-start.39 = (bf16[2,304,512]{2,1,0:T(8,128)(2,1)}, bf16[2,304,512]{2,1,0:T(8,128)(2,1)S(1)}, u32[]{:S(2)}, u32[]{:S(2)}) collective-permute-start(bf16[2,304,512]{2,1,0:T(8,128)(2,1)} %get-tuple-element.829), channel_id=1, source_target_pairs={{0,8},{4,12},{8,0},{12,4},{16,24},{20,28},{24,16},{28,20},{1,9},{5... | collective-permute-start | bytes 1867784 | tf_op jit(solution)/shard_map/cond/branch_1_fun/ppermute | solution.py:60
  714.8 22.1 %collective-permute-start.113 = (bf16[288,1152]{1,0:T(8,128)(2,1)S(1)}, bf16[288,1152]{1,0:T(8,128)(2,1)S(1)}, u32[]{:S(2)}, u32[]{:S(2)}) collective-permute-start(bf16[288,1152]{1,0:T(8,128)(2,1)S(1)} %get-tuple-element.1427), channel_id=1, source_target_pairs={{0,8},{4,12},{8,0},{12,4},{16,24},{20,28},{24,16},{28,20},{1,9},{5... | collective-permute-start | bytes 1990664 | tf_op jit(solution)/shard_map/ppermute | solution.py:60
  (151 other events, 1619.3 us)
